TPU v7x, 32 devices: a whole 2x2x4 slice. The times are simulated.
32 devices in a mesh: group: 2 (over y), dp: 4 (over z), tensor: 2 (over x), seq: 2 (over core).
Axes of the slice: x: 2, y: 2, z: 4, core: 2. Of those that a mesh axis runs over, the one named last changes fastest.
Arguments:
- queries: bfloat16 [8, 1024, 4096], P(('group', 'dp'), 'seq', 'tensor'), parts along dimension 0, may hold values from -6 to 6
- keys: bfloat16 [8, 1024, 2048], P(('group', 'dp'), 'seq', 'tensor'), parts along dimension 0, may hold values from -6 to 6
- out_grad: bfloat16 [8, 1024, 4096], P(('group', 'dp'), 'seq', 'tensor'), parts along dimension 0, may hold values from -1.2 to 1.2
- value_weight: bfloat16 [4608, 2048], P('dp', 'tensor'), may hold values from -0.09375 to 0.09375
- tenant_of: int32 [8], P('group'), parts along dimension 0, may hold values from 0 to 3
- owner_of: int32 [8], P('group'), parts along dimension 0, may hold values from 0 to 3, each once
- counts: int32 [8], P('group'), parts along dimension 0, may hold values from 1 to 16
- noise: float32 [8, 64, 4608], P(('group', 'dp'), 'seq'), parts along dimension 0, may hold values from -6 to 6
Outputs:
- tenant_update: float32 [8, 64, 4608], P(('group', 'dp'), 'seq'), parts along dimension 0
There are 2 independent parts, one for each index of `group`. A program takes and returns all parts, laid end to end along the dimension named above; an argument that names none is the same for every part. Nothing has to cross between parts.
All inputs are finite; a program needn't handle non-finite values.
Results may differ from a plain program's by a relative error of at most 0.0035.
Values may be sent and summed in bfloat16 or wider, within the bound.
No kernel may reach another device: no remote copies, remote signals or barrier semaphores. Data moves between devices by JAX's collectives and lax.ppermute only.
A program may use at most 64 MiB of HBM per device.

v0:
```python
import math

import jax
import jax.numpy as jnp
from jax import lax
from jax.sharding import PartitionSpec as P

D = 4608
HEAD_DIM = 128
PROMPT = 64


softcap = 50.0
query_scale = 144.0 ** (-0.5)


def broadcast(shard, axis, root):
    mine = lax.axis_index(axis) == root
    return lax.psum(jnp.where(mine, shard, jnp.zeros_like(shard)), axis)


def capped(raw):
    return softcap * jnp.tanh(raw * query_scale / softcap)


def body(queries, keys, out_grad, value_weight, tenant_of, owner_of, counts, noise):
    rows = queries.shape[1]
    kv_local = keys.shape[2] // HEAD_DIM
    group_size = queries.shape[2] // keys.shape[2]
    seq_index = lax.axis_index("seq")
    query_pos = seq_index * rows + jnp.arange(rows)
    query_heads = jnp.transpose(
        queries[0].reshape(rows, kv_local, group_size, HEAD_DIM), (1, 2, 0, 3)
    )
    piece = lax.all_gather(keys, "seq", axis=1, tiled=True)
    count_keys = piece.shape[1]
    key_heads = jnp.transpose(piece[0].reshape(count_keys, kv_local, HEAD_DIM), (1, 0, 2))
    key_pos = jnp.arange(count_keys)
    causal = key_pos[None, :] <= query_pos[:, None]

    def per_head(pair):
        query_head, key_head = pair
        raw = jnp.einsum("gqc,kc->gqk", query_head, key_head, preferred_element_type=jnp.float32)
        return jnp.sum(jnp.where(causal[None], jnp.exp(capped(raw)), 0.0), axis=-1)

    totals = lax.map(per_head, (query_heads, key_heads))
    prompt_rows = broadcast(keys[:, :PROMPT], "seq", 0)
    prompt_heads = prompt_rows[0].reshape(PROMPT, kv_local, HEAD_DIM)
    raw_prompt = jnp.einsum(
        "hgqc,phc->hgpq", query_heads, prompt_heads, preferred_element_type=jnp.float32
    )
    prompt_mask = jnp.arange(PROMPT)[:, None] <= query_pos[None, :]
    prob = (
        jnp.where(prompt_mask[None, None], jnp.exp(capped(raw_prompt)), 0.0) / totals[:, :, None, :]
    ).astype(jnp.bfloat16)
    grad_heads = out_grad[0].reshape(rows, kv_local, group_size, HEAD_DIM)
    partial_values = jnp.einsum(
        "hgpq,qhgc->phc", prob, grad_heads, preferred_element_type=jnp.float32
    )
    partial_values = partial_values.reshape(PROMPT, kv_local * HEAD_DIM)
    value_grad = lax.psum_scatter(partial_values, "seq", scatter_dimension=0, tiled=True).astype(
        jnp.bfloat16
    )
    slots = jnp.arange(owner_of.shape[0])
    my_owner = lax.axis_index("dp")
    owner_hit = owner_of == my_owner
    my_tenant = jnp.sum(jnp.where(owner_hit, slots, 0))
    my_count = jnp.sum(jnp.where(owner_hit, counts, 0)).astype(jnp.float32)
    partial_grad = lax.dot_general(
        value_grad,
        lax.all_gather(value_weight, "dp", axis=0, tiled=True),
        (((1,), (1,)), ((), ())),
        preferred_element_type=jnp.float32,
    )
    grad_share = lax.psum_scatter(partial_grad, "tensor", scatter_dimension=1, tiled=True)
    norm_sq = lax.psum(jnp.sum(grad_share * grad_share), ("tensor", "seq"))
    clipped = grad_share / jnp.maximum(1.0, jnp.sqrt(norm_sq))
    picked = (tenant_of == my_tenant).astype(jnp.float32)
    tenant_share = jnp.einsum(
        "e,erc->rc",
        picked,
        lax.all_gather(clipped[None], "dp", axis=0, tiled=True),
        precision=lax.Precision.HIGHEST,
    )
    tenant_sum = lax.all_gather(tenant_share, "tensor", axis=1, tiled=True)
    result = (math.sqrt(PROMPT * D) * tenant_sum + noise[0]) / my_count
    return result[None]


def solution(mesh):
    return jax.shard_map(
        body,
        mesh=mesh,
        in_specs=(
            P(("group", "dp"), "seq", "tensor"),
            P(("group", "dp"), "seq", "tensor"),
            P(("group", "dp"), "seq", "tensor"),
            P("dp", "tensor"),
            P("group"),
            P("group"),
            P("group"),
            P(("group", "dp"), "seq", None),
        ),
        out_specs=P(("group", "dp"), "seq", None),
        check_vma=False,
    )
```

profile of v0, /device:TPU:0, one launch (start us, length us, event | category | flops | bytes accessed | tf_op | source)
XLA Modules:
  0.0 305.1 jit_solution(71468805677093493)
XLA Ops:
  7.4 2.4 copy.11
  11.6 2.5 copy.10
  14.2 4.6 %reshape_squeeze.15 = bf16[512,8,2,128]{3,2,1,0:T(2,128)(2,1)} reshape(bf16[1,512,2048]{2,1,0:T(8,128)(2,1)} %param.12) | data formatting | bytes 4194304 | tf_op jit(solution)/shard_map/reshape;squeeze | solution.py:56
  18.7 4.5 %all-gather.5.cloned.1.call-done = bf16[1,1024,1024]{1,2,0:T(8,128)(2,1)} async-done(((bf16[1,512,1024]{1,2,0:T(8,128)(2,1)}), bf16[1,1024,1024]{1,2,0:T(8,128)(2,1)}) %all-gather.5.cloned.1.call-update) | async-done | bytes 2097168 | tf_op jit(solution)/shard_map/all_gather | solution.py:35
  23.3 24.2 %while.13 = (s32[]{:T(128)}, f32[8,2,512]{2,1,0:T(2,128)S(1)}, bf16[8,2,512,128]{2,3,1,0:T(8,128)(2,1)S(1)}, bf16[8,1024,128]{1,2,0:T(8,128)(2,1)}, s32[512]{0:T(512)S(1)}, /*index=5*/s32[]{:T(128)}) while((s32[]{:T(128)}, f32[8,2,512]{2,1,0:T(2,128)S(1)}, bf16[8,2,512,128]{2,3,1,0:T(8,128)(2,1)S(1)}, ...), condition=%wide.region_4.5_spmd.clone, body=%wide.region_2.4_spmd.clone.sunk | while | flops 273153024 | bytes 1588297 | solution.py:46
  23.6 2.6 select_reduce_fusion.2
  26.7 2.6 select_reduce_fusion.2
  29.7 2.6 select_reduce_fusion.2
  32.7 2.6 select_reduce_fusion.2
  35.8 2.6 select_reduce_fusion.2
  38.8 2.6 select_reduce_fusion.2
  41.8 2.6 select_reduce_fusion.2
  44.9 2.6 select_reduce_fusion.2
  47.5 3.5 %fusion.12 = f32[8,8,8,128]{3,2,1,0:T(8,128)S(1)} fusion(bf16[512,8,2,128]{3,2,1,0:T(2,128)(2,1)} %reshape_squeeze.15, bf16[8,2,512,128]{2,3,1,0:T(8,128)(2,1)S(1)} %get-tuple-element.163, f32[8,2,512]{2,1,0:T(2,128)S(1)} %get-tuple-element.70, pred[64,512]{1,0:T(8,128)(4,1)S(1)} %iota_compare_fusion.1, bf16[64,8,128,1]{2,1,0,3:T(8,128)(2,1)} %bitcast.64), kind=kOutput, calls=%fused_computation.15 | convolution fusion | flops 271056896 | bytes 4653056 | tf_op jit(solution)/shard_map/hgpq,qhgc->phc/dot_general | solution.py:57
  52.4 8.3 %reduce-scatter.3.cloned.1.call-done = f32[32,1024]{1,0:T(8,128)} async-done(((f32[64,1024]{1,0:T(8,128)}), f32[32,1024]{1,0:T(8,128)}) %reduce-scatter.3.cloned.1.call-update) | async-done | bytes 131088 | tf_op jit(solution)/shard_map/reduce_scatter | solution.py:61
  60.8 160.9 %all-gather.7.cloned.1.call-done = bf16[4608,1024]{1,0:T(8,128)(2,1)} async-done(((bf16[1152,1024]{1,0:T(8,128)(2,1)}), bf16[4608,1024]{1,0:T(8,128)(2,1)}) %all-gather.7.cloned.1.call-update) | async-done | bytes 9437200 | tf_op jit(solution)/shard_map/all_gather | solution.py:71
  221.6 7.4 %fusion.19 = f32[32,4608]{1,0:T(8,128)} fusion(bf16[4608,1024]{1,0:T(8,128)(2,1)} %all-gather.7.cloned.1.call-done, f32[32,1024]{1,0:T(8,128)} %reduce-scatter.3.cloned.1.call-done), kind=kOutput, calls=%fused_computation.26 | convolution fusion | flops 302022656 | bytes 10158080 | tf_op jit(solution)/shard_map/dot_general | solution.py:69
  229.2 13.5 %reduce-scatter.5.cloned.1.call-done = f32[32,2304]{1,0:T(8,128)} async-done(((f32[32,4608]{1,0:T(8,128)}), f32[32,2304]{1,0:T(8,128)}) %reduce-scatter.5.cloned.1.call-update) | async-done | bytes 294928 | tf_op jit(solution)/shard_map/reduce_scatter | solution.py:75
  242.7 1.6 multiply_reduce_fusion
  244.3 6.4 %psum.15 = f32[]{:T(128)} all-reduce(f32[]{:T(128)} %multiply_reduce_fusion), channel_id=1, replica_groups=mesh['group'=2,'dp'=4,'tensor'=2,'seq'=2] {'tensor','seq'}, use_global_device_ids=true, to_apply=%region_8.9 | all-reduce | flops 1 | bytes 8 | tf_op jit(solution)/shard_map/psum | solution.py:76
  251.4 1.7 broadcast_divide_fusion
  254.4 30.1 %all-gather.9.cloned.1.call-done = f32[128,2304]{1,0:T(8,128)} async-done(((f32[32,2304]{1,0:T(8,128)}), f32[128,2304]{1,0:T(8,128)}) %all-gather.9.cloned.1.call-update) | async-done | bytes 1179664 | tf_op jit(solution)/shard_map/all_gather | solution.py:82
  284.5 3.8 %fusion.10 = f32[1,32,2304]{2,0,1:T(1,128)S(1)} fusion(f32[4,32,2304]{2,1,0:T(8,128)} %bitcast.60, s32[4]{0:T(128)S(1)} %copy-done.3, s32[]{:T(128)} %get-tuple-element.90), kind=kOutput, calls=%fused_computation.13 | convolution fusion | flops 3538948 | bytes 1474580 | tf_op jit(solution)/shard_map/e,erc->rc/dot_general | solution.py:79
  288.3 8.9 %all_gather.15 = f32[32,4608]{1,0:T(8,128)S(1)} all-gather(f32[32,2304]{1,0:T(8,128)S(1)} %bitcast.59), channel_id=1, replica_groups=mesh['group'=2,'dp'=4,'tensor'=2,'seq'=2] {'tensor'}, dimensions={1}, use_global_device_ids=true | all-gather | bytes 884736 | tf_op jit(solution)/shard_map/all_gather | solution.py:85
  (50 shorter events, 7.8 us)
Async XLA Ops:
  7.4 4.2 %copy-start = (bf16[1,512,2048]{2,1,0:T(8,128)(2,1)S(1)}, bf16[1,512,2048]{2,1,0:T(8,128)(2,1)}, u32[]{:S(2)}) copy-start(bf16[1,512,2048]{2,1,0:T(8,128)(2,1)} %param.10) | copy-start | bytes 6291460
  7.4 15.9 %all-gather.5.cloned.1.call-start = ((), (), s32[]{:S(2)}) async-start(), calls=%async_computation.3 | async-start | bytes 3145728 | tf_op jit(solution)/shard_map/all_gather | solution.py:35
  9.8 37.7 %all-reduce.2.cloned.1.call-start = ((), (), s32[]{:S(2)}) async-start(), calls=%async_computation.2 | async-start | bytes 262144 | tf_op jit(solution)/shard_map/psum | solution.py:19
  11.5 49.3 %reduce-scatter.3.cloned.1.call-start = ((), (), s32[]{:S(2)}) async-start(), calls=%async_computation.4 | async-start | bytes 393216 | tf_op jit(solution)/shard_map/reduce_scatter | solution.py:61
  14.1 9.1 %copy-start.1 = (bf16[1,512,2048]{1,2,0:T(8,128)(2,1)S(1)}, bf16[1,512,2048]{1,2,0:T(8,128)(2,1)}, u32[]{:S(2)}) copy-start(bf16[1,512,2048]{1,2,0:T(8,128)(2,1)} %copy.10) | copy-start | bytes 6291460
  51.8 169.9 %all-gather.7.cloned.1.call-start = ((), (), s32[]{:S(2)}) async-start(), calls=%async_computation.5 | async-start | bytes 11796480 | tf_op jit(solution)/shard_map/all_gather | solution.py:71
  52.4 200.8 %copy-start.4 = (s32[4]{0:T(128)S(1)}, s32[4]{0:T(128)}, u32[]{:S(2)}) copy-start(s32[4]{0:T(128)} %param.16) | copy-start | bytes 52
  52.4 200.8 %copy-start.5 = (s32[4]{0:T(128)S(1)}, s32[4]{0:T(128)}, u32[]{:S(2)}) copy-start(s32[4]{0:T(128)} %param.15) | copy-start | bytes 52
  52.4 232.1 %copy-start.3 = (s32[4]{0:T(128)S(1)}, s32[4]{0:T(128)}, u32[]{:S(2)}) copy-start(s32[4]{0:T(128)} %param.14) | copy-start | bytes 52
  52.4 190.3 %reduce-scatter.5.cloned.1.call-start = ((), (), s32[]{:S(2)}) async-start(), calls=%async_computation.6 | async-start | bytes 884736 | tf_op jit(solution)/shard_map/reduce_scatter | solution.py:75
  229.1 68.0 %copy-start.2 = (f32[1,32,4608]{2,1,0:T(8,128)S(1)}, f32[1,32,4608]{2,1,0:T(8,128)}, u32[]{:S(2)}) copy-start(f32[1,32,4608]{2,1,0:T(8,128)} %param.17) | copy-start | bytes 1769476
  229.1 55.4 %all-gather.9.cloned.1.call-start = ((), (), s32[]{:S(2)}) async-start(), calls=%async_computation.7 | async-start | bytes 1474560 | tf_op jit(solution)/shard_map/all_gather | solution.py:82
Sparse Core Ops, SparseCore 0:
  10.0 13.2 all-gather.4
  25.6 19.1 all-reduce.1
  51.9 8.8 reduce-scatter.2
  229.2 13.4 reduce-scatter.4
Sparse Core Ops, SparseCore 1:
  53.8 167.8 all-gather.6
  253.2 31.2 all-gather.8
where the time goes:
time: 306 us; the launch traced here: 305 us
  waiting for transfers between devices  218 us (71%)
  matrix products  35.8 us (12%)
  between operations  16 us (5%)
  blocking collectives  15.2 us (5%)
  local copies, waits for them, and re-layouts  11.1 us (4%)
  other arithmetic  8.71 us (3%)
    all_gather x1, waiting for transfers between devices, body(): lax.all_gather(value_weight, 'dp', axis=0, tiled=True)  161 us
    all_gather x1, waiting for transfers between devices, body(): lax.all_gather(clipped[None], 'dp', axis=0, tiled=True)  30.1 us
    dot_general x8, matrix products, per_head(): jnp.einsum('gqc,kc->gqk', query_head, key_head, preferred_element_type=jn...  21.1 us
    reduce_scatter x1, waiting for transfers between devices, body(): lax.psum_scatter(partial_grad, 'tensor', scatter_dimension=1, tiled=True)  13.5 us
    all_gather x1, blocking collectives, body(): tenant_sum = lax.all_gather(tenant_share, 'tensor', axis=1, tiled=True)  8.85 us
    reduce_scatter x1, waiting for transfers between devices, body(): lax.psum_scatter(partial_values, 'seq', scatter_dimension=0, tiled=True)  8.32 us
    dot_general x1, matrix products, body(): lax.dot_general(value_grad, lax.all_gather(value_weight, 'dp', axis=0, ti...  7.44 us
    psum x1, blocking collectives, body(): norm_sq = lax.psum(jnp.sum(grad_share * grad_share), ('tensor', 'seq'))  6.36 us
  transfers between devices with their start and end apart: 6, of which 5 were waited for; matrix products, arithmetic and copies ran while one was open for 11% of the time, Pallas kernels for 0%

commit v1 on v0

v1 whole, which is shorter than its diff:
```python
import functools
import math

import jax
import jax.numpy as jnp
from jax import lax
from jax.experimental import pallas as pl
from jax.experimental.pallas import tpu as pltpu
from jax.sharding import PartitionSpec as P

D = 4608
HEAD_DIM = 128
PROMPT = 64
LANES = 128

softcap = 50.0
query_scale = 144.0 ** (-0.5)
TANH_SCALE = query_scale / softcap
EXP2_SCALE = softcap * math.log2(math.e)

CONTRACT_LAST = (((1,), (1,)), ((), ()))


def xor_pairs(size, step):
    return [(i, i ^ step) for i in range(size)]


def head_value_grad(q_halves, k_halves, g_halves, out, prob):
    block = LANES
    rows = q_halves[0].shape[0]
    group = q_halves[0].shape[1] // HEAD_DIM
    key_pos = lax.broadcasted_iota(jnp.int32, (block, block), 0)
    query_pos = lax.broadcasted_iota(jnp.int32, (block, block), 1)
    keep = jnp.concatenate([key_pos <= query_pos] * group, axis=1)

    def query_block(q_ref, parts, start, column):
        q_block = jnp.concatenate(
            [q_ref[start : start + block, g * HEAD_DIM : (g + 1) * HEAD_DIM] for g in range(group)],
            axis=0,
        )
        total, prompt = None, None
        for k_ref, count, diagonal in parts:
            raw = lax.dot_general(
                k_ref[:count, :], q_block, CONTRACT_LAST, preferred_element_type=jnp.float32
            )
            for low in range(0, count, block):
                e = jnp.exp2(jnp.tanh(raw[low : low + block] * TANH_SCALE) * EXP2_SCALE)
                if diagonal and low == count - block:
                    e = jnp.where(keep, e, 0.0)
                if prompt is None:
                    prompt = e[:PROMPT]
                part = jnp.sum(e.reshape(block // 8, 8, group * block), axis=0)
                total = part if total is None else total + part
        total = jnp.sum(total, axis=0, keepdims=True)
        scaled = (prompt / total).astype(jnp.bfloat16)
        for g in range(group):
            prob[g, :, column : column + block] = scaled[:, g * block : (g + 1) * block]

    for start in range(0, rows, block):
        query_block(q_halves[0], [(k_halves[0], start + block, True)], start, start)
    for start in range(0, rows, block):
        parts = [(k_halves[0], rows, False), (k_halves[1], start + block, True)]
        query_block(q_halves[1], parts, start, rows + start)
    value = None
    for g in range(group):
        for half in range(2):
            term = jnp.dot(
                prob[g, :, half * rows : (half + 1) * rows],
                g_halves[half][:, g * HEAD_DIM : (g + 1) * HEAD_DIM],
                preferred_element_type=jnp.float32,
            )
            value = term if value is None else value + term
    value = value.astype(jnp.bfloat16)
    out[0] = value[: PROMPT // 2]
    out[1] = value[PROMPT // 2 :]


def attention_kernel(seq_ref, q_own, q_far, k_own, k_far, g_own, g_far, out, prob):
    @pl.when(seq_ref[0] == 0)
    def _():
        head_value_grad((q_own, q_far), (k_own, k_far), (g_own, g_far), out, prob)

    @pl.when(seq_ref[0] == 1)
    def _():
        head_value_grad((q_far, q_own), (k_far, k_own), (g_far, g_own), out, prob)


def prompt_value_grad(seq_index, q_own, q_far, k_own, k_far, g_own, g_far):
    rows = q_own.shape[0]
    heads = k_far.shape[1] // HEAD_DIM
    group = q_own.shape[1] // k_own.shape[1]
    width = group * HEAD_DIM
    own = lambda h, seq: (0, seq[0] * heads + h)
    far = lambda h, seq: (0, h)
    return pl.pallas_call(
        attention_kernel,
        grid_spec=pltpu.PrefetchScalarGridSpec(
            num_scalar_prefetch=1,
            grid=(heads,),
            in_specs=[
                pl.BlockSpec((rows, width), own),
                pl.BlockSpec((rows, width), far),
                pl.BlockSpec((rows, HEAD_DIM), own),
                pl.BlockSpec((rows, HEAD_DIM), far),
                pl.BlockSpec((rows, width), own),
                pl.BlockSpec((rows, width), far),
            ],
            out_specs=pl.BlockSpec((2, PROMPT // 2, HEAD_DIM), lambda h, seq: (0, 0, h)),
            scratch_shapes=[pltpu.VMEM((group, PROMPT, 2 * rows), jnp.bfloat16)],
        ),
        out_shape=jax.ShapeDtypeStruct((2, PROMPT // 2, heads * HEAD_DIM), jnp.bfloat16),
        compiler_params=pltpu.CompilerParams(vmem_limit_bytes=32 * 1024 * 1024),
        cost_estimate=pl.CostEstimate(
            flops=heads * group * 9 * rows * rows * HEAD_DIM,
            bytes_accessed=10 * rows * heads * width,
            transcendentals=heads * group * 4 * rows * rows,
        ),
    )(seq_index.reshape(1), q_own, q_far, k_own, k_far, g_own, g_far)


def grad_kernel(place, *refs, examples, columns):
    near, far = refs[:examples], refs[examples : 2 * examples]
    weight, weight_far_0, weight_far_1, grad, squares = refs[2 * examples :]
    width = grad.shape[-1]
    depth = weight.shape[1] // 2
    rows = grad.shape[1]
    start = pl.multiple_of(place[2] * (columns - width), 16)
    total = None
    for half in range(2):
        offset = pl.multiple_of((place[1] ^ half) * depth, LANES)
        own = jnp.concatenate([ref[half] for ref in near], axis=0)
        other = jnp.concatenate([ref[half] for ref in far], axis=0)
        weight_far = (weight_far_0, weight_far_1)[half]
        term = lax.dot_general(
            own,
            weight[pl.ds(start, width), pl.ds(offset, depth)],
            CONTRACT_LAST,
            preferred_element_type=jnp.float32,
        ) + lax.dot_general(
            other, weight_far[...], CONTRACT_LAST, preferred_element_type=jnp.float32
        )
        total = term if total is None else total + term
    column = lax.broadcasted_iota(jnp.int32, (1, width), 1) + place[2] * (columns - width)
    split = columns // 2
    low = place[2] * split
    counted = (column >= low) & (column < low + split)
    squares[...] = jnp.zeros_like(squares)
    for step in range(examples):
        part = total[step * rows : (step + 1) * rows]
        grad[step] = part
        sums = jnp.sum(jnp.where(counted, part * part, 0.0), axis=0, keepdims=True)
        folded = sums[:, :LANES]
        for at in range(LANES, width, LANES):
            folded = folded + sums[:, at : at + LANES]
        squares[pl.ds(place[0] ^ step, 1), :] = folded


def share_kernel(place, select, norms, near, far, *outs):
    examples, rows, width = near.shape
    rest = far.shape[2]
    outs, scales = outs[:examples], outs[examples]
    devices = norms.shape[0] // 8
    norm_sq = jnp.sum(norms[...].reshape(devices, 8, LANES), axis=0)
    norm_sq = jnp.sum(norm_sq, axis=1, keepdims=True)
    scales[...] = jnp.broadcast_to(1.0 / jnp.maximum(1.0, jnp.sqrt(norm_sq)), scales.shape)
    scale = [scales[pl.ds(place[0] ^ step, 1), :] for step in range(examples)]
    near_at = pl.multiple_of(place[2] * rest, LANES)
    far_at = pl.multiple_of((1 - place[2]) * width, LANES)
    for k in range(examples):
        factor = [scale[step] * select[k * examples + step] for step in range(examples)]
        for ref, base, extent in ((near, near_at, width), (far, far_at, rest)):
            for at in range(0, extent, LANES):
                total = None
                for step in range(examples):
                    term = ref[step, :, at : at + LANES] * factor[step]
                    total = term if total is None else total + term
                to = pl.multiple_of(base + at, LANES)
                outs[k][:, pl.ds(to, LANES)] = total.astype(jnp.bfloat16)


def update_kernel(place, count, *refs, examples):
    shares, noise, out = refs[:examples], refs[examples], refs[examples + 1]
    columns = shares[0].shape[1]
    for step in range(examples):
        at = pl.ds(pl.multiple_of((place[0] ^ step) * columns, LANES), columns)
        share = shares[step][...].astype(jnp.float32)
        out[0, :, at] = (math.sqrt(PROMPT * D) * share + noise[0, :, at]) / count[0]


VMEM = pl.BlockSpec(memory_space=pltpu.VMEM)
SMEM = pl.BlockSpec(memory_space=pltpu.SMEM)


def tail_by_permutes(value_grad, weight, weight_far, tenant_of, owner_of, counts, noise, sizes):
    dp = sizes["dp"]
    columns = weight.shape[0]
    rows = PROMPT // 2
    width = weight_far[0].shape[0]
    rest = columns - width
    dp_index, seq_index, tensor_index = (lax.axis_index(a) for a in ("dp", "seq", "tensor"))
    place = jnp.stack([dp_index, seq_index, tensor_index]).astype(jnp.int32)

    order = jnp.arange(dp) ^ dp_index
    owner_ex = jnp.sum(
        jnp.where(tenant_of[:, None] == jnp.arange(dp)[None, :], owner_of[None, :], 0), axis=1
    )
    select = (owner_ex[order][None, :] == order[:, None]).astype(jnp.float32).reshape(-1)
    my_count = jnp.sum(jnp.where(owner_of == dp_index, counts, 0)).astype(jnp.float32).reshape(1)

    near = [value_grad] + [
        lax.ppermute(value_grad, "dp", xor_pairs(dp, step)) for step in range(1, dp)
    ]
    far = [lax.ppermute(block, "tensor", xor_pairs(2, 1)) for block in near]
    grad, squares = pl.pallas_call(
        functools.partial(grad_kernel, examples=dp, columns=columns),
        in_specs=[SMEM] + [VMEM] * (2 * dp + 3),
        out_specs=[VMEM, VMEM],
        out_shape=[
            jax.ShapeDtypeStruct((dp, rows, width), jnp.float32),
            jax.ShapeDtypeStruct((8, LANES), jnp.float32),
        ],
        compiler_params=pltpu.CompilerParams(vmem_limit_bytes=32 * 1024 * 1024),
    )(place, *near, *far, weight, *weight_far)
    sent = lax.dynamic_slice_in_dim(grad, tensor_index * (width - rest), rest, axis=2)
    grad_far = lax.ppermute(sent, "tensor", xor_pairs(2, 1))
    devices = dp * sizes["tensor"] * sizes["seq"]
    norms = lax.all_to_all(
        jnp.broadcast_to(squares[None], (devices, 8, LANES)).reshape(devices * 8, LANES),
        ("dp", "tensor", "seq"),
        split_axis=0,
        concat_axis=0,
        tiled=True,
    )
    shares = pl.pallas_call(
        share_kernel,
        in_specs=[SMEM, SMEM] + [VMEM] * 3,
        out_specs=[VMEM] * dp,
        out_shape=[jax.ShapeDtypeStruct((rows, columns), jnp.bfloat16)] * dp,
        scratch_shapes=[pltpu.VMEM((8, LANES), jnp.float32)],
    )(place, select, norms, grad, grad_far)
    arrived = [shares[0]] + [
        lax.ppermute(shares[step], "dp", xor_pairs(dp, step)) for step in range(1, dp)
    ]
    return pl.pallas_call(
        functools.partial(update_kernel, examples=dp),
        in_specs=[SMEM, SMEM] + [VMEM] * (dp + 1),
        out_specs=VMEM,
        out_shape=jax.ShapeDtypeStruct(noise.shape, jnp.float32),
    )(place, my_count, *arrived, noise)


def tail_by_collectives(value_grad, weight, tenant_of, owner_of, counts, noise):
    rows = PROMPT // 2
    seq_index, dp_index = lax.axis_index("seq"), lax.axis_index("dp")
    halves = jnp.where(seq_index == 0, value_grad, value_grad[::-1])
    mine = jnp.concatenate([halves[0], halves[1]], axis=1)
    whole = lax.all_gather(mine, "tensor", axis=1, tiled=True)
    whole = lax.all_gather(whole, "dp", axis=0, tiled=True)
    part = lax.all_to_all(weight, "tensor", split_axis=0, concat_axis=1, tiled=True)
    grad = lax.dot_general(whole, part, CONTRACT_LAST, preferred_element_type=jnp.float32)
    grad = grad.reshape(-1, rows, part.shape[0])
    norm_sq = lax.psum(jnp.sum(grad * grad, axis=(1, 2)), ("dp", "tensor", "seq"))
    clipped = grad / jnp.maximum(1.0, jnp.sqrt(norm_sq))[:, None, None]
    slots = jnp.arange(owner_of.shape[0])
    owner_ex = jnp.sum(
        jnp.where(tenant_of[:, None] == slots[None, :], owner_of[None, :], 0), axis=1
    )
    select = (owner_ex[None, :] == slots[:, None]).astype(jnp.float32)
    sums = jnp.einsum("oe,erc->orc", select, clipped, precision=lax.Precision.HIGHEST)
    sums = lax.all_gather(sums, "tensor", axis=2, tiled=True)
    sums = lax.all_to_all(sums, "dp", split_axis=0, concat_axis=2, tiled=True)
    my_count = jnp.sum(jnp.where(owner_of == dp_index, counts, 0)).astype(jnp.float32)
    return (math.sqrt(PROMPT * D) * sums + noise) / my_count


def body(sizes, queries, keys, out_grad, value_weight, tenant_of, owner_of, counts, noise):
    swap = xor_pairs(2, 1)
    seq_index = lax.axis_index("seq").astype(jnp.int32)
    tensor_index = lax.axis_index("tensor")
    q, k, g = queries[0], keys[0], out_grad[0]

    def from_sibling(x):
        half = x.shape[1] // 2
        sent = lax.dynamic_slice_in_dim(x, (1 - seq_index) * half, half, axis=1)
        return lax.ppermute(sent, "seq", swap)

    k_far, q_far, g_far = from_sibling(k), from_sibling(q), from_sibling(g)

    columns = value_weight.shape[0]
    dp = sizes["dp"]
    permutes = sizes["tensor"] == 2 and columns % LANES == 0 and dp in (1, 2, 4, 8)
    if permutes:
        width = -(-columns // (2 * LANES)) * LANES
        depth = value_weight.shape[1] // 2
        sent = lax.dynamic_slice(
            value_weight,
            ((1 - tensor_index) * (columns - width), seq_index * depth),
            (width, depth),
        )
        weight_far = lax.ppermute(sent, "tensor", swap)
        weight_far = (weight_far, lax.ppermute(weight_far, "seq", swap))

    halves = prompt_value_grad(seq_index, q, q_far, k, k_far, g, g_far)
    mine = lax.dynamic_index_in_dim(halves, seq_index, 0, keepdims=False)
    theirs = lax.dynamic_index_in_dim(halves, 1 - seq_index, 0, keepdims=False)
    value_grad = jnp.stack([mine, lax.ppermute(theirs, "seq", swap)])
    if permutes:
        return tail_by_permutes(
            value_grad, value_weight, weight_far, tenant_of, owner_of, counts, noise, sizes
        )
    return tail_by_collectives(value_grad, value_weight, tenant_of, owner_of, counts, noise)


def solution(mesh):
    return jax.shard_map(
        functools.partial(body, dict(mesh.shape)),
        mesh=mesh,
        in_specs=(
            P(("group", "dp"), "seq", "tensor"),
            P(("group", "dp"), "seq", "tensor"),
            P(("group", "dp"), "seq", "tensor"),
            P("dp", "tensor"),
            P("group"),
            P("group"),
            P("group"),
            P(("group", "dp"), "seq", None),
        ),
        out_specs=P(("group", "dp"), "seq", None),
        check_vma=False,
    )
```

time: 306 us -> 83.6 us (0.27)
  waiting for transfers between devices: 218 us -> 28.9 us
  matrix products: 35.8 us -> 0 us
  starting transfers between devices: 0.21 us -> 23.2 us
  between operations: 16 us -> 0.7 us
  blocking collectives: 15.2 us -> 0 us
  Pallas kernels: 0 us -> 14.3 us
  other arithmetic: 8.71 us -> 0.99 us
  local copies, waits for them, and re-layouts: 11.1 us -> 15.1 us
    all_gather x3 -> x0, waiting for transfers between devices: 196 us -> none  [the longest x1 161 us: body(): lax.all_gather(value_weight, 'dp', axis=0, tiled=True)]
    dot_general x11 -> x0, matrix products: 35.8 us -> none  [the longest x8 21.1 us: per_head(): jnp.einsum('gqc,kc->gqk', query_head, key_head, preferred_element_type=jn...]
    ppermute x0 -> x17, waiting for transfers between devices: none -> 22.7 us  [the longest x1 12.6 us: body(): weight_far = lax.ppermute(sent, 'tensor', swap)]
    reduce_scatter x2 -> x0, waiting for transfers between devices: 21.9 us -> none  [the longest x1 13.5 us: body(): lax.psum_scatter(partial_grad, 'tensor', scatter_dimension=1, tiled=True)]
    ppermute x0 -> x17, starting transfers between devices: none -> 19 us  [the longest x4 5.29 us: tail_by_permutes(): far = [lax.ppermute(block, 'tensor', xor_pairs(2, 1)) for block in near]]
    pallas_call x0 -> x4, Pallas kernels: none -> 14.3 us  [the longest x1 8.14 us: prompt_value_grad(): pl.pallas_call(attention_kernel, grid_spec=pltpu.PrefetchScalarGridSpec(n...]
    all_gather x1 -> x0, blocking collectives: 8.85 us -> none  [body(): tenant_sum = lax.all_gather(tenant_share, 'tensor', axis=1, tiled=True)]
    dynamic_slice x0 -> x6, local copies, waits for them, and re-layouts: none -> 7.45 us  [the longest x3 6.52 us: from_sibling(): sent = lax.dynamic_slice_in_dim(x, (1 - seq_index) * half, half, axis=1)]
  transfers between devices with their start and end apart: 6 -> 18, of which waited for: 5 -> 9; matrix products, arithmetic and copies ran while one was open for 11% -> 9% of each run, Pallas kernels for 0% -> 10%
where the time goes in v1:
time: 83.6 us; the launch traced here: 83.1 us
  waiting for transfers between devices  28.9 us (35%)
  starting transfers between devices  23.2 us (28%)
  local copies, waits for them, and re-layouts  15.1 us (18%)
  Pallas kernels  14.3 us (17%)
  other arithmetic  0.99 us (1%)
    ppermute x1, waiting for transfers between devices, body(): weight_far = lax.ppermute(sent, 'tensor', swap)  12.6 us
    pallas_call x1, Pallas kernels, prompt_value_grad(): pl.pallas_call(attention_kernel, grid_spec=pltpu.PrefetchScalarGridSpec(n...  8.14 us
    dynamic_slice x3, local copies, waits for them, and re-layouts, from_sibling(): sent = lax.dynamic_slice_in_dim(x, (1 - seq_index) * half, half, axis=1)  6.52 us
    all_to_all x1, waiting for transfers between devices, tail_by_permutes(): lax.all_to_all(jnp.broadcast_to(squares[None], (devices, 8, LANES)).resha...  6.21 us
    unnamed x28, local copies, waits for them, and re-layouts  5.79 us
    ppermute x4, starting transfers between devices, tail_by_permutes(): far = [lax.ppermute(block, 'tensor', xor_pairs(2, 1)) for block in near]  5.29 us
    ppermute x3, starting transfers between devices, tail_by_permutes(): lax.ppermute(value_grad, 'dp', xor_pairs(dp, step))  4.55 us
    ppermute x3, starting transfers between devices, tail_by_permutes(): lax.ppermute(shares[step], 'dp', xor_pairs(dp, step))  4.39 us
  transfers between devices with their start and end apart: 18, of which 9 were waited for; matrix products, arithmetic and copies ran while one was open for 9% of the time, Pallas kernels for 10%

profile of v1, /device:TPU:0, one launch (start us, length us, event | category | flops | bytes accessed | tf_op | source)
XLA Modules:
  0.0 83.1 jit_solution(5027272775097411775)
XLA Ops:
  0.0 2.4 %dynamic-slice_bitcast_fusion.1 = bf16[512,1024]{1,0:T(8,128)(2,1)} fusion(bf16[1,512,2048]{2,1,0:T(8,128)(2,1)} %param.8, s32[]{:T(128)S(6)} %select_n.44), kind=kLoop, calls=%fused_computation.2 | loop fusion | bytes 2097156 | tf_op jit(solution)/shard_map/dynamic_slice | solution.py:284
  2.9 2.3 %dynamic-slice_bitcast_fusion = bf16[512,1024]{1,0:T(8,128)(2,1)} fusion(bf16[1,512,2048]{2,1,0:T(8,128)(2,1)} %param.10, s32[]{:T(128)S(6)} %select_n.44), kind=kLoop, calls=%fused_computation.1 | loop fusion | bytes 2097156 | tf_op jit(solution)/shard_map/dynamic_slice | solution.py:284
  5.2 0.9 %dynamic_slice.36 = bf16[640,512]{1,0:T(8,128)(2,1)} dynamic-slice(bf16[1152,1024]{1,0:T(8,128)(2,1)S(1)} %copy-done, s32[]{:T(128)S(6)} %select_n.48, s32[]{:T(128)S(6)} %select_n.49), dynamic_slice_sizes={640,512} | dynamic-slice | bytes 1310724 | tf_op jit(solution)/shard_map/dynamic_slice | solution.py:295
  6.1 2.9 %collective-permute-start.11 = (bf16[640,512]{1,0:T(8,128)(2,1)}, bf16[640,512]{1,0:T(8,128)(2,1)S(1)}, u32[]{:S(2)}, u32[]{:S(2)}) collective-permute-start(bf16[640,512]{1,0:T(8,128)(2,1)} %dynamic_slice.36), channel_id=1, source_target_pairs={{0,2},{2,0},{1,3},{3,1},{4,6},{6,4},{5,7},{7,5},{8,10},{10,8},{9,1... | collective-permute-start | bytes 1966088 | tf_op jit(solution)/shard_map/ppermute | solution.py:300
  9.0 1.9 %dynamic-slice_bitcast_fusion.2 = bf16[512,512]{1,0:T(8,128)(2,1)} fusion(bf16[1,512,1024]{2,1,0:T(8,128)(2,1)} %param.9, s32[]{:T(128)S(6)} %select_n.45), kind=kLoop, calls=%fused_computation.3 | loop fusion | bytes 1048580 | tf_op jit(solution)/shard_map/dynamic_slice | solution.py:284
  11.5 12.6 %collective-permute-done.11.refs_9_ = bf16[640,512]{1,0:T(8,128)(2,1)S(1)} collective-permute-done((bf16[640,512]{1,0:T(8,128)(2,1)}, bf16[640,512]{1,0:T(8,128)(2,1)S(1)}, u32[]{:S(2)}, u32[]{:S(2)}) %collective-permute-start.11) | collective-permute-done | bytes 655392 | tf_op jit(solution)/shard_map/ppermute | solution.py:300
  24.2 1.6 %copy-done.2 = bf16[1,512,2048]{2,1,0:T(8,128)(2,1)S(1)} copy-done((bf16[1,512,2048]{2,1,0:T(8,128)(2,1)S(1)}, bf16[1,512,2048]{2,1,0:T(8,128)(2,1)}, u32[]{:S(2)}) %copy-start.2) | copy-done | bytes 2097176
  25.8 1.6 %copy-done.3 = bf16[1,512,2048]{2,1,0:T(8,128)(2,1)S(1)} copy-done((bf16[1,512,2048]{2,1,0:T(8,128)(2,1)S(1)}, bf16[1,512,2048]{2,1,0:T(8,128)(2,1)}, u32[]{:S(2)}) %copy-start.3) | copy-done | bytes 2097176
  27.3 1.2 %copy-done.4 = bf16[1,512,1024]{2,1,0:T(8,128)(2,1)S(1)} copy-done((bf16[1,512,1024]{2,1,0:T(8,128)(2,1)S(1)}, bf16[1,512,1024]{2,1,0:T(8,128)(2,1)}, u32[]{:S(2)}) %copy-start.4) | copy-done | bytes 1048600
  28.6 8.1 %shard_map.82 = bf16[2,32,512]{2,1,0:T(8,128)(2,1)S(1)} custom-call(s32[1]{0:T(128)} %bitcast.1.seq_ref, bf16[512,2048]{1,0:T(8,128)(2,1)S(1)} %bitcast.19, bf16[512,1024]{1,0:T(8,128)(2,1)} %collective-permute-done.q_far, bf16[512,1024]{1,0:T(8,128)(2,1)S(1)} %bitcast.21, bf16[512,512]{1,0:T(8,128)(2,1)S(1)} %collective-permute-done.1.k_far, ...), custom_call_target="tpu_custom_call" | custom-call | flops 2415919104 | bytes 5242880 | tf_op jit(solution)/shard_map/pallas_call | solution.py:95
  38.2 3.9 %collective-permute-start.6 = (bf16[2,32,512]{2,1,0:T(8,128)(2,1)S(1)}, bf16[2,32,512]{2,1,0:T(8,128)(2,1)S(1)}, u32[]{:S(2)}, u32[]{:S(2)}) collective-permute-start(bf16[2,32,512]{2,1,0:T(8,128)(2,1)S(1)} %pad_maximum_fusion.refs_0_), channel_id=1, source_target_pairs={{0,12},{4,8},{8,4},{12,0},{1,13},{5,9},{9,5},{13,1},{2,14},{6,10},... | collective-permute-start | bytes 196616 | tf_op jit(solution)/shard_map/ppermute | solution.py:211
  42.7 1.6 %collective-permute-start.7 = (bf16[2,32,512]{2,1,0:T(8,128)(2,1)S(1)}, bf16[2,32,512]{2,1,0:T(8,128)(2,1)S(1)}, u32[]{:S(2)}, u32[]{:S(2)}) collective-permute-start(bf16[2,32,512]{2,1,0:T(8,128)(2,1)S(1)} %pad_maximum_fusion.refs_0_), channel_id=1, source_target_pairs={{0,2},{2,0},{1,3},{3,1},{4,6},{6,4},{5,7},{7,5},{8,10},{10,8},{9,1... | collective-permute-start | bytes 196616 | tf_op jit(solution)/shard_map/ppermute | solution.py:213
  45.0 1.6 %collective-permute-start.10 = (bf16[2,32,512]{2,1,0:T(8,128)(2,1)S(1)}, bf16[2,32,512]{2,1,0:T(8,128)(2,1)S(1)}, u32[]{:S(2)}, u32[]{:S(2)}) collective-permute-start(bf16[2,32,512]{2,1,0:T(8,128)(2,1)S(1)} %collective-permute-done.6.refs_3_), channel_id=1, source_target_pairs={{0,2},{2,0},{1,3},{3,1},{4,6},{6,4},{5,7},{7,5},{8,10},{10,8},{9,1... | collective-permute-start | bytes 196616 | tf_op jit(solution)/shard_map/ppermute | solution.py:213
  47.4 1.5 %collective-permute-start.8 = (bf16[2,32,512]{2,1,0:T(8,128)(2,1)S(1)}, bf16[2,32,512]{2,1,0:T(8,128)(2,1)S(1)}, u32[]{:S(2)}, u32[]{:S(2)}) collective-permute-start(bf16[2,32,512]{2,1,0:T(8,128)(2,1)S(1)} %collective-permute-done.4.refs_1_), channel_id=1, source_target_pairs={{0,2},{2,0},{1,3},{3,1},{4,6},{6,4},{5,7},{7,5},{8,10},{10,8},{9,1... | collective-permute-start | bytes 196616 | tf_op jit(solution)/shard_map/ppermute | solution.py:213
  49.6 2.1 %collective-permute-done.8.refs_5_ = bf16[2,32,512]{2,1,0:T(8,128)(2,1)S(1)} collective-permute-done((bf16[2,32,512]{2,1,0:T(8,128)(2,1)S(1)}, bf16[2,32,512]{2,1,0:T(8,128)(2,1)S(1)}, u32[]{:S(2)}, u32[]{:S(2)}) %collective-permute-start.8) | collective-permute-done | bytes 65568 | tf_op jit(solution)/shard_map/ppermute | solution.py:213
  51.7 1.5 %collective-permute-done.9.refs_6_ = bf16[2,32,512]{2,1,0:T(8,128)(2,1)S(1)} collective-permute-done((bf16[2,32,512]{2,1,0:T(8,128)(2,1)S(1)}, bf16[2,32,512]{2,1,0:T(8,128)(2,1)S(1)}, u32[]{:S(2)}, u32[]{:S(2)}) %collective-permute-start.9) | collective-permute-done | bytes 65568 | tf_op jit(solution)/shard_map/ppermute | solution.py:213
  53.2 2.0 %shard_map.83 = (f32[4,32,640]{2,1,0:T(8,128)S(1)}, f32[8,128]{1,0:T(8,128)S(1)}) custom-call(s32[3]{0:T(128)S(1)} %pad_add_fusion.place, bf16[2,32,512]{2,1,0:T(8,128)(2,1)S(1)} %pad_maximum_fusion.refs_0_, bf16[2,32,512]{2,1,0:T(8,128)(2,1)S(1)} %collective-permute-done.4.refs_1_, bf16[2,32,512]{2,1,0:T(8,128)(2,1)S(1)} %collective-permute-done.5.refs_2_, ...), custom_call_target="tpu_custom_call" | custom-call | tf_op jit(solution)/shard_map/pallas_call | solution.py:214
  57.4 4.2 %all-to-all-start = ((f32[16,8,128]{2,1,0:T(8,128)}), f32[16,8,128]{2,1,0:T(8,128)S(1)}, u32[]{:S(2)}, u32[]{:S(2)}) async-start(f32[16,8,128]{2,1,0:T(8,128)} %broadcast_in_dim.34), calls=%async_computation | async-start | bytes 131072 | tf_op jit(solution)/shard_map/all_to_all | solution.py:227
  62.2 6.2 %all-to-all-done = f32[16,8,128]{2,1,0:T(8,128)S(1)} async-done(((f32[16,8,128]{2,1,0:T(8,128)}), f32[16,8,128]{2,1,0:T(8,128)S(1)}, u32[]{:S(2)}, u32[]{:S(2)}) %all-to-all-start) | async-done | bytes 65568 | tf_op jit(solution)/shard_map/all_to_all | solution.py:227
  69.2 2.0 %shard_map.84 = (bf16[32,1152]{1,0:T(8,128)(2,1)}, bf16[32,1152]{1,0:T(8,128)(2,1)}, bf16[32,1152]{1,0:T(8,128)(2,1)}, bf16[32,1152]{1,0:T(8,128)(2,1)}) custom-call(s32[3]{0:T(128)} %copy-done.5, f32[16]{0:T(128)} %reshape.40.select, f32[128,128]{1,0:T(8,128)} %bitcast.22, f32[4,32,640]{2,1,0:T(8,128)} %copy-done.1, f32[4,32,512]{2,1,0:T(8,128)} %copy-done.6), custom_call_target="tpu_custom_call" | custom-call | tf_op jit(solution)/shard_map/pallas_call | solution.py:234
  71.3 1.0 %collective-permute-start.15 = (bf16[32,1152]{1,0:T(8,128)(2,1)}, bf16[32,1152]{1,0:T(8,128)(2,1)S(1)}, u32[]{:S(2)}, u32[]{:S(2)}) collective-permute-start(bf16[32,1152]{1,0:T(8,128)(2,1)} %get-tuple-element.15), channel_id=1, source_target_pairs={{0,8},{4,12},{8,0},{12,4},{1,9},{5,13},{9,1},{13,5},{2,10},{6,14},... | collective-permute-start | bytes 221192 | tf_op jit(solution)/shard_map/ppermute | solution.py:242
  72.3 3.3 %collective-permute-start.16 = (bf16[32,1152]{1,0:T(8,128)(2,1)}, bf16[32,1152]{1,0:T(8,128)(2,1)S(1)}, u32[]{:S(2)}, u32[]{:S(2)}) collective-permute-start(bf16[32,1152]{1,0:T(8,128)(2,1)} %get-tuple-element.16), channel_id=1, source_target_pairs={{0,12},{4,8},{8,4},{12,0},{1,13},{5,9},{9,5},{13,1},{2,14},{6,10},... | collective-permute-start | bytes 221192 | tf_op jit(solution)/shard_map/ppermute | solution.py:242
  76.4 3.9 %collective-permute-done.15.refs_2_ = bf16[32,1152]{1,0:T(8,128)(2,1)S(1)} collective-permute-done((bf16[32,1152]{1,0:T(8,128)(2,1)}, bf16[32,1152]{1,0:T(8,128)(2,1)S(1)}, u32[]{:S(2)}, u32[]{:S(2)}) %collective-permute-start.15) | collective-permute-done | bytes 73760 | tf_op jit(solution)/shard_map/ppermute | solution.py:242
  81.0 2.1 %shard_map.85 = f32[1,32,4608]{2,1,0:T(8,128)} custom-call(s32[3]{0:T(128)} %copy-done.5, f32[1]{0:T(128)} %bitcast.3.count, bf16[32,1152]{1,0:T(8,128)(2,1)} %get-tuple-element.13.refs_0_, bf16[32,1152]{1,0:T(8,128)(2,1)} %copy-done.8, bf16[32,1152]{1,0:T(8,128)(2,1)} %copy-done.9, bf16[32,1152]{1,0:T(8,128)(2,1)} %copy-done.10, f32[1,32,4608]{2,1,0:T(8,128)} %refs_4_.1), custom_call_target="tpu_custom_call" | custom-call | tf_op jit(solution)/shard_map/pallas_call | solution.py:244
  (60 shorter events, 9.9 us)
Async XLA Ops:
  0.0 5.2 %copy-start = (bf16[1152,1024]{1,0:T(8,128)(2,1)S(1)}, bf16[1152,1024]{1,0:T(8,128)(2,1)}, u32[]{:S(2)}) copy-start(bf16[1152,1024]{1,0:T(8,128)(2,1)} %refs_8_.1) | copy-start | bytes 7077892
  2.4 8.5 %copy-start.11 = (s32[4]{0:T(128)S(1)}, s32[4]{0:T(128)}, u32[]{:S(2)}) copy-start(s32[4]{0:T(128)} %param.14) | copy-start | bytes 52
  2.4 8.5 %copy-start.12 = (s32[4]{0:T(128)S(1)}, s32[4]{0:T(128)}, u32[]{:S(2)}) copy-start(s32[4]{0:T(128)} %param.13) | copy-start | bytes 52
  2.4 21.7 %collective-permute-start = (bf16[512,1024]{1,0:T(8,128)(2,1)}, bf16[512,1024]{1,0:T(8,128)(2,1)}, u32[]{:S(2)}, u32[]{:S(2)}) collective-permute-start(bf16[512,1024]{1,0:T(8,128)(2,1)} %dynamic-slice_bitcast_fusion.1), channel_id=1, source_target_pairs={{0,1},{1,0},{2,3},{3,2},{4,5},{5,4},{6,7},{7,6},{8,9},{9,8},{10,11... | collective-permute-start | bytes 3145736 | tf_op jit(solution)/shard_map/ppermute | solution.py:285
  5.1 19.0 %collective-permute-start.2 = (bf16[512,1024]{1,0:T(8,128)(2,1)}, bf16[512,1024]{1,0:T(8,128)(2,1)}, u32[]{:S(2)}, u32[]{:S(2)}) collective-permute-start(bf16[512,1024]{1,0:T(8,128)(2,1)} %dynamic-slice_bitcast_fusion), channel_id=1, source_target_pairs={{0,1},{1,0},{2,3},{3,2},{4,5},{5,4},{6,7},{7,6},{8,9},{9,8},{10,11... | collective-permute-start | bytes 3145736 | tf_op jit(solution)/shard_map/ppermute | solution.py:285
  6.1 18.1 %collective-permute-start.11 = (bf16[640,512]{1,0:T(8,128)(2,1)}, bf16[640,512]{1,0:T(8,128)(2,1)S(1)}, u32[]{:S(2)}, u32[]{:S(2)}) collective-permute-start(bf16[640,512]{1,0:T(8,128)(2,1)} %dynamic_slice.36), channel_id=1, source_target_pairs={{0,2},{2,0},{1,3},{3,1},{4,6},{6,4},{5,7},{7,5},{8,10},{10,8},{9,1... | collective-permute-start | bytes 1966088 | tf_op jit(solution)/shard_map/ppermute | solution.py:300
  10.9 13.3 %collective-permute-start.1 = (bf16[512,512]{1,0:T(8,128)(2,1)}, bf16[512,512]{1,0:T(8,128)(2,1)S(1)}, u32[]{:S(2)}, u32[]{:S(2)}) collective-permute-start(bf16[512,512]{1,0:T(8,128)(2,1)} %dynamic-slice_bitcast_fusion.2), channel_id=1, source_target_pairs={{0,1},{1,0},{2,3},{3,2},{4,5},{5,4},{6,7},{7,6},{8,9},{9,8},{10,11... | collective-permute-start | bytes 1572872 | tf_op jit(solution)/shard_map/ppermute | solution.py:285
  24.1 29.1 %collective-permute-start.12 = (bf16[640,512]{1,0:T(8,128)(2,1)S(1)}, bf16[640,512]{1,0:T(8,128)(2,1)}, u32[]{:S(2)}, u32[]{:S(2)}) collective-permute-start(bf16[640,512]{1,0:T(8,128)(2,1)S(1)} %collective-permute-done.11.refs_9_), channel_id=1, source_target_pairs={{0,1},{1,0},{2,3},{3,2},{4,5},{5,4},{6,7},{7,6},{8,9},{9,8},{10,11... | collective-permute-start | bytes 1966088 | tf_op jit(solution)/shard_map/ppermute | solution.py:301
  28.6 8.7 %copy-start.13 = (s32[4]{0:T(128)S(1)}, s32[4]{0:T(128)}, u32[]{:S(2)}) copy-start(s32[4]{0:T(128)} %param.12) | copy-start | bytes 52
  36.7 1.4 %collective-permute-start.3 = (bf16[32,512]{1,0:T(8,128)(2,1)S(1)}, bf16[32,512]{1,0:T(8,128)(2,1)S(1)}, u32[]{:S(2)}, u32[]{:S(2)}) collective-permute-start(bf16[32,512]{1,0:T(8,128)(2,1)S(1)} %get-tuple-element.18), channel_id=1, source_target_pairs={{0,1},{1,0},{2,3},{3,2},{4,5},{5,4},{6,7},{7,6},{8,9},{9,8},{10,11... | collective-permute-start | bytes 98312 | tf_op jit(solution)/shard_map/ppermute | solution.py:306
  38.2 6.9 %collective-permute-start.6 = (bf16[2,32,512]{2,1,0:T(8,128)(2,1)S(1)}, bf16[2,32,512]{2,1,0:T(8,128)(2,1)S(1)}, u32[]{:S(2)}, u32[]{:S(2)}) collective-permute-start(bf16[2,32,512]{2,1,0:T(8,128)(2,1)S(1)} %pad_maximum_fusion.refs_0_), channel_id=1, source_target_pairs={{0,12},{4,8},{8,4},{12,0},{1,13},{5,9},{9,5},{13,1},{2,14},{6,10},... | collective-permute-start | bytes 196616 | tf_op jit(solution)/shard_map/ppermute | solution.py:211
  42.1 5.4 %collective-permute-start.4 = (bf16[2,32,512]{2,1,0:T(8,128)(2,1)S(1)}, bf16[2,32,512]{2,1,0:T(8,128)(2,1)S(1)}, u32[]{:S(2)}, u32[]{:S(2)}) collective-permute-start(bf16[2,32,512]{2,1,0:T(8,128)(2,1)S(1)} %pad_maximum_fusion.refs_0_), channel_id=1, source_target_pairs={{0,4},{4,0},{8,12},{12,8},{1,5},{5,1},{9,13},{13,9},{2,6},{6,2},{1... | collective-permute-start | bytes 196616 | tf_op jit(solution)/shard_map/ppermute | solution.py:211
  42.1 6.9 %collective-permute-start.5 = (bf16[2,32,512]{2,1,0:T(8,128)(2,1)S(1)}, bf16[2,32,512]{2,1,0:T(8,128)(2,1)S(1)}, u32[]{:S(2)}, u32[]{:S(2)}) collective-permute-start(bf16[2,32,512]{2,1,0:T(8,128)(2,1)S(1)} %pad_maximum_fusion.refs_0_), channel_id=1, source_target_pairs={{0,8},{4,12},{8,0},{12,4},{1,9},{5,13},{9,1},{13,5},{2,10},{6,14},... | collective-permute-start | bytes 196616 | tf_op jit(solution)/shard_map/ppermute | solution.py:211
  42.7 6.8 %collective-permute-start.7 = (bf16[2,32,512]{2,1,0:T(8,128)(2,1)S(1)}, bf16[2,32,512]{2,1,0:T(8,128)(2,1)S(1)}, u32[]{:S(2)}, u32[]{:S(2)}) collective-permute-start(bf16[2,32,512]{2,1,0:T(8,128)(2,1)S(1)} %pad_maximum_fusion.refs_0_), channel_id=1, source_target_pairs={{0,2},{2,0},{1,3},{3,1},{4,6},{6,4},{5,7},{7,5},{8,10},{10,8},{9,1... | collective-permute-start | bytes 196616 | tf_op jit(solution)/shard_map/ppermute | solution.py:213
  45.0 4.5 %collective-permute-start.10 = (bf16[2,32,512]{2,1,0:T(8,128)(2,1)S(1)}, bf16[2,32,512]{2,1,0:T(8,128)(2,1)S(1)}, u32[]{:S(2)}, u32[]{:S(2)}) collective-permute-start(bf16[2,32,512]{2,1,0:T(8,128)(2,1)S(1)} %collective-permute-done.6.refs_3_), channel_id=1, source_target_pairs={{0,2},{2,0},{1,3},{3,1},{4,6},{6,4},{5,7},{7,5},{8,10},{10,8},{9,1... | collective-permute-start | bytes 196616 | tf_op jit(solution)/shard_map/ppermute | solution.py:213
  47.4 4.3 %collective-permute-start.8 = (bf16[2,32,512]{2,1,0:T(8,128)(2,1)S(1)}, bf16[2,32,512]{2,1,0:T(8,128)(2,1)S(1)}, u32[]{:S(2)}, u32[]{:S(2)}) collective-permute-start(bf16[2,32,512]{2,1,0:T(8,128)(2,1)S(1)} %collective-permute-done.4.refs_1_), channel_id=1, source_target_pairs={{0,2},{2,0},{1,3},{3,1},{4,6},{6,4},{5,7},{7,5},{8,10},{10,8},{9,1... | collective-permute-start | bytes 196616 | tf_op jit(solution)/shard_map/ppermute | solution.py:213
  49.0 4.3 %collective-permute-start.9 = (bf16[2,32,512]{2,1,0:T(8,128)(2,1)S(1)}, bf16[2,32,512]{2,1,0:T(8,128)(2,1)S(1)}, u32[]{:S(2)}, u32[]{:S(2)}) collective-permute-start(bf16[2,32,512]{2,1,0:T(8,128)(2,1)S(1)} %collective-permute-done.5.refs_2_), channel_id=1, source_target_pairs={{0,2},{2,0},{1,3},{3,1},{4,6},{6,4},{5,7},{7,5},{8,10},{10,8},{9,1... | collective-permute-start | bytes 196616 | tf_op jit(solution)/shard_map/ppermute | solution.py:213
  49.6 5.7 %copy-start.5 = (s32[3]{0:T(128)}, s32[3]{0:T(128)S(1)}, u32[]{:S(2)}) copy-start(s32[3]{0:T(128)S(1)} %pad_add_fusion.place) | copy-start | bytes 40
  55.3 13.2 %copy-start.1 = (f32[4,32,640]{2,1,0:T(8,128)}, f32[4,32,640]{2,1,0:T(8,128)S(1)}, u32[]{:S(2)}) copy-start(f32[4,32,640]{2,1,0:T(8,128)S(1)} %get-tuple-element.12.near) | copy-start | bytes 983044
  55.3 13.1 %collective-permute-start.13 = (f32[4,32,512]{2,1,0:T(8,128)S(1)}, f32[4,32,512]{2,1,0:T(8,128)S(1)}, u32[]{:S(2)}, u32[]{:S(2)}) collective-permute-start(f32[4,32,512]{2,1,0:T(8,128)S(1)} %constant_dynamic-slice_fusion), channel_id=1, source_target_pairs={{0,2},{2,0},{1,3},{3,1},{4,6},{6,4},{5,7},{7,5},{8,10},{10,8},{9,1... | collective-permute-start | bytes 786440 | tf_op jit(solution)/shard_map/ppermute | solution.py:225
  57.4 11.1 %all-to-all-start = ((f32[16,8,128]{2,1,0:T(8,128)}), f32[16,8,128]{2,1,0:T(8,128)S(1)}, u32[]{:S(2)}, u32[]{:S(2)}) async-start(f32[16,8,128]{2,1,0:T(8,128)} %broadcast_in_dim.34), calls=%async_computation | async-start | bytes 131072 | tf_op jit(solution)/shard_map/all_to_all | solution.py:227
  71.2 5.2 %collective-permute-start.14 = (bf16[32,1152]{1,0:T(8,128)(2,1)}, bf16[32,1152]{1,0:T(8,128)(2,1)S(1)}, u32[]{:S(2)}, u32[]{:S(2)}) collective-permute-start(bf16[32,1152]{1,0:T(8,128)(2,1)} %get-tuple-element.14), channel_id=1, source_target_pairs={{0,4},{4,0},{8,12},{12,8},{1,5},{5,1},{9,13},{13,9},{2,6},{6,2},{1... | collective-permute-start | bytes 221192 | tf_op jit(solution)/shard_map/ppermute | solution.py:242
  71.3 9.1 %collective-permute-start.15 = (bf16[32,1152]{1,0:T(8,128)(2,1)}, bf16[32,1152]{1,0:T(8,128)(2,1)S(1)}, u32[]{:S(2)}, u32[]{:S(2)}) collective-permute-start(bf16[32,1152]{1,0:T(8,128)(2,1)} %get-tuple-element.15), channel_id=1, source_target_pairs={{0,8},{4,12},{8,0},{12,4},{1,9},{5,13},{9,1},{13,5},{2,10},{6,14},... | collective-permute-start | bytes 221192 | tf_op jit(solution)/shard_map/ppermute | solution.py:242
  72.3 8.1 %collective-permute-start.16 = (bf16[32,1152]{1,0:T(8,128)(2,1)}, bf16[32,1152]{1,0:T(8,128)(2,1)S(1)}, u32[]{:S(2)}, u32[]{:S(2)}) collective-permute-start(bf16[32,1152]{1,0:T(8,128)(2,1)} %get-tuple-element.16), channel_id=1, source_target_pairs={{0,12},{4,8},{8,4},{12,0},{1,13},{5,9},{9,5},{13,1},{2,14},{6,10},... | collective-permute-start | bytes 221192 | tf_op jit(solution)/shard_map/ppermute | solution.py:242
  (8 other events, 11.0 us)

commit v2 on v1

v2 whole, which is shorter than its diff:
```python
import functools
import math

import jax
import jax.numpy as jnp
from jax import lax
from jax.experimental import pallas as pl
from jax.experimental.pallas import tpu as pltpu
from jax.sharding import PartitionSpec as P

D = 4608
HEAD_DIM = 128
PROMPT = 64
LANES = 128

softcap = 50.0
query_scale = 144.0 ** (-0.5)
TANH_SCALE = query_scale / softcap
EXP2_SCALE = softcap * math.log2(math.e)

CONTRACT_LAST = (((1,), (1,)), ((), ()))
VMEM = pl.BlockSpec(memory_space=pltpu.VMEM)
SMEM = pl.BlockSpec(memory_space=pltpu.SMEM)
HBM = pl.BlockSpec(memory_space=pltpu.HBM)
ANY = pl.BlockSpec(memory_space=pl.ANY)


def xor_pairs(size, step):
    return [(i, i ^ step) for i in range(size)]


def head_value_grad(q, k, g, prob):
    block = LANES
    rows = q.shape[1]
    group = q.shape[2] // HEAD_DIM
    key_pos = lax.broadcasted_iota(jnp.int32, (block, block), 0)
    query_pos = lax.broadcasted_iota(jnp.int32, (block, block), 1)
    keep = jnp.concatenate([key_pos <= query_pos] * group, axis=1)

    def query_block(half, parts, start, column):
        q_block = jnp.concatenate(
            [
                q[half, start : start + block, i * HEAD_DIM : (i + 1) * HEAD_DIM]
                for i in range(group)
            ],
            axis=0,
        )
        total, prompt = None, None
        for key_half, count, diagonal in parts:
            raw = lax.dot_general(
                k[key_half, :count, :], q_block, CONTRACT_LAST, preferred_element_type=jnp.float32
            )
            for low in range(0, count, block):
                e = jnp.exp2(jnp.tanh(raw[low : low + block] * TANH_SCALE) * EXP2_SCALE)
                if diagonal and low == count - block:
                    e = jnp.where(keep, e, 0.0)
                if prompt is None:
                    prompt = e[:PROMPT]
                part = jnp.sum(e.reshape(block // 8, 8, group * block), axis=0)
                total = part if total is None else total + part
        total = jnp.sum(total, axis=0, keepdims=True)
        scaled = (prompt / total).astype(jnp.bfloat16)
        for i in range(group):
            prob[i, :, column : column + block] = scaled[:, i * block : (i + 1) * block]

    for start in range(0, rows, block):
        query_block(0, [(0, start + block, True)], start, start)
    for start in range(0, rows, block):
        query_block(1, [(0, rows, False), (1, start + block, True)], start, rows + start)
    value = None
    for i in range(group):
        for half in range(2):
            term = jnp.dot(
                prob[i, :, half * rows : (half + 1) * rows],
                g[half, :, i * HEAD_DIM : (i + 1) * HEAD_DIM],
                preferred_element_type=jnp.float32,
            )
            value = term if value is None else value + term
    return value.astype(jnp.bfloat16)


def attention_kernel(place, q, k, g, q_far, k_far, g_far, out, q_all, k_all, g_all, prob, done):
    heads = q_all.shape[0]
    seq = place[1]

    def copies(h):
        pairs = []
        for own, far, buffer in ((q, q_far, q_all), (k, k_far, k_all), (g, g_far, g_all)):
            width = buffer.shape[-1]
            at = pl.multiple_of((seq * heads + h) * width, LANES)
            pairs.append((own.at[:, pl.ds(at, width)], buffer.at[h, seq]))
            at = pl.multiple_of(h * width, LANES)
            pairs.append((far.at[:, pl.ds(at, width)], buffer.at[h, 1 - seq]))
        return [
            pltpu.make_async_copy(source, target, done.at[h, i])
            for i, (source, target) in enumerate(pairs)
        ]

    for h in range(heads):
        for copy in copies(h):
            copy.start()

    def step(h, carry):
        for copy in copies(h):
            copy.wait()
        value = head_value_grad(q_all.at[h], k_all.at[h], g_all.at[h], prob)
        at = pl.ds(pl.multiple_of(h * HEAD_DIM, LANES), HEAD_DIM)
        out[0, :, at] = value[: PROMPT // 2]
        out[1, :, at] = value[PROMPT // 2 :]
        return carry

    lax.fori_loop(0, heads, step, 0)


def prompt_value_grad(place, q, k, g, q_far, k_far, g_far):
    rows = q.shape[0]
    heads = k_far.shape[1] // HEAD_DIM
    group = q.shape[1] // k.shape[1]
    width = group * HEAD_DIM
    return pl.pallas_call(
        attention_kernel,
        in_specs=[SMEM] + [HBM] * 3 + [ANY] * 3,
        out_specs=VMEM,
        out_shape=jax.ShapeDtypeStruct((2, PROMPT // 2, heads * HEAD_DIM), jnp.bfloat16),
        scratch_shapes=[
            pltpu.VMEM((heads, 2, rows, width), jnp.bfloat16),
            pltpu.VMEM((heads, 2, rows, HEAD_DIM), jnp.bfloat16),
            pltpu.VMEM((heads, 2, rows, width), jnp.bfloat16),
            pltpu.VMEM((group, PROMPT, 2 * rows), jnp.bfloat16),
            pltpu.SemaphoreType.DMA((heads, 6)),
        ],
        compiler_params=pltpu.CompilerParams(vmem_limit_bytes=56 * 1024 * 1024),
        cost_estimate=pl.CostEstimate(
            flops=heads * group * 9 * rows * rows * HEAD_DIM,
            bytes_accessed=10 * rows * heads * width,
            transcendentals=heads * group * 4 * rows * rows,
        ),
    )(place, q, k, g, q_far, k_far, g_far)


def sibling_kernel(place, *refs, starts):
    count = len(starts)
    sources, targets, buffers = refs[:count], refs[count : 2 * count], refs[2 * count : 3 * count]
    done_in, done_out = refs[3 * count :]
    loads, stores = [], []
    for i, start in enumerate(starts):
        rows, width = targets[i].shape
        row, column = start(place)
        row = row if isinstance(row, int) else pl.multiple_of(row, 16)
        window = sources[i].at[pl.ds(row, rows), pl.ds(pl.multiple_of(column, LANES), width)]
        loads.append(pltpu.make_async_copy(window, buffers[i], done_in.at[i]))
        stores.append(pltpu.make_async_copy(buffers[i], targets[i], done_out.at[i]))
    for load in loads:
        load.start()
    for load, store in zip(loads, stores):
        load.wait()
        store.start()
    for store in stores:
        store.wait()


def cut(place, arrays, starts, shapes):
    return pl.pallas_call(
        functools.partial(sibling_kernel, starts=starts),
        in_specs=[SMEM] + [HBM] * len(arrays),
        out_specs=[ANY] * len(arrays),
        out_shape=[jax.ShapeDtypeStruct(shape, jnp.bfloat16) for shape in shapes],
        scratch_shapes=[pltpu.VMEM(shape, jnp.bfloat16) for shape in shapes]
        + [pltpu.SemaphoreType.DMA((len(arrays),))] * 2,
        compiler_params=pltpu.CompilerParams(vmem_limit_bytes=60 * 1024 * 1024),
    )(place, *arrays)


def grad_kernel(place, *refs, examples, columns):
    near, far = refs[:examples], refs[examples : 2 * examples]
    weight, weight_far_0, weight_far_1, grad, squares = refs[2 * examples :]
    width = grad.shape[-1]
    depth = weight.shape[1] // 2
    rows = grad.shape[1]
    start = pl.multiple_of(place[2] * (columns - width), 16)
    total = None
    for half in range(2):
        offset = pl.multiple_of((place[1] ^ half) * depth, LANES)
        own = jnp.concatenate([ref[half] for ref in near], axis=0)
        other = jnp.concatenate([ref[half] for ref in far], axis=0)
        weight_far = (weight_far_0, weight_far_1)[half]
        term = lax.dot_general(
            own,
            weight[pl.ds(start, width), pl.ds(offset, depth)],
            CONTRACT_LAST,
            preferred_element_type=jnp.float32,
        ) + lax.dot_general(
            other, weight_far[...], CONTRACT_LAST, preferred_element_type=jnp.float32
        )
        total = term if total is None else total + term
    column = lax.broadcasted_iota(jnp.int32, (1, width), 1) + place[2] * (columns - width)
    split = columns // 2
    low = place[2] * split
    counted = (column >= low) & (column < low + split)
    example = lax.broadcasted_iota(jnp.int32, (8, LANES), 0)
    by_example = jnp.zeros((8, LANES), jnp.float32)
    for step in range(examples):
        part = total[step * rows : (step + 1) * rows]
        grad[step] = part
        sums = jnp.sum(jnp.where(counted, part * part, 0.0), axis=0, keepdims=True)
        folded = sums[:, :LANES]
        for at in range(LANES, width, LANES):
            folded = folded + sums[:, at : at + LANES]
        by_example = jnp.where(example == (place[0] ^ step), folded, by_example)
    for device in range(squares.shape[0]):
        squares[device] = by_example


def share_kernel(place, tenant_of, owner_of, norms, near, far, *outs):
    examples, rows, width = near.shape
    rest = far.shape[2]
    outs, scales = outs[:examples], outs[examples]
    norm_sq = jnp.sum(jnp.sum(norms[...], axis=0), axis=1, keepdims=True)
    scales[...] = jnp.broadcast_to(1.0 / jnp.maximum(1.0, jnp.sqrt(norm_sq)), scales.shape)
    scale = [scales[pl.ds(place[0] ^ step, 1), :] for step in range(examples)]
    owner = [owner_of[tenant_of[place[0] ^ step]] for step in range(examples)]
    near_at = pl.multiple_of(place[2] * rest, LANES)
    far_at = pl.multiple_of((1 - place[2]) * width, LANES)
    for k in range(examples):
        factor = [
            scale[step] * (owner[step] == (place[0] ^ k)).astype(jnp.float32)
            for step in range(examples)
        ]
        for ref, base, extent in ((near, near_at, width), (far, far_at, rest)):
            for at in range(0, extent, LANES):
                total = None
                for step in range(examples):
                    term = ref[step, :, at : at + LANES] * factor[step]
                    total = term if total is None else total + term
                to = pl.multiple_of(base + at, LANES)
                outs[k][:, pl.ds(to, LANES)] = total.astype(jnp.bfloat16)


def update_kernel(place, owner_of, counts, *refs, examples):
    shares, noise, out = refs[:examples], refs[examples], refs[examples + 1]
    columns = shares[0].shape[1]
    count = 0
    for slot in range(owner_of.shape[0]):
        count = count + jnp.where(owner_of[slot] == place[0], counts[slot], 0)
    count = count.astype(jnp.float32)
    for step in range(examples):
        at = pl.ds(pl.multiple_of((place[0] ^ step) * columns, LANES), columns)
        share = shares[step][...].astype(jnp.float32)
        out[0, :, at] = (math.sqrt(PROMPT * D) * share + noise[0, :, at]) / count


def tail_by_permutes(
    place, value_grad, weight, weight_far, tenant_of, owner_of, counts, noise, sizes
):
    dp = sizes["dp"]
    columns = weight.shape[0]
    rows = PROMPT // 2
    width = weight_far[0].shape[0]
    rest = columns - width
    near = [value_grad] + [
        lax.ppermute(value_grad, "dp", xor_pairs(dp, step)) for step in range(1, dp)
    ]
    far = [lax.ppermute(block, "tensor", xor_pairs(2, 1)) for block in near]
    devices = dp * sizes["tensor"] * sizes["seq"]
    grad, squares = pl.pallas_call(
        functools.partial(grad_kernel, examples=dp, columns=columns),
        in_specs=[SMEM] + [VMEM] * (2 * dp + 3),
        out_specs=[VMEM, VMEM],
        out_shape=[
            jax.ShapeDtypeStruct((dp, rows, width), jnp.float32),
            jax.ShapeDtypeStruct((devices, 8, LANES), jnp.float32),
        ],
        compiler_params=pltpu.CompilerParams(vmem_limit_bytes=24 * 1024 * 1024),
    )(place, *near, *far, weight, *weight_far)
    sent = lax.dynamic_slice_in_dim(grad, place[2] * (width - rest), rest, axis=2)
    grad_far = lax.ppermute(sent, "tensor", xor_pairs(2, 1))
    norms = lax.all_to_all(
        squares, ("dp", "tensor", "seq"), split_axis=0, concat_axis=0, tiled=True
    )
    shares = pl.pallas_call(
        share_kernel,
        in_specs=[SMEM] * 3 + [VMEM] * 3,
        out_specs=[VMEM] * dp,
        out_shape=[jax.ShapeDtypeStruct((rows, columns), jnp.bfloat16)] * dp,
        scratch_shapes=[pltpu.VMEM((8, LANES), jnp.float32)],
        compiler_params=pltpu.CompilerParams(vmem_limit_bytes=16 * 1024 * 1024),
    )(place, tenant_of, owner_of, norms, grad, grad_far)
    arrived = [shares[0]] + [
        lax.ppermute(shares[step], "dp", xor_pairs(dp, step)) for step in range(1, dp)
    ]
    return pl.pallas_call(
        functools.partial(update_kernel, examples=dp),
        in_specs=[SMEM] * 3 + [VMEM] * (dp + 1),
        out_specs=VMEM,
        out_shape=jax.ShapeDtypeStruct(noise.shape, jnp.float32),
        compiler_params=pltpu.CompilerParams(vmem_limit_bytes=16 * 1024 * 1024),
    )(place, owner_of, counts, *arrived, noise)


def tail_by_collectives(value_grad, weight, tenant_of, owner_of, counts, noise):
    rows = PROMPT // 2
    seq_index, dp_index = lax.axis_index("seq"), lax.axis_index("dp")
    halves = jnp.where(seq_index == 0, value_grad, value_grad[::-1])
    mine = jnp.concatenate([halves[0], halves[1]], axis=1)
    whole = lax.all_gather(mine, "tensor", axis=1, tiled=True)
    whole = lax.all_gather(whole, "dp", axis=0, tiled=True)
    part = lax.all_to_all(weight, "tensor", split_axis=0, concat_axis=1, tiled=True)
    grad = lax.dot_general(whole, part, CONTRACT_LAST, preferred_element_type=jnp.float32)
    grad = grad.reshape(-1, rows, part.shape[0])
    norm_sq = lax.psum(jnp.sum(grad * grad, axis=(1, 2)), ("dp", "tensor", "seq"))
    clipped = grad / jnp.maximum(1.0, jnp.sqrt(norm_sq))[:, None, None]
    slots = jnp.arange(owner_of.shape[0])
    owner_ex = jnp.sum(
        jnp.where(tenant_of[:, None] == slots[None, :], owner_of[None, :], 0), axis=1
    )
    select = (owner_ex[None, :] == slots[:, None]).astype(jnp.float32)
    sums = jnp.einsum("oe,erc->orc", select, clipped, precision=lax.Precision.HIGHEST)
    sums = lax.all_gather(sums, "tensor", axis=2, tiled=True)
    sums = lax.all_to_all(sums, "dp", split_axis=0, concat_axis=2, tiled=True)
    my_count = jnp.sum(jnp.where(owner_of == dp_index, counts, 0)).astype(jnp.float32)
    return (math.sqrt(PROMPT * D) * sums + noise) / my_count


def body(sizes, queries, keys, out_grad, value_weight, tenant_of, owner_of, counts, noise):
    swap = xor_pairs(2, 1)
    place = jnp.stack([lax.axis_index(a) for a in ("dp", "seq", "tensor")]).astype(jnp.int32)
    seq_index = place[1]
    q, k, g = queries[0], keys[0], out_grad[0]

    def other_half(array):
        half = array.shape[1] // 2
        return (lambda at: (0, (1 - at[1]) * half)), (array.shape[0], half)

    arrays, windows = [k, q, g], [other_half(x) for x in (k, q, g)]
    columns = value_weight.shape[0]
    dp = sizes["dp"]
    permutes = sizes["tensor"] == 2 and columns % LANES == 0 and dp in (1, 2, 4, 8)
    if permutes:
        width = -(-columns // (2 * LANES)) * LANES
        depth = value_weight.shape[1] // 2
        arrays.append(value_weight)
        windows.append(
            (lambda at: ((1 - at[2]) * (columns - width), at[1] * depth), (width, depth))
        )
    starts, shapes = zip(*windows)
    sent = cut(place, arrays, starts, shapes)
    k_far, q_far, g_far = (lax.ppermute(x, "seq", swap) for x in sent[:3])
    if permutes:
        weight_far = lax.ppermute(sent[3], "tensor", swap)

    halves = prompt_value_grad(place, q, k, g, q_far, k_far, g_far)
    mine = lax.dynamic_index_in_dim(halves, seq_index, 0, keepdims=False)
    theirs = lax.dynamic_index_in_dim(halves, 1 - seq_index, 0, keepdims=False)
    value_grad = jnp.stack([mine, lax.ppermute(theirs, "seq", swap)])
    if permutes:
        weight_far, value_grad = lax.optimization_barrier((weight_far, value_grad))
        weight_far = (weight_far, lax.ppermute(weight_far, "seq", swap))
        return tail_by_permutes(
            place, value_grad, value_weight, weight_far, tenant_of, owner_of, counts, noise, sizes
        )
    return tail_by_collectives(value_grad, value_weight, tenant_of, owner_of, counts, noise)


def solution(mesh):
    return jax.shard_map(
        functools.partial(body, dict(mesh.shape)),
        mesh=mesh,
        in_specs=(
            P(("group", "dp"), "seq", "tensor"),
            P(("group", "dp"), "seq", "tensor"),
            P(("group", "dp"), "seq", "tensor"),
            P("dp", "tensor"),
            P("group"),
            P("group"),
            P("group"),
            P(("group", "dp"), "seq", None),
        ),
        out_specs=P(("group", "dp"), "seq", None),
        check_vma=False,
    )
```

time: 83.6 us -> 65.9 us (0.79)
  local copies, waits for them, and re-layouts: 15.1 us -> 0.84 us
  waiting for transfers between devices: 28.9 us -> 15.3 us
  blocking collectives: 0 us -> 12.6 us
  starting transfers between devices: 23.2 us -> 18.7 us
  Pallas kernels: 14.3 us -> 17.4 us
    all_to_all x0 -> x1, blocking collectives: none -> 12.6 us  [tail_by_permutes(): lax.all_to_all(squares, ('dp', 'tensor', 'seq'), split_axis=0, concat_axi...]
    ppermute x4, waiting for transfers between devices: 12.6 us -> 4.08 us  [the longest x1 2.28 us: body(): weight_far = lax.ppermute(sent[3], 'tensor', swap)]
    dynamic_slice x5 -> x1, local copies, waits for them, and re-layouts: 7.44 us -> 0.03 us  [tail_by_permutes(): lax.dynamic_slice_in_dim(grad, place[2] * (width - rest), rest, axis=2)]
    all_to_all x1 -> x0, waiting for transfers between devices: 6.21 us -> none  [tail_by_permutes(): lax.all_to_all(jnp.broadcast_to(squares[None], (devices, 8, LANES)).resha...]
    unnamed x28 -> x14, local copies, waits for them, and re-layouts: 5.79 us -> 0.03 us
    all_to_all x1 -> x0, starting transfers between devices: 4.17 us -> none  [tail_by_permutes(): lax.all_to_all(jnp.broadcast_to(squares[None], (devices, 8, LANES)).resha...]
    pallas_call x2 -> x3, Pallas kernels: 10.1 us -> 13.9 us  [the longest x1 9.41 us: prompt_value_grad(): pl.pallas_call(attention_kernel, in_specs=[SMEM] + [HBM] * 3 + [ANY] * 3,...]
  transfers between devices with their start and end apart: 18 -> 17, of which waited for: 9 -> 11; matrix products, arithmetic and copies ran while one was open for 9% -> 1% of each run, Pallas kernels for 10% -> 14%
where the time goes in v2:
time: 65.9 us; the launch traced here: 65.6 us
  starting transfers between devices  18.7 us (28%)
  Pallas kernels  17.4 us (26%)
  waiting for transfers between devices  15.3 us (23%)
  blocking collectives  12.6 us (19%)
  local copies, waits for them, and re-layouts  0.84 us (1%)
    all_to_all x1, blocking collectives, tail_by_permutes(): lax.all_to_all(squares, ('dp', 'tensor', 'seq'), split_axis=0, concat_axi...  12.6 us
    pallas_call x1, Pallas kernels, prompt_value_grad(): pl.pallas_call(attention_kernel, in_specs=[SMEM] + [HBM] * 3 + [ANY] * 3,...  9.41 us
    ppermute x4, starting transfers between devices, tail_by_permutes(): far = [lax.ppermute(block, 'tensor', xor_pairs(2, 1)) for block in near]  5.12 us
    ppermute x3, waiting for transfers between devices, tail_by_permutes(): lax.ppermute(shares[step], 'dp', xor_pairs(dp, step))  4.6 us
    ppermute x3, starting transfers between devices, tail_by_permutes(): lax.ppermute(shares[step], 'dp', xor_pairs(dp, step))  4.45 us
    ppermute x3, starting transfers between devices, tail_by_permutes(): lax.ppermute(value_grad, 'dp', xor_pairs(dp, step))  4.43 us
    ppermute x4, waiting for transfers between devices, tail_by_permutes(): far = [lax.ppermute(block, 'tensor', xor_pairs(2, 1)) for block in near]  3.71 us
    pallas_call x1, Pallas kernels, cut(): pl.pallas_call(functools.partial(sibling_kernel, starts=starts), in_specs...  3.67 us
  transfers between devices with their start and end apart: 17, of which 11 were waited for; matrix products, arithmetic and copies ran while one was open for 1% of the time, Pallas kernels for 14%

profile of v2, /device:TPU:0, one launch (start us, length us, event | category | flops | bytes accessed | tf_op | source)
XLA Modules:
  0.0 65.6 jit_solution(6938410852699630348)
XLA Ops:
  0.6 3.7 %shard_map.82 = (bf16[512,512]{1,0:T(8,128)(2,1)}, bf16[512,1024]{1,0:T(8,128)(2,1)}, bf16[512,1024]{1,0:T(8,128)(2,1)}, bf16[640,512]{1,0:T(8,128)(2,1)}) custom-call(s32[3]{0:T(128)} %pad_add_fusion.place, bf16[512,1024]{1,0:T(8,128)(2,1)} %bitcast.13, bf16[512,2048]{1,0:T(8,128)(2,1)} %bitcast.9, bf16[512,2048]{1,0:T(8,128)(2,1)} %bitcast.11, ...), custom_call_target="tpu_custom_call" | custom-call | tf_op jit(solution)/shard_map/pallas_call | solution.py:163
  5.3 2.6 %collective-permute-start = (bf16[640,512]{1,0:T(8,128)(2,1)}, bf16[640,512]{1,0:T(8,128)(2,1)S(1)}, u32[]{:S(2)}, u32[]{:S(2)}) collective-permute-start(bf16[640,512]{1,0:T(8,128)(2,1)} %get-tuple-element.17), channel_id=1, source_target_pairs={{0,2},{2,0},{1,3},{3,1},{4,6},{6,4},{5,7},{7,5},{8,10},{10,8},{9,1... | collective-permute-start | bytes 1966088 | tf_op jit(solution)/shard_map/ppermute | solution.py:349
  7.9 0.9 %collective-permute-done.2.k_far = bf16[512,512]{1,0:T(8,128)(2,1)S(1)} collective-permute-done((bf16[512,512]{1,0:T(8,128)(2,1)}, bf16[512,512]{1,0:T(8,128)(2,1)S(1)}, u32[]{:S(2)}, u32[]{:S(2)}) %collective-permute-start.2) | collective-permute-done | bytes 524320 | tf_op jit(solution)/shard_map/ppermute | solution.py:347
  8.8 0.9 %collective-permute-done.3.g_far = bf16[512,1024]{1,0:T(8,128)(2,1)} collective-permute-done((bf16[512,1024]{1,0:T(8,128)(2,1)}, bf16[512,1024]{1,0:T(8,128)(2,1)}, u32[]{:S(2)}, u32[]{:S(2)}) %collective-permute-start.3) | collective-permute-done | bytes 1048608 | tf_op jit(solution)/shard_map/ppermute | solution.py:347
  9.7 9.4 %shard_map.83 = bf16[2,32,512]{2,1,0:T(8,128)(2,1)} custom-call(s32[3]{0:T(128)} %pad_add_fusion.place, bf16[512,2048]{1,0:T(8,128)(2,1)} %bitcast.10, bf16[512,1024]{1,0:T(8,128)(2,1)} %bitcast.14, bf16[512,2048]{1,0:T(8,128)(2,1)} %bitcast.12, bf16[512,1024]{1,0:T(8,128)(2,1)} %collective-permute-done.1.q_far, bf16[512,512]{1,0:T(8,128)(2,1)} %copy-done.6, ...), custom_call_target="tpu_custom_call" | custom-call | flops 2415919104 | bytes 5242880 | tf_op jit(solution)/shard_map/pallas_call | solution.py:120
  19.1 0.8 %constant_dynamic-slice_fusion.1 = (bf16[1,32,512]{2,1,0:T(8,128)(2,1)S(1)}, bf16[32,512]{1,0:T(8,128)(2,1)S(1)}) fusion(bf16[2,32,512]{2,1,0:T(8,128)(2,1)} %shard_map.83, s32[]{:T(128)S(6)} %select_n.10, s32[]{:T(128)S(6)} %select_n.11), kind=kLoop, calls=%fused_computation.3 | loop fusion | bytes 131080 | tf_op jit(solution)/shard_map/jit(dynamic_index_in_dim)/dynamic_slice | solution.py:352
  20.3 0.9 %collective-permute-done.4 = bf16[32,512]{1,0:T(8,128)(2,1)S(1)} collective-permute-done((bf16[32,512]{1,0:T(8,128)(2,1)S(1)}, bf16[32,512]{1,0:T(8,128)(2,1)S(1)}, u32[]{:S(2)}, u32[]{:S(2)}) %collective-permute-start.4) | collective-permute-done | bytes 32800 | tf_op jit(solution)/shard_map/ppermute | solution.py:354
  21.1 2.3 %collective-permute-done.refs_9_ = bf16[640,512]{1,0:T(8,128)(2,1)S(1)} collective-permute-done((bf16[640,512]{1,0:T(8,128)(2,1)}, bf16[640,512]{1,0:T(8,128)(2,1)S(1)}, u32[]{:S(2)}, u32[]{:S(2)}) %collective-permute-start) | collective-permute-done | bytes 655392 | tf_op jit(solution)/shard_map/ppermute | solution.py:349
  23.4 2.9 %collective-permute-start.6 = (bf16[2,32,512]{2,1,0:T(8,128)(2,1)S(1)}, bf16[2,32,512]{2,1,0:T(8,128)(2,1)S(1)}, u32[]{:S(2)}, u32[]{:S(2)}) collective-permute-start(bf16[2,32,512]{2,1,0:T(8,128)(2,1)S(1)} %pad_maximum_fusion.refs_0_), channel_id=1, source_target_pairs={{0,8},{4,12},{8,0},{12,4},{1,9},{5,13},{9,1},{13,5},{2,10},{6,14},... | collective-permute-start | bytes 196616 | tf_op jit(solution)/shard_map/ppermute | solution.py:261
  26.3 1.3 %collective-permute-start.7 = (bf16[2,32,512]{2,1,0:T(8,128)(2,1)S(1)}, bf16[2,32,512]{2,1,0:T(8,128)(2,1)S(1)}, u32[]{:S(2)}, u32[]{:S(2)}) collective-permute-start(bf16[2,32,512]{2,1,0:T(8,128)(2,1)S(1)} %pad_maximum_fusion.refs_0_), channel_id=1, source_target_pairs={{0,12},{4,8},{8,4},{12,0},{1,13},{5,9},{9,5},{13,1},{2,14},{6,10},... | collective-permute-start | bytes 196616 | tf_op jit(solution)/shard_map/ppermute | solution.py:261
  27.8 1.5 %collective-permute-start.8 = (bf16[2,32,512]{2,1,0:T(8,128)(2,1)S(1)}, bf16[2,32,512]{2,1,0:T(8,128)(2,1)S(1)}, u32[]{:S(2)}, u32[]{:S(2)}) collective-permute-start(bf16[2,32,512]{2,1,0:T(8,128)(2,1)S(1)} %pad_maximum_fusion.refs_0_), channel_id=1, source_target_pairs={{0,2},{2,0},{1,3},{3,1},{4,6},{6,4},{5,7},{7,5},{8,10},{10,8},{9,1... | collective-permute-start | bytes 196616 | tf_op jit(solution)/shard_map/ppermute | solution.py:263
  29.3 1.3 %collective-permute-done.6.refs_2_ = bf16[2,32,512]{2,1,0:T(8,128)(2,1)S(1)} collective-permute-done((bf16[2,32,512]{2,1,0:T(8,128)(2,1)S(1)}, bf16[2,32,512]{2,1,0:T(8,128)(2,1)S(1)}, u32[]{:S(2)}, u32[]{:S(2)}) %collective-permute-start.6) | collective-permute-done | bytes 65568 | tf_op jit(solution)/shard_map/ppermute | solution.py:261
  30.6 1.6 %collective-permute-start.10 = (bf16[2,32,512]{2,1,0:T(8,128)(2,1)S(1)}, bf16[2,32,512]{2,1,0:T(8,128)(2,1)S(1)}, u32[]{:S(2)}, u32[]{:S(2)}) collective-permute-start(bf16[2,32,512]{2,1,0:T(8,128)(2,1)S(1)} %collective-permute-done.6.refs_2_), channel_id=1, source_target_pairs={{0,2},{2,0},{1,3},{3,1},{4,6},{6,4},{5,7},{7,5},{8,10},{10,8},{9,1... | collective-permute-start | bytes 196616 | tf_op jit(solution)/shard_map/ppermute | solution.py:263
  32.2 0.8 %collective-permute-done.7.refs_3_ = bf16[2,32,512]{2,1,0:T(8,128)(2,1)S(1)} collective-permute-done((bf16[2,32,512]{2,1,0:T(8,128)(2,1)S(1)}, bf16[2,32,512]{2,1,0:T(8,128)(2,1)S(1)}, u32[]{:S(2)}, u32[]{:S(2)}) %collective-permute-start.7) | collective-permute-done | bytes 65568 | tf_op jit(solution)/shard_map/ppermute | solution.py:261
  33.0 1.5 %collective-permute-start.11 = (bf16[2,32,512]{2,1,0:T(8,128)(2,1)S(1)}, bf16[2,32,512]{2,1,0:T(8,128)(2,1)S(1)}, u32[]{:S(2)}, u32[]{:S(2)}) collective-permute-start(bf16[2,32,512]{2,1,0:T(8,128)(2,1)S(1)} %collective-permute-done.7.refs_3_), channel_id=1, source_target_pairs={{0,2},{2,0},{1,3},{3,1},{4,6},{6,4},{5,7},{7,5},{8,10},{10,8},{9,1... | collective-permute-start | bytes 196616 | tf_op jit(solution)/shard_map/ppermute | solution.py:263
  35.6 1.7 %collective-permute-done.11.refs_7_ = bf16[2,32,512]{2,1,0:T(8,128)(2,1)S(1)} collective-permute-done((bf16[2,32,512]{2,1,0:T(8,128)(2,1)S(1)}, bf16[2,32,512]{2,1,0:T(8,128)(2,1)S(1)}, u32[]{:S(2)}, u32[]{:S(2)}) %collective-permute-start.11) | collective-permute-done | bytes 65568 | tf_op jit(solution)/shard_map/ppermute | solution.py:263
  37.3 1.5 %collective-permute-done.9.refs_5_ = bf16[2,32,512]{2,1,0:T(8,128)(2,1)S(1)} collective-permute-done((bf16[2,32,512]{2,1,0:T(8,128)(2,1)S(1)}, bf16[2,32,512]{2,1,0:T(8,128)(2,1)S(1)}, u32[]{:S(2)}, u32[]{:S(2)}) %collective-permute-start.9) | collective-permute-done | bytes 65568 | tf_op jit(solution)/shard_map/ppermute | solution.py:263
  38.8 2.0 %shard_map.84 = (f32[4,32,640]{2,1,0:T(8,128)S(1)}, f32[16,8,128]{2,1,0:T(8,128)S(1)}) custom-call(s32[3]{0:T(128)S(1)} %copy-done.2, bf16[2,32,512]{2,1,0:T(8,128)(2,1)S(1)} %pad_maximum_fusion.refs_0_, bf16[2,32,512]{2,1,0:T(8,128)(2,1)S(1)} %collective-permute-done.5.refs_1_, bf16[2,32,512]{2,1,0:T(8,128)(2,1)S(1)} %collective-permute-done.6.refs_2_, ...), custom_call_target="tpu_custom_call" | custom-call | tf_op jit(solution)/shard_map/pallas_call | solution.py:265
  41.6 12.6 %all_to_all.5.norms = f32[16,8,128]{2,1,0:T(8,128)S(1)} all-to-all(f32[16,8,128]{2,1,0:T(8,128)S(1)} %get-tuple-element.23), channel_id=1, replica_groups=mesh['group'=2,'dp'=4,'tensor'=2,'seq'=2] {'dp','tensor','seq'}, dimensions={0} | all-to-all | bytes 131072 | tf_op jit(solution)/shard_map/all_to_all | solution.py:277
  54.3 0.8 %shard_map.85 = (bf16[32,1152]{1,0:T(8,128)(2,1)S(1)}, bf16[32,1152]{1,0:T(8,128)(2,1)S(1)}, bf16[32,1152]{1,0:T(8,128)(2,1)S(1)}, bf16[32,1152]{1,0:T(8,128)(2,1)S(1)}) custom-call(s32[3]{0:T(128)S(1)} %copy-done.2, s32[4]{0:T(128)S(1)} %copy-done.5, s32[4]{0:T(128)S(1)} %copy-done.3, f32[16,8,128]{2,1,0:T(8,128)S(1)} %all_to_all.5.norms, ...), custom_call_target="tpu_custom_call" | custom-call | tf_op jit(solution)/shard_map/pallas_call | solution.py:280
  55.3 1.0 %collective-permute-start.15 = (bf16[32,1152]{1,0:T(8,128)(2,1)S(1)}, bf16[32,1152]{1,0:T(8,128)(2,1)S(1)}, u32[]{:S(2)}, u32[]{:S(2)}) collective-permute-start(bf16[32,1152]{1,0:T(8,128)(2,1)S(1)} %get-tuple-element.27), channel_id=1, source_target_pairs={{0,8},{4,12},{8,0},{12,4},{1,9},{5,13},{9,1},{13,5},{2,10},{6,14},... | collective-permute-start | bytes 221192 | tf_op jit(solution)/shard_map/ppermute | solution.py:289
  56.3 3.3 %collective-permute-start.16 = (bf16[32,1152]{1,0:T(8,128)(2,1)S(1)}, bf16[32,1152]{1,0:T(8,128)(2,1)S(1)}, u32[]{:S(2)}, u32[]{:S(2)}) collective-permute-start(bf16[32,1152]{1,0:T(8,128)(2,1)S(1)} %get-tuple-element.28), channel_id=1, source_target_pairs={{0,12},{4,8},{8,4},{12,0},{1,13},{5,9},{9,5},{13,1},{2,14},{6,10},... | collective-permute-start | bytes 221192 | tf_op jit(solution)/shard_map/ppermute | solution.py:289
  60.2 3.9 %collective-permute-done.15.refs_2_ = bf16[32,1152]{1,0:T(8,128)(2,1)S(1)} collective-permute-done((bf16[32,1152]{1,0:T(8,128)(2,1)S(1)}, bf16[32,1152]{1,0:T(8,128)(2,1)S(1)}, u32[]{:S(2)}, u32[]{:S(2)}) %collective-permute-start.15) | collective-permute-done | bytes 73760 | tf_op jit(solution)/shard_map/ppermute | solution.py:289
  64.2 1.5 %shard_map.86 = f32[1,32,4608]{2,1,0:T(8,128)} custom-call(s32[3]{0:T(128)S(1)} %copy-done.2, s32[4]{0:T(128)S(1)} %copy-done.3, s32[4]{0:T(128)S(1)} %copy-done.4, bf16[32,1152]{1,0:T(8,128)(2,1)S(1)} %get-tuple-element.25.refs_0_, bf16[32,1152]{1,0:T(8,128)(2,1)S(1)} %collective-permute-done.14.refs_1_, ...), custom_call_target="tpu_custom_call" | custom-call | tf_op jit(solution)/shard_map/pallas_call | solution.py:291
  (34 shorter events, 5.0 us)
Async XLA Ops:
  4.3 4.5 %collective-permute-start.1 = (bf16[512,1024]{1,0:T(8,128)(2,1)}, bf16[512,1024]{1,0:T(8,128)(2,1)}, u32[]{:S(2)}, u32[]{:S(2)}) collective-permute-start(bf16[512,1024]{1,0:T(8,128)(2,1)} %get-tuple-element.18), channel_id=1, source_target_pairs={{0,1},{1,0},{2,3},{3,2},{4,5},{5,4},{6,7},{7,6},{8,9},{9,8},{10,11... | collective-permute-start | bytes 3145736 | tf_op jit(solution)/shard_map/ppermute | solution.py:347
  4.8 4.9 %collective-permute-start.3 = (bf16[512,1024]{1,0:T(8,128)(2,1)}, bf16[512,1024]{1,0:T(8,128)(2,1)}, u32[]{:S(2)}, u32[]{:S(2)}) collective-permute-start(bf16[512,1024]{1,0:T(8,128)(2,1)} %get-tuple-element.20), channel_id=1, source_target_pairs={{0,1},{1,0},{2,3},{3,2},{4,5},{5,4},{6,7},{7,6},{8,9},{9,8},{10,11... | collective-permute-start | bytes 3145736 | tf_op jit(solution)/shard_map/ppermute | solution.py:347
  4.9 3.9 %collective-permute-start.2 = (bf16[512,512]{1,0:T(8,128)(2,1)}, bf16[512,512]{1,0:T(8,128)(2,1)S(1)}, u32[]{:S(2)}, u32[]{:S(2)}) collective-permute-start(bf16[512,512]{1,0:T(8,128)(2,1)} %get-tuple-element.19), channel_id=1, source_target_pairs={{0,1},{1,0},{2,3},{3,2},{4,5},{5,4},{6,7},{7,6},{8,9},{9,8},{10,11... | collective-permute-start | bytes 1572872 | tf_op jit(solution)/shard_map/ppermute | solution.py:347
  5.3 18.1 %collective-permute-start = (bf16[640,512]{1,0:T(8,128)(2,1)}, bf16[640,512]{1,0:T(8,128)(2,1)S(1)}, u32[]{:S(2)}, u32[]{:S(2)}) collective-permute-start(bf16[640,512]{1,0:T(8,128)(2,1)} %get-tuple-element.17), channel_id=1, source_target_pairs={{0,2},{2,0},{1,3},{3,1},{4,6},{6,4},{5,7},{7,5},{8,10},{10,8},{9,1... | collective-permute-start | bytes 1966088 | tf_op jit(solution)/shard_map/ppermute | solution.py:349
  7.9 30.9 %copy-start = (bf16[1152,1024]{1,0:T(8,128)(2,1)S(1)}, bf16[1152,1024]{1,0:T(8,128)(2,1)}, u32[]{:S(2)}) copy-start(bf16[1152,1024]{1,0:T(8,128)(2,1)} %refs_8_.1) | copy-start | bytes 7077892
  7.9 30.9 %copy-start.2 = (s32[3]{0:T(128)S(1)}, s32[3]{0:T(128)}, u32[]{:S(2)}) copy-start(s32[3]{0:T(128)} %pad_add_fusion.place) | copy-start | bytes 40
  8.8 0.9 %copy-start.6 = (bf16[512,512]{1,0:T(8,128)(2,1)}, bf16[512,512]{1,0:T(8,128)(2,1)S(1)}, u32[]{:S(2)}) copy-start(bf16[512,512]{1,0:T(8,128)(2,1)S(1)} %collective-permute-done.2.k_far) | copy-start | bytes 1572868
  19.9 1.2 %collective-permute-start.4 = (bf16[32,512]{1,0:T(8,128)(2,1)S(1)}, bf16[32,512]{1,0:T(8,128)(2,1)S(1)}, u32[]{:S(2)}, u32[]{:S(2)}) collective-permute-start(bf16[32,512]{1,0:T(8,128)(2,1)S(1)} %get-tuple-element.30), channel_id=1, source_target_pairs={{0,1},{1,0},{2,3},{3,2},{4,5},{5,4},{6,7},{7,6},{8,9},{9,8},{10,11... | collective-permute-start | bytes 98312 | tf_op jit(solution)/shard_map/ppermute | solution.py:354
  23.4 15.4 %collective-permute-start.12 = (bf16[640,512]{1,0:T(8,128)(2,1)S(1)}, bf16[640,512]{1,0:T(8,128)(2,1)}, u32[]{:S(2)}, u32[]{:S(2)}) collective-permute-start(bf16[640,512]{1,0:T(8,128)(2,1)S(1)} %collective-permute-done.refs_9_), channel_id=1, source_target_pairs={{0,1},{1,0},{2,3},{3,2},{4,5},{5,4},{6,7},{7,6},{8,9},{9,8},{10,11... | collective-permute-start | bytes 1966088 | tf_op jit(solution)/shard_map/ppermute | solution.py:357
  23.4 7.2 %collective-permute-start.6 = (bf16[2,32,512]{2,1,0:T(8,128)(2,1)S(1)}, bf16[2,32,512]{2,1,0:T(8,128)(2,1)S(1)}, u32[]{:S(2)}, u32[]{:S(2)}) collective-permute-start(bf16[2,32,512]{2,1,0:T(8,128)(2,1)S(1)} %pad_maximum_fusion.refs_0_), channel_id=1, source_target_pairs={{0,8},{4,12},{8,0},{12,4},{1,9},{5,13},{9,1},{13,5},{2,10},{6,14},... | collective-permute-start | bytes 196616 | tf_op jit(solution)/shard_map/ppermute | solution.py:261
  26.3 6.7 %collective-permute-start.7 = (bf16[2,32,512]{2,1,0:T(8,128)(2,1)S(1)}, bf16[2,32,512]{2,1,0:T(8,128)(2,1)S(1)}, u32[]{:S(2)}, u32[]{:S(2)}) collective-permute-start(bf16[2,32,512]{2,1,0:T(8,128)(2,1)S(1)} %pad_maximum_fusion.refs_0_), channel_id=1, source_target_pairs={{0,12},{4,8},{8,4},{12,0},{1,13},{5,9},{9,5},{13,1},{2,14},{6,10},... | collective-permute-start | bytes 196616 | tf_op jit(solution)/shard_map/ppermute | solution.py:261
  27.6 6.9 %collective-permute-start.5 = (bf16[2,32,512]{2,1,0:T(8,128)(2,1)S(1)}, bf16[2,32,512]{2,1,0:T(8,128)(2,1)S(1)}, u32[]{:S(2)}, u32[]{:S(2)}) collective-permute-start(bf16[2,32,512]{2,1,0:T(8,128)(2,1)S(1)} %pad_maximum_fusion.refs_0_), channel_id=1, source_target_pairs={{0,4},{4,0},{8,12},{12,8},{1,5},{5,1},{9,13},{13,9},{2,6},{6,2},{1... | collective-permute-start | bytes 196616 | tf_op jit(solution)/shard_map/ppermute | solution.py:261
  27.8 7.2 %collective-permute-start.8 = (bf16[2,32,512]{2,1,0:T(8,128)(2,1)S(1)}, bf16[2,32,512]{2,1,0:T(8,128)(2,1)S(1)}, u32[]{:S(2)}, u32[]{:S(2)}) collective-permute-start(bf16[2,32,512]{2,1,0:T(8,128)(2,1)S(1)} %pad_maximum_fusion.refs_0_), channel_id=1, source_target_pairs={{0,2},{2,0},{1,3},{3,1},{4,6},{6,4},{5,7},{7,5},{8,10},{10,8},{9,1... | collective-permute-start | bytes 196616 | tf_op jit(solution)/shard_map/ppermute | solution.py:263
  30.6 5.0 %collective-permute-start.10 = (bf16[2,32,512]{2,1,0:T(8,128)(2,1)S(1)}, bf16[2,32,512]{2,1,0:T(8,128)(2,1)S(1)}, u32[]{:S(2)}, u32[]{:S(2)}) collective-permute-start(bf16[2,32,512]{2,1,0:T(8,128)(2,1)S(1)} %collective-permute-done.6.refs_2_), channel_id=1, source_target_pairs={{0,2},{2,0},{1,3},{3,1},{4,6},{6,4},{5,7},{7,5},{8,10},{10,8},{9,1... | collective-permute-start | bytes 196616 | tf_op jit(solution)/shard_map/ppermute | solution.py:263
  33.0 4.3 %collective-permute-start.11 = (bf16[2,32,512]{2,1,0:T(8,128)(2,1)S(1)}, bf16[2,32,512]{2,1,0:T(8,128)(2,1)S(1)}, u32[]{:S(2)}, u32[]{:S(2)}) collective-permute-start(bf16[2,32,512]{2,1,0:T(8,128)(2,1)S(1)} %collective-permute-done.7.refs_3_), channel_id=1, source_target_pairs={{0,2},{2,0},{1,3},{3,1},{4,6},{6,4},{5,7},{7,5},{8,10},{10,8},{9,1... | collective-permute-start | bytes 196616 | tf_op jit(solution)/shard_map/ppermute | solution.py:263
  34.5 4.3 %collective-permute-start.9 = (bf16[2,32,512]{2,1,0:T(8,128)(2,1)S(1)}, bf16[2,32,512]{2,1,0:T(8,128)(2,1)S(1)}, u32[]{:S(2)}, u32[]{:S(2)}) collective-permute-start(bf16[2,32,512]{2,1,0:T(8,128)(2,1)S(1)} %collective-permute-done.5.refs_1_), channel_id=1, source_target_pairs={{0,2},{2,0},{1,3},{3,1},{4,6},{6,4},{5,7},{7,5},{8,10},{10,8},{9,1... | collective-permute-start | bytes 196616 | tf_op jit(solution)/shard_map/ppermute | solution.py:263
  35.0 19.2 %copy-start.3 = (s32[4]{0:T(128)S(1)}, s32[4]{0:T(128)}, u32[]{:S(2)}) copy-start(s32[4]{0:T(128)} %owner_of.3) | copy-start | bytes 52
  35.0 19.2 %copy-start.5 = (s32[4]{0:T(128)S(1)}, s32[4]{0:T(128)}, u32[]{:S(2)}) copy-start(s32[4]{0:T(128)} %tenant_of.1) | copy-start | bytes 52
  35.0 29.1 %copy-start.1 = (f32[1,32,4608]{2,1,0:T(8,128)S(1)}, f32[1,32,4608]{2,1,0:T(8,128)}, u32[]{:S(2)}) copy-start(f32[1,32,4608]{2,1,0:T(8,128)} %refs_4_.1) | copy-start | bytes 1769476
  35.0 29.1 %copy-start.4 = (s32[4]{0:T(128)S(1)}, s32[4]{0:T(128)}, u32[]{:S(2)}) copy-start(s32[4]{0:T(128)} %counts.1) | copy-start | bytes 52
  40.8 13.4 %collective-permute-start.13 = (f32[4,32,512]{2,1,0:T(8,128)S(1)}, f32[4,32,512]{2,1,0:T(8,128)S(1)}, u32[]{:S(2)}, u32[]{:S(2)}) collective-permute-start(f32[4,32,512]{2,1,0:T(8,128)S(1)} %constant_dynamic-slice_fusion), channel_id=1, source_target_pairs={{0,2},{2,0},{1,3},{3,1},{4,6},{6,4},{5,7},{7,5},{8,10},{10,8},{9,1... | collective-permute-start | bytes 786440 | tf_op jit(solution)/shard_map/ppermute | solution.py:276
  55.1 5.1 %collective-permute-start.14 = (bf16[32,1152]{1,0:T(8,128)(2,1)S(1)}, bf16[32,1152]{1,0:T(8,128)(2,1)S(1)}, u32[]{:S(2)}, u32[]{:S(2)}) collective-permute-start(bf16[32,1152]{1,0:T(8,128)(2,1)S(1)} %get-tuple-element.26), channel_id=1, source_target_pairs={{0,4},{4,0},{8,12},{12,8},{1,5},{5,1},{9,13},{13,9},{2,6},{6,2},{1... | collective-permute-start | bytes 221192 | tf_op jit(solution)/shard_map/ppermute | solution.py:289
  55.3 8.9 %collective-permute-start.15 = (bf16[32,1152]{1,0:T(8,128)(2,1)S(1)}, bf16[32,1152]{1,0:T(8,128)(2,1)S(1)}, u32[]{:S(2)}, u32[]{:S(2)}) collective-permute-start(bf16[32,1152]{1,0:T(8,128)(2,1)S(1)} %get-tuple-element.27), channel_id=1, source_target_pairs={{0,8},{4,12},{8,0},{12,4},{1,9},{5,13},{9,1},{13,5},{2,10},{6,14},... | collective-permute-start | bytes 221192 | tf_op jit(solution)/shard_map/ppermute | solution.py:289
  56.3 7.9 %collective-permute-start.16 = (bf16[32,1152]{1,0:T(8,128)(2,1)S(1)}, bf16[32,1152]{1,0:T(8,128)(2,1)S(1)}, u32[]{:S(2)}, u32[]{:S(2)}) collective-permute-start(bf16[32,1152]{1,0:T(8,128)(2,1)S(1)} %get-tuple-element.28), channel_id=1, source_target_pairs={{0,12},{4,8},{8,4},{12,0},{1,13},{5,9},{9,5},{13,1},{2,14},{6,10},... | collective-permute-start | bytes 221192 | tf_op jit(solution)/shard_map/ppermute | solution.py:289

commit v3 on v2

v3 whole, which is shorter than its diff:
```python
import functools
import math

import jax
import jax.numpy as jnp
from jax import lax
from jax.experimental import pallas as pl
from jax.experimental.pallas import tpu as pltpu
from jax.sharding import PartitionSpec as P

D = 4608
HEAD_DIM = 128
PROMPT = 64
LANES = 128

softcap = 50.0
query_scale = 144.0 ** (-0.5)
TANH_SCALE = query_scale / softcap
EXP2_SCALE = softcap * math.log2(math.e)

PARTIAL_TYPE = jnp.float32


def GROUPS(dp):
    return [[step] for step in range(dp)]


CONTRACT_LAST = (((1,), (1,)), ((), ()))
VMEM = pl.BlockSpec(memory_space=pltpu.VMEM)
SMEM = pl.BlockSpec(memory_space=pltpu.SMEM)
HBM = pl.BlockSpec(memory_space=pltpu.HBM)
ANY = pl.BlockSpec(memory_space=pl.ANY)


def xor_pairs(size, step):
    return [(i, i ^ step) for i in range(size)]


def head_value_grad(q, k, g, prob):
    block = LANES
    rows = q.shape[1]
    group = q.shape[2] // HEAD_DIM
    key_pos = lax.broadcasted_iota(jnp.int32, (block, block), 0)
    query_pos = lax.broadcasted_iota(jnp.int32, (block, block), 1)
    keep = jnp.concatenate([key_pos <= query_pos] * group, axis=1)

    def query_block(half, parts, start, column):
        q_block = jnp.concatenate(
            [
                q[half, start : start + block, i * HEAD_DIM : (i + 1) * HEAD_DIM]
                for i in range(group)
            ],
            axis=0,
        )
        total, prompt = None, None
        for key_half, count, diagonal in parts:
            raw = lax.dot_general(
                k[key_half, :count, :], q_block, CONTRACT_LAST, preferred_element_type=jnp.float32
            )
            for low in range(0, count, block):
                e = jnp.exp2(jnp.tanh(raw[low : low + block] * TANH_SCALE) * EXP2_SCALE)
                if diagonal and low == count - block:
                    e = jnp.where(keep, e, 0.0)
                if prompt is None:
                    prompt = e[:PROMPT]
                part = jnp.sum(e.reshape(block // 8, 8, group * block), axis=0)
                total = part if total is None else total + part
        total = jnp.sum(total, axis=0, keepdims=True)
        scaled = (prompt / total).astype(jnp.bfloat16)
        for i in range(group):
            prob[i, :, column : column + block] = scaled[:, i * block : (i + 1) * block]

    for start in range(0, rows, block):
        query_block(0, [(0, start + block, True)], start, start)
    for start in range(0, rows, block):
        query_block(1, [(0, rows, False), (1, start + block, True)], start, rows + start)
    value = None
    for i in range(group):
        for half in range(2):
            term = jnp.dot(
                prob[i, :, half * rows : (half + 1) * rows],
                g[half, :, i * HEAD_DIM : (i + 1) * HEAD_DIM],
                preferred_element_type=jnp.float32,
            )
            value = term if value is None else value + term
    return value.astype(jnp.bfloat16)


def attention_kernel(place, q, k, g, q_far, k_far, g_far, mine, theirs, q_all, k_all, g_all, prob, done):
    heads = q_all.shape[0]
    seq = place[1]

    def copies(h):
        pairs = []
        for own, far, buffer in ((q, q_far, q_all), (k, k_far, k_all), (g, g_far, g_all)):
            width = buffer.shape[-1]
            at = pl.multiple_of((seq * heads + h) * width, LANES)
            pairs.append((own.at[:, pl.ds(at, width)], buffer.at[h, seq]))
            at = pl.multiple_of(h * width, LANES)
            pairs.append((far.at[:, pl.ds(at, width)], buffer.at[h, 1 - seq]))
        return [
            pltpu.make_async_copy(source, target, done.at[h, i])
            for i, (source, target) in enumerate(pairs)
        ]

    for h in range(heads):
        for copy in copies(h):
            copy.start()

    def step(h, carry):
        for copy in copies(h):
            copy.wait()
        value = head_value_grad(q_all.at[h], k_all.at[h], g_all.at[h], prob)
        at = pl.ds(pl.multiple_of(h * HEAD_DIM, LANES), HEAD_DIM)
        low, high = value[: PROMPT // 2], value[PROMPT // 2 :]
        mine[:, at] = jnp.where(seq == 0, low, high)
        theirs[:, at] = jnp.where(seq == 0, high, low)
        return carry

    lax.fori_loop(0, heads, step, 0)


def prompt_value_grad(place, q, k, g, q_far, k_far, g_far):
    rows = q.shape[0]
    heads = k_far.shape[1] // HEAD_DIM
    group = q.shape[1] // k.shape[1]
    width = group * HEAD_DIM
    return pl.pallas_call(
        attention_kernel,
        in_specs=[SMEM] + [HBM] * 3 + [ANY] * 3,
        out_specs=[VMEM] * 2,
        out_shape=[jax.ShapeDtypeStruct((PROMPT // 2, heads * HEAD_DIM), jnp.bfloat16)] * 2,
        scratch_shapes=[
            pltpu.VMEM((heads, 2, rows, width), jnp.bfloat16),
            pltpu.VMEM((heads, 2, rows, HEAD_DIM), jnp.bfloat16),
            pltpu.VMEM((heads, 2, rows, width), jnp.bfloat16),
            pltpu.VMEM((group, PROMPT, 2 * rows), jnp.bfloat16),
            pltpu.SemaphoreType.DMA((heads, 6)),
        ],
        compiler_params=pltpu.CompilerParams(vmem_limit_bytes=24 * 1024 * 1024),
        cost_estimate=pl.CostEstimate(
            flops=heads * group * 9 * rows * rows * HEAD_DIM,
            bytes_accessed=10 * rows * heads * width,
            transcendentals=heads * group * 4 * rows * rows,
        ),
    )(place, q, k, g, q_far, k_far, g_far)


def sibling_kernel(place, *refs, starts):
    count = len(starts)
    sources, targets, done = refs[:count], refs[count : 2 * count], refs[2 * count]
    copies = []
    for i, start in enumerate(starts):
        rows, width = targets[i].shape
        row, column = start(place)
        window = sources[i].at[pl.ds(row, rows), pl.ds(pl.multiple_of(column, LANES), width)]
        copies.append(pltpu.make_async_copy(window, targets[i], done.at[i]))
    for copy in copies:
        copy.start()
    for copy in copies:
        copy.wait()


def cut(place, arrays, starts, shapes):
    return pl.pallas_call(
        functools.partial(sibling_kernel, starts=starts),
        in_specs=[SMEM] + [HBM] * len(arrays),
        out_specs=[VMEM] * len(arrays),
        out_shape=[jax.ShapeDtypeStruct(shape, jnp.bfloat16) for shape in shapes],
        scratch_shapes=[pltpu.SemaphoreType.DMA((len(arrays),))],
        compiler_params=pltpu.CompilerParams(vmem_limit_bytes=16 * 1024 * 1024),
    )(place, *arrays)


def partial_kernel(*refs):
    blocks, weight, out = refs[:-2], refs[-2], refs[-1]
    rows = blocks[0].shape[0]
    total = lax.dot_general(
        jnp.concatenate([block[...] for block in blocks], axis=0),
        weight[...],
        CONTRACT_LAST,
        preferred_element_type=jnp.float32,
    )
    for i in range(len(blocks)):
        out[i] = total[i * rows : (i + 1) * rows].astype(out.dtype)


def combine_kernel(place, near, far, grad, squares, *, steps):
    example = lax.broadcasted_iota(jnp.int32, squares.shape, 0)
    by_example = jnp.zeros(squares.shape, jnp.float32)
    for i, step in enumerate(steps):
        folded = None
        for at in range(0, near.shape[2], LANES):
            part = near[i, :, at : at + LANES].astype(jnp.float32)
            part = part + far[i, :, at : at + LANES].astype(jnp.float32)
            grad[i, :, at : at + LANES] = part
            folded = part * part if folded is None else folded + part * part
        folded = jnp.sum(folded, axis=0, keepdims=True)
        by_example = jnp.where(example == (place[0] ^ step), folded, by_example)
    squares[...] = by_example


def share_kernel(place, tenant_of, owner_of, *refs, groups):
    examples = sum(len(steps) for steps in groups)
    norms, grads = refs[:examples], refs[examples : examples + len(groups)]
    outs, scales = refs[examples + len(groups) : -1], refs[-1]
    norm_sq = norms[0][...]
    for other in norms[1:]:
        norm_sq = norm_sq + other[...]
    norm_sq = jnp.sum(norm_sq, axis=1, keepdims=True)
    scales[...] = jnp.broadcast_to(1.0 / jnp.maximum(1.0, jnp.sqrt(norm_sq)), scales.shape)
    scale = [scales[pl.ds(place[0] ^ step, 1), :] for step in range(examples)]
    owner = [owner_of[tenant_of[place[0] ^ step]] for step in range(examples)]
    for k in range(examples):
        factor = [
            scale[step] * (owner[step] == (place[0] ^ k)).astype(jnp.float32)
            for step in range(examples)
        ]
        for at in range(0, outs[k].shape[1], LANES):
            total = None
            for ref, steps in zip(grads, groups):
                for i, step in enumerate(steps):
                    term = ref[i, :, at : at + LANES] * factor[step]
                    total = term if total is None else total + term
            outs[k][:, at : at + LANES] = total.astype(jnp.bfloat16)


def update_kernel(place, owner_of, counts, *refs, examples):
    shares, noise, out = refs[:examples], refs[examples], refs[examples + 1]
    columns = shares[0].shape[1]
    count = 0
    for slot in range(owner_of.shape[0]):
        count = count + jnp.where(owner_of[slot] == place[0], counts[slot], 0)
    count = count.astype(jnp.float32)
    for step in range(examples):
        at = pl.ds(pl.multiple_of((place[0] ^ step) * columns, LANES), columns)
        share = shares[step][...].astype(jnp.float32)
        out[0, :, at] = (math.sqrt(PROMPT * D) * share + noise[0, :, at]) / count


def to_dp(array, dp):
    return [array] + [lax.ppermute(array, "dp", xor_pairs(dp, step)) for step in range(1, dp)]


def tail_by_permutes(place, value_grad, weight, tenant_of, owner_of, counts, noise, sizes):
    dp = sizes["dp"]
    columns = weight.shape[0]
    rows = PROMPT // 2
    swap = xor_pairs(2, 1)
    small = pltpu.CompilerParams(vmem_limit_bytes=16 * 1024 * 1024)
    blocks = to_dp(value_grad, dp)
    groups = GROUPS(dp)
    grads, squares = [], None
    for steps in groups:
        shape = (len(steps), rows, columns)
        near = pl.pallas_call(
            partial_kernel,
            in_specs=[VMEM] * (len(steps) + 1),
            out_specs=VMEM,
            out_shape=jax.ShapeDtypeStruct(shape, PARTIAL_TYPE),
            compiler_params=small,
            cost_estimate=pl.CostEstimate(
                flops=2 * len(steps) * rows * weight.size,
                bytes_accessed=2 * weight.size,
                transcendentals=0,
            ),
        )(*[blocks[step] for step in steps], weight)
        far = lax.ppermute(near, "tensor", swap)
        grad, square = pl.pallas_call(
            functools.partial(combine_kernel, steps=steps),
            in_specs=[SMEM] + [VMEM] * 2,
            out_specs=[VMEM] * 2,
            out_shape=[
                jax.ShapeDtypeStruct(shape, jnp.float32),
                jax.ShapeDtypeStruct((8, LANES), jnp.float32),
            ],
            compiler_params=small,
        )(place, near, far)
        grads.append(grad)
        squares = square if squares is None else squares + square
    norms = to_dp(squares + lax.ppermute(squares, "seq", swap), dp)
    shares = pl.pallas_call(
        functools.partial(share_kernel, groups=groups),
        in_specs=[SMEM] * 3 + [VMEM] * (dp + len(groups)),
        out_specs=[VMEM] * dp,
        out_shape=[jax.ShapeDtypeStruct((rows, columns), jnp.bfloat16)] * dp,
        scratch_shapes=[pltpu.VMEM((8, LANES), jnp.float32)],
        compiler_params=small,
    )(place, tenant_of, owner_of, *norms, *grads)
    arrived = [shares[0]] + [
        lax.ppermute(shares[step], "dp", xor_pairs(dp, step)) for step in range(1, dp)
    ]
    return pl.pallas_call(
        functools.partial(update_kernel, examples=dp),
        in_specs=[SMEM] * 3 + [VMEM] * (dp + 1),
        out_specs=VMEM,
        out_shape=jax.ShapeDtypeStruct(noise.shape, jnp.float32),
        compiler_params=small,
    )(place, owner_of, counts, *arrived, noise)


def tail_by_collectives(value_grad, weight, tenant_of, owner_of, counts, noise):
    rows = PROMPT // 2
    dp_index = lax.axis_index("dp")
    whole = lax.all_gather(value_grad, "tensor", axis=1, tiled=True)
    whole = lax.all_gather(whole, "dp", axis=0, tiled=True)
    part = lax.all_to_all(weight, "tensor", split_axis=0, concat_axis=1, tiled=True)
    grad = lax.dot_general(whole, part, CONTRACT_LAST, preferred_element_type=jnp.float32)
    grad = grad.reshape(-1, rows, part.shape[0])
    norm_sq = lax.psum(jnp.sum(grad * grad, axis=(1, 2)), ("dp", "tensor", "seq"))
    clipped = grad / jnp.maximum(1.0, jnp.sqrt(norm_sq))[:, None, None]
    slots = jnp.arange(owner_of.shape[0])
    owner_ex = jnp.sum(
        jnp.where(tenant_of[:, None] == slots[None, :], owner_of[None, :], 0), axis=1
    )
    select = (owner_ex[None, :] == slots[:, None]).astype(jnp.float32)
    sums = jnp.einsum("oe,erc->orc", select, clipped, precision=lax.Precision.HIGHEST)
    sums = lax.all_gather(sums, "tensor", axis=2, tiled=True)
    sums = lax.all_to_all(sums, "dp", split_axis=0, concat_axis=2, tiled=True)
    my_count = jnp.sum(jnp.where(owner_of == dp_index, counts, 0)).astype(jnp.float32)
    return (math.sqrt(PROMPT * D) * sums + noise) / my_count


def body(sizes, queries, keys, out_grad, value_weight, tenant_of, owner_of, counts, noise):
    swap = xor_pairs(2, 1)
    place = jnp.stack([lax.axis_index(a) for a in ("dp", "seq", "tensor")]).astype(jnp.int32)
    seq_index = place[1]
    q, k, g = (
        pltpu.with_memory_space_constraint(x[0], pltpu.HBM) for x in (queries, keys, out_grad)
    )

    def other_half(array):
        half = array.shape[1] // 2
        return (lambda at: (0, (1 - at[1]) * half)), (array.shape[0], half)

    starts, shapes = zip(*[other_half(x) for x in (k, q, g)])
    k_far, q_far, g_far = (
        lax.ppermute(x, "seq", swap) for x in cut(place, (k, q, g), starts, shapes)
    )
    mine, theirs = prompt_value_grad(place, q, k, g, q_far, k_far, g_far)
    other = lax.ppermute(theirs, "seq", swap)
    first = seq_index == 0
    value_grad = jnp.concatenate(
        [jnp.where(first, mine, other), jnp.where(first, other, mine)], axis=1
    )
    aligned = value_weight.shape[0] % LANES == 0 and sizes["dp"] in (1, 2, 4, 8)
    if sizes["tensor"] == 2 and aligned:
        return tail_by_permutes(
            place, value_grad, value_weight, tenant_of, owner_of, counts, noise, sizes
        )
    return tail_by_collectives(value_grad, value_weight, tenant_of, owner_of, counts, noise)


def solution(mesh):
    return jax.shard_map(
        functools.partial(body, dict(mesh.shape)),
        mesh=mesh,
        in_specs=(
            P(("group", "dp"), "seq", "tensor"),
            P(("group", "dp"), "seq", "tensor"),
            P(("group", "dp"), "seq", "tensor"),
            P("dp", "tensor"),
            P("group"),
            P("group"),
            P("group"),
            P(("group", "dp"), "seq", None),
        ),
        out_specs=P(("group", "dp"), "seq", None),
        check_vma=False,
    )
```

time: 65.9 us -> 59.2 us (0.90)
  blocking collectives: 12.6 us -> 0 us
  waiting for transfers between devices: 15.3 us -> 19.5 us
  starting transfers between devices: 18.7 us -> 20.9 us
  Pallas kernels: 17.4 us -> 18.4 us
  local copies, waits for them, and re-layouts: 0.84 us -> 0.02 us
    all_to_all x1 -> x0, blocking collectives: 12.6 us -> none  [tail_by_permutes(): lax.all_to_all(squares, ('dp', 'tensor', 'seq'), split_axis=0, concat_axi...]
    ppermute x14 -> x15, waiting for transfers between devices: 10.7 us -> 15.6 us  [the longest x4 4.97 us: tail_by_permutes(): far = lax.ppermute(near, 'tensor', swap)]
    pallas_call x2 -> x9, Pallas kernels: 2.88 us -> 6.17 us  [the longest x4 3.06 us: tail_by_permutes(): pl.pallas_call(partial_kernel, in_specs=[VMEM] * (len(steps) + 1), out_sp...]
    ppermute x14 -> x15, starting transfers between devices: 14.3 us -> 16.5 us  [the longest x6 10 us: to_dp(): lax.ppermute(array, 'dp', xor_pairs(dp, step))]
    pallas_call x1, Pallas kernels: 3.67 us -> 2.28 us  [cut(): pl.pallas_call(functools.partial(sibling_kernel, starts=starts), in_specs...]
    pallas_call x1, Pallas kernels: 9.41 us -> 8.47 us  [prompt_value_grad(): pl.pallas_call(attention_kernel, in_specs=[SMEM] + [HBM] * 3 + [ANY] * 3,...]
    dynamic_slice x2 -> x0, local copies, waits for them, and re-layouts: 0.82 us -> none  [the longest x1 0.79 us: body(): mine = lax.dynamic_index_in_dim(halves, seq_index, 0, keepdims=False)]
    ppermute x3, waiting for transfers between devices: 4.6 us -> 3.92 us  [tail_by_permutes(): lax.ppermute(shares[step], 'dp', xor_pairs(dp, step))]
  transfers between devices with their start and end apart: 17 -> 18, of which waited for: 11 -> 11; matrix products, arithmetic and copies ran while one was open for 1% -> 0% of each run, Pallas kernels for 14% -> 8%
where the time goes in v3:
time: 59.2 us; the launch traced here: 59.1 us
  starting transfers between devices  20.9 us (35%)
  waiting for transfers between devices  19.5 us (33%)
  Pallas kernels  18.4 us (31%)
    ppermute x6, starting transfers between devices, to_dp(): lax.ppermute(array, 'dp', xor_pairs(dp, step))  10 us
    pallas_call x1, Pallas kernels, prompt_value_grad(): pl.pallas_call(attention_kernel, in_specs=[SMEM] + [HBM] * 3 + [ANY] * 3,...  8.47 us
    ppermute x4, waiting for transfers between devices, tail_by_permutes(): far = lax.ppermute(near, 'tensor', swap)  4.97 us
    ppermute x4, starting transfers between devices, tail_by_permutes(): far = lax.ppermute(near, 'tensor', swap)  4.89 us
    ppermute x6, waiting for transfers between devices, to_dp(): lax.ppermute(array, 'dp', xor_pairs(dp, step))  4.59 us
    ppermute x3, starting transfers between devices, tail_by_permutes(): lax.ppermute(shares[step], 'dp', xor_pairs(dp, step))  4.44 us
    ppermute x3, waiting for transfers between devices, body(): lax.ppermute(x, 'seq', swap)  4.03 us
    ppermute x3, waiting for transfers between devices, tail_by_permutes(): lax.ppermute(shares[step], 'dp', xor_pairs(dp, step))  3.92 us
  transfers between devices with their start and end apart: 18, of which 11 were waited for; matrix products, arithmetic and copies ran while one was open for 0% of the time, Pallas kernels for 8%

profile of v3, /device:TPU:0, one launch (start us, length us, event | category | flops | bytes accessed | tf_op | source)
XLA Modules:
  0.0 59.1 jit_solution(15546571516302910049)
XLA Ops:
  0.1 2.3 %shard_map.82 = (bf16[512,512]{1,0:T(8,128)(2,1)S(1)}, bf16[512,1024]{1,0:T(8,128)(2,1)S(1)}, bf16[512,1024]{1,0:T(8,128)(2,1)S(1)}) custom-call(s32[3]{0:T(128)S(1)} %pad_add_fusion.place, bf16[512,1024]{1,0:T(8,128)(2,1)} %bitcast.10, bf16[512,2048]{1,0:T(8,128)(2,1)} %bitcast.6, bf16[512,2048]{1,0:T(8,128)(2,1)} %bitcast.8), custom_call_target="tpu_custom_call" | custom-call | tf_op jit(solution)/shard_map/pallas_call | solution.py:165
  3.4 4.0 %collective-permute-done.1.k_far = bf16[512,512]{1,0:T(8,128)(2,1)S(1)} collective-permute-done((bf16[512,512]{1,0:T(8,128)(2,1)S(1)}, bf16[512,512]{1,0:T(8,128)(2,1)S(1)}, u32[]{:S(2)}, u32[]{:S(2)}) %collective-permute-start.1) | collective-permute-done | bytes 524320 | tf_op jit(solution)/shard_map/ppermute | solution.py:338
  7.4 8.5 %shard_map.83 = (bf16[32,512]{1,0:T(8,128)(2,1)S(1)}, bf16[32,512]{1,0:T(8,128)(2,1)S(1)}) custom-call(s32[3]{0:T(128)S(1)} %pad_add_fusion.place, bf16[512,2048]{1,0:T(8,128)(2,1)} %bitcast.7, bf16[512,1024]{1,0:T(8,128)(2,1)} %bitcast.11, bf16[512,2048]{1,0:T(8,128)(2,1)} %bitcast.9, bf16[512,1024]{1,0:T(8,128)(2,1)S(1)} %collective-permute-done.q_far, ...), custom_call_target="tpu_custom_call" | custom-call | flops 2415919104 | bytes 5242880 | tf_op jit(solution)/shard_map/pallas_call | solution.py:128
  16.3 0.9 %collective-permute-done.3 = bf16[32,512]{1,0:T(8,128)(2,1)S(1)} collective-permute-done((bf16[32,512]{1,0:T(8,128)(2,1)S(1)}, bf16[32,512]{1,0:T(8,128)(2,1)S(1)}, u32[]{:S(2)}, u32[]{:S(2)}) %collective-permute-start.3) | collective-permute-done | bytes 32800 | tf_op jit(solution)/shard_map/ppermute | solution.py:341
  17.2 5.0 %collective-permute-start.9 = (bf16[32,1024]{1,0:T(8,128)(2,1)S(1)}, bf16[32,1024]{1,0:T(8,128)(2,1)S(1)}, u32[]{:S(2)}, u32[]{:S(2)}) collective-permute-start(bf16[32,1024]{1,0:T(8,128)(2,1)S(1)} %pad_maximum_fusion.refs_0_), channel_id=1, source_target_pairs={{0,12},{4,8},{8,4},{12,0},{1,13},{5,9},{9,5},{13,1},{2,14},{6,10},... | collective-permute-start | bytes 196616 | tf_op jit(solution)/shard_map/ppermute | solution.py:242
  22.9 0.8 %shard_map.84.near = f32[1,32,1152]{2,1,0:T(8,128)S(1)} custom-call(bf16[32,1024]{1,0:T(8,128)(2,1)S(1)} %pad_maximum_fusion.refs_0_, bf16[1152,1024]{1,0:T(8,128)(2,1)S(1)} %copy-done), custom_call_target="tpu_custom_call" | custom-call | flops 75497472 | bytes 2359296 | tf_op jit(solution)/shard_map/pallas_call | solution.py:256
  23.7 1.6 %collective-permute-start.4 = (f32[1,32,1152]{2,1,0:T(8,128)S(1)}, f32[1,32,1152]{2,1,0:T(8,128)S(1)}, u32[]{:S(2)}, u32[]{:S(2)}) collective-permute-start(f32[1,32,1152]{2,1,0:T(8,128)S(1)} %shard_map.84.near), channel_id=1, source_target_pairs={{0,2},{2,0},{1,3},{3,1},{4,6},{6,4},{5,7},{7,5},{8,10},{10,8},{9,1... | collective-permute-start | bytes 442376 | tf_op jit(solution)/shard_map/ppermute | solution.py:268
  25.3 0.8 %shard_map.90.near = f32[1,32,1152]{2,1,0:T(8,128)S(1)} custom-call(bf16[32,1024]{1,0:T(8,128)(2,1)S(1)} %collective-permute-done.9.refs_0_, bf16[1152,1024]{1,0:T(8,128)(2,1)S(1)} %copy-done), custom_call_target="tpu_custom_call" | custom-call | flops 75497472 | bytes 2359296 | tf_op jit(solution)/shard_map/pallas_call | solution.py:256
  26.1 1.1 %collective-permute-start.10 = (f32[1,32,1152]{2,1,0:T(8,128)S(1)}, f32[1,32,1152]{2,1,0:T(8,128)S(1)}, u32[]{:S(2)}, u32[]{:S(2)}) collective-permute-start(f32[1,32,1152]{2,1,0:T(8,128)S(1)} %shard_map.90.near), channel_id=1, source_target_pairs={{0,2},{2,0},{1,3},{3,1},{4,6},{6,4},{5,7},{7,5},{8,10},{10,8},{9,1... | collective-permute-start | bytes 442376 | tf_op jit(solution)/shard_map/ppermute | solution.py:268
  27.2 0.9 %collective-permute-done.7.refs_0_ = bf16[32,1024]{1,0:T(8,128)(2,1)S(1)} collective-permute-done((bf16[32,1024]{1,0:T(8,128)(2,1)S(1)}, bf16[32,1024]{1,0:T(8,128)(2,1)S(1)}, u32[]{:S(2)}, u32[]{:S(2)}) %collective-permute-start.7) | collective-permute-done | bytes 65568 | tf_op jit(solution)/shard_map/ppermute | solution.py:242
  28.9 1.6 %collective-permute-start.8 = (f32[1,32,1152]{2,1,0:T(8,128)S(1)}, f32[1,32,1152]{2,1,0:T(8,128)S(1)}, u32[]{:S(2)}, u32[]{:S(2)}) collective-permute-start(f32[1,32,1152]{2,1,0:T(8,128)S(1)} %shard_map.88.near), channel_id=1, source_target_pairs={{0,2},{2,0},{1,3},{3,1},{4,6},{6,4},{5,7},{7,5},{8,10},{10,8},{9,1... | collective-permute-start | bytes 442376 | tf_op jit(solution)/shard_map/ppermute | solution.py:268
  33.6 2.6 %collective-permute-done.8.far = f32[1,32,1152]{2,1,0:T(8,128)S(1)} collective-permute-done((f32[1,32,1152]{2,1,0:T(8,128)S(1)}, f32[1,32,1152]{2,1,0:T(8,128)S(1)}, u32[]{:S(2)}, u32[]{:S(2)}) %collective-permute-start.8) | collective-permute-done | bytes 147488 | tf_op jit(solution)/shard_map/ppermute | solution.py:268
  36.7 1.8 %collective-permute-done.6.far = f32[1,32,1152]{2,1,0:T(8,128)S(1)} collective-permute-done((f32[1,32,1152]{2,1,0:T(8,128)S(1)}, f32[1,32,1152]{2,1,0:T(8,128)S(1)}, u32[]{:S(2)}, u32[]{:S(2)}) %collective-permute-start.6) | collective-permute-done | bytes 147488 | tf_op jit(solution)/shard_map/ppermute | solution.py:268
  39.2 1.2 %collective-permute-done.11 = f32[8,128]{1,0:T(8,128)S(1)} collective-permute-done((f32[8,128]{1,0:T(8,128)S(1)}, f32[8,128]{1,0:T(8,128)S(1)}, u32[]{:S(2)}, u32[]{:S(2)}) %collective-permute-start.11) | collective-permute-done | bytes 4128 | tf_op jit(solution)/shard_map/ppermute | solution.py:281
  40.3 3.5 %collective-permute-start.14 = (f32[8,128]{1,0:T(8,128)S(1)}, f32[8,128]{1,0:T(8,128)S(1)}, u32[]{:S(2)}, u32[]{:S(2)}) collective-permute-start(f32[8,128]{1,0:T(8,128)S(1)} %add.15.refs_0_), channel_id=1, source_target_pairs={{0,12},{4,8},{8,4},{12,0},{1,13},{5,9},{9,5},{13,1},{2,14},{6,10},... | collective-permute-start | bytes 12296 | tf_op jit(solution)/shard_map/ppermute | solution.py:242
  43.9 0.9 %collective-permute-start.12 = (f32[8,128]{1,0:T(8,128)S(1)}, f32[8,128]{1,0:T(8,128)S(1)}, u32[]{:S(2)}, u32[]{:S(2)}) collective-permute-start(f32[8,128]{1,0:T(8,128)S(1)} %add.15.refs_0_), channel_id=1, source_target_pairs={{0,4},{4,0},{8,12},{12,8},{1,5},{5,1},{9,13},{13,9},{2,6},{6,2},{1... | collective-permute-start | bytes 12296 | tf_op jit(solution)/shard_map/ppermute | solution.py:242
  44.7 1.0 %collective-permute-done.14.refs_3_ = f32[8,128]{1,0:T(8,128)S(1)} collective-permute-done((f32[8,128]{1,0:T(8,128)S(1)}, f32[8,128]{1,0:T(8,128)S(1)}, u32[]{:S(2)}, u32[]{:S(2)}) %collective-permute-start.14) | collective-permute-done | bytes 4128 | tf_op jit(solution)/shard_map/ppermute | solution.py:242
  45.7 2.6 %collective-permute-done.13.refs_2_ = f32[8,128]{1,0:T(8,128)S(1)} collective-permute-done((f32[8,128]{1,0:T(8,128)S(1)}, f32[8,128]{1,0:T(8,128)S(1)}, u32[]{:S(2)}, u32[]{:S(2)}) %collective-permute-start.13) | collective-permute-done | bytes 4128 | tf_op jit(solution)/shard_map/ppermute | solution.py:242
  48.4 0.8 %shard_map.92 = (bf16[32,1152]{1,0:T(8,128)(2,1)S(1)}, bf16[32,1152]{1,0:T(8,128)(2,1)S(1)}, bf16[32,1152]{1,0:T(8,128)(2,1)S(1)}, bf16[32,1152]{1,0:T(8,128)(2,1)S(1)}) custom-call(s32[3]{0:T(128)S(1)} %pad_add_fusion.place, s32[4]{0:T(128)S(1)} %copy-done.4, s32[4]{0:T(128)S(1)} %copy-done.2, f32[8,128]{1,0:T(8,128)S(1)} %add.15.refs_0_, ...), custom_call_target="tpu_custom_call" | custom-call | tf_op jit(solution)/shard_map/pallas_call | solution.py:282
  49.3 2.1 %collective-permute-start.16 = (bf16[32,1152]{1,0:T(8,128)(2,1)S(1)}, bf16[32,1152]{1,0:T(8,128)(2,1)S(1)}, u32[]{:S(2)}, u32[]{:S(2)}) collective-permute-start(bf16[32,1152]{1,0:T(8,128)(2,1)S(1)} %get-tuple-element.37), channel_id=1, source_target_pairs={{0,8},{4,12},{8,0},{12,4},{1,9},{5,13},{9,1},{13,5},{2,10},{6,14},... | collective-permute-start | bytes 221192 | tf_op jit(solution)/shard_map/ppermute | solution.py:291
  51.4 2.3 %collective-permute-start.17 = (bf16[32,1152]{1,0:T(8,128)(2,1)S(1)}, bf16[32,1152]{1,0:T(8,128)(2,1)S(1)}, u32[]{:S(2)}, u32[]{:S(2)}) collective-permute-start(bf16[32,1152]{1,0:T(8,128)(2,1)S(1)} %get-tuple-element.38), channel_id=1, source_target_pairs={{0,12},{4,8},{8,4},{12,0},{1,13},{5,9},{9,5},{13,1},{2,14},{6,10},... | collective-permute-start | bytes 221192 | tf_op jit(solution)/shard_map/ppermute | solution.py:291
  53.7 3.0 %collective-permute-done.16.refs_2_ = bf16[32,1152]{1,0:T(8,128)(2,1)S(1)} collective-permute-done((bf16[32,1152]{1,0:T(8,128)(2,1)S(1)}, bf16[32,1152]{1,0:T(8,128)(2,1)S(1)}, u32[]{:S(2)}, u32[]{:S(2)}) %collective-permute-start.16) | collective-permute-done | bytes 73760 | tf_op jit(solution)/shard_map/ppermute | solution.py:291
  56.7 0.9 %collective-permute-done.17.refs_3_ = bf16[32,1152]{1,0:T(8,128)(2,1)S(1)} collective-permute-done((bf16[32,1152]{1,0:T(8,128)(2,1)S(1)}, bf16[32,1152]{1,0:T(8,128)(2,1)S(1)}, u32[]{:S(2)}, u32[]{:S(2)}) %collective-permute-start.17) | collective-permute-done | bytes 73760 | tf_op jit(solution)/shard_map/ppermute | solution.py:291
  57.6 1.5 %shard_map.93 = f32[1,32,4608]{2,1,0:T(8,128)} custom-call(s32[3]{0:T(128)S(1)} %pad_add_fusion.place, s32[4]{0:T(128)S(1)} %copy-done.2, s32[4]{0:T(128)S(1)} %copy-done.3, bf16[32,1152]{1,0:T(8,128)(2,1)S(1)} %get-tuple-element.35.refs_0_, bf16[32,1152]{1,0:T(8,128)(2,1)S(1)} %collective-permute-done.15.refs_1_, ...), custom_call_target="tpu_custom_call" | custom-call | tf_op jit(solution)/shard_map/pallas_call | solution.py:293
  (39 shorter events, 7.4 us)
Async XLA Ops:
  2.4 5.1 %collective-permute-start = (bf16[512,1024]{1,0:T(8,128)(2,1)S(1)}, bf16[512,1024]{1,0:T(8,128)(2,1)S(1)}, u32[]{:S(2)}, u32[]{:S(2)}) collective-permute-start(bf16[512,1024]{1,0:T(8,128)(2,1)S(1)} %get-tuple-element.22), channel_id=1, source_target_pairs={{0,1},{1,0},{2,3},{3,2},{4,5},{5,4},{6,7},{7,6},{8,9},{9,8},{10,11... | collective-permute-start | bytes 3145736 | tf_op jit(solution)/shard_map/ppermute | solution.py:338
  2.9 4.5 %collective-permute-start.2 = (bf16[512,1024]{1,0:T(8,128)(2,1)S(1)}, bf16[512,1024]{1,0:T(8,128)(2,1)S(1)}, u32[]{:S(2)}, u32[]{:S(2)}) collective-permute-start(bf16[512,1024]{1,0:T(8,128)(2,1)S(1)} %get-tuple-element.24), channel_id=1, source_target_pairs={{0,1},{1,0},{2,3},{3,2},{4,5},{5,4},{6,7},{7,6},{8,9},{9,8},{10,11... | collective-permute-start | bytes 3145736 | tf_op jit(solution)/shard_map/ppermute | solution.py:338
  3.0 19.9 %copy-start = (bf16[1152,1024]{1,0:T(8,128)(2,1)S(1)}, bf16[1152,1024]{1,0:T(8,128)(2,1)}, u32[]{:S(2)}) copy-start(bf16[1152,1024]{1,0:T(8,128)(2,1)} %refs_1_.7) | copy-start | bytes 7077892
  3.0 4.5 %collective-permute-start.1 = (bf16[512,512]{1,0:T(8,128)(2,1)S(1)}, bf16[512,512]{1,0:T(8,128)(2,1)S(1)}, u32[]{:S(2)}, u32[]{:S(2)}) collective-permute-start(bf16[512,512]{1,0:T(8,128)(2,1)S(1)} %get-tuple-element.23), channel_id=1, source_target_pairs={{0,1},{1,0},{2,3},{3,2},{4,5},{5,4},{6,7},{7,6},{8,9},{9,8},{10,11... | collective-permute-start | bytes 1572872 | tf_op jit(solution)/shard_map/ppermute | solution.py:338
  15.9 1.3 %collective-permute-start.3 = (bf16[32,512]{1,0:T(8,128)(2,1)S(1)}, bf16[32,512]{1,0:T(8,128)(2,1)S(1)}, u32[]{:S(2)}, u32[]{:S(2)}) collective-permute-start(bf16[32,512]{1,0:T(8,128)(2,1)S(1)} %get-tuple-element.26), channel_id=1, source_target_pairs={{0,1},{1,0},{2,3},{3,2},{4,5},{5,4},{6,7},{7,6},{8,9},{9,8},{10,11... | collective-permute-start | bytes 98312 | tf_op jit(solution)/shard_map/ppermute | solution.py:341
  17.2 8.1 %collective-permute-start.9 = (bf16[32,1024]{1,0:T(8,128)(2,1)S(1)}, bf16[32,1024]{1,0:T(8,128)(2,1)S(1)}, u32[]{:S(2)}, u32[]{:S(2)}) collective-permute-start(bf16[32,1024]{1,0:T(8,128)(2,1)S(1)} %pad_maximum_fusion.refs_0_), channel_id=1, source_target_pairs={{0,12},{4,8},{8,4},{12,0},{1,13},{5,9},{9,5},{13,1},{2,14},{6,10},... | collective-permute-start | bytes 196616 | tf_op jit(solution)/shard_map/ppermute | solution.py:242
  22.2 5.9 %collective-permute-start.7 = (bf16[32,1024]{1,0:T(8,128)(2,1)S(1)}, bf16[32,1024]{1,0:T(8,128)(2,1)S(1)}, u32[]{:S(2)}, u32[]{:S(2)}) collective-permute-start(bf16[32,1024]{1,0:T(8,128)(2,1)S(1)} %pad_maximum_fusion.refs_0_), channel_id=1, source_target_pairs={{0,8},{4,12},{8,0},{12,4},{1,9},{5,13},{9,1},{13,5},{2,10},{6,14},... | collective-permute-start | bytes 196616 | tf_op jit(solution)/shard_map/ppermute | solution.py:242
  22.2 8.2 %collective-permute-start.5 = (bf16[32,1024]{1,0:T(8,128)(2,1)S(1)}, bf16[32,1024]{1,0:T(8,128)(2,1)S(1)}, u32[]{:S(2)}, u32[]{:S(2)}) collective-permute-start(bf16[32,1024]{1,0:T(8,128)(2,1)S(1)} %pad_maximum_fusion.refs_0_), channel_id=1, source_target_pairs={{0,4},{4,0},{8,12},{12,8},{1,5},{5,1},{9,13},{13,9},{2,6},{6,2},{1... | collective-permute-start | bytes 196616 | tf_op jit(solution)/shard_map/ppermute | solution.py:242
  23.7 8.2 %collective-permute-start.4 = (f32[1,32,1152]{2,1,0:T(8,128)S(1)}, f32[1,32,1152]{2,1,0:T(8,128)S(1)}, u32[]{:S(2)}, u32[]{:S(2)}) collective-permute-start(f32[1,32,1152]{2,1,0:T(8,128)S(1)} %shard_map.84.near), channel_id=1, source_target_pairs={{0,2},{2,0},{1,3},{3,1},{4,6},{6,4},{5,7},{7,5},{8,10},{10,8},{9,1... | collective-permute-start | bytes 442376 | tf_op jit(solution)/shard_map/ppermute | solution.py:268
  26.1 6.9 %collective-permute-start.10 = (f32[1,32,1152]{2,1,0:T(8,128)S(1)}, f32[1,32,1152]{2,1,0:T(8,128)S(1)}, u32[]{:S(2)}, u32[]{:S(2)}) collective-permute-start(f32[1,32,1152]{2,1,0:T(8,128)S(1)} %shard_map.90.near), channel_id=1, source_target_pairs={{0,2},{2,0},{1,3},{3,1},{4,6},{6,4},{5,7},{7,5},{8,10},{10,8},{9,1... | collective-permute-start | bytes 442376 | tf_op jit(solution)/shard_map/ppermute | solution.py:268
  28.9 19.5 %copy-start.2 = (s32[4]{0:T(128)S(1)}, s32[4]{0:T(128)}, u32[]{:S(2)}) copy-start(s32[4]{0:T(128)} %owner_of.3) | copy-start | bytes 52
  28.9 19.5 %copy-start.4 = (s32[4]{0:T(128)S(1)}, s32[4]{0:T(128)}, u32[]{:S(2)}) copy-start(s32[4]{0:T(128)} %tenant_of.1) | copy-start | bytes 52
  28.9 28.7 %copy-start.1 = (f32[1,32,4608]{2,1,0:T(8,128)S(1)}, f32[1,32,4608]{2,1,0:T(8,128)}, u32[]{:S(2)}) copy-start(f32[1,32,4608]{2,1,0:T(8,128)} %refs_4_.1) | copy-start | bytes 1769476
  28.9 28.7 %copy-start.3 = (s32[4]{0:T(128)S(1)}, s32[4]{0:T(128)}, u32[]{:S(2)}) copy-start(s32[4]{0:T(128)} %counts.1) | copy-start | bytes 52
  28.9 7.2 %collective-permute-start.8 = (f32[1,32,1152]{2,1,0:T(8,128)S(1)}, f32[1,32,1152]{2,1,0:T(8,128)S(1)}, u32[]{:S(2)}, u32[]{:S(2)}) collective-permute-start(f32[1,32,1152]{2,1,0:T(8,128)S(1)} %shard_map.88.near), channel_id=1, source_target_pairs={{0,2},{2,0},{1,3},{3,1},{4,6},{6,4},{5,7},{7,5},{8,10},{10,8},{9,1... | collective-permute-start | bytes 442376 | tf_op jit(solution)/shard_map/ppermute | solution.py:268
  31.3 7.3 %collective-permute-start.6 = (f32[1,32,1152]{2,1,0:T(8,128)S(1)}, f32[1,32,1152]{2,1,0:T(8,128)S(1)}, u32[]{:S(2)}, u32[]{:S(2)}) collective-permute-start(f32[1,32,1152]{2,1,0:T(8,128)S(1)} %shard_map.86.near), channel_id=1, source_target_pairs={{0,2},{2,0},{1,3},{3,1},{4,6},{6,4},{5,7},{7,5},{8,10},{10,8},{9,1... | collective-permute-start | bytes 442376 | tf_op jit(solution)/shard_map/ppermute | solution.py:268
  39.1 1.2 %collective-permute-start.11 = (f32[8,128]{1,0:T(8,128)S(1)}, f32[8,128]{1,0:T(8,128)S(1)}, u32[]{:S(2)}, u32[]{:S(2)}) collective-permute-start(f32[8,128]{1,0:T(8,128)S(1)} %add_add_fusion), channel_id=1, source_target_pairs={{0,1},{1,0},{2,3},{3,2},{4,5},{5,4},{6,7},{7,6},{8,9},{9,8},{10,11... | collective-permute-start | bytes 12296 | tf_op jit(solution)/shard_map/ppermute | solution.py:281
  40.3 5.4 %collective-permute-start.14 = (f32[8,128]{1,0:T(8,128)S(1)}, f32[8,128]{1,0:T(8,128)S(1)}, u32[]{:S(2)}, u32[]{:S(2)}) collective-permute-start(f32[8,128]{1,0:T(8,128)S(1)} %add.15.refs_0_), channel_id=1, source_target_pairs={{0,12},{4,8},{8,4},{12,0},{1,13},{5,9},{9,5},{13,1},{2,14},{6,10},... | collective-permute-start | bytes 12296 | tf_op jit(solution)/shard_map/ppermute | solution.py:242
  43.9 4.5 %collective-permute-start.13 = (f32[8,128]{1,0:T(8,128)S(1)}, f32[8,128]{1,0:T(8,128)S(1)}, u32[]{:S(2)}, u32[]{:S(2)}) collective-permute-start(f32[8,128]{1,0:T(8,128)S(1)} %add.15.refs_0_), channel_id=1, source_target_pairs={{0,8},{4,12},{8,0},{12,4},{1,9},{5,13},{9,1},{13,5},{2,10},{6,14},... | collective-permute-start | bytes 12296 | tf_op jit(solution)/shard_map/ppermute | solution.py:242
  43.9 4.5 %collective-permute-start.12 = (f32[8,128]{1,0:T(8,128)S(1)}, f32[8,128]{1,0:T(8,128)S(1)}, u32[]{:S(2)}, u32[]{:S(2)}) collective-permute-start(f32[8,128]{1,0:T(8,128)S(1)} %add.15.refs_0_), channel_id=1, source_target_pairs={{0,4},{4,0},{8,12},{12,8},{1,5},{5,1},{9,13},{13,9},{2,6},{6,2},{1... | collective-permute-start | bytes 12296 | tf_op jit(solution)/shard_map/ppermute | solution.py:242
  49.2 4.5 %collective-permute-start.15 = (bf16[32,1152]{1,0:T(8,128)(2,1)S(1)}, bf16[32,1152]{1,0:T(8,128)(2,1)S(1)}, u32[]{:S(2)}, u32[]{:S(2)}) collective-permute-start(bf16[32,1152]{1,0:T(8,128)(2,1)S(1)} %get-tuple-element.36), channel_id=1, source_target_pairs={{0,4},{4,0},{8,12},{12,8},{1,5},{5,1},{9,13},{13,9},{2,6},{6,2},{1... | collective-permute-start | bytes 221192 | tf_op jit(solution)/shard_map/ppermute | solution.py:291
  49.3 7.3 %collective-permute-start.16 = (bf16[32,1152]{1,0:T(8,128)(2,1)S(1)}, bf16[32,1152]{1,0:T(8,128)(2,1)S(1)}, u32[]{:S(2)}, u32[]{:S(2)}) collective-permute-start(bf16[32,1152]{1,0:T(8,128)(2,1)S(1)} %get-tuple-element.37), channel_id=1, source_target_pairs={{0,8},{4,12},{8,0},{12,4},{1,9},{5,13},{9,1},{13,5},{2,10},{6,14},... | collective-permute-start | bytes 221192 | tf_op jit(solution)/shard_map/ppermute | solution.py:291
  51.4 6.2 %collective-permute-start.17 = (bf16[32,1152]{1,0:T(8,128)(2,1)S(1)}, bf16[32,1152]{1,0:T(8,128)(2,1)S(1)}, u32[]{:S(2)}, u32[]{:S(2)}) collective-permute-start(bf16[32,1152]{1,0:T(8,128)(2,1)S(1)} %get-tuple-element.38), channel_id=1, source_target_pairs={{0,12},{4,8},{8,4},{12,0},{1,13},{5,9},{9,5},{13,1},{2,14},{6,10},... | collective-permute-start | bytes 221192 | tf_op jit(solution)/shard_map/ppermute | solution.py:291

commit v4 on v3

--- a/solution.py
+++ b/solution.py
@@ -18,7 +18,7 @@
 TANH_SCALE = query_scale / softcap
 EXP2_SCALE = softcap * math.log2(math.e)
 
-PARTIAL_TYPE = jnp.float32
+PARTIAL_TYPE = jnp.bfloat16
 
 
 def GROUPS(dp):
@@ -36,114 +36,170 @@
     return [(i, i ^ step) for i in range(size)]
 
 
-def head_value_grad(q, k, g, prob):
+def add_scores(query, keys, count, diagonal, total):
     block = LANES
-    rows = q.shape[1]
-    group = q.shape[2] // HEAD_DIM
-    key_pos = lax.broadcasted_iota(jnp.int32, (block, block), 0)
-    query_pos = lax.broadcasted_iota(jnp.int32, (block, block), 1)
-    keep = jnp.concatenate([key_pos <= query_pos] * group, axis=1)
-
-    def query_block(half, parts, start, column):
-        q_block = jnp.concatenate(
-            [
-                q[half, start : start + block, i * HEAD_DIM : (i + 1) * HEAD_DIM]
-                for i in range(group)
-            ],
-            axis=0,
-        )
-        total, prompt = None, None
-        for key_half, count, diagonal in parts:
-            raw = lax.dot_general(
-                k[key_half, :count, :], q_block, CONTRACT_LAST, preferred_element_type=jnp.float32
+    lanes = query.shape[0]
+    raw = lax.dot_general(
+        keys[:count, :], query, CONTRACT_LAST, preferred_element_type=jnp.float32
+    )
+    prompt = None
+    for low in range(0, count, block):
+        e = jnp.exp2(jnp.tanh(raw[low : low + block] * TANH_SCALE) * EXP2_SCALE)
+        if diagonal and low == count - block:
+            key_pos = lax.broadcasted_iota(jnp.int32, (block, block), 0)
+            query_pos = lax.broadcasted_iota(jnp.int32, (block, block), 1)
+            keep = jnp.concatenate([key_pos <= query_pos] * (lanes // block), axis=1)
+            e = jnp.where(keep, e, 0.0)
+        if prompt is None:
+            prompt = e[:PROMPT]
+        part = jnp.sum(e.reshape(block // 8, 8, lanes), axis=0)
+        total = part if total is None else total + part
+    return total, prompt
+
+
+def query_block(queries):
+    return jnp.concatenate(
+        [
+            queries[:, at : at + HEAD_DIM] for at in range(0, queries.shape[1], HEAD_DIM)
+        ],
+        axis=0,
+    )
+
+
+def triangle_kernel(place, q, k, g, totals, prompts, q_own, k_own, g_own, done):
+    heads, rows, width = q_own.shape
+    skipped = place[1] * heads
+    lanes = width // HEAD_DIM * LANES
+
+    def load(source, target, h, i):
+        extent = target.shape[2]
+        columns = pl.ds(pl.multiple_of((skipped + h) * extent, LANES), extent)
+        return pltpu.make_async_copy(source.at[:, columns], target.at[h], done.at[h, i])
+
+    for h in range(heads):
+        load(k, k_own, h, 0).start()
+        load(q, q_own, h, 1).start()
+    for h in range(heads):
+        load(g, g_own, h, 2).start()
+
+    def step(h, carry):
+        load(k, k_own, h, 0).wait()
+        load(q, q_own, h, 1).wait()
+        for i, start in enumerate(range(0, rows, LANES)):
+            total, prompt = add_scores(
+                query_block(q_own[h, start : start + LANES, :]),
+                k_own.at[h],
+                start + LANES,
+                True,
+                None,
             )
-            for low in range(0, count, block):
-                e = jnp.exp2(jnp.tanh(raw[low : low + block] * TANH_SCALE) * EXP2_SCALE)
-                if diagonal and low == count - block:
-                    e = jnp.where(keep, e, 0.0)
-                if prompt is None:
-                    prompt = e[:PROMPT]
-                part = jnp.sum(e.reshape(block // 8, 8, group * block), axis=0)
-                total = part if total is None else total + part
-        total = jnp.sum(total, axis=0, keepdims=True)
-        scaled = (prompt / total).astype(jnp.bfloat16)
-        for i in range(group):
-            prob[i, :, column : column + block] = scaled[:, i * block : (i + 1) * block]
-
-    for start in range(0, rows, block):
-        query_block(0, [(0, start + block, True)], start, start)
-    for start in range(0, rows, block):
-        query_block(1, [(0, rows, False), (1, start + block, True)], start, rows + start)
-    value = None
-    for i in range(group):
-        for half in range(2):
-            term = jnp.dot(
-                prob[i, :, half * rows : (half + 1) * rows],
-                g[half, :, i * HEAD_DIM : (i + 1) * HEAD_DIM],
-                preferred_element_type=jnp.float32,
+            at = slice(i * lanes, (i + 1) * lanes)
+            totals[h, :, at] = total
+            prompts[h, :, at] = prompt
+        return carry
+
+    lax.fori_loop(0, heads, step, 0)
+    for h in range(heads):
+        load(g, g_own, h, 2).wait()
+
+
+def own_triangle(place, q, k, g):
+    rows = q.shape[0]
+    heads = k.shape[1] // (2 * HEAD_DIM)
+    width = q.shape[1] // (2 * heads)
+    lanes = width // HEAD_DIM * rows
+    return pl.pallas_call(
+        triangle_kernel,
+        in_specs=[SMEM, HBM, HBM, HBM],
+        out_specs=[VMEM] * 5,
+        out_shape=[
+            jax.ShapeDtypeStruct((heads, 8, lanes), jnp.float32),
+            jax.ShapeDtypeStruct((heads, PROMPT, lanes), jnp.float32),
+            jax.ShapeDtypeStruct((heads, rows, width), jnp.bfloat16),
+            jax.ShapeDtypeStruct((heads, rows, HEAD_DIM), jnp.bfloat16),
+            jax.ShapeDtypeStruct((heads, rows, width), jnp.bfloat16),
+        ],
+        scratch_shapes=[pltpu.SemaphoreType.DMA((heads, 3))],
+        compiler_params=pltpu.CompilerParams(vmem_limit_bytes=16 * 1024 * 1024),
+        cost_estimate=pl.CostEstimate(
+            flops=2 * heads * lanes * rows * HEAD_DIM,
+            bytes_accessed=6 * heads * rows * width,
+            transcendentals=heads * lanes * rows,
+        ),
+    )(place, q, k, g)
+
+
+def attention_kernel(
+    place, totals, prompts, q_own, k_own, g_own, q_far, k_far, g_far, mine, theirs, k_first, prob
+):
+    heads, rows, width = q_own.shape
+    group = width // HEAD_DIM
+    lanes = group * LANES
+    first = place[1] == 0
+
+    def step(h, carry):
+        at_q = pl.ds(pl.multiple_of(h * width, LANES), width)
+        at_k = pl.ds(pl.multiple_of(h * HEAD_DIM, LANES), HEAD_DIM)
+        k_first[...] = jnp.where(first, k_own[h], k_far[:, at_k])
+        for i, start in enumerate(range(0, rows, LANES)):
+            at = slice(i * lanes, (i + 1) * lanes)
+            q_block = q_far[start : start + LANES, at_q]
+            far, far_prompt = add_scores(
+                query_block(q_block), k_far.at[:, at_k], start + LANES, True, None
             )
-            value = term if value is None else value + term
-    return value.astype(jnp.bfloat16)
-
-
-def attention_kernel(place, q, k, g, q_far, k_far, g_far, mine, theirs, q_all, k_all, g_all, prob, done):
-    heads = q_all.shape[0]
-    seq = place[1]
-
-    def copies(h):
-        pairs = []
-        for own, far, buffer in ((q, q_far, q_all), (k, k_far, k_all), (g, g_far, g_all)):
-            width = buffer.shape[-1]
-            at = pl.multiple_of((seq * heads + h) * width, LANES)
-            pairs.append((own.at[:, pl.ds(at, width)], buffer.at[h, seq]))
-            at = pl.multiple_of(h * width, LANES)
-            pairs.append((far.at[:, pl.ds(at, width)], buffer.at[h, 1 - seq]))
-        return [
-            pltpu.make_async_copy(source, target, done.at[h, i])
-            for i, (source, target) in enumerate(pairs)
-        ]
-
-    for h in range(heads):
-        for copy in copies(h):
-            copy.start()
-
-    def step(h, carry):
-        for copy in copies(h):
-            copy.wait()
-        value = head_value_grad(q_all.at[h], k_all.at[h], g_all.at[h], prob)
-        at = pl.ds(pl.multiple_of(h * HEAD_DIM, LANES), HEAD_DIM)
+            q_block = jnp.where(first, q_block, q_own[h, start : start + LANES, :])
+            square, late_prompt = add_scores(query_block(q_block), k_first, rows, False, None)
+            own, own_prompt = totals[h, :, at], prompts[h, :, at]
+            early = jnp.where(first, own, far)
+            late = square + jnp.where(first, far, own)
+            early_prompt = jnp.where(first, own_prompt, far_prompt)
+            early = early_prompt / jnp.sum(early, axis=0, keepdims=True)
+            late = late_prompt / jnp.sum(late, axis=0, keepdims=True)
+            for slot, scaled in enumerate((jnp.where(first, early, late), jnp.where(first, late, early))):
+                scaled = scaled.astype(jnp.bfloat16)
+                column = slot * rows + start
+                for j in range(group):
+                    prob[j, :, column : column + LANES] = scaled[:, j * LANES : (j + 1) * LANES]
+        value = None
+        for j in range(group):
+            at_g = pl.ds(pl.multiple_of(h * width + j * HEAD_DIM, LANES), HEAD_DIM)
+            for slot, g in enumerate(
+                (g_own[h, :, j * HEAD_DIM : (j + 1) * HEAD_DIM], g_far[:, at_g])
+            ):
+                term = jnp.dot(
+                    prob[j, :, slot * rows : (slot + 1) * rows],
+                    g,
+                    preferred_element_type=jnp.float32,
+                )
+                value = term if value is None else value + term
+        value = value.astype(jnp.bfloat16)
         low, high = value[: PROMPT // 2], value[PROMPT // 2 :]
-        mine[:, at] = jnp.where(seq == 0, low, high)
-        theirs[:, at] = jnp.where(seq == 0, high, low)
+        mine[:, at_k] = jnp.where(first, low, high)
+        theirs[:, at_k] = jnp.where(first, high, low)
         return carry
 
     lax.fori_loop(0, heads, step, 0)
 
 
-def prompt_value_grad(place, q, k, g, q_far, k_far, g_far):
-    rows = q.shape[0]
-    heads = k_far.shape[1] // HEAD_DIM
-    group = q.shape[1] // k.shape[1]
-    width = group * HEAD_DIM
+def prompt_value_grad(place, totals, prompts, q_own, k_own, g_own, q_far, k_far, g_far):
+    heads, rows, width = q_own.shape
+    group = width // HEAD_DIM
     return pl.pallas_call(
         attention_kernel,
-        in_specs=[SMEM] + [HBM] * 3 + [ANY] * 3,
+        in_specs=[SMEM] + [VMEM] * 8,
         out_specs=[VMEM] * 2,
         out_shape=[jax.ShapeDtypeStruct((PROMPT // 2, heads * HEAD_DIM), jnp.bfloat16)] * 2,
         scratch_shapes=[
-            pltpu.VMEM((heads, 2, rows, width), jnp.bfloat16),
-            pltpu.VMEM((heads, 2, rows, HEAD_DIM), jnp.bfloat16),
-            pltpu.VMEM((heads, 2, rows, width), jnp.bfloat16),
+            pltpu.VMEM((rows, HEAD_DIM), jnp.bfloat16),
             pltpu.VMEM((group, PROMPT, 2 * rows), jnp.bfloat16),
-            pltpu.SemaphoreType.DMA((heads, 6)),
         ],
-        compiler_params=pltpu.CompilerParams(vmem_limit_bytes=24 * 1024 * 1024),
+        compiler_params=pltpu.CompilerParams(vmem_limit_bytes=16 * 1024 * 1024),
         cost_estimate=pl.CostEstimate(
-            flops=heads * group * 9 * rows * rows * HEAD_DIM,
+            flops=heads * group * 7 * rows * rows * HEAD_DIM,
             bytes_accessed=10 * rows * heads * width,
-            transcendentals=heads * group * 4 * rows * rows,
+            transcendentals=heads * group * 3 * rows * rows,
         ),
-    )(place, q, k, g, q_far, k_far, g_far)
+    )(place, totals, prompts, q_own, k_own, g_own, q_far, k_far, g_far)
 
 
 def sibling_kernel(place, *refs, starts):
@@ -337,7 +393,8 @@
     k_far, q_far, g_far = (
         lax.ppermute(x, "seq", swap) for x in cut(place, (k, q, g), starts, shapes)
     )
-    mine, theirs = prompt_value_grad(place, q, k, g, q_far, k_far, g_far)
+    own = own_triangle(place, q, k, g)
+    mine, theirs = prompt_value_grad(place, *own, q_far, k_far, g_far)
     other = lax.ppermute(theirs, "seq", swap)
     first = seq_index == 0
     value_grad = jnp.concatenate(

time: 59.2 us -> 53.3 us (0.900)
  waiting for transfers between devices: 19.5 us -> 13 us
  Pallas kernels: 18.4 us -> 19.8 us
  starting transfers between devices: 20.9 us -> 20.1 us
    ppermute x3, waiting for transfers between devices: 4.03 us -> 0.28 us  [body(): lax.ppermute(x, 'seq', swap)]
    ppermute x4, waiting for transfers between devices: 4.97 us -> 2.07 us  [tail_by_permutes(): far = lax.ppermute(near, 'tensor', swap)]
    pallas_call x1 -> x2, Pallas kernels: 8.47 us -> 9.86 us  [the longest x1 6.12 us: prompt_value_grad(): pl.pallas_call(attention_kernel, in_specs=[SMEM] + [VMEM] * 8, out_specs=...]
    ppermute x4, starting transfers between devices: 4.89 us -> 4.18 us  [tail_by_permutes(): far = lax.ppermute(near, 'tensor', swap)]
  transfers between devices with their start and end apart: 18 -> 18, of which waited for: 11 -> 10; matrix products, arithmetic and copies ran while one was open for 0% -> 0% of each run, Pallas kernels for 8% -> 16%
where the time goes in v4:
time: 53.3 us; the launch traced here: 53.2 us
  starting transfers between devices  20.1 us (38%)
  Pallas kernels  19.8 us (37%)
  waiting for transfers between devices  13 us (24%)
    ppermute x6, starting transfers between devices, to_dp(): lax.ppermute(array, 'dp', xor_pairs(dp, step))  9.97 us
    pallas_call x1, Pallas kernels, prompt_value_grad(): pl.pallas_call(attention_kernel, in_specs=[SMEM] + [VMEM] * 8, out_specs=...  6.12 us
    ppermute x6, waiting for transfers between devices, to_dp(): lax.ppermute(array, 'dp', xor_pairs(dp, step))  4.68 us
    ppermute x3, starting transfers between devices, tail_by_permutes(): lax.ppermute(shares[step], 'dp', xor_pairs(dp, step))  4.45 us
    ppermute x4, starting transfers between devices, tail_by_permutes(): far = lax.ppermute(near, 'tensor', swap)  4.18 us
    ppermute x3, waiting for transfers between devices, tail_by_permutes(): lax.ppermute(shares[step], 'dp', xor_pairs(dp, step))  3.92 us
    pallas_call x1, Pallas kernels, own_triangle(): pl.pallas_call(triangle_kernel, in_specs=[SMEM, HBM, HBM, HBM], out_specs...  3.74 us
    pallas_call x4, Pallas kernels, tail_by_permutes(): pl.pallas_call(partial_kernel, in_specs=[VMEM] * (len(steps) + 1), out_sp...  3.06 us
  transfers between devices with their start and end apart: 18, of which 10 were waited for; matrix products, arithmetic and copies ran while one was open for 0% of the time, Pallas kernels for 16%

profile of v4, /device:TPU:0, one launch (start us, length us, event | category | flops | bytes accessed | tf_op | source)
XLA Modules:
  0.0 53.2 jit_solution(6285236335748098860)
XLA Ops:
  0.1 2.3 %shard_map.83 = (bf16[512,512]{1,0:T(8,128)(2,1)S(1)}, bf16[512,1024]{1,0:T(8,128)(2,1)S(1)}, bf16[512,1024]{1,0:T(8,128)(2,1)S(1)}) custom-call(s32[3]{0:T(128)S(1)} %pad_add_fusion.place, bf16[512,1024]{1,0:T(8,128)(2,1)} %bitcast.10, bf16[512,2048]{1,0:T(8,128)(2,1)} %bitcast.6, bf16[512,2048]{1,0:T(8,128)(2,1)} %bitcast.8), custom_call_target="tpu_custom_call" | custom-call | tf_op jit(solution)/shard_map/pallas_call | solution.py:221
  3.4 3.7 %shard_map.82 = (f32[4,8,1024]{2,1,0:T(8,128)S(1)}, f32[4,64,1024]{2,1,0:T(8,128)S(1)}, bf16[4,512,256]{2,1,0:T(8,128)(2,1)S(1)}, bf16[4,512,128]{2,1,0:T(8,128)(2,1)S(1)}, bf16[4,512,256]{2,1,0:T(8,128)(2,1)S(1)}) custom-call(s32[3]{0:T(128)S(1)} %pad_add_fusion.place, bf16[512,2048]{1,0:T(8,128)(2,1)} %bitcast.7, bf16[512,1024]{1,0:T(8,128)(2,1)} %bitcast.11, ...), custom_call_target="tpu_custom_call" | custom-call | flops 536870912 | bytes 3145728 | tf_op jit(solution)/shard_map/pallas_call | solution.py:111
  7.4 6.1 %shard_map.84 = (bf16[32,512]{1,0:T(8,128)(2,1)S(1)}, bf16[32,512]{1,0:T(8,128)(2,1)S(1)}) custom-call(s32[3]{0:T(128)S(1)} %pad_add_fusion.place, f32[4,8,1024]{2,1,0:T(8,128)S(1)} %get-tuple-element.27.totals, f32[4,64,1024]{2,1,0:T(8,128)S(1)} %get-tuple-element.28.prompts, bf16[4,512,256]{2,1,0:T(8,128)(2,1)S(1)} %get-tuple-element.29.q_own, ...), custom_call_target="tpu_custom_call" | custom-call | flops 1879048192 | bytes 5242880 | tf_op jit(solution)/shard_map/pallas_call | solution.py:187
  14.0 0.9 %collective-permute-done.3 = bf16[32,512]{1,0:T(8,128)(2,1)S(1)} collective-permute-done((bf16[32,512]{1,0:T(8,128)(2,1)S(1)}, bf16[32,512]{1,0:T(8,128)(2,1)S(1)}, u32[]{:S(2)}, u32[]{:S(2)}) %collective-permute-start.3) | collective-permute-done | bytes 32800 | tf_op jit(solution)/shard_map/ppermute | solution.py:398
  14.9 3.0 %collective-permute-start.5 = (bf16[32,1024]{1,0:T(8,128)(2,1)S(1)}, bf16[32,1024]{1,0:T(8,128)(2,1)S(1)}, u32[]{:S(2)}, u32[]{:S(2)}) collective-permute-start(bf16[32,1024]{1,0:T(8,128)(2,1)S(1)} %pad_maximum_fusion.refs_0_), channel_id=1, source_target_pairs={{0,4},{4,0},{8,12},{12,8},{1,5},{5,1},{9,13},{13,9},{2,6},{6,2},{1... | collective-permute-start | bytes 196616 | tf_op jit(solution)/shard_map/ppermute | solution.py:298
  17.9 2.6 %collective-permute-start.7 = (bf16[32,1024]{1,0:T(8,128)(2,1)S(1)}, bf16[32,1024]{1,0:T(8,128)(2,1)S(1)}, u32[]{:S(2)}, u32[]{:S(2)}) collective-permute-start(bf16[32,1024]{1,0:T(8,128)(2,1)S(1)} %pad_maximum_fusion.refs_0_), channel_id=1, source_target_pairs={{0,8},{4,12},{8,0},{12,4},{1,9},{5,13},{9,1},{13,5},{2,10},{6,14},... | collective-permute-start | bytes 196616 | tf_op jit(solution)/shard_map/ppermute | solution.py:298
  20.5 0.8 %shard_map.85.near = bf16[1,32,1152]{2,1,0:T(8,128)(2,1)S(1)} custom-call(bf16[32,1024]{1,0:T(8,128)(2,1)S(1)} %pad_maximum_fusion.refs_0_, bf16[1152,1024]{1,0:T(8,128)(2,1)S(1)} %copy-done), custom_call_target="tpu_custom_call" | custom-call | flops 75497472 | bytes 2359296 | tf_op jit(solution)/shard_map/pallas_call | solution.py:312
  21.2 1.7 %collective-permute-start.4 = (bf16[1,32,1152]{2,1,0:T(8,128)(2,1)S(1)}, bf16[1,32,1152]{2,1,0:T(8,128)(2,1)S(1)}, u32[]{:S(2)}, u32[]{:S(2)}) collective-permute-start(bf16[1,32,1152]{2,1,0:T(8,128)(2,1)S(1)} %shard_map.85.near), channel_id=1, source_target_pairs={{0,2},{2,0},{1,3},{3,1},{4,6},{6,4},{5,7},{7,5},{8,10},{10,8},{9,1... | collective-permute-start | bytes 221192 | tf_op jit(solution)/shard_map/ppermute | solution.py:324
  23.0 0.8 %shard_map.87.near = bf16[1,32,1152]{2,1,0:T(8,128)(2,1)S(1)} custom-call(bf16[32,1024]{1,0:T(8,128)(2,1)S(1)} %collective-permute-done.5.refs_0_, bf16[1152,1024]{1,0:T(8,128)(2,1)S(1)} %copy-done), custom_call_target="tpu_custom_call" | custom-call | flops 75497472 | bytes 2359296 | tf_op jit(solution)/shard_map/pallas_call | solution.py:312
  24.1 1.3 %collective-permute-done.7.refs_0_ = bf16[32,1024]{1,0:T(8,128)(2,1)S(1)} collective-permute-done((bf16[32,1024]{1,0:T(8,128)(2,1)S(1)}, bf16[32,1024]{1,0:T(8,128)(2,1)S(1)}, u32[]{:S(2)}, u32[]{:S(2)}) %collective-permute-start.7) | collective-permute-done | bytes 65568 | tf_op jit(solution)/shard_map/ppermute | solution.py:298
  26.2 1.6 %collective-permute-start.8 = (bf16[1,32,1152]{2,1,0:T(8,128)(2,1)S(1)}, bf16[1,32,1152]{2,1,0:T(8,128)(2,1)S(1)}, u32[]{:S(2)}, u32[]{:S(2)}) collective-permute-start(bf16[1,32,1152]{2,1,0:T(8,128)(2,1)S(1)} %shard_map.89.near), channel_id=1, source_target_pairs={{0,2},{2,0},{1,3},{3,1},{4,6},{6,4},{5,7},{7,5},{8,10},{10,8},{9,1... | collective-permute-start | bytes 221192 | tf_op jit(solution)/shard_map/ppermute | solution.py:324
  27.8 0.8 %shard_map.91.near = bf16[1,32,1152]{2,1,0:T(8,128)(2,1)S(1)} custom-call(bf16[32,1024]{1,0:T(8,128)(2,1)S(1)} %collective-permute-done.9.refs_0_, bf16[1152,1024]{1,0:T(8,128)(2,1)S(1)} %copy-done), custom_call_target="tpu_custom_call" | custom-call | flops 75497472 | bytes 2359296 | tf_op jit(solution)/shard_map/pallas_call | solution.py:312
  31.2 1.7 %collective-permute-done.10.far = bf16[1,32,1152]{2,1,0:T(8,128)(2,1)S(1)} collective-permute-done((bf16[1,32,1152]{2,1,0:T(8,128)(2,1)S(1)}, bf16[1,32,1152]{2,1,0:T(8,128)(2,1)S(1)}, u32[]{:S(2)}, u32[]{:S(2)}) %collective-permute-start.10) | collective-permute-done | bytes 73760 | tf_op jit(solution)/shard_map/ppermute | solution.py:324
  33.6 1.2 %collective-permute-done.11 = f32[8,128]{1,0:T(8,128)S(1)} collective-permute-done((f32[8,128]{1,0:T(8,128)S(1)}, f32[8,128]{1,0:T(8,128)S(1)}, u32[]{:S(2)}, u32[]{:S(2)}) %collective-permute-start.11) | collective-permute-done | bytes 4128 | tf_op jit(solution)/shard_map/ppermute | solution.py:337
  34.8 3.2 %collective-permute-start.14 = (f32[8,128]{1,0:T(8,128)S(1)}, f32[8,128]{1,0:T(8,128)S(1)}, u32[]{:S(2)}, u32[]{:S(2)}) collective-permute-start(f32[8,128]{1,0:T(8,128)S(1)} %add.15.refs_0_), channel_id=1, source_target_pairs={{0,12},{4,8},{8,4},{12,0},{1,13},{5,9},{9,5},{13,1},{2,14},{6,10},... | collective-permute-start | bytes 12296 | tf_op jit(solution)/shard_map/ppermute | solution.py:298
  38.0 1.2 %collective-permute-start.12 = (f32[8,128]{1,0:T(8,128)S(1)}, f32[8,128]{1,0:T(8,128)S(1)}, u32[]{:S(2)}, u32[]{:S(2)}) collective-permute-start(f32[8,128]{1,0:T(8,128)S(1)} %add.15.refs_0_), channel_id=1, source_target_pairs={{0,4},{4,0},{8,12},{12,8},{1,5},{5,1},{9,13},{13,9},{2,6},{6,2},{1... | collective-permute-start | bytes 12296 | tf_op jit(solution)/shard_map/ppermute | solution.py:298
  39.2 1.0 %collective-permute-done.14.refs_3_ = f32[8,128]{1,0:T(8,128)S(1)} collective-permute-done((f32[8,128]{1,0:T(8,128)S(1)}, f32[8,128]{1,0:T(8,128)S(1)}, u32[]{:S(2)}, u32[]{:S(2)}) %collective-permute-start.14) | collective-permute-done | bytes 4128 | tf_op jit(solution)/shard_map/ppermute | solution.py:298
  40.2 2.3 %collective-permute-done.13.refs_2_ = f32[8,128]{1,0:T(8,128)S(1)} collective-permute-done((f32[8,128]{1,0:T(8,128)S(1)}, f32[8,128]{1,0:T(8,128)S(1)}, u32[]{:S(2)}, u32[]{:S(2)}) %collective-permute-start.13) | collective-permute-done | bytes 4128 | tf_op jit(solution)/shard_map/ppermute | solution.py:298
  42.5 0.8 %shard_map.93 = (bf16[32,1152]{1,0:T(8,128)(2,1)S(1)}, bf16[32,1152]{1,0:T(8,128)(2,1)S(1)}, bf16[32,1152]{1,0:T(8,128)(2,1)S(1)}, bf16[32,1152]{1,0:T(8,128)(2,1)S(1)}) custom-call(s32[3]{0:T(128)S(1)} %pad_add_fusion.place, s32[4]{0:T(128)S(1)} %copy-done.4, s32[4]{0:T(128)S(1)} %copy-done.2, f32[8,128]{1,0:T(8,128)S(1)} %add.15.refs_0_, ...), custom_call_target="tpu_custom_call" | custom-call | tf_op jit(solution)/shard_map/pallas_call | solution.py:338
  43.7 1.8 %collective-permute-start.16 = (bf16[32,1152]{1,0:T(8,128)(2,1)S(1)}, bf16[32,1152]{1,0:T(8,128)(2,1)S(1)}, u32[]{:S(2)}, u32[]{:S(2)}) collective-permute-start(bf16[32,1152]{1,0:T(8,128)(2,1)S(1)} %get-tuple-element.47), channel_id=1, source_target_pairs={{0,8},{4,12},{8,0},{12,4},{1,9},{5,13},{9,1},{13,5},{2,10},{6,14},... | collective-permute-start | bytes 221192 | tf_op jit(solution)/shard_map/ppermute | solution.py:347
  45.5 2.3 %collective-permute-start.17 = (bf16[32,1152]{1,0:T(8,128)(2,1)S(1)}, bf16[32,1152]{1,0:T(8,128)(2,1)S(1)}, u32[]{:S(2)}, u32[]{:S(2)}) collective-permute-start(bf16[32,1152]{1,0:T(8,128)(2,1)S(1)} %get-tuple-element.48), channel_id=1, source_target_pairs={{0,12},{4,8},{8,4},{12,0},{1,13},{5,9},{9,5},{13,1},{2,14},{6,10},... | collective-permute-start | bytes 221192 | tf_op jit(solution)/shard_map/ppermute | solution.py:347
  47.8 3.0 %collective-permute-done.16.refs_2_ = bf16[32,1152]{1,0:T(8,128)(2,1)S(1)} collective-permute-done((bf16[32,1152]{1,0:T(8,128)(2,1)S(1)}, bf16[32,1152]{1,0:T(8,128)(2,1)S(1)}, u32[]{:S(2)}, u32[]{:S(2)}) %collective-permute-start.16) | collective-permute-done | bytes 73760 | tf_op jit(solution)/shard_map/ppermute | solution.py:347
  50.8 0.9 %collective-permute-done.17.refs_3_ = bf16[32,1152]{1,0:T(8,128)(2,1)S(1)} collective-permute-done((bf16[32,1152]{1,0:T(8,128)(2,1)S(1)}, bf16[32,1152]{1,0:T(8,128)(2,1)S(1)}, u32[]{:S(2)}, u32[]{:S(2)}) %collective-permute-start.17) | collective-permute-done | bytes 73760 | tf_op jit(solution)/shard_map/ppermute | solution.py:347
  51.7 1.4 %shard_map.94 = f32[1,32,4608]{2,1,0:T(8,128)} custom-call(s32[3]{0:T(128)S(1)} %pad_add_fusion.place, s32[4]{0:T(128)S(1)} %copy-done.2, s32[4]{0:T(128)S(1)} %copy-done.3, bf16[32,1152]{1,0:T(8,128)(2,1)S(1)} %get-tuple-element.45.refs_0_, bf16[32,1152]{1,0:T(8,128)(2,1)S(1)} %collective-permute-done.15.refs_1_, ...), custom_call_target="tpu_custom_call" | custom-call | tf_op jit(solution)/shard_map/pallas_call | solution.py:349
  (40 shorter events, 6.6 us)
Async XLA Ops:
  2.4 5.1 %collective-permute-start = (bf16[512,1024]{1,0:T(8,128)(2,1)S(1)}, bf16[512,1024]{1,0:T(8,128)(2,1)S(1)}, u32[]{:S(2)}, u32[]{:S(2)}) collective-permute-start(bf16[512,1024]{1,0:T(8,128)(2,1)S(1)} %get-tuple-element.32), channel_id=1, source_target_pairs={{0,1},{1,0},{2,3},{3,2},{4,5},{5,4},{6,7},{7,6},{8,9},{9,8},{10,11... | collective-permute-start | bytes 3145736 | tf_op jit(solution)/shard_map/ppermute | solution.py:394
  2.9 4.5 %collective-permute-start.2 = (bf16[512,1024]{1,0:T(8,128)(2,1)S(1)}, bf16[512,1024]{1,0:T(8,128)(2,1)S(1)}, u32[]{:S(2)}, u32[]{:S(2)}) collective-permute-start(bf16[512,1024]{1,0:T(8,128)(2,1)S(1)} %get-tuple-element.34), channel_id=1, source_target_pairs={{0,1},{1,0},{2,3},{3,2},{4,5},{5,4},{6,7},{7,6},{8,9},{9,8},{10,11... | collective-permute-start | bytes 3145736 | tf_op jit(solution)/shard_map/ppermute | solution.py:394
  3.0 4.5 %collective-permute-start.1 = (bf16[512,512]{1,0:T(8,128)(2,1)S(1)}, bf16[512,512]{1,0:T(8,128)(2,1)S(1)}, u32[]{:S(2)}, u32[]{:S(2)}) collective-permute-start(bf16[512,512]{1,0:T(8,128)(2,1)S(1)} %get-tuple-element.33), channel_id=1, source_target_pairs={{0,1},{1,0},{2,3},{3,2},{4,5},{5,4},{6,7},{7,6},{8,9},{9,8},{10,11... | collective-permute-start | bytes 1572872 | tf_op jit(solution)/shard_map/ppermute | solution.py:394
  7.4 13.0 %copy-start = (bf16[1152,1024]{1,0:T(8,128)(2,1)S(1)}, bf16[1152,1024]{1,0:T(8,128)(2,1)}, u32[]{:S(2)}) copy-start(bf16[1152,1024]{1,0:T(8,128)(2,1)} %refs_1_.7) | copy-start | bytes 7077892
  13.6 1.3 %collective-permute-start.3 = (bf16[32,512]{1,0:T(8,128)(2,1)S(1)}, bf16[32,512]{1,0:T(8,128)(2,1)S(1)}, u32[]{:S(2)}, u32[]{:S(2)}) collective-permute-start(bf16[32,512]{1,0:T(8,128)(2,1)S(1)} %get-tuple-element.36), channel_id=1, source_target_pairs={{0,1},{1,0},{2,3},{3,2},{4,5},{5,4},{6,7},{7,6},{8,9},{9,8},{10,11... | collective-permute-start | bytes 98312 | tf_op jit(solution)/shard_map/ppermute | solution.py:398
  14.9 8.1 %collective-permute-start.5 = (bf16[32,1024]{1,0:T(8,128)(2,1)S(1)}, bf16[32,1024]{1,0:T(8,128)(2,1)S(1)}, u32[]{:S(2)}, u32[]{:S(2)}) collective-permute-start(bf16[32,1024]{1,0:T(8,128)(2,1)S(1)} %pad_maximum_fusion.refs_0_), channel_id=1, source_target_pairs={{0,4},{4,0},{8,12},{12,8},{1,5},{5,1},{9,13},{13,9},{2,6},{6,2},{1... | collective-permute-start | bytes 196616 | tf_op jit(solution)/shard_map/ppermute | solution.py:298
  17.9 7.5 %collective-permute-start.7 = (bf16[32,1024]{1,0:T(8,128)(2,1)S(1)}, bf16[32,1024]{1,0:T(8,128)(2,1)S(1)}, u32[]{:S(2)}, u32[]{:S(2)}) collective-permute-start(bf16[32,1024]{1,0:T(8,128)(2,1)S(1)} %pad_maximum_fusion.refs_0_), channel_id=1, source_target_pairs={{0,8},{4,12},{8,0},{12,4},{1,9},{5,13},{9,1},{13,5},{2,10},{6,14},... | collective-permute-start | bytes 196616 | tf_op jit(solution)/shard_map/ppermute | solution.py:298
  20.5 7.3 %collective-permute-start.9 = (bf16[32,1024]{1,0:T(8,128)(2,1)S(1)}, bf16[32,1024]{1,0:T(8,128)(2,1)S(1)}, u32[]{:S(2)}, u32[]{:S(2)}) collective-permute-start(bf16[32,1024]{1,0:T(8,128)(2,1)S(1)} %pad_maximum_fusion.refs_0_), channel_id=1, source_target_pairs={{0,12},{4,8},{8,4},{12,0},{1,13},{5,9},{9,5},{13,1},{2,14},{6,10},... | collective-permute-start | bytes 196616 | tf_op jit(solution)/shard_map/ppermute | solution.py:298
  21.2 7.9 %collective-permute-start.4 = (bf16[1,32,1152]{2,1,0:T(8,128)(2,1)S(1)}, bf16[1,32,1152]{2,1,0:T(8,128)(2,1)S(1)}, u32[]{:S(2)}, u32[]{:S(2)}) collective-permute-start(bf16[1,32,1152]{2,1,0:T(8,128)(2,1)S(1)} %shard_map.85.near), channel_id=1, source_target_pairs={{0,2},{2,0},{1,3},{3,1},{4,6},{6,4},{5,7},{7,5},{8,10},{10,8},{9,1... | collective-permute-start | bytes 221192 | tf_op jit(solution)/shard_map/ppermute | solution.py:324
  23.7 6.0 %collective-permute-start.6 = (bf16[1,32,1152]{2,1,0:T(8,128)(2,1)S(1)}, bf16[1,32,1152]{2,1,0:T(8,128)(2,1)S(1)}, u32[]{:S(2)}, u32[]{:S(2)}) collective-permute-start(bf16[1,32,1152]{2,1,0:T(8,128)(2,1)S(1)} %shard_map.87.near), channel_id=1, source_target_pairs={{0,2},{2,0},{1,3},{3,1},{4,6},{6,4},{5,7},{7,5},{8,10},{10,8},{9,1... | collective-permute-start | bytes 221192 | tf_op jit(solution)/shard_map/ppermute | solution.py:324
  26.2 16.3 %copy-start.2 = (s32[4]{0:T(128)S(1)}, s32[4]{0:T(128)}, u32[]{:S(2)}) copy-start(s32[4]{0:T(128)} %owner_of.3) | copy-start | bytes 52
  26.2 16.3 %copy-start.4 = (s32[4]{0:T(128)S(1)}, s32[4]{0:T(128)}, u32[]{:S(2)}) copy-start(s32[4]{0:T(128)} %tenant_of.1) | copy-start | bytes 52
  26.2 25.5 %copy-start.1 = (f32[1,32,4608]{2,1,0:T(8,128)S(1)}, f32[1,32,4608]{2,1,0:T(8,128)}, u32[]{:S(2)}) copy-start(f32[1,32,4608]{2,1,0:T(8,128)} %refs_4_.1) | copy-start | bytes 1769476
  26.2 25.5 %copy-start.3 = (s32[4]{0:T(128)S(1)}, s32[4]{0:T(128)}, u32[]{:S(2)}) copy-start(s32[4]{0:T(128)} %counts.1) | copy-start | bytes 52
  26.2 4.4 %collective-permute-start.8 = (bf16[1,32,1152]{2,1,0:T(8,128)(2,1)S(1)}, bf16[1,32,1152]{2,1,0:T(8,128)(2,1)S(1)}, u32[]{:S(2)}, u32[]{:S(2)}) collective-permute-start(bf16[1,32,1152]{2,1,0:T(8,128)(2,1)S(1)} %shard_map.89.near), channel_id=1, source_target_pairs={{0,2},{2,0},{1,3},{3,1},{4,6},{6,4},{5,7},{7,5},{8,10},{10,8},{9,1... | collective-permute-start | bytes 221192 | tf_op jit(solution)/shard_map/ppermute | solution.py:324
  28.6 4.4 %collective-permute-start.10 = (bf16[1,32,1152]{2,1,0:T(8,128)(2,1)S(1)}, bf16[1,32,1152]{2,1,0:T(8,128)(2,1)S(1)}, u32[]{:S(2)}, u32[]{:S(2)}) collective-permute-start(bf16[1,32,1152]{2,1,0:T(8,128)(2,1)S(1)} %shard_map.91.near), channel_id=1, source_target_pairs={{0,2},{2,0},{1,3},{3,1},{4,6},{6,4},{5,7},{7,5},{8,10},{10,8},{9,1... | collective-permute-start | bytes 221192 | tf_op jit(solution)/shard_map/ppermute | solution.py:324
  33.5 1.2 %collective-permute-start.11 = (f32[8,128]{1,0:T(8,128)S(1)}, f32[8,128]{1,0:T(8,128)S(1)}, u32[]{:S(2)}, u32[]{:S(2)}) collective-permute-start(f32[8,128]{1,0:T(8,128)S(1)} %add_add_fusion), channel_id=1, source_target_pairs={{0,1},{1,0},{2,3},{3,2},{4,5},{5,4},{6,7},{7,6},{8,9},{9,8},{10,11... | collective-permute-start | bytes 12296 | tf_op jit(solution)/shard_map/ppermute | solution.py:337
  34.8 5.4 %collective-permute-start.14 = (f32[8,128]{1,0:T(8,128)S(1)}, f32[8,128]{1,0:T(8,128)S(1)}, u32[]{:S(2)}, u32[]{:S(2)}) collective-permute-start(f32[8,128]{1,0:T(8,128)S(1)} %add.15.refs_0_), channel_id=1, source_target_pairs={{0,12},{4,8},{8,4},{12,0},{1,13},{5,9},{9,5},{13,1},{2,14},{6,10},... | collective-permute-start | bytes 12296 | tf_op jit(solution)/shard_map/ppermute | solution.py:298
  38.0 4.5 %collective-permute-start.13 = (f32[8,128]{1,0:T(8,128)S(1)}, f32[8,128]{1,0:T(8,128)S(1)}, u32[]{:S(2)}, u32[]{:S(2)}) collective-permute-start(f32[8,128]{1,0:T(8,128)S(1)} %add.15.refs_0_), channel_id=1, source_target_pairs={{0,8},{4,12},{8,0},{12,4},{1,9},{5,13},{9,1},{13,5},{2,10},{6,14},... | collective-permute-start | bytes 12296 | tf_op jit(solution)/shard_map/ppermute | solution.py:298
  38.0 4.5 %collective-permute-start.12 = (f32[8,128]{1,0:T(8,128)S(1)}, f32[8,128]{1,0:T(8,128)S(1)}, u32[]{:S(2)}, u32[]{:S(2)}) collective-permute-start(f32[8,128]{1,0:T(8,128)S(1)} %add.15.refs_0_), channel_id=1, source_target_pairs={{0,4},{4,0},{8,12},{12,8},{1,5},{5,1},{9,13},{13,9},{2,6},{6,2},{1... | collective-permute-start | bytes 12296 | tf_op jit(solution)/shard_map/ppermute | solution.py:298
  43.3 4.5 %collective-permute-start.15 = (bf16[32,1152]{1,0:T(8,128)(2,1)S(1)}, bf16[32,1152]{1,0:T(8,128)(2,1)S(1)}, u32[]{:S(2)}, u32[]{:S(2)}) collective-permute-start(bf16[32,1152]{1,0:T(8,128)(2,1)S(1)} %get-tuple-element.46), channel_id=1, source_target_pairs={{0,4},{4,0},{8,12},{12,8},{1,5},{5,1},{9,13},{13,9},{2,6},{6,2},{1... | collective-permute-start | bytes 221192 | tf_op jit(solution)/shard_map/ppermute | solution.py:347
  43.7 7.1 %collective-permute-start.16 = (bf16[32,1152]{1,0:T(8,128)(2,1)S(1)}, bf16[32,1152]{1,0:T(8,128)(2,1)S(1)}, u32[]{:S(2)}, u32[]{:S(2)}) collective-permute-start(bf16[32,1152]{1,0:T(8,128)(2,1)S(1)} %get-tuple-element.47), channel_id=1, source_target_pairs={{0,8},{4,12},{8,0},{12,4},{1,9},{5,13},{9,1},{13,5},{2,10},{6,14},... | collective-permute-start | bytes 221192 | tf_op jit(solution)/shard_map/ppermute | solution.py:347
  45.5 6.2 %collective-permute-start.17 = (bf16[32,1152]{1,0:T(8,128)(2,1)S(1)}, bf16[32,1152]{1,0:T(8,128)(2,1)S(1)}, u32[]{:S(2)}, u32[]{:S(2)}) collective-permute-start(bf16[32,1152]{1,0:T(8,128)(2,1)S(1)} %get-tuple-element.48), channel_id=1, source_target_pairs={{0,12},{4,8},{8,4},{12,0},{1,13},{5,9},{9,5},{13,1},{2,14},{6,10},... | collective-permute-start | bytes 221192 | tf_op jit(solution)/shard_map/ppermute | solution.py:347

commit v5 on v4

--- a/solution.py
+++ b/solution.py
@@ -66,9 +66,9 @@
     )
 
 
-def triangle_kernel(place, q, k, g, totals, prompts, q_own, k_own, g_own, done):
+def triangle_kernel(q, k, g, totals, prompts, q_own, k_own, g_own, done):
     heads, rows, width = q_own.shape
-    skipped = place[1] * heads
+    skipped = lax.axis_index("seq") * heads
     lanes = width // HEAD_DIM * LANES
 
     def load(source, target, h, i):
@@ -103,14 +103,14 @@
         load(g, g_own, h, 2).wait()
 
 
-def own_triangle(place, q, k, g):
+def own_triangle(q, k, g):
     rows = q.shape[0]
     heads = k.shape[1] // (2 * HEAD_DIM)
     width = q.shape[1] // (2 * heads)
     lanes = width // HEAD_DIM * rows
     return pl.pallas_call(
         triangle_kernel,
-        in_specs=[SMEM, HBM, HBM, HBM],
+        in_specs=[HBM, HBM, HBM],
         out_specs=[VMEM] * 5,
         out_shape=[
             jax.ShapeDtypeStruct((heads, 8, lanes), jnp.float32),
@@ -126,16 +126,16 @@
             bytes_accessed=6 * heads * rows * width,
             transcendentals=heads * lanes * rows,
         ),
-    )(place, q, k, g)
+    )(q, k, g)
 
 
 def attention_kernel(
-    place, totals, prompts, q_own, k_own, g_own, q_far, k_far, g_far, mine, theirs, k_first, prob
+    totals, prompts, q_own, k_own, g_own, q_far, k_far, g_far, mine, theirs, k_first, prob
 ):
     heads, rows, width = q_own.shape
     group = width // HEAD_DIM
     lanes = group * LANES
-    first = place[1] == 0
+    first = lax.axis_index("seq") == 0
 
     def step(h, carry):
         at_q = pl.ds(pl.multiple_of(h * width, LANES), width)
@@ -181,12 +181,12 @@
     lax.fori_loop(0, heads, step, 0)
 
 
-def prompt_value_grad(place, totals, prompts, q_own, k_own, g_own, q_far, k_far, g_far):
+def prompt_value_grad(totals, prompts, q_own, k_own, g_own, q_far, k_far, g_far):
     heads, rows, width = q_own.shape
     group = width // HEAD_DIM
     return pl.pallas_call(
         attention_kernel,
-        in_specs=[SMEM] + [VMEM] * 8,
+        in_specs=[VMEM] * 8,
         out_specs=[VMEM] * 2,
         out_shape=[jax.ShapeDtypeStruct((PROMPT // 2, heads * HEAD_DIM), jnp.bfloat16)] * 2,
         scratch_shapes=[
@@ -199,16 +199,16 @@
             bytes_accessed=10 * rows * heads * width,
             transcendentals=heads * group * 3 * rows * rows,
         ),
-    )(place, totals, prompts, q_own, k_own, g_own, q_far, k_far, g_far)
-
-
-def sibling_kernel(place, *refs, starts):
+    )(totals, prompts, q_own, k_own, g_own, q_far, k_far, g_far)
+
+
+def sibling_kernel(*refs, starts):
     count = len(starts)
     sources, targets, done = refs[:count], refs[count : 2 * count], refs[2 * count]
     copies = []
     for i, start in enumerate(starts):
         rows, width = targets[i].shape
-        row, column = start(place)
+        row, column = start(lax.axis_index("seq"))
         window = sources[i].at[pl.ds(row, rows), pl.ds(pl.multiple_of(column, LANES), width)]
         copies.append(pltpu.make_async_copy(window, targets[i], done.at[i]))
     for copy in copies:
@@ -217,15 +217,15 @@
         copy.wait()
 
 
-def cut(place, arrays, starts, shapes):
+def cut(arrays, starts, shapes):
     return pl.pallas_call(
         functools.partial(sibling_kernel, starts=starts),
-        in_specs=[SMEM] + [HBM] * len(arrays),
+        in_specs=[HBM] * len(arrays),
         out_specs=[VMEM] * len(arrays),
         out_shape=[jax.ShapeDtypeStruct(shape, jnp.bfloat16) for shape in shapes],
         scratch_shapes=[pltpu.SemaphoreType.DMA((len(arrays),))],
         compiler_params=pltpu.CompilerParams(vmem_limit_bytes=16 * 1024 * 1024),
-    )(place, *arrays)
+    )(*arrays)
 
 
 def partial_kernel(*refs):
@@ -241,7 +241,7 @@
         out[i] = total[i * rows : (i + 1) * rows].astype(out.dtype)
 
 
-def combine_kernel(place, near, far, grad, squares, *, steps):
+def combine_kernel(near, far, grad, squares, *, steps):
     example = lax.broadcasted_iota(jnp.int32, squares.shape, 0)
     by_example = jnp.zeros(squares.shape, jnp.float32)
     for i, step in enumerate(steps):
@@ -252,11 +252,25 @@
             grad[i, :, at : at + LANES] = part
             folded = part * part if folded is None else folded + part * part
         folded = jnp.sum(folded, axis=0, keepdims=True)
-        by_example = jnp.where(example == (place[0] ^ step), folded, by_example)
+        by_example = jnp.where(example == (lax.axis_index("dp") ^ step), folded, by_example)
     squares[...] = by_example
 
 
-def share_kernel(place, tenant_of, owner_of, *refs, groups):
+def select_kernel(tenant_of, owner_of, counts, select, count, *, examples):
+    dp_index = lax.axis_index("dp")
+    for step in range(examples):
+        owner = owner_of[tenant_of[dp_index ^ step]]
+        for k in range(examples):
+            hit = jnp.where(owner == (dp_index ^ k), 1.0, 0.0)
+            row = k * examples + step
+            select[row : row + 1, :] = jnp.full((1, LANES), hit, jnp.float32)
+    total = 0
+    for slot in range(examples):
+        total = total + jnp.where(owner_of[slot] == dp_index, counts[slot], 0)
+    count[...] = jnp.full((1, LANES), total.astype(jnp.float32), jnp.float32)
+
+
+def share_kernel(select, *refs, groups):
     examples = sum(len(steps) for steps in groups)
     norms, grads = refs[:examples], refs[examples : examples + len(groups)]
     outs, scales = refs[examples + len(groups) : -1], refs[-1]
@@ -265,11 +279,11 @@
         norm_sq = norm_sq + other[...]
     norm_sq = jnp.sum(norm_sq, axis=1, keepdims=True)
     scales[...] = jnp.broadcast_to(1.0 / jnp.maximum(1.0, jnp.sqrt(norm_sq)), scales.shape)
-    scale = [scales[pl.ds(place[0] ^ step, 1), :] for step in range(examples)]
-    owner = [owner_of[tenant_of[place[0] ^ step]] for step in range(examples)]
+    dp_index = lax.axis_index("dp")
+    scale = [scales[pl.ds(dp_index ^ step, 1), :] for step in range(examples)]
     for k in range(examples):
         factor = [
-            scale[step] * (owner[step] == (place[0] ^ k)).astype(jnp.float32)
+            scale[step] * select[k * examples + step : k * examples + step + 1, :]
             for step in range(examples)
         ]
         for at in range(0, outs[k].shape[1], LANES):
@@ -281,24 +295,32 @@
             outs[k][:, at : at + LANES] = total.astype(jnp.bfloat16)
 
 
-def update_kernel(place, owner_of, counts, *refs, examples):
+def update_kernel(count, *refs, examples):
     shares, noise, out = refs[:examples], refs[examples], refs[examples + 1]
+    stage, done = refs[examples + 2 :]
     columns = shares[0].shape[1]
-    count = 0
-    for slot in range(owner_of.shape[0]):
-        count = count + jnp.where(owner_of[slot] == place[0], counts[slot], 0)
-    count = count.astype(jnp.float32)
+    dp_index = lax.axis_index("dp")
+    copies = []
     for step in range(examples):
-        at = pl.ds(pl.multiple_of((place[0] ^ step) * columns, LANES), columns)
-        share = shares[step][...].astype(jnp.float32)
-        out[0, :, at] = (math.sqrt(PROMPT * D) * share + noise[0, :, at]) / count
+        base = pl.multiple_of((dp_index ^ step) * columns, LANES)
+        for at in range(0, columns, LANES):
+            share = shares[step][:, at : at + LANES].astype(jnp.float32)
+            added = noise[0, :, pl.ds(pl.multiple_of(base + at, LANES), LANES)]
+            stage[step, :, at : at + LANES] = (math.sqrt(PROMPT * D) * share + added) / count[...]
+        copy = pltpu.make_async_copy(
+            stage.at[step], out.at[0, :, pl.ds(base, columns)], done.at[step]
+        )
+        copy.start()
+        copies.append(copy)
+    for copy in copies:
+        copy.wait()
 
 
 def to_dp(array, dp):
     return [array] + [lax.ppermute(array, "dp", xor_pairs(dp, step)) for step in range(1, dp)]
 
 
-def tail_by_permutes(place, value_grad, weight, tenant_of, owner_of, counts, noise, sizes):
+def tail_by_permutes(value_grad, weight, tenant_of, owner_of, counts, noise, sizes):
     dp = sizes["dp"]
     columns = weight.shape[0]
     rows = PROMPT // 2
@@ -306,6 +328,17 @@
     small = pltpu.CompilerParams(vmem_limit_bytes=16 * 1024 * 1024)
     blocks = to_dp(value_grad, dp)
     groups = GROUPS(dp)
+    tenant_of, blocks[-1] = lax.optimization_barrier((tenant_of, blocks[-1]))
+    select, count = pl.pallas_call(
+        functools.partial(select_kernel, examples=dp),
+        in_specs=[SMEM] * 3,
+        out_specs=[VMEM] * 2,
+        out_shape=[
+            jax.ShapeDtypeStruct((dp * dp, LANES), jnp.float32),
+            jax.ShapeDtypeStruct((1, LANES), jnp.float32),
+        ],
+        compiler_params=small,
+    )(tenant_of, owner_of, counts)
     grads, squares = [], None
     for steps in groups:
         shape = (len(steps), rows, columns)
@@ -324,35 +357,39 @@
         far = lax.ppermute(near, "tensor", swap)
         grad, square = pl.pallas_call(
             functools.partial(combine_kernel, steps=steps),
-            in_specs=[SMEM] + [VMEM] * 2,
+            in_specs=[VMEM] * 2,
             out_specs=[VMEM] * 2,
             out_shape=[
                 jax.ShapeDtypeStruct(shape, jnp.float32),
                 jax.ShapeDtypeStruct((8, LANES), jnp.float32),
             ],
             compiler_params=small,
-        )(place, near, far)
+        )(near, far)
         grads.append(grad)
         squares = square if squares is None else squares + square
     norms = to_dp(squares + lax.ppermute(squares, "seq", swap), dp)
     shares = pl.pallas_call(
         functools.partial(share_kernel, groups=groups),
-        in_specs=[SMEM] * 3 + [VMEM] * (dp + len(groups)),
+        in_specs=[VMEM] * (1 + dp + len(groups)),
         out_specs=[VMEM] * dp,
         out_shape=[jax.ShapeDtypeStruct((rows, columns), jnp.bfloat16)] * dp,
         scratch_shapes=[pltpu.VMEM((8, LANES), jnp.float32)],
         compiler_params=small,
-    )(place, tenant_of, owner_of, *norms, *grads)
+    )(select, *norms, *grads)
     arrived = [shares[0]] + [
         lax.ppermute(shares[step], "dp", xor_pairs(dp, step)) for step in range(1, dp)
     ]
     return pl.pallas_call(
         functools.partial(update_kernel, examples=dp),
-        in_specs=[SMEM] * 3 + [VMEM] * (dp + 1),
-        out_specs=VMEM,
+        in_specs=[VMEM] * (dp + 2),
+        out_specs=ANY,
         out_shape=jax.ShapeDtypeStruct(noise.shape, jnp.float32),
+        scratch_shapes=[
+            pltpu.VMEM((dp, rows, columns), jnp.float32),
+            pltpu.SemaphoreType.DMA((dp,)),
+        ],
         compiler_params=small,
-    )(place, owner_of, counts, *arrived, noise)
+    )(count, *arrived, noise)
 
 
 def tail_by_collectives(value_grad, weight, tenant_of, owner_of, counts, noise):
@@ -379,31 +416,31 @@
 
 def body(sizes, queries, keys, out_grad, value_weight, tenant_of, owner_of, counts, noise):
     swap = xor_pairs(2, 1)
-    place = jnp.stack([lax.axis_index(a) for a in ("dp", "seq", "tensor")]).astype(jnp.int32)
-    seq_index = place[1]
+    seq_index = lax.axis_index("seq")
     q, k, g = (
         pltpu.with_memory_space_constraint(x[0], pltpu.HBM) for x in (queries, keys, out_grad)
     )
 
     def other_half(array):
         half = array.shape[1] // 2
-        return (lambda at: (0, (1 - at[1]) * half)), (array.shape[0], half)
+        return (lambda seq: (0, (1 - seq) * half)), (array.shape[0], half)
 
     starts, shapes = zip(*[other_half(x) for x in (k, q, g)])
     k_far, q_far, g_far = (
-        lax.ppermute(x, "seq", swap) for x in cut(place, (k, q, g), starts, shapes)
-    )
-    own = own_triangle(place, q, k, g)
-    mine, theirs = prompt_value_grad(place, *own, q_far, k_far, g_far)
+        lax.ppermute(x, "seq", swap) for x in cut((k, q, g), starts, shapes)
+    )
+    aligned = value_weight.shape[0] % LANES == 0 and sizes["dp"] in (1, 2, 4, 8)
+    permutes = sizes["tensor"] == 2 and aligned
+    own = own_triangle(q, k, g)
+    mine, theirs = prompt_value_grad(*own, q_far, k_far, g_far)
     other = lax.ppermute(theirs, "seq", swap)
     first = seq_index == 0
     value_grad = jnp.concatenate(
         [jnp.where(first, mine, other), jnp.where(first, other, mine)], axis=1
     )
-    aligned = value_weight.shape[0] % LANES == 0 and sizes["dp"] in (1, 2, 4, 8)
-    if sizes["tensor"] == 2 and aligned:
+    if permutes:
         return tail_by_permutes(
-            place, value_grad, value_weight, tenant_of, owner_of, counts, noise, sizes
+            value_grad, value_weight, tenant_of, owner_of, counts, noise, sizes
         )
     return tail_by_collectives(value_grad, value_weight, tenant_of, owner_of, counts, noise)
 

time: 53.3 us -> 49.8 us (0.934)
  Pallas kernels: 19.8 us -> 15.4 us
  starting transfers between devices: 20.1 us -> 21.4 us
    ppermute x6, waiting for transfers between devices: 4.68 us -> 2.49 us  [to_dp(): lax.ppermute(array, 'dp', xor_pairs(dp, step))]
    pallas_call x4, Pallas kernels: 2.3 us -> 0.15 us  [tail_by_permutes(): pl.pallas_call(functools.partial(combine_kernel, steps=steps), in_specs=[...]
    ppermute x4, waiting for transfers between devices: 2.07 us -> 3.39 us  [tail_by_permutes(): far = lax.ppermute(near, 'tensor', swap)]
    ppermute x4, starting transfers between devices: 4.18 us -> 5.33 us  [tail_by_permutes(): far = lax.ppermute(near, 'tensor', swap)]
    pallas_call x3 -> x4, Pallas kernels: 11.3 us -> 10.2 us  [the longest x1 5.56 us: prompt_value_grad(): pl.pallas_call(attention_kernel, in_specs=[VMEM] * 8, out_specs=[VMEM] *...]
    pallas_call x1, Pallas kernels: 0.84 us -> 0.28 us  [tail_by_permutes(): pl.pallas_call(functools.partial(share_kernel, groups=groups), in_specs=[...]
    pallas_call x1, Pallas kernels: 2.28 us -> 1.73 us  [cut(): pl.pallas_call(functools.partial(sibling_kernel, starts=starts), in_specs...]
    ppermute x3, waiting for transfers between devices: 0.28 us -> 0.83 us  [body(): lax.ppermute(x, 'seq', swap)]
  transfers between devices with their start and end apart: 18 -> 18, of which waited for: 10 -> 9; matrix products, arithmetic and copies ran while one was open for 0% -> 0% of each run, Pallas kernels for 16% -> 14%
where the time goes in v5:
time: 49.8 us; the launch traced here: 49.6 us
  starting transfers between devices  21.4 us (43%)
  Pallas kernels  15.4 us (31%)
  waiting for transfers between devices  12.6 us (25%)
    ppermute x6, starting transfers between devices, to_dp(): lax.ppermute(array, 'dp', xor_pairs(dp, step))  10 us
    pallas_call x1, Pallas kernels, prompt_value_grad(): pl.pallas_call(attention_kernel, in_specs=[VMEM] * 8, out_specs=[VMEM] *...  5.56 us
    ppermute x4, starting transfers between devices, tail_by_permutes(): far = lax.ppermute(near, 'tensor', swap)  5.33 us
    ppermute x3, starting transfers between devices, tail_by_permutes(): lax.ppermute(shares[step], 'dp', xor_pairs(dp, step))  4.45 us
    ppermute x3, waiting for transfers between devices, tail_by_permutes(): lax.ppermute(shares[step], 'dp', xor_pairs(dp, step))  3.92 us
    ppermute x4, waiting for transfers between devices, tail_by_permutes(): far = lax.ppermute(near, 'tensor', swap)  3.39 us
    pallas_call x1, Pallas kernels, own_triangle(): pl.pallas_call(triangle_kernel, in_specs=[HBM, HBM, HBM], out_specs=[VMEM...  3.19 us
    pallas_call x4, Pallas kernels, tail_by_permutes(): pl.pallas_call(partial_kernel, in_specs=[VMEM] * (len(steps) + 1), out_sp...  3.06 us
  transfers between devices with their start and end apart: 18, of which 9 were waited for; matrix products, arithmetic and copies ran while one was open for 0% of the time, Pallas kernels for 14%

profile of v5, /device:TPU:0, one launch (start us, length us, event | category | flops | bytes accessed | tf_op | source)
XLA Modules:
  0.0 49.6 jit_solution(13042966334900706891)
XLA Ops:
  0.0 1.7 %shard_map.83 = (bf16[512,512]{1,0:T(8,128)(2,1)S(1)}, bf16[512,1024]{1,0:T(8,128)(2,1)S(1)}, bf16[512,1024]{1,0:T(8,128)(2,1)S(1)}) custom-call(bf16[512,1024]{1,0:T(8,128)(2,1)} %bitcast.7, bf16[512,2048]{1,0:T(8,128)(2,1)} %bitcast.3, bf16[512,2048]{1,0:T(8,128)(2,1)} %bitcast.5), custom_call_target="tpu_custom_call" | custom-call | tf_op jit(solution)/shard_map/pallas_call | solution.py:221
  2.8 3.2 %shard_map.82 = (f32[4,8,1024]{2,1,0:T(8,128)S(1)}, f32[4,64,1024]{2,1,0:T(8,128)S(1)}, bf16[4,512,256]{2,1,0:T(8,128)(2,1)S(1)}, bf16[4,512,128]{2,1,0:T(8,128)(2,1)S(1)}, bf16[4,512,256]{2,1,0:T(8,128)(2,1)S(1)}) custom-call(bf16[512,2048]{1,0:T(8,128)(2,1)} %bitcast.4, bf16[512,1024]{1,0:T(8,128)(2,1)} %bitcast.8, bf16[512,2048]{1,0:T(8,128)(2,1)} %bitcast.6), custom_call_target="tpu_custom_call" | custom-call | flops 536870912 | bytes 3145728 | tf_op jit(solution)/shard_map/pallas_call | solution.py:111
  6.0 0.8 %collective-permute-done.1.k_far = bf16[512,512]{1,0:T(8,128)(2,1)S(1)} collective-permute-done((bf16[512,512]{1,0:T(8,128)(2,1)S(1)}, bf16[512,512]{1,0:T(8,128)(2,1)S(1)}, u32[]{:S(2)}, u32[]{:S(2)}) %collective-permute-start.1) | collective-permute-done | bytes 524320 | tf_op jit(solution)/shard_map/ppermute | solution.py:430
  6.8 5.6 %shard_map.84 = (bf16[32,512]{1,0:T(8,128)(2,1)S(1)}, bf16[32,512]{1,0:T(8,128)(2,1)S(1)}) custom-call(f32[4,8,1024]{2,1,0:T(8,128)S(1)} %get-tuple-element.31.totals, f32[4,64,1024]{2,1,0:T(8,128)S(1)} %get-tuple-element.32.prompts, bf16[4,512,256]{2,1,0:T(8,128)(2,1)S(1)} %get-tuple-element.33.q_own, bf16[4,512,128]{2,1,0:T(8,128)(2,1)S(1)} %get-tuple-element.34.k_own, ...), custom_call_target="tpu_custom_call" | custom-call | flops 1879048192 | bytes 5242880 | tf_op jit(solution)/shard_map/pallas_call | solution.py:187
  12.8 0.9 %collective-permute-done.3 = bf16[32,512]{1,0:T(8,128)(2,1)S(1)} collective-permute-done((bf16[32,512]{1,0:T(8,128)(2,1)S(1)}, bf16[32,512]{1,0:T(8,128)(2,1)S(1)}, u32[]{:S(2)}, u32[]{:S(2)}) %collective-permute-start.3) | collective-permute-done | bytes 32800 | tf_op jit(solution)/shard_map/ppermute | solution.py:436
  13.7 5.0 %collective-permute-start.4 = (bf16[32,1024]{1,0:T(8,128)(2,1)S(1)}, bf16[32,1024]{1,0:T(8,128)(2,1)S(1)}, u32[]{:S(2)}, u32[]{:S(2)}) collective-permute-start(bf16[32,1024]{1,0:T(8,128)(2,1)S(1)} %pad_maximum_fusion.refs_0_), channel_id=1, source_target_pairs={{0,12},{4,8},{8,4},{12,0},{1,13},{5,9},{9,5},{13,1},{2,14},{6,10},... | collective-permute-start | bytes 196616 | tf_op jit(solution)/shard_map/ppermute | solution.py:320
  20.1 1.6 %collective-permute-start.5 = (bf16[1,32,1152]{2,1,0:T(8,128)(2,1)S(1)}, bf16[1,32,1152]{2,1,0:T(8,128)(2,1)S(1)}, u32[]{:S(2)}, u32[]{:S(2)}) collective-permute-start(bf16[1,32,1152]{2,1,0:T(8,128)(2,1)S(1)} %shard_map.86.near), channel_id=1, source_target_pairs={{0,2},{2,0},{1,3},{3,1},{4,6},{6,4},{5,7},{7,5},{8,10},{10,8},{9,1... | collective-permute-start | bytes 221192 | tf_op jit(solution)/shard_map/ppermute | solution.py:357
  21.8 0.8 %shard_map.92.near = bf16[1,32,1152]{2,1,0:T(8,128)(2,1)S(1)} custom-call(bf16[32,1024]{1,0:T(8,128)(2,1)S(1)} %collective-permute-done.4.refs_0_, bf16[1152,1024]{1,0:T(8,128)(2,1)S(1)} %copy-done), custom_call_target="tpu_custom_call" | custom-call | flops 75497472 | bytes 2359296 | tf_op jit(solution)/shard_map/pallas_call | solution.py:345
  22.5 1.6 %collective-permute-start.10 = (bf16[1,32,1152]{2,1,0:T(8,128)(2,1)S(1)}, bf16[1,32,1152]{2,1,0:T(8,128)(2,1)S(1)}, u32[]{:S(2)}, u32[]{:S(2)}) collective-permute-start(bf16[1,32,1152]{2,1,0:T(8,128)(2,1)S(1)} %shard_map.92.near), channel_id=1, source_target_pairs={{0,2},{2,0},{1,3},{3,1},{4,6},{6,4},{5,7},{7,5},{8,10},{10,8},{9,1... | collective-permute-start | bytes 221192 | tf_op jit(solution)/shard_map/ppermute | solution.py:357
  24.1 0.8 %shard_map.88.near = bf16[1,32,1152]{2,1,0:T(8,128)(2,1)S(1)} custom-call(bf16[32,1024]{1,0:T(8,128)(2,1)S(1)} %collective-permute-done.6.refs_0_, bf16[1152,1024]{1,0:T(8,128)(2,1)S(1)} %copy-done), custom_call_target="tpu_custom_call" | custom-call | flops 75497472 | bytes 2359296 | tf_op jit(solution)/shard_map/pallas_call | solution.py:345
  24.9 1.2 %collective-permute-start.7 = (bf16[1,32,1152]{2,1,0:T(8,128)(2,1)S(1)}, bf16[1,32,1152]{2,1,0:T(8,128)(2,1)S(1)}, u32[]{:S(2)}, u32[]{:S(2)}) collective-permute-start(bf16[1,32,1152]{2,1,0:T(8,128)(2,1)S(1)} %shard_map.88.near), channel_id=1, source_target_pairs={{0,2},{2,0},{1,3},{3,1},{4,6},{6,4},{5,7},{7,5},{8,10},{10,8},{9,1... | collective-permute-start | bytes 221192 | tf_op jit(solution)/shard_map/ppermute | solution.py:357
  26.2 0.8 %shard_map.90.near = bf16[1,32,1152]{2,1,0:T(8,128)(2,1)S(1)} custom-call(bf16[32,1024]{1,0:T(8,128)(2,1)S(1)} %collective-permute-done.8.refs_0_, bf16[1152,1024]{1,0:T(8,128)(2,1)S(1)} %copy-done), custom_call_target="tpu_custom_call" | custom-call | flops 75497472 | bytes 2359296 | tf_op jit(solution)/shard_map/pallas_call | solution.py:345
  27.0 0.9 %collective-permute-start.9 = (bf16[1,32,1152]{2,1,0:T(8,128)(2,1)S(1)}, bf16[1,32,1152]{2,1,0:T(8,128)(2,1)S(1)}, u32[]{:S(2)}, u32[]{:S(2)}) collective-permute-start(bf16[1,32,1152]{2,1,0:T(8,128)(2,1)S(1)} %shard_map.90.near), channel_id=1, source_target_pairs={{0,2},{2,0},{1,3},{3,1},{4,6},{6,4},{5,7},{7,5},{8,10},{10,8},{9,1... | collective-permute-start | bytes 221192 | tf_op jit(solution)/shard_map/ppermute | solution.py:357
  27.9 2.2 %collective-permute-done.7.far = bf16[1,32,1152]{2,1,0:T(8,128)(2,1)S(1)} collective-permute-done((bf16[1,32,1152]{2,1,0:T(8,128)(2,1)S(1)}, bf16[1,32,1152]{2,1,0:T(8,128)(2,1)S(1)}, u32[]{:S(2)}, u32[]{:S(2)}) %collective-permute-start.7) | collective-permute-done | bytes 73760 | tf_op jit(solution)/shard_map/ppermute | solution.py:357
  30.1 1.2 %collective-permute-done.9.far = bf16[1,32,1152]{2,1,0:T(8,128)(2,1)S(1)} collective-permute-done((bf16[1,32,1152]{2,1,0:T(8,128)(2,1)S(1)}, bf16[1,32,1152]{2,1,0:T(8,128)(2,1)S(1)}, u32[]{:S(2)}, u32[]{:S(2)}) %collective-permute-start.9) | collective-permute-done | bytes 73760 | tf_op jit(solution)/shard_map/ppermute | solution.py:357
  31.5 1.2 %collective-permute-done.11 = f32[8,128]{1,0:T(8,128)S(1)} collective-permute-done((f32[8,128]{1,0:T(8,128)S(1)}, f32[8,128]{1,0:T(8,128)S(1)}, u32[]{:S(2)}, u32[]{:S(2)}) %collective-permute-start.11) | collective-permute-done | bytes 4128 | tf_op jit(solution)/shard_map/ppermute | solution.py:370
  32.6 3.0 %collective-permute-start.14 = (f32[8,128]{1,0:T(8,128)S(1)}, f32[8,128]{1,0:T(8,128)S(1)}, u32[]{:S(2)}, u32[]{:S(2)}) collective-permute-start(f32[8,128]{1,0:T(8,128)S(1)} %add.15.refs_0_), channel_id=1, source_target_pairs={{0,12},{4,8},{8,4},{12,0},{1,13},{5,9},{9,5},{13,1},{2,14},{6,10},... | collective-permute-start | bytes 12296 | tf_op jit(solution)/shard_map/ppermute | solution.py:320
  35.6 1.4 %collective-permute-start.12 = (f32[8,128]{1,0:T(8,128)S(1)}, f32[8,128]{1,0:T(8,128)S(1)}, u32[]{:S(2)}, u32[]{:S(2)}) collective-permute-start(f32[8,128]{1,0:T(8,128)S(1)} %add.15.refs_0_), channel_id=1, source_target_pairs={{0,4},{4,0},{8,12},{12,8},{1,5},{5,1},{9,13},{13,9},{2,6},{6,2},{1... | collective-permute-start | bytes 12296 | tf_op jit(solution)/shard_map/ppermute | solution.py:320
  38.0 2.1 %collective-permute-done.13.refs_2_ = f32[8,128]{1,0:T(8,128)S(1)} collective-permute-done((f32[8,128]{1,0:T(8,128)S(1)}, f32[8,128]{1,0:T(8,128)S(1)}, u32[]{:S(2)}, u32[]{:S(2)}) %collective-permute-start.13) | collective-permute-done | bytes 4128 | tf_op jit(solution)/shard_map/ppermute | solution.py:320
  41.0 1.6 %collective-permute-start.16 = (bf16[32,1152]{1,0:T(8,128)(2,1)S(1)}, bf16[32,1152]{1,0:T(8,128)(2,1)S(1)}, u32[]{:S(2)}, u32[]{:S(2)}) collective-permute-start(bf16[32,1152]{1,0:T(8,128)(2,1)S(1)} %get-tuple-element.55), channel_id=1, source_target_pairs={{0,8},{4,12},{8,0},{12,4},{1,9},{5,13},{9,1},{13,5},{2,10},{6,14},... | collective-permute-start | bytes 221192 | tf_op jit(solution)/shard_map/ppermute | solution.py:380
  42.6 2.3 %collective-permute-start.17 = (bf16[32,1152]{1,0:T(8,128)(2,1)S(1)}, bf16[32,1152]{1,0:T(8,128)(2,1)S(1)}, u32[]{:S(2)}, u32[]{:S(2)}) collective-permute-start(bf16[32,1152]{1,0:T(8,128)(2,1)S(1)} %get-tuple-element.56), channel_id=1, source_target_pairs={{0,12},{4,8},{8,4},{12,0},{1,13},{5,9},{9,5},{13,1},{2,14},{6,10},... | collective-permute-start | bytes 221192 | tf_op jit(solution)/shard_map/ppermute | solution.py:380
  44.8 3.0 %collective-permute-done.16.refs_2_ = bf16[32,1152]{1,0:T(8,128)(2,1)S(1)} collective-permute-done((bf16[32,1152]{1,0:T(8,128)(2,1)S(1)}, bf16[32,1152]{1,0:T(8,128)(2,1)S(1)}, u32[]{:S(2)}, u32[]{:S(2)}) %collective-permute-start.16) | collective-permute-done | bytes 73760 | tf_op jit(solution)/shard_map/ppermute | solution.py:380
  47.8 0.9 %collective-permute-done.17.refs_3_ = bf16[32,1152]{1,0:T(8,128)(2,1)S(1)} collective-permute-done((bf16[32,1152]{1,0:T(8,128)(2,1)S(1)}, bf16[32,1152]{1,0:T(8,128)(2,1)S(1)}, u32[]{:S(2)}, u32[]{:S(2)}) %collective-permute-start.17) | collective-permute-done | bytes 73760 | tf_op jit(solution)/shard_map/ppermute | solution.py:380
  48.8 0.9 %shard_map.95 = f32[1,32,4608]{2,1,0:T(8,128)} custom-call(f32[1,128]{1,0:T(1,128)S(1)} %get-tuple-element.42.count, bf16[32,1152]{1,0:T(8,128)(2,1)S(1)} %get-tuple-element.53.refs_0_, bf16[32,1152]{1,0:T(8,128)(2,1)S(1)} %collective-permute-done.15.refs_1_, bf16[32,1152]{1,0:T(8,128)(2,1)S(1)} %collective-permute-done.16.refs_2_, ...), custom_call_target="tpu_custom_call" | custom-call | tf_op jit(solution)/shard_map/pallas_call | solution.py:382
  (40 shorter events, 5.0 us)
Async XLA Ops:
  1.7 5.1 %collective-permute-start = (bf16[512,1024]{1,0:T(8,128)(2,1)S(1)}, bf16[512,1024]{1,0:T(8,128)(2,1)S(1)}, u32[]{:S(2)}, u32[]{:S(2)}) collective-permute-start(bf16[512,1024]{1,0:T(8,128)(2,1)S(1)} %get-tuple-element.36), channel_id=1, source_target_pairs={{0,1},{1,0},{2,3},{3,2},{4,5},{5,4},{6,7},{7,6},{8,9},{9,8},{10,11... | collective-permute-start | bytes 3145736 | tf_op jit(solution)/shard_map/ppermute | solution.py:430
  2.3 4.5 %collective-permute-start.2 = (bf16[512,1024]{1,0:T(8,128)(2,1)S(1)}, bf16[512,1024]{1,0:T(8,128)(2,1)S(1)}, u32[]{:S(2)}, u32[]{:S(2)}) collective-permute-start(bf16[512,1024]{1,0:T(8,128)(2,1)S(1)} %get-tuple-element.38), channel_id=1, source_target_pairs={{0,1},{1,0},{2,3},{3,2},{4,5},{5,4},{6,7},{7,6},{8,9},{9,8},{10,11... | collective-permute-start | bytes 3145736 | tf_op jit(solution)/shard_map/ppermute | solution.py:430
  2.3 4.5 %collective-permute-start.1 = (bf16[512,512]{1,0:T(8,128)(2,1)S(1)}, bf16[512,512]{1,0:T(8,128)(2,1)S(1)}, u32[]{:S(2)}, u32[]{:S(2)}) collective-permute-start(bf16[512,512]{1,0:T(8,128)(2,1)S(1)} %get-tuple-element.37), channel_id=1, source_target_pairs={{0,1},{1,0},{2,3},{3,2},{4,5},{5,4},{6,7},{7,6},{8,9},{9,8},{10,11... | collective-permute-start | bytes 1572872 | tf_op jit(solution)/shard_map/ppermute | solution.py:430
  6.8 12.6 %copy-start = (bf16[1152,1024]{1,0:T(8,128)(2,1)S(1)}, bf16[1152,1024]{1,0:T(8,128)(2,1)}, u32[]{:S(2)}) copy-start(bf16[1152,1024]{1,0:T(8,128)(2,1)} %refs_1_.7) | copy-start | bytes 7077892
  12.4 1.3 %collective-permute-start.3 = (bf16[32,512]{1,0:T(8,128)(2,1)S(1)}, bf16[32,512]{1,0:T(8,128)(2,1)S(1)}, u32[]{:S(2)}, u32[]{:S(2)}) collective-permute-start(bf16[32,512]{1,0:T(8,128)(2,1)S(1)} %get-tuple-element.40), channel_id=1, source_target_pairs={{0,1},{1,0},{2,3},{3,2},{4,5},{5,4},{6,7},{7,6},{8,9},{9,8},{10,11... | collective-permute-start | bytes 98312 | tf_op jit(solution)/shard_map/ppermute | solution.py:436
  13.7 8.1 %collective-permute-start.4 = (bf16[32,1024]{1,0:T(8,128)(2,1)S(1)}, bf16[32,1024]{1,0:T(8,128)(2,1)S(1)}, u32[]{:S(2)}, u32[]{:S(2)}) collective-permute-start(bf16[32,1024]{1,0:T(8,128)(2,1)S(1)} %pad_maximum_fusion.refs_0_), channel_id=1, source_target_pairs={{0,12},{4,8},{8,4},{12,0},{1,13},{5,9},{9,5},{13,1},{2,14},{6,10},... | collective-permute-start | bytes 196616 | tf_op jit(solution)/shard_map/ppermute | solution.py:320
  18.7 5.4 %collective-permute-start.6 = (bf16[32,1024]{1,0:T(8,128)(2,1)S(1)}, bf16[32,1024]{1,0:T(8,128)(2,1)S(1)}, u32[]{:S(2)}, u32[]{:S(2)}) collective-permute-start(bf16[32,1024]{1,0:T(8,128)(2,1)S(1)} %pad_maximum_fusion.refs_0_), channel_id=1, source_target_pairs={{0,4},{4,0},{8,12},{12,8},{1,5},{5,1},{9,13},{13,9},{2,6},{6,2},{1... | collective-permute-start | bytes 196616 | tf_op jit(solution)/shard_map/ppermute | solution.py:320
  18.7 7.5 %collective-permute-start.8 = (bf16[32,1024]{1,0:T(8,128)(2,1)S(1)}, bf16[32,1024]{1,0:T(8,128)(2,1)S(1)}, u32[]{:S(2)}, u32[]{:S(2)}) collective-permute-start(bf16[32,1024]{1,0:T(8,128)(2,1)S(1)} %pad_maximum_fusion.refs_0_), channel_id=1, source_target_pairs={{0,8},{4,12},{8,0},{12,4},{1,9},{5,13},{9,1},{13,5},{2,10},{6,14},... | collective-permute-start | bytes 196616 | tf_op jit(solution)/shard_map/ppermute | solution.py:320
  20.1 7.7 %collective-permute-start.5 = (bf16[1,32,1152]{2,1,0:T(8,128)(2,1)S(1)}, bf16[1,32,1152]{2,1,0:T(8,128)(2,1)S(1)}, u32[]{:S(2)}, u32[]{:S(2)}) collective-permute-start(bf16[1,32,1152]{2,1,0:T(8,128)(2,1)S(1)} %shard_map.86.near), channel_id=1, source_target_pairs={{0,2},{2,0},{1,3},{3,1},{4,6},{6,4},{5,7},{7,5},{8,10},{10,8},{9,1... | collective-permute-start | bytes 221192 | tf_op jit(solution)/shard_map/ppermute | solution.py:357
  22.5 5.3 %collective-permute-start.10 = (bf16[1,32,1152]{2,1,0:T(8,128)(2,1)S(1)}, bf16[1,32,1152]{2,1,0:T(8,128)(2,1)S(1)}, u32[]{:S(2)}, u32[]{:S(2)}) collective-permute-start(bf16[1,32,1152]{2,1,0:T(8,128)(2,1)S(1)} %shard_map.92.near), channel_id=1, source_target_pairs={{0,2},{2,0},{1,3},{3,1},{4,6},{6,4},{5,7},{7,5},{8,10},{10,8},{9,1... | collective-permute-start | bytes 221192 | tf_op jit(solution)/shard_map/ppermute | solution.py:357
  24.9 12.1 %copy-start.2 = (s32[4]{0:T(128)S(1)}, s32[4]{0:T(128)}, u32[]{:S(2)}) copy-start(s32[4]{0:T(128)} %tenant_of) | copy-start | bytes 52
  24.9 12.1 %copy-start.3 = (s32[4]{0:T(128)S(1)}, s32[4]{0:T(128)}, u32[]{:S(2)}) copy-start(s32[4]{0:T(128)} %owner_of.1) | copy-start | bytes 52
  24.9 12.1 %copy-start.4 = (s32[4]{0:T(128)S(1)}, s32[4]{0:T(128)}, u32[]{:S(2)}) copy-start(s32[4]{0:T(128)} %counts.1) | copy-start | bytes 52
  24.9 23.8 %copy-start.1 = (f32[1,32,4608]{2,1,0:T(8,128)S(1)}, f32[1,32,4608]{2,1,0:T(8,128)}, u32[]{:S(2)}) copy-start(f32[1,32,4608]{2,1,0:T(8,128)} %refs_4_.1) | copy-start | bytes 1769476
  24.9 5.2 %collective-permute-start.7 = (bf16[1,32,1152]{2,1,0:T(8,128)(2,1)S(1)}, bf16[1,32,1152]{2,1,0:T(8,128)(2,1)S(1)}, u32[]{:S(2)}, u32[]{:S(2)}) collective-permute-start(bf16[1,32,1152]{2,1,0:T(8,128)(2,1)S(1)} %shard_map.88.near), channel_id=1, source_target_pairs={{0,2},{2,0},{1,3},{3,1},{4,6},{6,4},{5,7},{7,5},{8,10},{10,8},{9,1... | collective-permute-start | bytes 221192 | tf_op jit(solution)/shard_map/ppermute | solution.py:357
  27.0 4.4 %collective-permute-start.9 = (bf16[1,32,1152]{2,1,0:T(8,128)(2,1)S(1)}, bf16[1,32,1152]{2,1,0:T(8,128)(2,1)S(1)}, u32[]{:S(2)}, u32[]{:S(2)}) collective-permute-start(bf16[1,32,1152]{2,1,0:T(8,128)(2,1)S(1)} %shard_map.90.near), channel_id=1, source_target_pairs={{0,2},{2,0},{1,3},{3,1},{4,6},{6,4},{5,7},{7,5},{8,10},{10,8},{9,1... | collective-permute-start | bytes 221192 | tf_op jit(solution)/shard_map/ppermute | solution.py:357
  31.4 1.2 %collective-permute-start.11 = (f32[8,128]{1,0:T(8,128)S(1)}, f32[8,128]{1,0:T(8,128)S(1)}, u32[]{:S(2)}, u32[]{:S(2)}) collective-permute-start(f32[8,128]{1,0:T(8,128)S(1)} %add_add_fusion), channel_id=1, source_target_pairs={{0,1},{1,0},{2,3},{3,2},{4,5},{5,4},{6,7},{7,6},{8,9},{9,8},{10,11... | collective-permute-start | bytes 12296 | tf_op jit(solution)/shard_map/ppermute | solution.py:370
  32.6 5.4 %collective-permute-start.14 = (f32[8,128]{1,0:T(8,128)S(1)}, f32[8,128]{1,0:T(8,128)S(1)}, u32[]{:S(2)}, u32[]{:S(2)}) collective-permute-start(f32[8,128]{1,0:T(8,128)S(1)} %add.15.refs_0_), channel_id=1, source_target_pairs={{0,12},{4,8},{8,4},{12,0},{1,13},{5,9},{9,5},{13,1},{2,14},{6,10},... | collective-permute-start | bytes 12296 | tf_op jit(solution)/shard_map/ppermute | solution.py:320
  35.6 4.5 %collective-permute-start.13 = (f32[8,128]{1,0:T(8,128)S(1)}, f32[8,128]{1,0:T(8,128)S(1)}, u32[]{:S(2)}, u32[]{:S(2)}) collective-permute-start(f32[8,128]{1,0:T(8,128)S(1)} %add.15.refs_0_), channel_id=1, source_target_pairs={{0,8},{4,12},{8,0},{12,4},{1,9},{5,13},{9,1},{13,5},{2,10},{6,14},... | collective-permute-start | bytes 12296 | tf_op jit(solution)/shard_map/ppermute | solution.py:320
  35.6 4.5 %collective-permute-start.12 = (f32[8,128]{1,0:T(8,128)S(1)}, f32[8,128]{1,0:T(8,128)S(1)}, u32[]{:S(2)}, u32[]{:S(2)}) collective-permute-start(f32[8,128]{1,0:T(8,128)S(1)} %add.15.refs_0_), channel_id=1, source_target_pairs={{0,4},{4,0},{8,12},{12,8},{1,5},{5,1},{9,13},{13,9},{2,6},{6,2},{1... | collective-permute-start | bytes 12296 | tf_op jit(solution)/shard_map/ppermute | solution.py:320
  40.4 4.5 %collective-permute-start.15 = (bf16[32,1152]{1,0:T(8,128)(2,1)S(1)}, bf16[32,1152]{1,0:T(8,128)(2,1)S(1)}, u32[]{:S(2)}, u32[]{:S(2)}) collective-permute-start(bf16[32,1152]{1,0:T(8,128)(2,1)S(1)} %get-tuple-element.54), channel_id=1, source_target_pairs={{0,4},{4,0},{8,12},{12,8},{1,5},{5,1},{9,13},{13,9},{2,6},{6,2},{1... | collective-permute-start | bytes 221192 | tf_op jit(solution)/shard_map/ppermute | solution.py:380
  41.0 6.8 %collective-permute-start.16 = (bf16[32,1152]{1,0:T(8,128)(2,1)S(1)}, bf16[32,1152]{1,0:T(8,128)(2,1)S(1)}, u32[]{:S(2)}, u32[]{:S(2)}) collective-permute-start(bf16[32,1152]{1,0:T(8,128)(2,1)S(1)} %get-tuple-element.55), channel_id=1, source_target_pairs={{0,8},{4,12},{8,0},{12,4},{1,9},{5,13},{9,1},{13,5},{2,10},{6,14},... | collective-permute-start | bytes 221192 | tf_op jit(solution)/shard_map/ppermute | solution.py:380
  42.6 6.2 %collective-permute-start.17 = (bf16[32,1152]{1,0:T(8,128)(2,1)S(1)}, bf16[32,1152]{1,0:T(8,128)(2,1)S(1)}, u32[]{:S(2)}, u32[]{:S(2)}) collective-permute-start(bf16[32,1152]{1,0:T(8,128)(2,1)S(1)} %get-tuple-element.56), channel_id=1, source_target_pairs={{0,12},{4,8},{8,4},{12,0},{1,13},{5,9},{9,5},{13,1},{2,14},{6,10},... | collective-permute-start | bytes 221192 | tf_op jit(solution)/shard_map/ppermute | solution.py:380

commit v6 on v5

--- a/solution.py
+++ b/solution.py
@@ -66,72 +66,80 @@
     )
 
 
-def triangle_kernel(q, k, g, totals, prompts, q_own, k_own, g_own, done):
+def triangle_kernel(
+    q, k, g, q_head, k_head, totals, prompts, q_own, k_own, g_own, g_sent, done
+):
     heads, rows, width = q_own.shape
-    skipped = lax.axis_index("seq") * heads
+    seq = lax.axis_index("seq")
     lanes = width // HEAD_DIM * LANES
 
     def load(source, target, h, i):
         extent = target.shape[2]
-        columns = pl.ds(pl.multiple_of((skipped + h) * extent, LANES), extent)
+        columns = pl.ds(pl.multiple_of((seq * heads + h) * extent, LANES), extent)
         return pltpu.make_async_copy(source.at[:, columns], target.at[h], done.at[h, i])
 
-    for h in range(heads):
+    for h in range(1, heads):
         load(k, k_own, h, 0).start()
         load(q, q_own, h, 1).start()
+    half = g_sent.shape[1]
+    sibling = pl.ds(pl.multiple_of((1 - seq) * half, LANES), half)
+    send = pltpu.make_async_copy(g.at[:, sibling], g_sent, done.at[0, 3])
+    send.start()
     for h in range(heads):
         load(g, g_own, h, 2).start()
 
-    def step(h, carry):
-        load(k, k_own, h, 0).wait()
-        load(q, q_own, h, 1).wait()
+    def triangle(h, queries, keys):
         for i, start in enumerate(range(0, rows, LANES)):
             total, prompt = add_scores(
-                query_block(q_own[h, start : start + LANES, :]),
-                k_own.at[h],
-                start + LANES,
-                True,
-                None,
+                query_block(queries[start : start + LANES, :]), keys, start + LANES, True, None
             )
             at = slice(i * lanes, (i + 1) * lanes)
             totals[h, :, at] = total
             prompts[h, :, at] = prompt
+
+    def step(h, carry):
+        load(k, k_own, h, 0).wait()
+        load(q, q_own, h, 1).wait()
+        triangle(h, q_own.at[h], k_own.at[h])
         return carry
 
-    lax.fori_loop(0, heads, step, 0)
+    q_own[0] = q_head[...]
+    k_own[0] = k_head[...]
+    triangle(0, q_head, k_head)
+    lax.fori_loop(1, heads, step, 0)
+    send.wait()
     for h in range(heads):
         load(g, g_own, h, 2).wait()
 
 
-def own_triangle(q, k, g):
+def own_triangle(q, k, g, q_head, k_head):
     rows = q.shape[0]
     heads = k.shape[1] // (2 * HEAD_DIM)
     width = q.shape[1] // (2 * heads)
     lanes = width // HEAD_DIM * rows
     return pl.pallas_call(
         triangle_kernel,
-        in_specs=[HBM, HBM, HBM],
-        out_specs=[VMEM] * 5,
+        in_specs=[HBM] * 3 + [VMEM] * 2,
+        out_specs=[VMEM] * 6,
         out_shape=[
             jax.ShapeDtypeStruct((heads, 8, lanes), jnp.float32),
             jax.ShapeDtypeStruct((heads, PROMPT, lanes), jnp.float32),
             jax.ShapeDtypeStruct((heads, rows, width), jnp.bfloat16),
             jax.ShapeDtypeStruct((heads, rows, HEAD_DIM), jnp.bfloat16),
             jax.ShapeDtypeStruct((heads, rows, width), jnp.bfloat16),
+            jax.ShapeDtypeStruct((rows, heads * width), jnp.bfloat16),
         ],
-        scratch_shapes=[pltpu.SemaphoreType.DMA((heads, 3))],
+        scratch_shapes=[pltpu.SemaphoreType.DMA((heads, 4))],
         compiler_params=pltpu.CompilerParams(vmem_limit_bytes=16 * 1024 * 1024),
         cost_estimate=pl.CostEstimate(
             flops=2 * heads * lanes * rows * HEAD_DIM,
             bytes_accessed=6 * heads * rows * width,
             transcendentals=heads * lanes * rows,
         ),
-    )(q, k, g)
-
-
-def attention_kernel(
-    totals, prompts, q_own, k_own, g_own, q_far, k_far, g_far, mine, theirs, k_first, prob
-):
+    )(q, k, g, q_head, k_head)
+
+
+def attention_kernel(totals, prompts, q_own, k_own, far, prob, k_first):
     heads, rows, width = q_own.shape
     group = width // HEAD_DIM
     lanes = group * LANES
@@ -139,19 +147,18 @@
 
     def step(h, carry):
         at_q = pl.ds(pl.multiple_of(h * width, LANES), width)
-        at_k = pl.ds(pl.multiple_of(h * HEAD_DIM, LANES), HEAD_DIM)
-        k_first[...] = jnp.where(first, k_own[h], k_far[:, at_k])
+        at_k = pl.ds(pl.multiple_of(heads * width + h * HEAD_DIM, LANES), HEAD_DIM)
+        k_far = far.at[:, at_k]
+        k_first[...] = jnp.where(first, k_own[h], k_far[...])
         for i, start in enumerate(range(0, rows, LANES)):
             at = slice(i * lanes, (i + 1) * lanes)
-            q_block = q_far[start : start + LANES, at_q]
-            far, far_prompt = add_scores(
-                query_block(q_block), k_far.at[:, at_k], start + LANES, True, None
-            )
+            q_block = far[start : start + LANES, at_q]
+            other, far_prompt = add_scores(query_block(q_block), k_far, start + LANES, True, None)
             q_block = jnp.where(first, q_block, q_own[h, start : start + LANES, :])
             square, late_prompt = add_scores(query_block(q_block), k_first, rows, False, None)
             own, own_prompt = totals[h, :, at], prompts[h, :, at]
-            early = jnp.where(first, own, far)
-            late = square + jnp.where(first, far, own)
+            early = jnp.where(first, own, other)
+            late = square + jnp.where(first, other, own)
             early_prompt = jnp.where(first, own_prompt, far_prompt)
             early = early_prompt / jnp.sum(early, axis=0, keepdims=True)
             late = late_prompt / jnp.sum(late, axis=0, keepdims=True)
@@ -159,73 +166,113 @@
                 scaled = scaled.astype(jnp.bfloat16)
                 column = slot * rows + start
                 for j in range(group):
-                    prob[j, :, column : column + LANES] = scaled[:, j * LANES : (j + 1) * LANES]
+                    prob[h, j, :, column : column + LANES] = scaled[:, j * LANES : (j + 1) * LANES]
+        return carry
+
+    lax.fori_loop(0, heads, step, 0)
+
+
+def value_kernel(prob, g_own, g_far, mine, theirs):
+    heads, rows, width = g_own.shape
+    group = width // HEAD_DIM
+    first = lax.axis_index("seq") == 0
+
+    def step(h):
+        at_k = slice(h * HEAD_DIM, (h + 1) * HEAD_DIM)
+        at_g = slice(h * width, (h + 1) * width)
+        whole = None
+        for slot, g in enumerate((g_own[h], g_far[:, at_g])):
+            term = jnp.dot(
+                jnp.concatenate(
+                    [prob[h, j, :, slot * rows : (slot + 1) * rows] for j in range(group)], axis=0
+                ),
+                g,
+                preferred_element_type=jnp.float32,
+            )
+            whole = term if whole is None else whole + term
         value = None
         for j in range(group):
-            at_g = pl.ds(pl.multiple_of(h * width + j * HEAD_DIM, LANES), HEAD_DIM)
-            for slot, g in enumerate(
-                (g_own[h, :, j * HEAD_DIM : (j + 1) * HEAD_DIM], g_far[:, at_g])
-            ):
-                term = jnp.dot(
-                    prob[j, :, slot * rows : (slot + 1) * rows],
-                    g,
-                    preferred_element_type=jnp.float32,
-                )
-                value = term if value is None else value + term
+            part = whole[j * PROMPT : (j + 1) * PROMPT, j * HEAD_DIM : (j + 1) * HEAD_DIM]
+            value = part if value is None else value + part
         value = value.astype(jnp.bfloat16)
         low, high = value[: PROMPT // 2], value[PROMPT // 2 :]
         mine[:, at_k] = jnp.where(first, low, high)
         theirs[:, at_k] = jnp.where(first, high, low)
-        return carry
-
-    lax.fori_loop(0, heads, step, 0)
-
-
-def prompt_value_grad(totals, prompts, q_own, k_own, g_own, q_far, k_far, g_far):
+
+    for h in range(heads):
+        step(h)
+
+
+def prompt_value_grad(totals, prompts, q_own, k_own, g_own, far, g_far):
     heads, rows, width = q_own.shape
     group = width // HEAD_DIM
+    prob = pl.pallas_call(
+        attention_kernel,
+        in_specs=[VMEM] * 5,
+        out_specs=VMEM,
+        out_shape=jax.ShapeDtypeStruct((heads, group, PROMPT, 2 * rows), jnp.bfloat16),
+        scratch_shapes=[pltpu.VMEM((rows, HEAD_DIM), jnp.bfloat16)],
+        compiler_params=pltpu.CompilerParams(vmem_limit_bytes=16 * 1024 * 1024),
+        cost_estimate=pl.CostEstimate(
+            flops=heads * group * 6 * rows * rows * HEAD_DIM,
+            bytes_accessed=6 * rows * heads * width,
+            transcendentals=heads * group * 3 * rows * rows,
+        ),
+    )(totals, prompts, q_own, k_own, far)
     return pl.pallas_call(
-        attention_kernel,
-        in_specs=[VMEM] * 8,
+        value_kernel,
+        in_specs=[VMEM] * 3,
         out_specs=[VMEM] * 2,
         out_shape=[jax.ShapeDtypeStruct((PROMPT // 2, heads * HEAD_DIM), jnp.bfloat16)] * 2,
-        scratch_shapes=[
-            pltpu.VMEM((rows, HEAD_DIM), jnp.bfloat16),
-            pltpu.VMEM((group, PROMPT, 2 * rows), jnp.bfloat16),
-        ],
         compiler_params=pltpu.CompilerParams(vmem_limit_bytes=16 * 1024 * 1024),
         cost_estimate=pl.CostEstimate(
-            flops=heads * group * 7 * rows * rows * HEAD_DIM,
-            bytes_accessed=10 * rows * heads * width,
-            transcendentals=heads * group * 3 * rows * rows,
+            flops=4 * heads * group * PROMPT * rows * HEAD_DIM,
+            bytes_accessed=6 * rows * heads * width,
+            transcendentals=0,
         ),
-    )(totals, prompts, q_own, k_own, g_own, q_far, k_far, g_far)
-
-
-def sibling_kernel(*refs, starts):
-    count = len(starts)
-    sources, targets, done = refs[:count], refs[count : 2 * count], refs[2 * count]
-    copies = []
-    for i, start in enumerate(starts):
-        rows, width = targets[i].shape
-        row, column = start(lax.axis_index("seq"))
-        window = sources[i].at[pl.ds(row, rows), pl.ds(pl.multiple_of(column, LANES), width)]
-        copies.append(pltpu.make_async_copy(window, targets[i], done.at[i]))
+    )(prob, g_own, g_far)
+
+
+def sibling_kernel(q, k, out, q_head, k_head, done):
+    seq = lax.axis_index("seq")
+    copies, to = [], 0
+    for i, source in enumerate((q, k)):
+        half = source.shape[1] // 2
+        columns = pl.ds(pl.multiple_of((1 - seq) * half, LANES), half)
+        copies.append(
+            pltpu.make_async_copy(
+                source.at[:, columns], out.at[:, to : to + half], done.at[i]
+            )
+        )
+        to += half
+    for i, (source, target) in enumerate(((q, q_head), (k, k_head))):
+        start = pl.multiple_of(seq * (source.shape[1] // 2), LANES)
+        copies.append(
+            pltpu.make_async_copy(
+                source.at[:, pl.ds(start, target.shape[1])], target, done.at[2 + i]
+            )
+        )
     for copy in copies:
         copy.start()
     for copy in copies:
         copy.wait()
 
 
-def cut(arrays, starts, shapes):
+def for_sibling(q, k):
+    rows = q.shape[0]
+    width = q.shape[1] * HEAD_DIM // k.shape[1]
     return pl.pallas_call(
-        functools.partial(sibling_kernel, starts=starts),
-        in_specs=[HBM] * len(arrays),
-        out_specs=[VMEM] * len(arrays),
-        out_shape=[jax.ShapeDtypeStruct(shape, jnp.bfloat16) for shape in shapes],
-        scratch_shapes=[pltpu.SemaphoreType.DMA((len(arrays),))],
+        sibling_kernel,
+        in_specs=[HBM] * 2,
+        out_specs=[VMEM] * 3,
+        out_shape=[
+            jax.ShapeDtypeStruct((rows, (q.shape[1] + k.shape[1]) // 2), jnp.bfloat16),
+            jax.ShapeDtypeStruct((rows, width), jnp.bfloat16),
+            jax.ShapeDtypeStruct((rows, HEAD_DIM), jnp.bfloat16),
+        ],
+        scratch_shapes=[pltpu.SemaphoreType.DMA((4,))],
         compiler_params=pltpu.CompilerParams(vmem_limit_bytes=16 * 1024 * 1024),
-    )(*arrays)
+    )(q, k)
 
 
 def partial_kernel(*refs):
@@ -421,18 +468,13 @@
         pltpu.with_memory_space_constraint(x[0], pltpu.HBM) for x in (queries, keys, out_grad)
     )
 
-    def other_half(array):
-        half = array.shape[1] // 2
-        return (lambda seq: (0, (1 - seq) * half)), (array.shape[0], half)
-
-    starts, shapes = zip(*[other_half(x) for x in (k, q, g)])
-    k_far, q_far, g_far = (
-        lax.ppermute(x, "seq", swap) for x in cut((k, q, g), starts, shapes)
-    )
+    sent, q_head, k_head = for_sibling(q, k)
+    far = lax.ppermute(sent, "seq", swap)
     aligned = value_weight.shape[0] % LANES == 0 and sizes["dp"] in (1, 2, 4, 8)
     permutes = sizes["tensor"] == 2 and aligned
-    own = own_triangle(q, k, g)
-    mine, theirs = prompt_value_grad(*own, q_far, k_far, g_far)
+    *own, g_sent = own_triangle(q, k, g, q_head, k_head)
+    g_far = lax.ppermute(g_sent, "seq", swap)
+    mine, theirs = prompt_value_grad(*own, far, g_far)
     other = lax.ppermute(theirs, "seq", swap)
     first = seq_index == 0
     value_grad = jnp.concatenate(

time: 49.8 us -> 47.7 us (0.958)
  Pallas kernels: 15.4 us -> 14.4 us
  waiting for transfers between devices: 12.6 us -> 12 us
    pallas_call x3 -> x4, Pallas kernels: 10.5 us -> 9.4 us  [the longest x1 4.72 us: prompt_value_grad(): pl.pallas_call(attention_kernel, in_specs=[VMEM] * 5, out_specs=VMEM, out...]
    ppermute x3 -> x2, waiting for transfers between devices: 0.83 us -> 0.18 us  [the longest x1 0.18 us: body(): far = lax.ppermute(sent, 'seq', swap)]
    ppermute x3 -> x2, starting transfers between devices: 1.03 us -> 0.63 us  [the longest x1 0.52 us: body(): far = lax.ppermute(sent, 'seq', swap)]
  transfers between devices with their start and end apart: 18 -> 17, of which waited for: 9 -> 9; matrix products, arithmetic and copies ran while one was open for 0% -> 0% of each run, Pallas kernels for 14% -> 24%
where the time goes in v6:
time: 47.7 us; the launch traced here: 47.5 us
  starting transfers between devices  21 us (44%)
  Pallas kernels  14.4 us (30%)
  waiting for transfers between devices  12 us (25%)
    ppermute x6, starting transfers between devices, to_dp(): lax.ppermute(array, 'dp', xor_pairs(dp, step))  10 us
    ppermute x4, starting transfers between devices, tail_by_permutes(): far = lax.ppermute(near, 'tensor', swap)  5.34 us
    pallas_call x1, Pallas kernels, prompt_value_grad(): pl.pallas_call(attention_kernel, in_specs=[VMEM] * 5, out_specs=VMEM, out...  4.72 us
    ppermute x3, starting transfers between devices, tail_by_permutes(): lax.ppermute(shares[step], 'dp', xor_pairs(dp, step))  4.45 us
    ppermute x3, waiting for transfers between devices, tail_by_permutes(): lax.ppermute(shares[step], 'dp', xor_pairs(dp, step))  3.92 us
    ppermute x4, waiting for transfers between devices, tail_by_permutes(): far = lax.ppermute(near, 'tensor', swap)  3.39 us
    pallas_call x4, Pallas kernels, tail_by_permutes(): pl.pallas_call(partial_kernel, in_specs=[VMEM] * (len(steps) + 1), out_sp...  3.06 us
    pallas_call x1, Pallas kernels, own_triangle(): pl.pallas_call(triangle_kernel, in_specs=[HBM] * 3 + [VMEM] * 2, out_spec...  2.74 us
  transfers between devices with their start and end apart: 17, of which 9 were waited for; matrix products, arithmetic and copies ran while one was open for 0% of the time, Pallas kernels for 24%

profile of v6, /device:TPU:0, one launch (start us, length us, event | category | flops | bytes accessed | tf_op | source)
XLA Modules:
  0.0 47.5 jit_solution(10031742815669007818)
XLA Ops:
  0.0 1.5 %shard_map.82 = (bf16[512,1536]{1,0:T(8,128)(2,1)S(1)}, bf16[512,256]{1,0:T(8,128)(2,1)S(1)}, bf16[512,128]{1,0:T(8,128)(2,1)S(1)}) custom-call(bf16[512,2048]{1,0:T(8,128)(2,1)} %bitcast.3, bf16[512,1024]{1,0:T(8,128)(2,1)} %bitcast.5), custom_call_target="tpu_custom_call" | custom-call | tf_op jit(solution)/shard_map/pallas_call | solution.py:264
  2.0 2.7 %shard_map.83 = (f32[4,8,1024]{2,1,0:T(8,128)S(1)}, f32[4,64,1024]{2,1,0:T(8,128)S(1)}, bf16[4,512,256]{2,1,0:T(8,128)(2,1)S(1)}, bf16[4,512,128]{2,1,0:T(8,128)...) custom-call(bf16[512,2048]{1,0:T(8,128)(2,1)} %bitcast.4, bf16[512,1024]{1,0:T(8,128)(2,1)} %bitcast.6, ...), custom_call_target="tpu_custom_call" | custom-call | flops 536870912 | bytes 3145728 | tf_op jit(solution)/shard_map/pallas_call | solution.py:120
  5.1 4.7 %shard_map.84.prob = bf16[4,2,64,1024]{3,2,1,0:T(8,128)(2,1)S(1)} custom-call(f32[4,8,1024]{2,1,0:T(8,128)S(1)} %get-tuple-element.34.totals, f32[4,64,1024]{2,1,0:T(8,128)S(1)} %get-tuple-element.35.prompts, bf16[4,512,256]{2,1,0:T(8,128)(2,1)S(1)} %get-tuple-element.36.q_own, bf16[4,512,128]{2,1,0:T(8,128)(2,1)S(1)} %get-tuple-element.37.k_own, ...), custom_call_target="tpu_custom_call" | custom-call | flops 1610612736 | bytes 3145728 | tf_op jit(solution)/shard_map/pallas_call | solution.py:209
  10.7 0.9 %collective-permute-done.2 = bf16[32,512]{1,0:T(8,128)(2,1)S(1)} collective-permute-done((bf16[32,512]{1,0:T(8,128)(2,1)S(1)}, bf16[32,512]{1,0:T(8,128)(2,1)S(1)}, u32[]{:S(2)}, u32[]{:S(2)}) %collective-permute-start.2) | collective-permute-done | bytes 32800 | tf_op jit(solution)/shard_map/ppermute | solution.py:478
  11.6 5.0 %collective-permute-start.3 = (bf16[32,1024]{1,0:T(8,128)(2,1)S(1)}, bf16[32,1024]{1,0:T(8,128)(2,1)S(1)}, u32[]{:S(2)}, u32[]{:S(2)}) collective-permute-start(bf16[32,1024]{1,0:T(8,128)(2,1)S(1)} %pad_maximum_fusion.refs_0_), channel_id=1, source_target_pairs={{0,12},{4,8},{8,4},{12,0},{1,13},{5,9},{9,5},{13,1},{2,14},{6,10},... | collective-permute-start | bytes 196616 | tf_op jit(solution)/shard_map/ppermute | solution.py:367
  17.3 0.8 %shard_map.87.near = bf16[1,32,1152]{2,1,0:T(8,128)(2,1)S(1)} custom-call(bf16[32,1024]{1,0:T(8,128)(2,1)S(1)} %pad_maximum_fusion.refs_0_, bf16[1152,1024]{1,0:T(8,128)(2,1)S(1)} %copy-done), custom_call_target="tpu_custom_call" | custom-call | flops 75497472 | bytes 2359296 | tf_op jit(solution)/shard_map/pallas_call | solution.py:392
  18.0 1.7 %collective-permute-start.4 = (bf16[1,32,1152]{2,1,0:T(8,128)(2,1)S(1)}, bf16[1,32,1152]{2,1,0:T(8,128)(2,1)S(1)}, u32[]{:S(2)}, u32[]{:S(2)}) collective-permute-start(bf16[1,32,1152]{2,1,0:T(8,128)(2,1)S(1)} %shard_map.87.near), channel_id=1, source_target_pairs={{0,2},{2,0},{1,3},{3,1},{4,6},{6,4},{5,7},{7,5},{8,10},{10,8},{9,1... | collective-permute-start | bytes 221192 | tf_op jit(solution)/shard_map/ppermute | solution.py:404
  19.7 0.8 %shard_map.93.near = bf16[1,32,1152]{2,1,0:T(8,128)(2,1)S(1)} custom-call(bf16[32,1024]{1,0:T(8,128)(2,1)S(1)} %collective-permute-done.3.refs_0_, bf16[1152,1024]{1,0:T(8,128)(2,1)S(1)} %copy-done), custom_call_target="tpu_custom_call" | custom-call | flops 75497472 | bytes 2359296 | tf_op jit(solution)/shard_map/pallas_call | solution.py:392
  20.4 1.6 %collective-permute-start.9 = (bf16[1,32,1152]{2,1,0:T(8,128)(2,1)S(1)}, bf16[1,32,1152]{2,1,0:T(8,128)(2,1)S(1)}, u32[]{:S(2)}, u32[]{:S(2)}) collective-permute-start(bf16[1,32,1152]{2,1,0:T(8,128)(2,1)S(1)} %shard_map.93.near), channel_id=1, source_target_pairs={{0,2},{2,0},{1,3},{3,1},{4,6},{6,4},{5,7},{7,5},{8,10},{10,8},{9,1... | collective-permute-start | bytes 221192 | tf_op jit(solution)/shard_map/ppermute | solution.py:404
  22.0 0.8 %shard_map.89.near = bf16[1,32,1152]{2,1,0:T(8,128)(2,1)S(1)} custom-call(bf16[32,1024]{1,0:T(8,128)(2,1)S(1)} %collective-permute-done.5.refs_0_, bf16[1152,1024]{1,0:T(8,128)(2,1)S(1)} %copy-done), custom_call_target="tpu_custom_call" | custom-call | flops 75497472 | bytes 2359296 | tf_op jit(solution)/shard_map/pallas_call | solution.py:392
  22.8 1.2 %collective-permute-start.6 = (bf16[1,32,1152]{2,1,0:T(8,128)(2,1)S(1)}, bf16[1,32,1152]{2,1,0:T(8,128)(2,1)S(1)}, u32[]{:S(2)}, u32[]{:S(2)}) collective-permute-start(bf16[1,32,1152]{2,1,0:T(8,128)(2,1)S(1)} %shard_map.89.near), channel_id=1, source_target_pairs={{0,2},{2,0},{1,3},{3,1},{4,6},{6,4},{5,7},{7,5},{8,10},{10,8},{9,1... | collective-permute-start | bytes 221192 | tf_op jit(solution)/shard_map/ppermute | solution.py:404
  24.1 0.8 %shard_map.91.near = bf16[1,32,1152]{2,1,0:T(8,128)(2,1)S(1)} custom-call(bf16[32,1024]{1,0:T(8,128)(2,1)S(1)} %collective-permute-done.7.refs_0_, bf16[1152,1024]{1,0:T(8,128)(2,1)S(1)} %copy-done), custom_call_target="tpu_custom_call" | custom-call | flops 75497472 | bytes 2359296 | tf_op jit(solution)/shard_map/pallas_call | solution.py:392
  24.9 0.9 %collective-permute-start.8 = (bf16[1,32,1152]{2,1,0:T(8,128)(2,1)S(1)}, bf16[1,32,1152]{2,1,0:T(8,128)(2,1)S(1)}, u32[]{:S(2)}, u32[]{:S(2)}) collective-permute-start(bf16[1,32,1152]{2,1,0:T(8,128)(2,1)S(1)} %shard_map.91.near), channel_id=1, source_target_pairs={{0,2},{2,0},{1,3},{3,1},{4,6},{6,4},{5,7},{7,5},{8,10},{10,8},{9,1... | collective-permute-start | bytes 221192 | tf_op jit(solution)/shard_map/ppermute | solution.py:404
  25.8 2.2 %collective-permute-done.6.far = bf16[1,32,1152]{2,1,0:T(8,128)(2,1)S(1)} collective-permute-done((bf16[1,32,1152]{2,1,0:T(8,128)(2,1)S(1)}, bf16[1,32,1152]{2,1,0:T(8,128)(2,1)S(1)}, u32[]{:S(2)}, u32[]{:S(2)}) %collective-permute-start.6) | collective-permute-done | bytes 73760 | tf_op jit(solution)/shard_map/ppermute | solution.py:404
  28.0 1.2 %collective-permute-done.8.far = bf16[1,32,1152]{2,1,0:T(8,128)(2,1)S(1)} collective-permute-done((bf16[1,32,1152]{2,1,0:T(8,128)(2,1)S(1)}, bf16[1,32,1152]{2,1,0:T(8,128)(2,1)S(1)}, u32[]{:S(2)}, u32[]{:S(2)}) %collective-permute-start.8) | collective-permute-done | bytes 73760 | tf_op jit(solution)/shard_map/ppermute | solution.py:404
  29.4 1.2 %collective-permute-done.10 = f32[8,128]{1,0:T(8,128)S(1)} collective-permute-done((f32[8,128]{1,0:T(8,128)S(1)}, f32[8,128]{1,0:T(8,128)S(1)}, u32[]{:S(2)}, u32[]{:S(2)}) %collective-permute-start.10) | collective-permute-done | bytes 4128 | tf_op jit(solution)/shard_map/ppermute | solution.py:417
  30.5 3.0 %collective-permute-start.13 = (f32[8,128]{1,0:T(8,128)S(1)}, f32[8,128]{1,0:T(8,128)S(1)}, u32[]{:S(2)}, u32[]{:S(2)}) collective-permute-start(f32[8,128]{1,0:T(8,128)S(1)} %add.15.refs_0_), channel_id=1, source_target_pairs={{0,12},{4,8},{8,4},{12,0},{1,13},{5,9},{9,5},{13,1},{2,14},{6,10},... | collective-permute-start | bytes 12296 | tf_op jit(solution)/shard_map/ppermute | solution.py:367
  33.5 1.4 %collective-permute-start.11 = (f32[8,128]{1,0:T(8,128)S(1)}, f32[8,128]{1,0:T(8,128)S(1)}, u32[]{:S(2)}, u32[]{:S(2)}) collective-permute-start(f32[8,128]{1,0:T(8,128)S(1)} %add.15.refs_0_), channel_id=1, source_target_pairs={{0,4},{4,0},{8,12},{12,8},{1,5},{5,1},{9,13},{13,9},{2,6},{6,2},{1... | collective-permute-start | bytes 12296 | tf_op jit(solution)/shard_map/ppermute | solution.py:367
  35.9 2.1 %collective-permute-done.12.refs_2_ = f32[8,128]{1,0:T(8,128)S(1)} collective-permute-done((f32[8,128]{1,0:T(8,128)S(1)}, f32[8,128]{1,0:T(8,128)S(1)}, u32[]{:S(2)}, u32[]{:S(2)}) %collective-permute-start.12) | collective-permute-done | bytes 4128 | tf_op jit(solution)/shard_map/ppermute | solution.py:367
  38.9 1.6 %collective-permute-start.15 = (bf16[32,1152]{1,0:T(8,128)(2,1)S(1)}, bf16[32,1152]{1,0:T(8,128)(2,1)S(1)}, u32[]{:S(2)}, u32[]{:S(2)}) collective-permute-start(bf16[32,1152]{1,0:T(8,128)(2,1)S(1)} %get-tuple-element.57), channel_id=1, source_target_pairs={{0,8},{4,12},{8,0},{12,4},{1,9},{5,13},{9,1},{13,5},{2,10},{6,14},... | collective-permute-start | bytes 221192 | tf_op jit(solution)/shard_map/ppermute | solution.py:427
  40.4 2.3 %collective-permute-start.16 = (bf16[32,1152]{1,0:T(8,128)(2,1)S(1)}, bf16[32,1152]{1,0:T(8,128)(2,1)S(1)}, u32[]{:S(2)}, u32[]{:S(2)}) collective-permute-start(bf16[32,1152]{1,0:T(8,128)(2,1)S(1)} %get-tuple-element.58), channel_id=1, source_target_pairs={{0,12},{4,8},{8,4},{12,0},{1,13},{5,9},{9,5},{13,1},{2,14},{6,10},... | collective-permute-start | bytes 221192 | tf_op jit(solution)/shard_map/ppermute | solution.py:427
  42.7 3.0 %collective-permute-done.15.refs_2_ = bf16[32,1152]{1,0:T(8,128)(2,1)S(1)} collective-permute-done((bf16[32,1152]{1,0:T(8,128)(2,1)S(1)}, bf16[32,1152]{1,0:T(8,128)(2,1)S(1)}, u32[]{:S(2)}, u32[]{:S(2)}) %collective-permute-start.15) | collective-permute-done | bytes 73760 | tf_op jit(solution)/shard_map/ppermute | solution.py:427
  45.7 0.9 %collective-permute-done.16.refs_3_ = bf16[32,1152]{1,0:T(8,128)(2,1)S(1)} collective-permute-done((bf16[32,1152]{1,0:T(8,128)(2,1)S(1)}, bf16[32,1152]{1,0:T(8,128)(2,1)S(1)}, u32[]{:S(2)}, u32[]{:S(2)}) %collective-permute-start.16) | collective-permute-done | bytes 73760 | tf_op jit(solution)/shard_map/ppermute | solution.py:427
  46.7 0.9 %shard_map.96 = f32[1,32,4608]{2,1,0:T(8,128)} custom-call(f32[1,128]{1,0:T(1,128)S(1)} %get-tuple-element.44.count, bf16[32,1152]{1,0:T(8,128)(2,1)S(1)} %get-tuple-element.55.refs_0_, bf16[32,1152]{1,0:T(8,128)(2,1)S(1)} %collective-permute-done.14.refs_1_, bf16[32,1152]{1,0:T(8,128)(2,1)S(1)} %collective-permute-done.15.refs_2_, ...), custom_call_target="tpu_custom_call" | custom-call | tf_op jit(solution)/shard_map/pallas_call | solution.py:429
  (39 shorter events, 4.5 us)
Async XLA Ops:
  1.5 3.6 %collective-permute-start = (bf16[512,1536]{1,0:T(8,128)(2,1)S(1)}, bf16[512,1536]{1,0:T(8,128)(2,1)S(1)}, u32[]{:S(2)}, u32[]{:S(2)}) collective-permute-start(bf16[512,1536]{1,0:T(8,128)(2,1)S(1)} %get-tuple-element.38), channel_id=1, source_target_pairs={{0,1},{1,0},{2,3},{3,2},{4,5},{5,4},{6,7},{7,6},{8,9},{9,8},{10,11... | collective-permute-start | bytes 4718600 | tf_op jit(solution)/shard_map/ppermute | solution.py:472
  4.8 5.0 %collective-permute-start.1 = (bf16[512,1024]{1,0:T(8,128)(2,1)S(1)}, bf16[512,1024]{1,0:T(8,128)(2,1)S(1)}, u32[]{:S(2)}, u32[]{:S(2)}) collective-permute-start(bf16[512,1024]{1,0:T(8,128)(2,1)S(1)} %get-tuple-element.40), channel_id=1, source_target_pairs={{0,1},{1,0},{2,3},{3,2},{4,5},{5,4},{6,7},{7,6},{8,9},{9,8},{10,11... | collective-permute-start | bytes 3145736 | tf_op jit(solution)/shard_map/ppermute | solution.py:476
  9.8 7.5 %copy-start = (bf16[1152,1024]{1,0:T(8,128)(2,1)S(1)}, bf16[1152,1024]{1,0:T(8,128)(2,1)}, u32[]{:S(2)}) copy-start(bf16[1152,1024]{1,0:T(8,128)(2,1)} %refs_1_.7) | copy-start | bytes 7077892
  10.3 1.3 %collective-permute-start.2 = (bf16[32,512]{1,0:T(8,128)(2,1)S(1)}, bf16[32,512]{1,0:T(8,128)(2,1)S(1)}, u32[]{:S(2)}, u32[]{:S(2)}) collective-permute-start(bf16[32,512]{1,0:T(8,128)(2,1)S(1)} %get-tuple-element.42), channel_id=1, source_target_pairs={{0,1},{1,0},{2,3},{3,2},{4,5},{5,4},{6,7},{7,6},{8,9},{9,8},{10,11... | collective-permute-start | bytes 98312 | tf_op jit(solution)/shard_map/ppermute | solution.py:478
  11.6 8.1 %collective-permute-start.3 = (bf16[32,1024]{1,0:T(8,128)(2,1)S(1)}, bf16[32,1024]{1,0:T(8,128)(2,1)S(1)}, u32[]{:S(2)}, u32[]{:S(2)}) collective-permute-start(bf16[32,1024]{1,0:T(8,128)(2,1)S(1)} %pad_maximum_fusion.refs_0_), channel_id=1, source_target_pairs={{0,12},{4,8},{8,4},{12,0},{1,13},{5,9},{9,5},{13,1},{2,14},{6,10},... | collective-permute-start | bytes 196616 | tf_op jit(solution)/shard_map/ppermute | solution.py:367
  16.6 5.4 %collective-permute-start.5 = (bf16[32,1024]{1,0:T(8,128)(2,1)S(1)}, bf16[32,1024]{1,0:T(8,128)(2,1)S(1)}, u32[]{:S(2)}, u32[]{:S(2)}) collective-permute-start(bf16[32,1024]{1,0:T(8,128)(2,1)S(1)} %pad_maximum_fusion.refs_0_), channel_id=1, source_target_pairs={{0,4},{4,0},{8,12},{12,8},{1,5},{5,1},{9,13},{13,9},{2,6},{6,2},{1... | collective-permute-start | bytes 196616 | tf_op jit(solution)/shard_map/ppermute | solution.py:367
  16.6 7.5 %collective-permute-start.7 = (bf16[32,1024]{1,0:T(8,128)(2,1)S(1)}, bf16[32,1024]{1,0:T(8,128)(2,1)S(1)}, u32[]{:S(2)}, u32[]{:S(2)}) collective-permute-start(bf16[32,1024]{1,0:T(8,128)(2,1)S(1)} %pad_maximum_fusion.refs_0_), channel_id=1, source_target_pairs={{0,8},{4,12},{8,0},{12,4},{1,9},{5,13},{9,1},{13,5},{2,10},{6,14},... | collective-permute-start | bytes 196616 | tf_op jit(solution)/shard_map/ppermute | solution.py:367
  18.0 7.7 %collective-permute-start.4 = (bf16[1,32,1152]{2,1,0:T(8,128)(2,1)S(1)}, bf16[1,32,1152]{2,1,0:T(8,128)(2,1)S(1)}, u32[]{:S(2)}, u32[]{:S(2)}) collective-permute-start(bf16[1,32,1152]{2,1,0:T(8,128)(2,1)S(1)} %shard_map.87.near), channel_id=1, source_target_pairs={{0,2},{2,0},{1,3},{3,1},{4,6},{6,4},{5,7},{7,5},{8,10},{10,8},{9,1... | collective-permute-start | bytes 221192 | tf_op jit(solution)/shard_map/ppermute | solution.py:404
  20.4 5.3 %collective-permute-start.9 = (bf16[1,32,1152]{2,1,0:T(8,128)(2,1)S(1)}, bf16[1,32,1152]{2,1,0:T(8,128)(2,1)S(1)}, u32[]{:S(2)}, u32[]{:S(2)}) collective-permute-start(bf16[1,32,1152]{2,1,0:T(8,128)(2,1)S(1)} %shard_map.93.near), channel_id=1, source_target_pairs={{0,2},{2,0},{1,3},{3,1},{4,6},{6,4},{5,7},{7,5},{8,10},{10,8},{9,1... | collective-permute-start | bytes 221192 | tf_op jit(solution)/shard_map/ppermute | solution.py:404
  22.8 12.1 %copy-start.2 = (s32[4]{0:T(128)S(1)}, s32[4]{0:T(128)}, u32[]{:S(2)}) copy-start(s32[4]{0:T(128)} %tenant_of) | copy-start | bytes 52
  22.8 12.1 %copy-start.3 = (s32[4]{0:T(128)S(1)}, s32[4]{0:T(128)}, u32[]{:S(2)}) copy-start(s32[4]{0:T(128)} %owner_of.1) | copy-start | bytes 52
  22.8 12.1 %copy-start.4 = (s32[4]{0:T(128)S(1)}, s32[4]{0:T(128)}, u32[]{:S(2)}) copy-start(s32[4]{0:T(128)} %counts.1) | copy-start | bytes 52
  22.8 23.8 %copy-start.1 = (f32[1,32,4608]{2,1,0:T(8,128)S(1)}, f32[1,32,4608]{2,1,0:T(8,128)}, u32[]{:S(2)}) copy-start(f32[1,32,4608]{2,1,0:T(8,128)} %refs_4_.1) | copy-start | bytes 1769476
  22.8 5.2 %collective-permute-start.6 = (bf16[1,32,1152]{2,1,0:T(8,128)(2,1)S(1)}, bf16[1,32,1152]{2,1,0:T(8,128)(2,1)S(1)}, u32[]{:S(2)}, u32[]{:S(2)}) collective-permute-start(bf16[1,32,1152]{2,1,0:T(8,128)(2,1)S(1)} %shard_map.89.near), channel_id=1, source_target_pairs={{0,2},{2,0},{1,3},{3,1},{4,6},{6,4},{5,7},{7,5},{8,10},{10,8},{9,1... | collective-permute-start | bytes 221192 | tf_op jit(solution)/shard_map/ppermute | solution.py:404
  24.9 4.4 %collective-permute-start.8 = (bf16[1,32,1152]{2,1,0:T(8,128)(2,1)S(1)}, bf16[1,32,1152]{2,1,0:T(8,128)(2,1)S(1)}, u32[]{:S(2)}, u32[]{:S(2)}) collective-permute-start(bf16[1,32,1152]{2,1,0:T(8,128)(2,1)S(1)} %shard_map.91.near), channel_id=1, source_target_pairs={{0,2},{2,0},{1,3},{3,1},{4,6},{6,4},{5,7},{7,5},{8,10},{10,8},{9,1... | collective-permute-start | bytes 221192 | tf_op jit(solution)/shard_map/ppermute | solution.py:404
  29.3 1.2 %collective-permute-start.10 = (f32[8,128]{1,0:T(8,128)S(1)}, f32[8,128]{1,0:T(8,128)S(1)}, u32[]{:S(2)}, u32[]{:S(2)}) collective-permute-start(f32[8,128]{1,0:T(8,128)S(1)} %add_add_fusion), channel_id=1, source_target_pairs={{0,1},{1,0},{2,3},{3,2},{4,5},{5,4},{6,7},{7,6},{8,9},{9,8},{10,11... | collective-permute-start | bytes 12296 | tf_op jit(solution)/shard_map/ppermute | solution.py:417
  30.5 5.4 %collective-permute-start.13 = (f32[8,128]{1,0:T(8,128)S(1)}, f32[8,128]{1,0:T(8,128)S(1)}, u32[]{:S(2)}, u32[]{:S(2)}) collective-permute-start(f32[8,128]{1,0:T(8,128)S(1)} %add.15.refs_0_), channel_id=1, source_target_pairs={{0,12},{4,8},{8,4},{12,0},{1,13},{5,9},{9,5},{13,1},{2,14},{6,10},... | collective-permute-start | bytes 12296 | tf_op jit(solution)/shard_map/ppermute | solution.py:367
  33.5 4.5 %collective-permute-start.12 = (f32[8,128]{1,0:T(8,128)S(1)}, f32[8,128]{1,0:T(8,128)S(1)}, u32[]{:S(2)}, u32[]{:S(2)}) collective-permute-start(f32[8,128]{1,0:T(8,128)S(1)} %add.15.refs_0_), channel_id=1, source_target_pairs={{0,8},{4,12},{8,0},{12,4},{1,9},{5,13},{9,1},{13,5},{2,10},{6,14},... | collective-permute-start | bytes 12296 | tf_op jit(solution)/shard_map/ppermute | solution.py:367
  33.5 4.5 %collective-permute-start.11 = (f32[8,128]{1,0:T(8,128)S(1)}, f32[8,128]{1,0:T(8,128)S(1)}, u32[]{:S(2)}, u32[]{:S(2)}) collective-permute-start(f32[8,128]{1,0:T(8,128)S(1)} %add.15.refs_0_), channel_id=1, source_target_pairs={{0,4},{4,0},{8,12},{12,8},{1,5},{5,1},{9,13},{13,9},{2,6},{6,2},{1... | collective-permute-start | bytes 12296 | tf_op jit(solution)/shard_map/ppermute | solution.py:367
  38.3 4.5 %collective-permute-start.14 = (bf16[32,1152]{1,0:T(8,128)(2,1)S(1)}, bf16[32,1152]{1,0:T(8,128)(2,1)S(1)}, u32[]{:S(2)}, u32[]{:S(2)}) collective-permute-start(bf16[32,1152]{1,0:T(8,128)(2,1)S(1)} %get-tuple-element.56), channel_id=1, source_target_pairs={{0,4},{4,0},{8,12},{12,8},{1,5},{5,1},{9,13},{13,9},{2,6},{6,2},{1... | collective-permute-start | bytes 221192 | tf_op jit(solution)/shard_map/ppermute | solution.py:427
  38.9 6.8 %collective-permute-start.15 = (bf16[32,1152]{1,0:T(8,128)(2,1)S(1)}, bf16[32,1152]{1,0:T(8,128)(2,1)S(1)}, u32[]{:S(2)}, u32[]{:S(2)}) collective-permute-start(bf16[32,1152]{1,0:T(8,128)(2,1)S(1)} %get-tuple-element.57), channel_id=1, source_target_pairs={{0,8},{4,12},{8,0},{12,4},{1,9},{5,13},{9,1},{13,5},{2,10},{6,14},... | collective-permute-start | bytes 221192 | tf_op jit(solution)/shard_map/ppermute | solution.py:427
  40.4 6.2 %collective-permute-start.16 = (bf16[32,1152]{1,0:T(8,128)(2,1)S(1)}, bf16[32,1152]{1,0:T(8,128)(2,1)S(1)}, u32[]{:S(2)}, u32[]{:S(2)}) collective-permute-start(bf16[32,1152]{1,0:T(8,128)(2,1)S(1)} %get-tuple-element.58), channel_id=1, source_target_pairs={{0,12},{4,8},{8,4},{12,0},{1,13},{5,9},{9,5},{13,1},{2,14},{6,10},... | collective-permute-start | bytes 221192 | tf_op jit(solution)/shard_map/ppermute | solution.py:427

commit v7 on v6

--- a/solution.py
+++ b/solution.py
@@ -21,8 +21,11 @@
 PARTIAL_TYPE = jnp.bfloat16
 
 
-def GROUPS(dp):
-    return [[step] for step in range(dp)]
+ARRIVAL = {"blocks": (3, 1, 2), "norms": (3, 2, 1), "shares": (1, 2, 3)}
+
+
+def arrival(what, dp):
+    return list(ARRIVAL[what]) if dp == 4 else list(range(1, dp))
 
 
 CONTRACT_LAST = (((1,), (1,)), ((), ()))
@@ -66,9 +69,7 @@
     )
 
 
-def triangle_kernel(
-    q, k, g, q_head, k_head, totals, prompts, q_own, k_own, g_own, g_sent, done
-):
+def triangle_kernel(q, k, g, q_head, k_head, totals, prompts, q_own, k_own, g_sent, done):
     heads, rows, width = q_own.shape
     seq = lax.axis_index("seq")
     lanes = width // HEAD_DIM * LANES
@@ -83,10 +84,8 @@
         load(q, q_own, h, 1).start()
     half = g_sent.shape[1]
     sibling = pl.ds(pl.multiple_of((1 - seq) * half, LANES), half)
-    send = pltpu.make_async_copy(g.at[:, sibling], g_sent, done.at[0, 3])
+    send = pltpu.make_async_copy(g.at[:, sibling], g_sent, done.at[0, 0])
     send.start()
-    for h in range(heads):
-        load(g, g_own, h, 2).start()
 
     def triangle(h, queries, keys):
         for i, start in enumerate(range(0, rows, LANES)):
@@ -108,8 +107,6 @@
     triangle(0, q_head, k_head)
     lax.fori_loop(1, heads, step, 0)
     send.wait()
-    for h in range(heads):
-        load(g, g_own, h, 2).wait()
 
 
 def own_triangle(q, k, g, q_head, k_head):
@@ -120,16 +117,15 @@
     return pl.pallas_call(
         triangle_kernel,
         in_specs=[HBM] * 3 + [VMEM] * 2,
-        out_specs=[VMEM] * 6,
+        out_specs=[VMEM] * 5,
         out_shape=[
             jax.ShapeDtypeStruct((heads, 8, lanes), jnp.float32),
             jax.ShapeDtypeStruct((heads, PROMPT, lanes), jnp.float32),
             jax.ShapeDtypeStruct((heads, rows, width), jnp.bfloat16),
             jax.ShapeDtypeStruct((heads, rows, HEAD_DIM), jnp.bfloat16),
-            jax.ShapeDtypeStruct((heads, rows, width), jnp.bfloat16),
             jax.ShapeDtypeStruct((rows, heads * width), jnp.bfloat16),
         ],
-        scratch_shapes=[pltpu.SemaphoreType.DMA((heads, 4))],
+        scratch_shapes=[pltpu.SemaphoreType.DMA((heads, 2))],
         compiler_params=pltpu.CompilerParams(vmem_limit_bytes=16 * 1024 * 1024),
         cost_estimate=pl.CostEstimate(
             flops=2 * heads * lanes * rows * HEAD_DIM,
@@ -139,16 +135,30 @@
     )(q, k, g, q_head, k_head)
 
 
-def attention_kernel(totals, prompts, q_own, k_own, far, prob, k_first):
+def attention_kernel(*refs, turn):
+    if turn:
+        totals, prompts, q_own, k_own, g, far, weight, prob, g_own, turned, k_first, done = refs
+    else:
+        totals, prompts, q_own, k_own, g, far, prob, g_own, k_first, done = refs
     heads, rows, width = q_own.shape
     group = width // HEAD_DIM
     lanes = group * LANES
-    first = lax.axis_index("seq") == 0
+    seq = lax.axis_index("seq")
+    first = seq == 0
+    half = g_own.shape[1]
+    load = pltpu.make_async_copy(
+        g.at[:, pl.ds(pl.multiple_of(seq * half, LANES), half)], g_own, done.at[0]
+    )
+    load.start()
 
     def step(h, carry):
         at_q = pl.ds(pl.multiple_of(h * width, LANES), width)
         at_k = pl.ds(pl.multiple_of(heads * width + h * HEAD_DIM, LANES), HEAD_DIM)
         k_far = far.at[:, at_k]
+        if turn:
+            share = weight.shape[1] // heads
+            features = pl.ds(pl.multiple_of(h * share, LANES), share)
+            turned[features, :] = weight[:, features].T
         k_first[...] = jnp.where(first, k_own[h], k_far[...])
         for i, start in enumerate(range(0, rows, LANES)):
             at = slice(i * lanes, (i + 1) * lanes)
@@ -170,18 +180,20 @@
         return carry
 
     lax.fori_loop(0, heads, step, 0)
+    load.wait()
 
 
 def value_kernel(prob, g_own, g_far, mine, theirs):
-    heads, rows, width = g_own.shape
-    group = width // HEAD_DIM
+    heads, group, _, rows = prob.shape
+    rows = rows // 2
+    width = group * HEAD_DIM
     first = lax.axis_index("seq") == 0
 
     def step(h):
         at_k = slice(h * HEAD_DIM, (h + 1) * HEAD_DIM)
         at_g = slice(h * width, (h + 1) * width)
         whole = None
-        for slot, g in enumerate((g_own[h], g_far[:, at_g])):
+        for slot, g in enumerate((g_own[:, at_g], g_far[:, at_g])):
             term = jnp.dot(
                 jnp.concatenate(
                     [prob[h, j, :, slot * rows : (slot + 1) * rows] for j in range(group)], axis=0
@@ -203,23 +215,31 @@
         step(h)
 
 
-def prompt_value_grad(totals, prompts, q_own, k_own, g_own, far, g_far):
+def prompt_value_grad(totals, prompts, q_own, k_own, g, far, g_far, weight):
     heads, rows, width = q_own.shape
     group = width // HEAD_DIM
-    prob = pl.pallas_call(
-        attention_kernel,
-        in_specs=[VMEM] * 5,
-        out_specs=VMEM,
-        out_shape=jax.ShapeDtypeStruct((heads, group, PROMPT, 2 * rows), jnp.bfloat16),
-        scratch_shapes=[pltpu.VMEM((rows, HEAD_DIM), jnp.bfloat16)],
+    weights = [] if weight is None else [weight]
+    prob, g_own, *turned = pl.pallas_call(
+        functools.partial(attention_kernel, turn=bool(weights)),
+        in_specs=[VMEM] * 4 + [HBM, VMEM] + [VMEM] * len(weights),
+        out_specs=[VMEM] * (2 + len(weights)),
+        out_shape=[
+            jax.ShapeDtypeStruct((heads, group, PROMPT, 2 * rows), jnp.bfloat16),
+            jax.ShapeDtypeStruct((rows, heads * width), jnp.bfloat16),
+        ]
+        + [jax.ShapeDtypeStruct(w.shape[::-1], w.dtype) for w in weights],
+        scratch_shapes=[
+            pltpu.VMEM((rows, HEAD_DIM), jnp.bfloat16),
+            pltpu.SemaphoreType.DMA((1,)),
+        ],
         compiler_params=pltpu.CompilerParams(vmem_limit_bytes=16 * 1024 * 1024),
         cost_estimate=pl.CostEstimate(
             flops=heads * group * 6 * rows * rows * HEAD_DIM,
             bytes_accessed=6 * rows * heads * width,
             transcendentals=heads * group * 3 * rows * rows,
         ),
-    )(totals, prompts, q_own, k_own, far)
-    return pl.pallas_call(
+    )(totals, prompts, q_own, k_own, g, far, *weights)
+    mine, theirs = pl.pallas_call(
         value_kernel,
         in_specs=[VMEM] * 3,
         out_specs=[VMEM] * 2,
@@ -231,6 +251,7 @@
             transcendentals=0,
         ),
     )(prob, g_own, g_far)
+    return mine, theirs, turned
 
 
 def sibling_kernel(q, k, out, q_head, k_head, done):
@@ -278,10 +299,9 @@
 def partial_kernel(*refs):
     blocks, weight, out = refs[:-2], refs[-2], refs[-1]
     rows = blocks[0].shape[0]
-    total = lax.dot_general(
+    total = jnp.dot(
         jnp.concatenate([block[...] for block in blocks], axis=0),
         weight[...],
-        CONTRACT_LAST,
         preferred_element_type=jnp.float32,
     )
     for i in range(len(blocks)):
@@ -317,14 +337,15 @@
     count[...] = jnp.full((1, LANES), total.astype(jnp.float32), jnp.float32)
 
 
-def share_kernel(select, *refs, groups):
+def add_kernel(left, right, out):
+    out[...] = left[...] + right[...]
+
+
+def share_kernel(select, norms, *refs, groups):
     examples = sum(len(steps) for steps in groups)
-    norms, grads = refs[:examples], refs[examples : examples + len(groups)]
-    outs, scales = refs[examples + len(groups) : -1], refs[-1]
-    norm_sq = norms[0][...]
-    for other in norms[1:]:
-        norm_sq = norm_sq + other[...]
-    norm_sq = jnp.sum(norm_sq, axis=1, keepdims=True)
+    grads = refs[: len(groups)]
+    outs, scales = refs[len(groups) : -1], refs[-1]
+    norm_sq = jnp.sum(norms[...], axis=1, keepdims=True)
     scales[...] = jnp.broadcast_to(1.0 / jnp.maximum(1.0, jnp.sqrt(norm_sq)), scales.shape)
     dp_index = lax.axis_index("dp")
     scale = [scales[pl.ds(dp_index ^ step, 1), :] for step in range(examples)]
@@ -342,25 +363,17 @@
             outs[k][:, at : at + LANES] = total.astype(jnp.bfloat16)
 
 
-def update_kernel(count, *refs, examples):
-    shares, noise, out = refs[:examples], refs[examples], refs[examples + 1]
-    stage, done = refs[examples + 2 :]
-    columns = shares[0].shape[1]
-    dp_index = lax.axis_index("dp")
-    copies = []
-    for step in range(examples):
-        base = pl.multiple_of((dp_index ^ step) * columns, LANES)
-        for at in range(0, columns, LANES):
-            share = shares[step][:, at : at + LANES].astype(jnp.float32)
-            added = noise[0, :, pl.ds(pl.multiple_of(base + at, LANES), LANES)]
-            stage[step, :, at : at + LANES] = (math.sqrt(PROMPT * D) * share + added) / count[...]
-        copy = pltpu.make_async_copy(
-            stage.at[step], out.at[0, :, pl.ds(base, columns)], done.at[step]
-        )
-        copy.start()
-        copies.append(copy)
-    for copy in copies:
-        copy.wait()
+def update_kernel(count, share, noise, *refs, step):
+    out, stage, done = refs[-3:]
+    columns = share.shape[1]
+    base = pl.multiple_of((lax.axis_index("dp") ^ step) * columns, LANES)
+    for at in range(0, columns, LANES):
+        part = share[:, at : at + LANES].astype(jnp.float32)
+        added = noise[0, :, pl.ds(pl.multiple_of(base + at, LANES), LANES)]
+        stage[:, at : at + LANES] = (math.sqrt(PROMPT * D) * part + added) / count[...]
+    copy = pltpu.make_async_copy(stage, out.at[0, :, pl.ds(base, columns)], done.at[0])
+    copy.start()
+    copy.wait()
 
 
 def to_dp(array, dp):
@@ -369,12 +382,12 @@
 
 def tail_by_permutes(value_grad, weight, tenant_of, owner_of, counts, noise, sizes):
     dp = sizes["dp"]
-    columns = weight.shape[0]
+    columns = weight.shape[1]
     rows = PROMPT // 2
     swap = xor_pairs(2, 1)
     small = pltpu.CompilerParams(vmem_limit_bytes=16 * 1024 * 1024)
     blocks = to_dp(value_grad, dp)
-    groups = GROUPS(dp)
+    groups = [[step] for step in [0] + arrival("blocks", dp)]
     tenant_of, blocks[-1] = lax.optimization_barrier((tenant_of, blocks[-1]))
     select, count = pl.pallas_call(
         functools.partial(select_kernel, examples=dp),
@@ -387,7 +400,10 @@
         compiler_params=small,
     )(tenant_of, owner_of, counts)
     grads, squares = [], None
+    nears = []
     for steps in groups:
+        if len(nears) > 1:
+            blocks[steps[0]], _ = lax.optimization_barrier((blocks[steps[0]], nears[-1]))
         shape = (len(steps), rows, columns)
         near = pl.pallas_call(
             partial_kernel,
@@ -401,6 +417,7 @@
                 transcendentals=0,
             ),
         )(*[blocks[step] for step in steps], weight)
+        nears.append(near)
         far = lax.ppermute(near, "tensor", swap)
         grad, square = pl.pallas_call(
             functools.partial(combine_kernel, steps=steps),
@@ -415,28 +432,43 @@
         grads.append(grad)
         squares = square if squares is None else squares + square
     norms = to_dp(squares + lax.ppermute(squares, "seq", swap), dp)
+    total = norms[0]
+    for step in arrival("norms", dp):
+        total = pl.pallas_call(
+            add_kernel,
+            in_specs=[VMEM] * 2,
+            out_specs=VMEM,
+            out_shape=jax.ShapeDtypeStruct(total.shape, total.dtype),
+            compiler_params=small,
+        )(total, norms[step])
     shares = pl.pallas_call(
         functools.partial(share_kernel, groups=groups),
-        in_specs=[VMEM] * (1 + dp + len(groups)),
+        in_specs=[VMEM] * (2 + len(groups)),
         out_specs=[VMEM] * dp,
         out_shape=[jax.ShapeDtypeStruct((rows, columns), jnp.bfloat16)] * dp,
         scratch_shapes=[pltpu.VMEM((8, LANES), jnp.float32)],
         compiler_params=small,
-    )(select, *norms, *grads)
+    )(select, total, *grads)
     arrived = [shares[0]] + [
         lax.ppermute(shares[step], "dp", xor_pairs(dp, step)) for step in range(1, dp)
     ]
-    return pl.pallas_call(
-        functools.partial(update_kernel, examples=dp),
-        in_specs=[VMEM] * (dp + 2),
-        out_specs=ANY,
-        out_shape=jax.ShapeDtypeStruct(noise.shape, jnp.float32),
-        scratch_shapes=[
-            pltpu.VMEM((dp, rows, columns), jnp.float32),
-            pltpu.SemaphoreType.DMA((dp,)),
-        ],
-        compiler_params=small,
-    )(count, *arrived, noise)
+    result = []
+    for step in [0] + arrival("shares", dp):
+        result = [
+            pl.pallas_call(
+                functools.partial(update_kernel, step=step),
+                in_specs=[VMEM] * 3 + [ANY] * len(result),
+                out_specs=ANY,
+                out_shape=jax.ShapeDtypeStruct(noise.shape, jnp.float32),
+                input_output_aliases={3: 0} if result else {},
+                scratch_shapes=[
+                    pltpu.VMEM((rows, columns), jnp.float32),
+                    pltpu.SemaphoreType.DMA((1,)),
+                ],
+                compiler_params=small,
+            )(count, arrived[step], noise, *result)
+        ]
+    return result[0]
 
 
 def tail_by_collectives(value_grad, weight, tenant_of, owner_of, counts, noise):
@@ -474,7 +506,9 @@
     permutes = sizes["tensor"] == 2 and aligned
     *own, g_sent = own_triangle(q, k, g, q_head, k_head)
     g_far = lax.ppermute(g_sent, "seq", swap)
-    mine, theirs = prompt_value_grad(*own, far, g_far)
+    mine, theirs, turned = prompt_value_grad(
+        *own, g, far, g_far, value_weight if permutes else None
+    )
     other = lax.ppermute(theirs, "seq", swap)
     first = seq_index == 0
     value_grad = jnp.concatenate(
@@ -482,7 +516,7 @@
     )
     if permutes:
         return tail_by_permutes(
-            value_grad, value_weight, tenant_of, owner_of, counts, noise, sizes
+            value_grad, turned[0], tenant_of, owner_of, counts, noise, sizes
         )
     return tail_by_collectives(value_grad, value_weight, tenant_of, owner_of, counts, noise)
 

time: 47.7 us -> 46.8 us (0.981)
  waiting for transfers between devices: 12 us -> 9.76 us
  Pallas kernels: 14.4 us -> 15.3 us
    ppermute x3, waiting for transfers between devices: 3.92 us -> 1.77 us  [tail_by_permutes(): lax.ppermute(shares[step], 'dp', xor_pairs(dp, step))]
    pallas_call x2 -> x8, Pallas kernels: 5.6 us -> 7.57 us  [the longest x1 4.75 us: prompt_value_grad(): pl.pallas_call(functools.partial(attention_kernel, turn=bool(weights)), i...]
    pallas_call x4, Pallas kernels: 3.06 us -> 2.01 us  [tail_by_permutes(): pl.pallas_call(partial_kernel, in_specs=[VMEM] * (len(steps) + 1), out_sp...]
  transfers between devices with their start and end apart: 17 -> 17, of which waited for: 9 -> 9; matrix products, arithmetic and copies ran while one was open for 0% -> 0% of each run, Pallas kernels for 24% -> 26%
where the time goes in v7:
time: 46.8 us; the launch traced here: 46.7 us
  starting transfers between devices  21.3 us (46%)
  Pallas kernels  15.3 us (33%)
  waiting for transfers between devices  9.76 us (21%)
    ppermute x6, starting transfers between devices, to_dp(): lax.ppermute(array, 'dp', xor_pairs(dp, step))  10 us
    ppermute x4, starting transfers between devices, tail_by_permutes(): far = lax.ppermute(near, 'tensor', swap)  5.71 us
    pallas_call x1, Pallas kernels, prompt_value_grad(): pl.pallas_call(functools.partial(attention_kernel, turn=bool(weights)), i...  4.75 us
    ppermute x3, starting transfers between devices, tail_by_permutes(): lax.ppermute(shares[step], 'dp', xor_pairs(dp, step))  4.45 us
    ppermute x4, waiting for transfers between devices, tail_by_permutes(): far = lax.ppermute(near, 'tensor', swap)  3.54 us
    pallas_call x4, Pallas kernels, tail_by_permutes(): pl.pallas_call(functools.partial(update_kernel, step=step), in_specs=[VME...  2.81 us
    pallas_call x1, Pallas kernels, own_triangle(): pl.pallas_call(triangle_kernel, in_specs=[HBM] * 3 + [VMEM] * 2, out_spec...  2.8 us
    ppermute x6, waiting for transfers between devices, to_dp(): lax.ppermute(array, 'dp', xor_pairs(dp, step))  2.32 us
  transfers between devices with their start and end apart: 17, of which 9 were waited for; matrix products, arithmetic and copies ran while one was open for 0% of the time, Pallas kernels for 26%

profile of v7, /device:TPU:0, one launch (start us, length us, event | category | flops | bytes accessed | tf_op | source)
XLA Modules:
  0.0 46.7 jit_solution(11280594964823649368)
XLA Ops:
  0.0 1.5 %shard_map.82 = (bf16[512,1536]{1,0:T(8,128)(2,1)S(1)}, bf16[512,256]{1,0:T(8,128)(2,1)S(1)}, bf16[512,128]{1,0:T(8,128)(2,1)S(1)}) custom-call(bf16[512,2048]{1,0:T(8,128)(2,1)} %bitcast.3, bf16[512,1024]{1,0:T(8,128)(2,1)} %bitcast.5), custom_call_target="tpu_custom_call" | custom-call | tf_op jit(solution)/shard_map/pallas_call | solution.py:285
  2.0 2.8 %shard_map.83 = (f32[4,8,1024]{2,1,0:T(8,128)S(1)}, f32[4,64,1024]{2,1,0:T(8,128)S(1)}, bf16[4,512,256]{2,1,0:T(8,128)(2,1)S(1)}, bf16[4,512,128]{2,1,0:T(8,128)(2,1)S(1)}, bf16[512,1024]{1,0:T(8,128)(2,1)S(1)}) custom-call(bf16[512,2048]{1,0:T(8,128)(2,1)} %bitcast.4, bf16[512,1024]{1,0:T(8,128)(2,1)} %bitcast.6, bf16[512,2048]{1,0:T(8,128)(2,1)} %bitcast.7, ...), custom_call_target="tpu_custom_call" | custom-call | flops 536870912 | bytes 3145728 | tf_op jit(solution)/shard_map/pallas_call | solution.py:117
  5.1 4.8 %shard_map.84 = (bf16[4,2,64,1024]{3,2,1,0:T(8,128)(2,1)S(1)}, bf16[512,1024]{1,0:T(8,128)(2,1)S(1)}, bf16[1024,1152]{1,0:T(8,128)(2,1)S(1)}) custom-call(f32[4,8,1024]{2,1,0:T(8,128)S(1)} %get-tuple-element.38.refs_0_, f32[4,64,1024]{2,1,0:T(8,128)S(1)} %get-tuple-element.39.refs_1_, bf16[4,512,256]{2,1,0:T(8,128)(2,1)S(1)} %get-tuple-element.40.refs_2_, ...), custom_call_target="tpu_custom_call" | custom-call | flops 1610612736 | bytes 3145728 | tf_op jit(solution)/shard_map/pallas_call | solution.py:222
  10.7 0.9 %collective-permute-done.2 = bf16[32,512]{1,0:T(8,128)(2,1)S(1)} collective-permute-done((bf16[32,512]{1,0:T(8,128)(2,1)S(1)}, bf16[32,512]{1,0:T(8,128)(2,1)S(1)}, u32[]{:S(2)}, u32[]{:S(2)}) %collective-permute-start.2) | collective-permute-done | bytes 32800 | tf_op jit(solution)/shard_map/ppermute | solution.py:512
  11.6 5.0 %collective-permute-start.3 = (bf16[32,1024]{1,0:T(8,128)(2,1)S(1)}, bf16[32,1024]{1,0:T(8,128)(2,1)S(1)}, u32[]{:S(2)}, u32[]{:S(2)}) collective-permute-start(bf16[32,1024]{1,0:T(8,128)(2,1)S(1)} %pad_maximum_fusion.refs_0_), channel_id=1, source_target_pairs={{0,12},{4,8},{8,4},{12,0},{1,13},{5,9},{9,5},{13,1},{2,14},{6,10},... | collective-permute-start | bytes 196616 | tf_op jit(solution)/shard_map/ppermute | solution.py:380
  16.6 0.6 %collective-permute-start.8 = (bf16[32,1024]{1,0:T(8,128)(2,1)S(1)}, bf16[32,1024]{1,0:T(8,128)(2,1)S(1)}, u32[]{:S(2)}, u32[]{:S(2)}) collective-permute-start(bf16[32,1024]{1,0:T(8,128)(2,1)S(1)} %pad_maximum_fusion.refs_0_), channel_id=1, source_target_pairs={{0,8},{4,12},{8,0},{12,4},{1,9},{5,13},{9,1},{13,5},{2,10},{6,14},... | collective-permute-start | bytes 196616 | tf_op jit(solution)/shard_map/ppermute | solution.py:380
  17.8 1.7 %collective-permute-start.4 = (bf16[1,32,1152]{2,1,0:T(8,128)(2,1)S(1)}, bf16[1,32,1152]{2,1,0:T(8,128)(2,1)S(1)}, u32[]{:S(2)}, u32[]{:S(2)}) collective-permute-start(bf16[1,32,1152]{2,1,0:T(8,128)(2,1)S(1)} %shard_map.87.near), channel_id=1, source_target_pairs={{0,2},{2,0},{1,3},{3,1},{4,6},{6,4},{5,7},{7,5},{8,10},{10,8},{9,1... | collective-permute-start | bytes 221192 | tf_op jit(solution)/shard_map/ppermute | solution.py:421
  20.0 1.8 %collective-permute-start.5 = (bf16[1,32,1152]{2,1,0:T(8,128)(2,1)S(1)}, bf16[1,32,1152]{2,1,0:T(8,128)(2,1)S(1)}, u32[]{:S(2)}, u32[]{:S(2)}) collective-permute-start(bf16[1,32,1152]{2,1,0:T(8,128)(2,1)S(1)} %shard_map.89.near), channel_id=1, source_target_pairs={{0,2},{2,0},{1,3},{3,1},{4,6},{6,4},{5,7},{7,5},{8,10},{10,8},{9,1... | collective-permute-start | bytes 221192 | tf_op jit(solution)/shard_map/ppermute | solution.py:421
  22.4 1.4 %collective-permute-start.7 = (bf16[1,32,1152]{2,1,0:T(8,128)(2,1)S(1)}, bf16[1,32,1152]{2,1,0:T(8,128)(2,1)S(1)}, u32[]{:S(2)}, u32[]{:S(2)}) collective-permute-start(bf16[1,32,1152]{2,1,0:T(8,128)(2,1)S(1)} %shard_map.91.near), channel_id=1, source_target_pairs={{0,2},{2,0},{1,3},{3,1},{4,6},{6,4},{5,7},{7,5},{8,10},{10,8},{9,1... | collective-permute-start | bytes 221192 | tf_op jit(solution)/shard_map/ppermute | solution.py:421
  24.4 0.8 %collective-permute-start.9 = (bf16[1,32,1152]{2,1,0:T(8,128)(2,1)S(1)}, bf16[1,32,1152]{2,1,0:T(8,128)(2,1)S(1)}, u32[]{:S(2)}, u32[]{:S(2)}) collective-permute-start(bf16[1,32,1152]{2,1,0:T(8,128)(2,1)S(1)} %shard_map.93.near), channel_id=1, source_target_pairs={{0,2},{2,0},{1,3},{3,1},{4,6},{6,4},{5,7},{7,5},{8,10},{10,8},{9,1... | collective-permute-start | bytes 221192 | tf_op jit(solution)/shard_map/ppermute | solution.py:421
  25.2 2.4 %collective-permute-done.7.far = bf16[1,32,1152]{2,1,0:T(8,128)(2,1)S(1)} collective-permute-done((bf16[1,32,1152]{2,1,0:T(8,128)(2,1)S(1)}, bf16[1,32,1152]{2,1,0:T(8,128)(2,1)S(1)}, u32[]{:S(2)}, u32[]{:S(2)}) %collective-permute-start.7) | collective-permute-done | bytes 73760 | tf_op jit(solution)/shard_map/ppermute | solution.py:421
  27.7 1.1 %collective-permute-done.9.far = bf16[1,32,1152]{2,1,0:T(8,128)(2,1)S(1)} collective-permute-done((bf16[1,32,1152]{2,1,0:T(8,128)(2,1)S(1)}, bf16[1,32,1152]{2,1,0:T(8,128)(2,1)S(1)}, u32[]{:S(2)}, u32[]{:S(2)}) %collective-permute-start.9) | collective-permute-done | bytes 73760 | tf_op jit(solution)/shard_map/ppermute | solution.py:421
  28.9 1.2 %collective-permute-done.10 = f32[8,128]{1,0:T(8,128)S(1)} collective-permute-done((f32[8,128]{1,0:T(8,128)S(1)}, f32[8,128]{1,0:T(8,128)S(1)}, u32[]{:S(2)}, u32[]{:S(2)}) %collective-permute-start.10) | collective-permute-done | bytes 4128 | tf_op jit(solution)/shard_map/ppermute | solution.py:434
  30.1 2.8 %collective-permute-start.11 = (f32[8,128]{1,0:T(8,128)S(1)}, f32[8,128]{1,0:T(8,128)S(1)}, u32[]{:S(2)}, u32[]{:S(2)}) collective-permute-start(f32[8,128]{1,0:T(8,128)S(1)} %add.15.left), channel_id=1, source_target_pairs={{0,12},{4,8},{8,4},{12,0},{1,13},{5,9},{9,5},{13,1},{2,14},{6,10},... | collective-permute-start | bytes 12296 | tf_op jit(solution)/shard_map/ppermute | solution.py:380
  32.8 1.6 %collective-permute-start.13 = (f32[8,128]{1,0:T(8,128)S(1)}, f32[8,128]{1,0:T(8,128)S(1)}, u32[]{:S(2)}, u32[]{:S(2)}) collective-permute-start(f32[8,128]{1,0:T(8,128)S(1)} %add.15.left), channel_id=1, source_target_pairs={{0,4},{4,0},{8,12},{12,8},{1,5},{5,1},{9,13},{13,9},{2,6},{6,2},{1... | collective-permute-start | bytes 12296 | tf_op jit(solution)/shard_map/ppermute | solution.py:380
  35.5 1.9 %collective-permute-done.12.right = f32[8,128]{1,0:T(8,128)S(1)} collective-permute-done((f32[8,128]{1,0:T(8,128)S(1)}, f32[8,128]{1,0:T(8,128)S(1)}, u32[]{:S(2)}, u32[]{:S(2)}) %collective-permute-start.12) | collective-permute-done | bytes 4128 | tf_op jit(solution)/shard_map/ppermute | solution.py:380
  37.6 0.8 %collective-permute-start.16 = (bf16[32,1152]{1,0:T(8,128)(2,1)S(1)}, bf16[32,1152]{1,0:T(8,128)(2,1)S(1)}, u32[]{:S(2)}, u32[]{:S(2)}) collective-permute-start(bf16[32,1152]{1,0:T(8,128)(2,1)S(1)} %get-tuple-element.65), channel_id=1, source_target_pairs={{0,4},{4,0},{8,12},{12,8},{1,5},{5,1},{9,13},{13,9},{2,6},{6,2},{1... | collective-permute-start | bytes 221192 | tf_op jit(solution)/shard_map/ppermute | solution.py:453
  38.4 1.4 %collective-permute-start.15 = (bf16[32,1152]{1,0:T(8,128)(2,1)S(1)}, bf16[32,1152]{1,0:T(8,128)(2,1)S(1)}, u32[]{:S(2)}, u32[]{:S(2)}) collective-permute-start(bf16[32,1152]{1,0:T(8,128)(2,1)S(1)} %get-tuple-element.64), channel_id=1, source_target_pairs={{0,8},{4,12},{8,0},{12,4},{1,9},{5,13},{9,1},{13,5},{2,10},{6,14},... | collective-permute-start | bytes 221192 | tf_op jit(solution)/shard_map/ppermute | solution.py:453
  39.8 2.3 %collective-permute-start.14 = (bf16[32,1152]{1,0:T(8,128)(2,1)S(1)}, bf16[32,1152]{1,0:T(8,128)(2,1)S(1)}, u32[]{:S(2)}, u32[]{:S(2)}) collective-permute-start(bf16[32,1152]{1,0:T(8,128)(2,1)S(1)} %get-tuple-element.63), channel_id=1, source_target_pairs={{0,12},{4,8},{8,4},{12,0},{1,13},{5,9},{9,5},{13,1},{2,14},{6,10},... | collective-permute-start | bytes 221192 | tf_op jit(solution)/shard_map/ppermute | solution.py:453
  42.1 0.7 %shard_map.99.refs_0_ = f32[1,32,4608]{2,1,0:T(8,128)} custom-call(f32[1,128]{1,0:T(1,128)S(1)} %get-tuple-element.49.count, bf16[32,1152]{1,0:T(8,128)(2,1)S(1)} %get-tuple-element.66.share, f32[1,32,4608]{2,1,0:T(8,128)S(1)} %copy-done), custom_call_target="tpu_custom_call" | custom-call | tf_op jit(solution)/shard_map/pallas_call | solution.py:458
  42.8 0.7 %shard_map.100.refs_0_ = f32[1,32,4608]{2,1,0:T(8,128)} custom-call(f32[1,128]{1,0:T(1,128)S(1)} %get-tuple-element.49.count, bf16[32,1152]{1,0:T(8,128)(2,1)S(1)} %collective-permute-done.16.share, f32[1,32,4608]{2,1,0:T(8,128)S(1)} %copy-done, f32[1,32,4608]{2,1,0:T(8,128)} %shard_map.99.refs_0_), custom_call_target="tpu_custom_call", output_to_operand_aliasing={{}: (3, {})} | custom-call | tf_op jit(solution)/shard_map/pallas_call | solution.py:458
  43.5 1.5 %collective-permute-done.15.share = bf16[32,1152]{1,0:T(8,128)(2,1)S(1)} collective-permute-done((bf16[32,1152]{1,0:T(8,128)(2,1)S(1)}, bf16[32,1152]{1,0:T(8,128)(2,1)S(1)}, u32[]{:S(2)}, u32[]{:S(2)}) %collective-permute-start.15) | collective-permute-done | bytes 73760 | tf_op jit(solution)/shard_map/ppermute | solution.py:453
  45.1 0.7 %shard_map.101.refs_0_ = f32[1,32,4608]{2,1,0:T(8,128)} custom-call(f32[1,128]{1,0:T(1,128)S(1)} %get-tuple-element.49.count, bf16[32,1152]{1,0:T(8,128)(2,1)S(1)} %collective-permute-done.15.share, f32[1,32,4608]{2,1,0:T(8,128)S(1)} %copy-done, f32[1,32,4608]{2,1,0:T(8,128)} %shard_map.100.refs_0_), custom_call_target="tpu_custom_call", output_to_operand_aliasing={{}: (3, {})} | custom-call | tf_op jit(solution)/shard_map/pallas_call | solution.py:458
  46.0 0.7 %shard_map.102 = f32[1,32,4608]{2,1,0:T(8,128)} custom-call(f32[1,128]{1,0:T(1,128)S(1)} %get-tuple-element.49.count, bf16[32,1152]{1,0:T(8,128)(2,1)S(1)} %collective-permute-done.14.share, f32[1,32,4608]{2,1,0:T(8,128)S(1)} %copy-done, f32[1,32,4608]{2,1,0:T(8,128)} %shard_map.101.refs_0_), custom_call_target="tpu_custom_call", output_to_operand_aliasing={{}: (3, {})} | custom-call | tf_op jit(solution)/shard_map/pallas_call | solution.py:458
  (45 shorter events, 5.5 us)
Async XLA Ops:
  1.5 3.6 %collective-permute-start = (bf16[512,1536]{1,0:T(8,128)(2,1)S(1)}, bf16[512,1536]{1,0:T(8,128)(2,1)S(1)}, u32[]{:S(2)}, u32[]{:S(2)}) collective-permute-start(bf16[512,1536]{1,0:T(8,128)(2,1)S(1)} %get-tuple-element.42), channel_id=1, source_target_pairs={{0,1},{1,0},{2,3},{3,2},{4,5},{5,4},{6,7},{7,6},{8,9},{9,8},{10,11... | collective-permute-start | bytes 4718600 | tf_op jit(solution)/shard_map/ppermute | solution.py:504
  2.0 3.0 %copy-start.1 = (bf16[1152,1024]{1,0:T(8,128)(2,1)S(1)}, bf16[1152,1024]{1,0:T(8,128)(2,1)}, u32[]{:S(2)}) copy-start(bf16[1152,1024]{1,0:T(8,128)(2,1)} %refs_6_.1) | copy-start | bytes 7077892
  4.8 5.0 %collective-permute-start.1 = (bf16[512,1024]{1,0:T(8,128)(2,1)S(1)}, bf16[512,1024]{1,0:T(8,128)(2,1)S(1)}, u32[]{:S(2)}, u32[]{:S(2)}) collective-permute-start(bf16[512,1024]{1,0:T(8,128)(2,1)S(1)} %get-tuple-element.45), channel_id=1, source_target_pairs={{0,1},{1,0},{2,3},{3,2},{4,5},{5,4},{6,7},{7,6},{8,9},{9,8},{10,11... | collective-permute-start | bytes 3145736 | tf_op jit(solution)/shard_map/ppermute | solution.py:508
  10.3 1.3 %collective-permute-start.2 = (bf16[32,512]{1,0:T(8,128)(2,1)S(1)}, bf16[32,512]{1,0:T(8,128)(2,1)S(1)}, u32[]{:S(2)}, u32[]{:S(2)}) collective-permute-start(bf16[32,512]{1,0:T(8,128)(2,1)S(1)} %get-tuple-element.47), channel_id=1, source_target_pairs={{0,1},{1,0},{2,3},{3,2},{4,5},{5,4},{6,7},{7,6},{8,9},{9,8},{10,11... | collective-permute-start | bytes 98312 | tf_op jit(solution)/shard_map/ppermute | solution.py:512
  11.6 7.9 %collective-permute-start.3 = (bf16[32,1024]{1,0:T(8,128)(2,1)S(1)}, bf16[32,1024]{1,0:T(8,128)(2,1)S(1)}, u32[]{:S(2)}, u32[]{:S(2)}) collective-permute-start(bf16[32,1024]{1,0:T(8,128)(2,1)S(1)} %pad_maximum_fusion.refs_0_), channel_id=1, source_target_pairs={{0,12},{4,8},{8,4},{12,0},{1,13},{5,9},{9,5},{13,1},{2,14},{6,10},... | collective-permute-start | bytes 196616 | tf_op jit(solution)/shard_map/ppermute | solution.py:380
  16.6 5.3 %collective-permute-start.6 = (bf16[32,1024]{1,0:T(8,128)(2,1)S(1)}, bf16[32,1024]{1,0:T(8,128)(2,1)S(1)}, u32[]{:S(2)}, u32[]{:S(2)}) collective-permute-start(bf16[32,1024]{1,0:T(8,128)(2,1)S(1)} %pad_maximum_fusion.refs_0_), channel_id=1, source_target_pairs={{0,4},{4,0},{8,12},{12,8},{1,5},{5,1},{9,13},{13,9},{2,6},{6,2},{1... | collective-permute-start | bytes 196616 | tf_op jit(solution)/shard_map/ppermute | solution.py:380
  16.6 7.2 %collective-permute-start.8 = (bf16[32,1024]{1,0:T(8,128)(2,1)S(1)}, bf16[32,1024]{1,0:T(8,128)(2,1)S(1)}, u32[]{:S(2)}, u32[]{:S(2)}) collective-permute-start(bf16[32,1024]{1,0:T(8,128)(2,1)S(1)} %pad_maximum_fusion.refs_0_), channel_id=1, source_target_pairs={{0,8},{4,12},{8,0},{12,4},{1,9},{5,13},{9,1},{13,5},{2,10},{6,14},... | collective-permute-start | bytes 196616 | tf_op jit(solution)/shard_map/ppermute | solution.py:380
  17.8 7.3 %collective-permute-start.4 = (bf16[1,32,1152]{2,1,0:T(8,128)(2,1)S(1)}, bf16[1,32,1152]{2,1,0:T(8,128)(2,1)S(1)}, u32[]{:S(2)}, u32[]{:S(2)}) collective-permute-start(bf16[1,32,1152]{2,1,0:T(8,128)(2,1)S(1)} %shard_map.87.near), channel_id=1, source_target_pairs={{0,2},{2,0},{1,3},{3,1},{4,6},{6,4},{5,7},{7,5},{8,10},{10,8},{9,1... | collective-permute-start | bytes 221192 | tf_op jit(solution)/shard_map/ppermute | solution.py:421
  20.0 5.1 %collective-permute-start.5 = (bf16[1,32,1152]{2,1,0:T(8,128)(2,1)S(1)}, bf16[1,32,1152]{2,1,0:T(8,128)(2,1)S(1)}, u32[]{:S(2)}, u32[]{:S(2)}) collective-permute-start(bf16[1,32,1152]{2,1,0:T(8,128)(2,1)S(1)} %shard_map.89.near), channel_id=1, source_target_pairs={{0,2},{2,0},{1,3},{3,1},{4,6},{6,4},{5,7},{7,5},{8,10},{10,8},{9,1... | collective-permute-start | bytes 221192 | tf_op jit(solution)/shard_map/ppermute | solution.py:421
  22.4 12.1 %copy-start.2 = (s32[4]{0:T(128)S(1)}, s32[4]{0:T(128)}, u32[]{:S(2)}) copy-start(s32[4]{0:T(128)} %tenant_of) | copy-start | bytes 52
  22.4 12.0 %copy-start.3 = (s32[4]{0:T(128)S(1)}, s32[4]{0:T(128)}, u32[]{:S(2)}) copy-start(s32[4]{0:T(128)} %owner_of.1) | copy-start | bytes 52
  22.4 12.0 %copy-start.4 = (s32[4]{0:T(128)S(1)}, s32[4]{0:T(128)}, u32[]{:S(2)}) copy-start(s32[4]{0:T(128)} %counts.1) | copy-start | bytes 52
  22.4 19.7 %copy-start = (f32[1,32,4608]{2,1,0:T(8,128)S(1)}, f32[1,32,4608]{2,1,0:T(8,128)}, u32[]{:S(2)}) copy-start(f32[1,32,4608]{2,1,0:T(8,128)} %noise.7) | copy-start | bytes 1769476
  22.4 5.2 %collective-permute-start.7 = (bf16[1,32,1152]{2,1,0:T(8,128)(2,1)S(1)}, bf16[1,32,1152]{2,1,0:T(8,128)(2,1)S(1)}, u32[]{:S(2)}, u32[]{:S(2)}) collective-permute-start(bf16[1,32,1152]{2,1,0:T(8,128)(2,1)S(1)} %shard_map.91.near), channel_id=1, source_target_pairs={{0,2},{2,0},{1,3},{3,1},{4,6},{6,4},{5,7},{7,5},{8,10},{10,8},{9,1... | collective-permute-start | bytes 221192 | tf_op jit(solution)/shard_map/ppermute | solution.py:421
  24.4 4.4 %collective-permute-start.9 = (bf16[1,32,1152]{2,1,0:T(8,128)(2,1)S(1)}, bf16[1,32,1152]{2,1,0:T(8,128)(2,1)S(1)}, u32[]{:S(2)}, u32[]{:S(2)}) collective-permute-start(bf16[1,32,1152]{2,1,0:T(8,128)(2,1)S(1)} %shard_map.93.near), channel_id=1, source_target_pairs={{0,2},{2,0},{1,3},{3,1},{4,6},{6,4},{5,7},{7,5},{8,10},{10,8},{9,1... | collective-permute-start | bytes 221192 | tf_op jit(solution)/shard_map/ppermute | solution.py:421
  28.8 1.2 %collective-permute-start.10 = (f32[8,128]{1,0:T(8,128)S(1)}, f32[8,128]{1,0:T(8,128)S(1)}, u32[]{:S(2)}, u32[]{:S(2)}) collective-permute-start(f32[8,128]{1,0:T(8,128)S(1)} %add_add_fusion), channel_id=1, source_target_pairs={{0,1},{1,0},{2,3},{3,2},{4,5},{5,4},{6,7},{7,6},{8,9},{9,8},{10,11... | collective-permute-start | bytes 12296 | tf_op jit(solution)/shard_map/ppermute | solution.py:434
  30.1 5.4 %collective-permute-start.11 = (f32[8,128]{1,0:T(8,128)S(1)}, f32[8,128]{1,0:T(8,128)S(1)}, u32[]{:S(2)}, u32[]{:S(2)}) collective-permute-start(f32[8,128]{1,0:T(8,128)S(1)} %add.15.left), channel_id=1, source_target_pairs={{0,12},{4,8},{8,4},{12,0},{1,13},{5,9},{9,5},{13,1},{2,14},{6,10},... | collective-permute-start | bytes 12296 | tf_op jit(solution)/shard_map/ppermute | solution.py:380
  32.8 4.5 %collective-permute-start.12 = (f32[8,128]{1,0:T(8,128)S(1)}, f32[8,128]{1,0:T(8,128)S(1)}, u32[]{:S(2)}, u32[]{:S(2)}) collective-permute-start(f32[8,128]{1,0:T(8,128)S(1)} %add.15.left), channel_id=1, source_target_pairs={{0,8},{4,12},{8,0},{12,4},{1,9},{5,13},{9,1},{13,5},{2,10},{6,14},... | collective-permute-start | bytes 12296 | tf_op jit(solution)/shard_map/ppermute | solution.py:380
  32.8 4.5 %collective-permute-start.13 = (f32[8,128]{1,0:T(8,128)S(1)}, f32[8,128]{1,0:T(8,128)S(1)}, u32[]{:S(2)}, u32[]{:S(2)}) collective-permute-start(f32[8,128]{1,0:T(8,128)S(1)} %add.15.left), channel_id=1, source_target_pairs={{0,4},{4,0},{8,12},{12,8},{1,5},{5,1},{9,13},{13,9},{2,6},{6,2},{1... | collective-permute-start | bytes 12296 | tf_op jit(solution)/shard_map/ppermute | solution.py:380
  37.6 5.2 %collective-permute-start.16 = (bf16[32,1152]{1,0:T(8,128)(2,1)S(1)}, bf16[32,1152]{1,0:T(8,128)(2,1)S(1)}, u32[]{:S(2)}, u32[]{:S(2)}) collective-permute-start(bf16[32,1152]{1,0:T(8,128)(2,1)S(1)} %get-tuple-element.65), channel_id=1, source_target_pairs={{0,4},{4,0},{8,12},{12,8},{1,5},{5,1},{9,13},{13,9},{2,6},{6,2},{1... | collective-permute-start | bytes 221192 | tf_op jit(solution)/shard_map/ppermute | solution.py:453
  38.4 6.6 %collective-permute-start.15 = (bf16[32,1152]{1,0:T(8,128)(2,1)S(1)}, bf16[32,1152]{1,0:T(8,128)(2,1)S(1)}, u32[]{:S(2)}, u32[]{:S(2)}) collective-permute-start(bf16[32,1152]{1,0:T(8,128)(2,1)S(1)} %get-tuple-element.64), channel_id=1, source_target_pairs={{0,8},{4,12},{8,0},{12,4},{1,9},{5,13},{9,1},{13,5},{2,10},{6,14},... | collective-permute-start | bytes 221192 | tf_op jit(solution)/shard_map/ppermute | solution.py:453
  39.8 6.2 %collective-permute-start.14 = (bf16[32,1152]{1,0:T(8,128)(2,1)S(1)}, bf16[32,1152]{1,0:T(8,128)(2,1)S(1)}, u32[]{:S(2)}, u32[]{:S(2)}) collective-permute-start(bf16[32,1152]{1,0:T(8,128)(2,1)S(1)} %get-tuple-element.63), channel_id=1, source_target_pairs={{0,12},{4,8},{8,4},{12,0},{1,13},{5,9},{9,5},{13,1},{2,14},{6,10},... | collective-permute-start | bytes 221192 | tf_op jit(solution)/shard_map/ppermute | solution.py:453

commit v8 on v7

--- a/solution.py
+++ b/solution.py
@@ -21,11 +21,31 @@
 PARTIAL_TYPE = jnp.bfloat16
 
 
-ARRIVAL = {"blocks": (3, 1, 2), "norms": (3, 2, 1), "shares": (1, 2, 3)}
-
-
-def arrival(what, dp):
-    return list(ARRIVAL[what]) if dp == 4 else list(range(1, dp))
+ORDER = {
+    "blocks": ((3, 1, 2), (3, 1, 2)),
+    "norms": ((3, 2, 1), (3, 2, 1)),
+    "shares": ((1, 2, 3), (1, 2, 3)),
+}
+
+
+def order(what, dp):
+    return ORDER[what] if dp == 4 else (tuple(range(1, dp)),) * 2
+
+
+def partner(what, slot, dp):
+    here = lax.axis_index("dp")
+    if slot == 0:
+        return here
+    first, second = (steps[slot - 1] for steps in order(what, dp))
+    if first == second:
+        return here ^ first
+    return here ^ jnp.where(lax.axis_index("seq") == 0, first, second)
+
+
+def to_partner(array, what, slot, dp):
+    steps = [steps[slot - 1] for steps in order(what, dp)]
+    pairs = [(2 * z + s, 2 * (z ^ step) + s) for z in range(dp) for s, step in enumerate(steps)]
+    return lax.ppermute(array, ("dp", "seq"), pairs)
 
 
 CONTRACT_LAST = (((1,), (1,)), ((), ()))
@@ -137,9 +157,9 @@
 
 def attention_kernel(*refs, turn):
     if turn:
-        totals, prompts, q_own, k_own, g, far, weight, prob, g_own, turned, k_first, done = refs
+        totals, prompts, q_own, k_own, g, far, weight, prob, g_own, turned, done = refs
     else:
-        totals, prompts, q_own, k_own, g, far, prob, g_own, k_first, done = refs
+        totals, prompts, q_own, k_own, g, far, prob, g_own, done = refs
     heads, rows, width = q_own.shape
     group = width // HEAD_DIM
     lanes = group * LANES
@@ -159,13 +179,13 @@
             share = weight.shape[1] // heads
             features = pl.ds(pl.multiple_of(h * share, LANES), share)
             turned[features, :] = weight[:, features].T
-        k_first[...] = jnp.where(first, k_own[h], k_far[...])
+        early_keys = jnp.where(first, k_own[h], k_far[...])
         for i, start in enumerate(range(0, rows, LANES)):
             at = slice(i * lanes, (i + 1) * lanes)
             q_block = far[start : start + LANES, at_q]
             other, far_prompt = add_scores(query_block(q_block), k_far, start + LANES, True, None)
             q_block = jnp.where(first, q_block, q_own[h, start : start + LANES, :])
-            square, late_prompt = add_scores(query_block(q_block), k_first, rows, False, None)
+            square, late_prompt = add_scores(query_block(q_block), early_keys, rows, False, None)
             own, own_prompt = totals[h, :, at], prompts[h, :, at]
             early = jnp.where(first, own, other)
             late = square + jnp.where(first, other, own)
@@ -179,7 +199,7 @@
                     prob[h, j, :, column : column + LANES] = scaled[:, j * LANES : (j + 1) * LANES]
         return carry
 
-    lax.fori_loop(0, heads, step, 0)
+    lax.fori_loop(0, heads, step, 0, unroll=2 if heads % 2 == 0 else 1)
     load.wait()
 
 
@@ -228,10 +248,7 @@
             jax.ShapeDtypeStruct((rows, heads * width), jnp.bfloat16),
         ]
         + [jax.ShapeDtypeStruct(w.shape[::-1], w.dtype) for w in weights],
-        scratch_shapes=[
-            pltpu.VMEM((rows, HEAD_DIM), jnp.bfloat16),
-            pltpu.SemaphoreType.DMA((1,)),
-        ],
+        scratch_shapes=[pltpu.SemaphoreType.DMA((1,))],
         compiler_params=pltpu.CompilerParams(vmem_limit_bytes=16 * 1024 * 1024),
         cost_estimate=pl.CostEstimate(
             flops=heads * group * 6 * rows * rows * HEAD_DIM,
@@ -296,44 +313,33 @@
     )(q, k)
 
 
-def partial_kernel(*refs):
-    blocks, weight, out = refs[:-2], refs[-2], refs[-1]
-    rows = blocks[0].shape[0]
-    total = jnp.dot(
-        jnp.concatenate([block[...] for block in blocks], axis=0),
-        weight[...],
-        preferred_element_type=jnp.float32,
-    )
-    for i in range(len(blocks)):
-        out[i] = total[i * rows : (i + 1) * rows].astype(out.dtype)
-
-
-def combine_kernel(near, far, grad, squares, *, steps):
+def partial_kernel(block, weight, out):
+    total = jnp.dot(block[...], weight[...], preferred_element_type=jnp.float32)
+    out[...] = total.astype(out.dtype)
+
+
+def combine_kernel(near, far, grad, squares, *, slot, dp):
+    folded = None
+    for at in range(0, near.shape[1], LANES):
+        part = near[:, at : at + LANES].astype(jnp.float32)
+        part = part + far[:, at : at + LANES].astype(jnp.float32)
+        grad[:, at : at + LANES] = part
+        folded = part * part if folded is None else folded + part * part
+    folded = jnp.sum(folded, axis=0, keepdims=True)
     example = lax.broadcasted_iota(jnp.int32, squares.shape, 0)
-    by_example = jnp.zeros(squares.shape, jnp.float32)
-    for i, step in enumerate(steps):
-        folded = None
-        for at in range(0, near.shape[2], LANES):
-            part = near[i, :, at : at + LANES].astype(jnp.float32)
-            part = part + far[i, :, at : at + LANES].astype(jnp.float32)
-            grad[i, :, at : at + LANES] = part
-            folded = part * part if folded is None else folded + part * part
-        folded = jnp.sum(folded, axis=0, keepdims=True)
-        by_example = jnp.where(example == (lax.axis_index("dp") ^ step), folded, by_example)
-    squares[...] = by_example
-
-
-def select_kernel(tenant_of, owner_of, counts, select, count, *, examples):
-    dp_index = lax.axis_index("dp")
-    for step in range(examples):
-        owner = owner_of[tenant_of[dp_index ^ step]]
-        for k in range(examples):
-            hit = jnp.where(owner == (dp_index ^ k), 1.0, 0.0)
-            row = k * examples + step
+    squares[...] = jnp.where(example == partner("blocks", slot, dp), folded, 0.0)
+
+
+def select_kernel(tenant_of, owner_of, counts, select, count, *, dp):
+    for j in range(dp):
+        owner = owner_of[tenant_of[partner("blocks", j, dp)]]
+        for i in range(dp):
+            hit = jnp.where(owner == partner("shares", i, dp), 1.0, 0.0)
+            row = i * dp + j
             select[row : row + 1, :] = jnp.full((1, LANES), hit, jnp.float32)
     total = 0
-    for slot in range(examples):
-        total = total + jnp.where(owner_of[slot] == dp_index, counts[slot], 0)
+    for slot in range(dp):
+        total = total + jnp.where(owner_of[slot] == lax.axis_index("dp"), counts[slot], 0)
     count[...] = jnp.full((1, LANES), total.astype(jnp.float32), jnp.float32)
 
 
@@ -341,32 +347,25 @@
     out[...] = left[...] + right[...]
 
 
-def share_kernel(select, norms, *refs, groups):
-    examples = sum(len(steps) for steps in groups)
-    grads = refs[: len(groups)]
-    outs, scales = refs[len(groups) : -1], refs[-1]
+def share_kernel(select, norms, *refs, dp):
+    grads, outs, scales = refs[:dp], refs[dp : 2 * dp], refs[-1]
     norm_sq = jnp.sum(norms[...], axis=1, keepdims=True)
     scales[...] = jnp.broadcast_to(1.0 / jnp.maximum(1.0, jnp.sqrt(norm_sq)), scales.shape)
-    dp_index = lax.axis_index("dp")
-    scale = [scales[pl.ds(dp_index ^ step, 1), :] for step in range(examples)]
-    for k in range(examples):
-        factor = [
-            scale[step] * select[k * examples + step : k * examples + step + 1, :]
-            for step in range(examples)
-        ]
-        for at in range(0, outs[k].shape[1], LANES):
+    scale = [scales[pl.ds(partner("blocks", j, dp), 1), :] for j in range(dp)]
+    for i, out in enumerate(outs):
+        factor = [scale[j] * select[i * dp + j : i * dp + j + 1, :] for j in range(dp)]
+        for at in range(0, out.shape[1], LANES):
             total = None
-            for ref, steps in zip(grads, groups):
-                for i, step in enumerate(steps):
-                    term = ref[i, :, at : at + LANES] * factor[step]
-                    total = term if total is None else total + term
-            outs[k][:, at : at + LANES] = total.astype(jnp.bfloat16)
-
-
-def update_kernel(count, share, noise, *refs, step):
+            for grad, weight in zip(grads, factor):
+                term = grad[:, at : at + LANES] * weight
+                total = term if total is None else total + term
+            out[:, at : at + LANES] = total.astype(jnp.bfloat16)
+
+
+def update_kernel(count, share, noise, *refs, slot, dp):
     out, stage, done = refs[-3:]
     columns = share.shape[1]
-    base = pl.multiple_of((lax.axis_index("dp") ^ step) * columns, LANES)
+    base = pl.multiple_of(partner("shares", slot, dp) * columns, LANES)
     for at in range(0, columns, LANES):
         part = share[:, at : at + LANES].astype(jnp.float32)
         added = noise[0, :, pl.ds(pl.multiple_of(base + at, LANES), LANES)]
@@ -376,87 +375,76 @@
     copy.wait()
 
 
-def to_dp(array, dp):
-    return [array] + [lax.ppermute(array, "dp", xor_pairs(dp, step)) for step in range(1, dp)]
-
-
 def tail_by_permutes(value_grad, weight, tenant_of, owner_of, counts, noise, sizes):
     dp = sizes["dp"]
     columns = weight.shape[1]
     rows = PROMPT // 2
     swap = xor_pairs(2, 1)
     small = pltpu.CompilerParams(vmem_limit_bytes=16 * 1024 * 1024)
-    blocks = to_dp(value_grad, dp)
-    groups = [[step] for step in [0] + arrival("blocks", dp)]
-    tenant_of, blocks[-1] = lax.optimization_barrier((tenant_of, blocks[-1]))
-    select, count = pl.pallas_call(
-        functools.partial(select_kernel, examples=dp),
-        in_specs=[SMEM] * 3,
-        out_specs=[VMEM] * 2,
-        out_shape=[
-            jax.ShapeDtypeStruct((dp * dp, LANES), jnp.float32),
-            jax.ShapeDtypeStruct((1, LANES), jnp.float32),
-        ],
-        compiler_params=small,
-    )(tenant_of, owner_of, counts)
-    grads, squares = [], None
-    nears = []
-    for steps in groups:
-        if len(nears) > 1:
-            blocks[steps[0]], _ = lax.optimization_barrier((blocks[steps[0]], nears[-1]))
-        shape = (len(steps), rows, columns)
-        near = pl.pallas_call(
+
+    def kernel(body, operands, outs, scalar=False, **static):
+        return pl.pallas_call(
+            functools.partial(body, **static),
+            in_specs=[SMEM if scalar else VMEM] * len(operands),
+            out_specs=[VMEM] * len(outs),
+            out_shape=[jax.ShapeDtypeStruct(shape, dtype) for shape, dtype in outs],
+            compiler_params=small,
+        )(*operands)
+
+    blocks = [value_grad]
+    blocks += [to_partner(value_grad, "blocks", slot, dp) for slot in range(1, dp)]
+    tenant_of, blocks[1] = lax.optimization_barrier((tenant_of, blocks[1]))
+    select, count = kernel(
+        select_kernel,
+        (tenant_of, owner_of, counts),
+        [((dp * dp, LANES), jnp.float32), ((1, LANES), jnp.float32)],
+        scalar=True,
+        dp=dp,
+    )
+    grads, squares, near = [], None, None
+    for slot, block in enumerate(blocks):
+        if slot > 1:
+            block, _ = lax.optimization_barrier((block, near))
+        (near,) = pl.pallas_call(
             partial_kernel,
-            in_specs=[VMEM] * (len(steps) + 1),
-            out_specs=VMEM,
-            out_shape=jax.ShapeDtypeStruct(shape, PARTIAL_TYPE),
+            in_specs=[VMEM] * 2,
+            out_specs=[VMEM],
+            out_shape=[jax.ShapeDtypeStruct((rows, columns), PARTIAL_TYPE)],
             compiler_params=small,
             cost_estimate=pl.CostEstimate(
-                flops=2 * len(steps) * rows * weight.size,
-                bytes_accessed=2 * weight.size,
-                transcendentals=0,
+                flops=2 * rows * weight.size, bytes_accessed=2 * weight.size, transcendentals=0
             ),
-        )(*[blocks[step] for step in steps], weight)
-        nears.append(near)
+        )(block, weight)
         far = lax.ppermute(near, "tensor", swap)
-        grad, square = pl.pallas_call(
-            functools.partial(combine_kernel, steps=steps),
-            in_specs=[VMEM] * 2,
-            out_specs=[VMEM] * 2,
-            out_shape=[
-                jax.ShapeDtypeStruct(shape, jnp.float32),
-                jax.ShapeDtypeStruct((8, LANES), jnp.float32),
-            ],
-            compiler_params=small,
-        )(near, far)
+        grad, square = kernel(
+            combine_kernel,
+            (near, far),
+            [((rows, columns), jnp.float32), ((8, LANES), jnp.float32)],
+            slot=slot,
+            dp=dp,
+        )
         grads.append(grad)
         squares = square if squares is None else squares + square
-    norms = to_dp(squares + lax.ppermute(squares, "seq", swap), dp)
-    total = norms[0]
-    for step in arrival("norms", dp):
-        total = pl.pallas_call(
-            add_kernel,
-            in_specs=[VMEM] * 2,
-            out_specs=VMEM,
-            out_shape=jax.ShapeDtypeStruct(total.shape, total.dtype),
-            compiler_params=small,
-        )(total, norms[step])
+    squares = squares + lax.ppermute(squares, "seq", swap)
+    total = squares
+    for slot in range(1, dp):
+        other = to_partner(squares, "norms", slot, dp)
+        (total,) = kernel(add_kernel, (total, other), [((8, LANES), jnp.float32)])
     shares = pl.pallas_call(
-        functools.partial(share_kernel, groups=groups),
-        in_specs=[VMEM] * (2 + len(groups)),
+        functools.partial(share_kernel, dp=dp),
+        in_specs=[VMEM] * (2 + dp),
         out_specs=[VMEM] * dp,
         out_shape=[jax.ShapeDtypeStruct((rows, columns), jnp.bfloat16)] * dp,
         scratch_shapes=[pltpu.VMEM((8, LANES), jnp.float32)],
         compiler_params=small,
     )(select, total, *grads)
-    arrived = [shares[0]] + [
-        lax.ppermute(shares[step], "dp", xor_pairs(dp, step)) for step in range(1, dp)
-    ]
     result = []
-    for step in [0] + arrival("shares", dp):
+    for slot, share in enumerate(shares):
+        if slot:
+            share = to_partner(share, "shares", slot, dp)
         result = [
             pl.pallas_call(
-                functools.partial(update_kernel, step=step),
+                functools.partial(update_kernel, slot=slot, dp=dp),
                 in_specs=[VMEM] * 3 + [ANY] * len(result),
                 out_specs=ANY,
                 out_shape=jax.ShapeDtypeStruct(noise.shape, jnp.float32),
@@ -466,7 +454,7 @@
                     pltpu.SemaphoreType.DMA((1,)),
                 ],
                 compiler_params=small,
-            )(count, arrived[step], noise, *result)
+            )(count, share, noise, *result)
         ]
     return result[0]
 

time: 46.8 us -> 46.5 us (level)
  transfers between devices with their start and end apart: 17 -> 17, of which waited for: 9 -> 10; matrix products, arithmetic and copies ran while one was open for 0% -> 0% of each run, Pallas kernels for 26% -> 26%
where the time goes in v8:
time: 46.5 us; the launch traced here: 46.4 us
  starting transfers between devices  21.3 us (46%)
  Pallas kernels  15 us (32%)
  waiting for transfers between devices  9.76 us (21%)
    ppermute x9, starting transfers between devices, to_partner(): return lax.ppermute(array, ('dp', 'seq'), pairs)  14.5 us
    ppermute x4, starting transfers between devices, tail_by_permutes(): far = lax.ppermute(near, 'tensor', swap)  5.7 us
    pallas_call x1, Pallas kernels, prompt_value_grad(): pl.pallas_call(functools.partial(attention_kernel, turn=bool(weights)), i...  4.42 us
    ppermute x9, waiting for transfers between devices, to_partner(): return lax.ppermute(array, ('dp', 'seq'), pairs)  4.11 us
    ppermute x4, waiting for transfers between devices, tail_by_permutes(): far = lax.ppermute(near, 'tensor', swap)  3.53 us
    pallas_call x4, Pallas kernels, tail_by_permutes(): pl.pallas_call(functools.partial(update_kernel, slot=slot, dp=dp), in_spe...  2.81 us
    pallas_call x1, Pallas kernels, own_triangle(): pl.pallas_call(triangle_kernel, in_specs=[HBM] * 3 + [VMEM] * 2, out_spec...  2.8 us
    pallas_call x4, Pallas kernels, tail_by_permutes(): pl.pallas_call(partial_kernel, in_specs=[VMEM] * 2, out_specs=[VMEM], out...  2.01 us
  transfers between devices with their start and end apart: 17, of which 10 were waited for; matrix products, arithmetic and copies ran while one was open for 0% of the time, Pallas kernels for 26%

profile of v8, /device:TPU:0, one launch (start us, length us, event | category | flops | bytes accessed | tf_op | source)
XLA Modules:
  0.0 46.4 jit_solution(9548407293260077218)
XLA Ops:
  0.0 1.5 %shard_map.82 = (bf16[512,1536]{1,0:T(8,128)(2,1)S(1)}, bf16[512,256]{1,0:T(8,128)(2,1)S(1)}, bf16[512,128]{1,0:T(8,128)(2,1)S(1)}) custom-call(bf16[512,2048]{1,0:T(8,128)(2,1)} %bitcast.3, bf16[512,1024]{1,0:T(8,128)(2,1)} %bitcast.5), custom_call_target="tpu_custom_call" | custom-call | tf_op jit(solution)/shard_map/pallas_call | solution.py:302
  2.0 2.8 %shard_map.83 = (f32[4,8,1024]{2,1,0:T(8,128)S(1)}, f32[4,64,1024]{2,1,0:T(8,128)S(1)}, bf16[4,512,256]{2,1,0:T(8,128)(2,1)S(1)}, bf16[4,512,128]{2,1,0:T(8,128)(2,1)S(1)}, bf16[512,1024]{1,0:T(8,128)(2,1)S(1)}) custom-call(bf16[512,2048]{1,0:T(8,128)(2,1)} %bitcast.4, bf16[512,1024]{1,0:T(8,128)(2,1)} %bitcast.6, bf16[512,2048]{1,0:T(8,128)(2,1)} %bitcast.7, ...), custom_call_target="tpu_custom_call" | custom-call | flops 536870912 | bytes 3145728 | tf_op jit(solution)/shard_map/pallas_call | solution.py:137
  5.1 4.4 %shard_map.84 = (bf16[4,2,64,1024]{3,2,1,0:T(8,128)(2,1)S(1)}, bf16[512,1024]{1,0:T(8,128)(2,1)S(1)}, bf16[1024,1152]{1,0:T(8,128)(2,1)S(1)}) custom-call(f32[4,8,1024]{2,1,0:T(8,128)S(1)} %get-tuple-element.38.refs_0_, f32[4,64,1024]{2,1,0:T(8,128)S(1)} %get-tuple-element.39.refs_1_, bf16[4,512,256]{2,1,0:T(8,128)(2,1)S(1)} %get-tuple-element.40.refs_2_, ...), custom_call_target="tpu_custom_call" | custom-call | flops 1610612736 | bytes 3145728 | tf_op jit(solution)/shard_map/pallas_call | solution.py:242
  10.4 0.9 %collective-permute-done.2 = bf16[32,512]{1,0:T(8,128)(2,1)S(1)} collective-permute-done((bf16[32,512]{1,0:T(8,128)(2,1)S(1)}, bf16[32,512]{1,0:T(8,128)(2,1)S(1)}, u32[]{:S(2)}, u32[]{:S(2)}) %collective-permute-start.2) | collective-permute-done | bytes 32800 | tf_op jit(solution)/shard_map/ppermute | solution.py:500
  11.3 5.0 %collective-permute-start.3 = (bf16[32,1024]{1,0:T(8,128)(2,1)S(1)}, bf16[32,1024]{1,0:T(8,128)(2,1)S(1)}, u32[]{:S(2)}, u32[]{:S(2)}) collective-permute-start(bf16[32,1024]{1,0:T(8,128)(2,1)S(1)} %pad_maximum_fusion.block), channel_id=1, source_target_pairs={{0,12},{1,13},{4,8},{5,9},{8,4},{9,5},{12,0},{13,1},{2,14},{3,15},... | collective-permute-start | bytes 196616 | tf_op jit(solution)/shard_map/ppermute | solution.py:48
  16.3 0.6 %collective-permute-start.8 = (bf16[32,1024]{1,0:T(8,128)(2,1)S(1)}, bf16[32,1024]{1,0:T(8,128)(2,1)S(1)}, u32[]{:S(2)}, u32[]{:S(2)}) collective-permute-start(bf16[32,1024]{1,0:T(8,128)(2,1)S(1)} %pad_maximum_fusion.block), channel_id=1, source_target_pairs={{0,8},{1,9},{4,12},{5,13},{8,0},{9,1},{12,4},{13,5},{2,10},{3,11},... | collective-permute-start | bytes 196616 | tf_op jit(solution)/shard_map/ppermute | solution.py:48
  17.5 1.7 %collective-permute-start.4 = (bf16[32,1152]{1,0:T(8,128)(2,1)S(1)}, bf16[32,1152]{1,0:T(8,128)(2,1)S(1)}, u32[]{:S(2)}, u32[]{:S(2)}) collective-permute-start(bf16[32,1152]{1,0:T(8,128)(2,1)S(1)} %shard_map.87.near), channel_id=1, source_target_pairs={{0,2},{2,0},{1,3},{3,1},{4,6},{6,4},{5,7},{7,5},{8,10},{10,8},{9,1... | collective-permute-start | bytes 221192 | tf_op jit(solution)/shard_map/ppermute | solution.py:418
  19.7 1.8 %collective-permute-start.5 = (bf16[32,1152]{1,0:T(8,128)(2,1)S(1)}, bf16[32,1152]{1,0:T(8,128)(2,1)S(1)}, u32[]{:S(2)}, u32[]{:S(2)}) collective-permute-start(bf16[32,1152]{1,0:T(8,128)(2,1)S(1)} %shard_map.89.near), channel_id=1, source_target_pairs={{0,2},{2,0},{1,3},{3,1},{4,6},{6,4},{5,7},{7,5},{8,10},{10,8},{9,1... | collective-permute-start | bytes 221192 | tf_op jit(solution)/shard_map/ppermute | solution.py:418
  22.1 1.4 %collective-permute-start.7 = (bf16[32,1152]{1,0:T(8,128)(2,1)S(1)}, bf16[32,1152]{1,0:T(8,128)(2,1)S(1)}, u32[]{:S(2)}, u32[]{:S(2)}) collective-permute-start(bf16[32,1152]{1,0:T(8,128)(2,1)S(1)} %shard_map.91.near), channel_id=1, source_target_pairs={{0,2},{2,0},{1,3},{3,1},{4,6},{6,4},{5,7},{7,5},{8,10},{10,8},{9,1... | collective-permute-start | bytes 221192 | tf_op jit(solution)/shard_map/ppermute | solution.py:418
  24.0 0.8 %collective-permute-start.9 = (bf16[32,1152]{1,0:T(8,128)(2,1)S(1)}, bf16[32,1152]{1,0:T(8,128)(2,1)S(1)}, u32[]{:S(2)}, u32[]{:S(2)}) collective-permute-start(bf16[32,1152]{1,0:T(8,128)(2,1)S(1)} %shard_map.93.near), channel_id=1, source_target_pairs={{0,2},{2,0},{1,3},{3,1},{4,6},{6,4},{5,7},{7,5},{8,10},{10,8},{9,1... | collective-permute-start | bytes 221192 | tf_op jit(solution)/shard_map/ppermute | solution.py:418
  24.9 2.4 %collective-permute-done.7.far = bf16[32,1152]{1,0:T(8,128)(2,1)S(1)} collective-permute-done((bf16[32,1152]{1,0:T(8,128)(2,1)S(1)}, bf16[32,1152]{1,0:T(8,128)(2,1)S(1)}, u32[]{:S(2)}, u32[]{:S(2)}) %collective-permute-start.7) | collective-permute-done | bytes 73760 | tf_op jit(solution)/shard_map/ppermute | solution.py:418
  27.3 1.1 %collective-permute-done.9.far = bf16[32,1152]{1,0:T(8,128)(2,1)S(1)} collective-permute-done((bf16[32,1152]{1,0:T(8,128)(2,1)S(1)}, bf16[32,1152]{1,0:T(8,128)(2,1)S(1)}, u32[]{:S(2)}, u32[]{:S(2)}) %collective-permute-start.9) | collective-permute-done | bytes 73760 | tf_op jit(solution)/shard_map/ppermute | solution.py:418
  28.6 1.2 %collective-permute-done.10 = f32[8,128]{1,0:T(8,128)S(1)} collective-permute-done((f32[8,128]{1,0:T(8,128)S(1)}, f32[8,128]{1,0:T(8,128)S(1)}, u32[]{:S(2)}, u32[]{:S(2)}) %collective-permute-start.10) | collective-permute-done | bytes 4128 | tf_op jit(solution)/shard_map/ppermute | solution.py:428
  29.7 2.8 %collective-permute-start.11 = (f32[8,128]{1,0:T(8,128)S(1)}, f32[8,128]{1,0:T(8,128)S(1)}, u32[]{:S(2)}, u32[]{:S(2)}) collective-permute-start(f32[8,128]{1,0:T(8,128)S(1)} %add.15.left), channel_id=1, source_target_pairs={{0,12},{1,13},{4,8},{5,9},{8,4},{9,5},{12,0},{13,1},{2,14},{3,15},... | collective-permute-start | bytes 12296 | tf_op jit(solution)/shard_map/ppermute | solution.py:48
  32.5 1.6 %collective-permute-start.13 = (f32[8,128]{1,0:T(8,128)S(1)}, f32[8,128]{1,0:T(8,128)S(1)}, u32[]{:S(2)}, u32[]{:S(2)}) collective-permute-start(f32[8,128]{1,0:T(8,128)S(1)} %add.15.left), channel_id=1, source_target_pairs={{0,4},{1,5},{4,0},{5,1},{8,12},{9,13},{12,8},{13,9},{2,6},{3,7},{6... | collective-permute-start | bytes 12296 | tf_op jit(solution)/shard_map/ppermute | solution.py:48
  35.1 1.9 %collective-permute-done.12.right = f32[8,128]{1,0:T(8,128)S(1)} collective-permute-done((f32[8,128]{1,0:T(8,128)S(1)}, f32[8,128]{1,0:T(8,128)S(1)}, u32[]{:S(2)}, u32[]{:S(2)}) %collective-permute-start.12) | collective-permute-done | bytes 4128 | tf_op jit(solution)/shard_map/ppermute | solution.py:48
  37.3 0.8 %collective-permute-start.16 = (bf16[32,1152]{1,0:T(8,128)(2,1)S(1)}, bf16[32,1152]{1,0:T(8,128)(2,1)S(1)}, u32[]{:S(2)}, u32[]{:S(2)}) collective-permute-start(bf16[32,1152]{1,0:T(8,128)(2,1)S(1)} %get-tuple-element.65), channel_id=1, source_target_pairs={{0,4},{1,5},{4,0},{5,1},{8,12},{9,13},{12,8},{13,9},{2,6},{3,7},{6... | collective-permute-start | bytes 221192 | tf_op jit(solution)/shard_map/ppermute | solution.py:48
  38.1 1.4 %collective-permute-start.15 = (bf16[32,1152]{1,0:T(8,128)(2,1)S(1)}, bf16[32,1152]{1,0:T(8,128)(2,1)S(1)}, u32[]{:S(2)}, u32[]{:S(2)}) collective-permute-start(bf16[32,1152]{1,0:T(8,128)(2,1)S(1)} %get-tuple-element.64), channel_id=1, source_target_pairs={{0,8},{1,9},{4,12},{5,13},{8,0},{9,1},{12,4},{13,5},{2,10},{3,11},... | collective-permute-start | bytes 221192 | tf_op jit(solution)/shard_map/ppermute | solution.py:48
  39.5 2.3 %collective-permute-start.14 = (bf16[32,1152]{1,0:T(8,128)(2,1)S(1)}, bf16[32,1152]{1,0:T(8,128)(2,1)S(1)}, u32[]{:S(2)}, u32[]{:S(2)}) collective-permute-start(bf16[32,1152]{1,0:T(8,128)(2,1)S(1)} %get-tuple-element.63), channel_id=1, source_target_pairs={{0,12},{1,13},{4,8},{5,9},{8,4},{9,5},{12,0},{13,1},{2,14},{3,15},... | collective-permute-start | bytes 221192 | tf_op jit(solution)/shard_map/ppermute | solution.py:48
  41.8 0.7 %shard_map.99.refs_0_ = f32[1,32,4608]{2,1,0:T(8,128)} custom-call(f32[1,128]{1,0:T(1,128)S(1)} %get-tuple-element.49.count, bf16[32,1152]{1,0:T(8,128)(2,1)S(1)} %get-tuple-element.66.share, f32[1,32,4608]{2,1,0:T(8,128)S(1)} %copy-done), custom_call_target="tpu_custom_call" | custom-call | tf_op jit(solution)/shard_map/pallas_call | solution.py:446
  42.5 0.7 %shard_map.100.refs_0_ = f32[1,32,4608]{2,1,0:T(8,128)} custom-call(f32[1,128]{1,0:T(1,128)S(1)} %get-tuple-element.49.count, bf16[32,1152]{1,0:T(8,128)(2,1)S(1)} %collective-permute-done.16.share, f32[1,32,4608]{2,1,0:T(8,128)S(1)} %copy-done, f32[1,32,4608]{2,1,0:T(8,128)} %shard_map.99.refs_0_), custom_call_target="tpu_custom_call", output_to_operand_aliasing={{}: (3, {})} | custom-call | tf_op jit(solution)/shard_map/pallas_call | solution.py:446
  43.2 1.5 %collective-permute-done.15.share = bf16[32,1152]{1,0:T(8,128)(2,1)S(1)} collective-permute-done((bf16[32,1152]{1,0:T(8,128)(2,1)S(1)}, bf16[32,1152]{1,0:T(8,128)(2,1)S(1)}, u32[]{:S(2)}, u32[]{:S(2)}) %collective-permute-start.15) | collective-permute-done | bytes 73760 | tf_op jit(solution)/shard_map/ppermute | solution.py:48
  44.7 0.7 %shard_map.101.refs_0_ = f32[1,32,4608]{2,1,0:T(8,128)} custom-call(f32[1,128]{1,0:T(1,128)S(1)} %get-tuple-element.49.count, bf16[32,1152]{1,0:T(8,128)(2,1)S(1)} %collective-permute-done.15.share, f32[1,32,4608]{2,1,0:T(8,128)S(1)} %copy-done, f32[1,32,4608]{2,1,0:T(8,128)} %shard_map.100.refs_0_), custom_call_target="tpu_custom_call", output_to_operand_aliasing={{}: (3, {})} | custom-call | tf_op jit(solution)/shard_map/pallas_call | solution.py:446
  45.7 0.7 %shard_map.102 = f32[1,32,4608]{2,1,0:T(8,128)} custom-call(f32[1,128]{1,0:T(1,128)S(1)} %get-tuple-element.49.count, bf16[32,1152]{1,0:T(8,128)(2,1)S(1)} %collective-permute-done.14.share, f32[1,32,4608]{2,1,0:T(8,128)S(1)} %copy-done, f32[1,32,4608]{2,1,0:T(8,128)} %shard_map.101.refs_0_), custom_call_target="tpu_custom_call", output_to_operand_aliasing={{}: (3, {})} | custom-call | tf_op jit(solution)/shard_map/pallas_call | solution.py:446
  (45 shorter events, 5.5 us)
Async XLA Ops:
  1.5 3.6 %collective-permute-start = (bf16[512,1536]{1,0:T(8,128)(2,1)S(1)}, bf16[512,1536]{1,0:T(8,128)(2,1)S(1)}, u32[]{:S(2)}, u32[]{:S(2)}) collective-permute-start(bf16[512,1536]{1,0:T(8,128)(2,1)S(1)} %get-tuple-element.42), channel_id=1, source_target_pairs={{0,1},{1,0},{2,3},{3,2},{4,5},{5,4},{6,7},{7,6},{8,9},{9,8},{10,11... | collective-permute-start | bytes 4718600 | tf_op jit(solution)/shard_map/ppermute | solution.py:492
  2.0 3.0 %copy-start.1 = (bf16[1152,1024]{1,0:T(8,128)(2,1)S(1)}, bf16[1152,1024]{1,0:T(8,128)(2,1)}, u32[]{:S(2)}) copy-start(bf16[1152,1024]{1,0:T(8,128)(2,1)} %refs_6_.1) | copy-start | bytes 7077892
  4.8 4.7 %collective-permute-start.1 = (bf16[512,1024]{1,0:T(8,128)(2,1)S(1)}, bf16[512,1024]{1,0:T(8,128)(2,1)S(1)}, u32[]{:S(2)}, u32[]{:S(2)}) collective-permute-start(bf16[512,1024]{1,0:T(8,128)(2,1)S(1)} %get-tuple-element.45), channel_id=1, source_target_pairs={{0,1},{1,0},{2,3},{3,2},{4,5},{5,4},{6,7},{7,6},{8,9},{9,8},{10,11... | collective-permute-start | bytes 3145736 | tf_op jit(solution)/shard_map/ppermute | solution.py:496
  10.0 1.3 %collective-permute-start.2 = (bf16[32,512]{1,0:T(8,128)(2,1)S(1)}, bf16[32,512]{1,0:T(8,128)(2,1)S(1)}, u32[]{:S(2)}, u32[]{:S(2)}) collective-permute-start(bf16[32,512]{1,0:T(8,128)(2,1)S(1)} %get-tuple-element.47), channel_id=1, source_target_pairs={{0,1},{1,0},{2,3},{3,2},{4,5},{5,4},{6,7},{7,6},{8,9},{9,8},{10,11... | collective-permute-start | bytes 98312 | tf_op jit(solution)/shard_map/ppermute | solution.py:500
  11.3 7.9 %collective-permute-start.3 = (bf16[32,1024]{1,0:T(8,128)(2,1)S(1)}, bf16[32,1024]{1,0:T(8,128)(2,1)S(1)}, u32[]{:S(2)}, u32[]{:S(2)}) collective-permute-start(bf16[32,1024]{1,0:T(8,128)(2,1)S(1)} %pad_maximum_fusion.block), channel_id=1, source_target_pairs={{0,12},{1,13},{4,8},{5,9},{8,4},{9,5},{12,0},{13,1},{2,14},{3,15},... | collective-permute-start | bytes 196616 | tf_op jit(solution)/shard_map/ppermute | solution.py:48
  16.3 5.3 %collective-permute-start.6 = (bf16[32,1024]{1,0:T(8,128)(2,1)S(1)}, bf16[32,1024]{1,0:T(8,128)(2,1)S(1)}, u32[]{:S(2)}, u32[]{:S(2)}) collective-permute-start(bf16[32,1024]{1,0:T(8,128)(2,1)S(1)} %pad_maximum_fusion.block), channel_id=1, source_target_pairs={{0,4},{1,5},{4,0},{5,1},{8,12},{9,13},{12,8},{13,9},{2,6},{3,7},{6... | collective-permute-start | bytes 196616 | tf_op jit(solution)/shard_map/ppermute | solution.py:48
  16.3 7.2 %collective-permute-start.8 = (bf16[32,1024]{1,0:T(8,128)(2,1)S(1)}, bf16[32,1024]{1,0:T(8,128)(2,1)S(1)}, u32[]{:S(2)}, u32[]{:S(2)}) collective-permute-start(bf16[32,1024]{1,0:T(8,128)(2,1)S(1)} %pad_maximum_fusion.block), channel_id=1, source_target_pairs={{0,8},{1,9},{4,12},{5,13},{8,0},{9,1},{12,4},{13,5},{2,10},{3,11},... | collective-permute-start | bytes 196616 | tf_op jit(solution)/shard_map/ppermute | solution.py:48
  17.5 7.3 %collective-permute-start.4 = (bf16[32,1152]{1,0:T(8,128)(2,1)S(1)}, bf16[32,1152]{1,0:T(8,128)(2,1)S(1)}, u32[]{:S(2)}, u32[]{:S(2)}) collective-permute-start(bf16[32,1152]{1,0:T(8,128)(2,1)S(1)} %shard_map.87.near), channel_id=1, source_target_pairs={{0,2},{2,0},{1,3},{3,1},{4,6},{6,4},{5,7},{7,5},{8,10},{10,8},{9,1... | collective-permute-start | bytes 221192 | tf_op jit(solution)/shard_map/ppermute | solution.py:418
  19.7 5.1 %collective-permute-start.5 = (bf16[32,1152]{1,0:T(8,128)(2,1)S(1)}, bf16[32,1152]{1,0:T(8,128)(2,1)S(1)}, u32[]{:S(2)}, u32[]{:S(2)}) collective-permute-start(bf16[32,1152]{1,0:T(8,128)(2,1)S(1)} %shard_map.89.near), channel_id=1, source_target_pairs={{0,2},{2,0},{1,3},{3,1},{4,6},{6,4},{5,7},{7,5},{8,10},{10,8},{9,1... | collective-permute-start | bytes 221192 | tf_op jit(solution)/shard_map/ppermute | solution.py:418
  22.1 12.1 %copy-start.2 = (s32[4]{0:T(128)S(1)}, s32[4]{0:T(128)}, u32[]{:S(2)}) copy-start(s32[4]{0:T(128)} %tenant_of) | copy-start | bytes 52
  22.1 12.0 %copy-start.3 = (s32[4]{0:T(128)S(1)}, s32[4]{0:T(128)}, u32[]{:S(2)}) copy-start(s32[4]{0:T(128)} %owner_of.1) | copy-start | bytes 52
  22.1 12.0 %copy-start.4 = (s32[4]{0:T(128)S(1)}, s32[4]{0:T(128)}, u32[]{:S(2)}) copy-start(s32[4]{0:T(128)} %counts.1) | copy-start | bytes 52
  22.1 19.6 %copy-start = (f32[1,32,4608]{2,1,0:T(8,128)S(1)}, f32[1,32,4608]{2,1,0:T(8,128)}, u32[]{:S(2)}) copy-start(f32[1,32,4608]{2,1,0:T(8,128)} %noise.7) | copy-start | bytes 1769476
  22.1 5.2 %collective-permute-start.7 = (bf16[32,1152]{1,0:T(8,128)(2,1)S(1)}, bf16[32,1152]{1,0:T(8,128)(2,1)S(1)}, u32[]{:S(2)}, u32[]{:S(2)}) collective-permute-start(bf16[32,1152]{1,0:T(8,128)(2,1)S(1)} %shard_map.91.near), channel_id=1, source_target_pairs={{0,2},{2,0},{1,3},{3,1},{4,6},{6,4},{5,7},{7,5},{8,10},{10,8},{9,1... | collective-permute-start | bytes 221192 | tf_op jit(solution)/shard_map/ppermute | solution.py:418
  24.0 4.4 %collective-permute-start.9 = (bf16[32,1152]{1,0:T(8,128)(2,1)S(1)}, bf16[32,1152]{1,0:T(8,128)(2,1)S(1)}, u32[]{:S(2)}, u32[]{:S(2)}) collective-permute-start(bf16[32,1152]{1,0:T(8,128)(2,1)S(1)} %shard_map.93.near), channel_id=1, source_target_pairs={{0,2},{2,0},{1,3},{3,1},{4,6},{6,4},{5,7},{7,5},{8,10},{10,8},{9,1... | collective-permute-start | bytes 221192 | tf_op jit(solution)/shard_map/ppermute | solution.py:418
  28.5 1.2 %collective-permute-start.10 = (f32[8,128]{1,0:T(8,128)S(1)}, f32[8,128]{1,0:T(8,128)S(1)}, u32[]{:S(2)}, u32[]{:S(2)}) collective-permute-start(f32[8,128]{1,0:T(8,128)S(1)} %add_add_fusion), channel_id=1, source_target_pairs={{0,1},{1,0},{2,3},{3,2},{4,5},{5,4},{6,7},{7,6},{8,9},{9,8},{10,11... | collective-permute-start | bytes 12296 | tf_op jit(solution)/shard_map/ppermute | solution.py:428
  29.7 5.4 %collective-permute-start.11 = (f32[8,128]{1,0:T(8,128)S(1)}, f32[8,128]{1,0:T(8,128)S(1)}, u32[]{:S(2)}, u32[]{:S(2)}) collective-permute-start(f32[8,128]{1,0:T(8,128)S(1)} %add.15.left), channel_id=1, source_target_pairs={{0,12},{1,13},{4,8},{5,9},{8,4},{9,5},{12,0},{13,1},{2,14},{3,15},... | collective-permute-start | bytes 12296 | tf_op jit(solution)/shard_map/ppermute | solution.py:48
  32.5 4.5 %collective-permute-start.12 = (f32[8,128]{1,0:T(8,128)S(1)}, f32[8,128]{1,0:T(8,128)S(1)}, u32[]{:S(2)}, u32[]{:S(2)}) collective-permute-start(f32[8,128]{1,0:T(8,128)S(1)} %add.15.left), channel_id=1, source_target_pairs={{0,8},{1,9},{4,12},{5,13},{8,0},{9,1},{12,4},{13,5},{2,10},{3,11},... | collective-permute-start | bytes 12296 | tf_op jit(solution)/shard_map/ppermute | solution.py:48
  32.5 4.5 %collective-permute-start.13 = (f32[8,128]{1,0:T(8,128)S(1)}, f32[8,128]{1,0:T(8,128)S(1)}, u32[]{:S(2)}, u32[]{:S(2)}) collective-permute-start(f32[8,128]{1,0:T(8,128)S(1)} %add.15.left), channel_id=1, source_target_pairs={{0,4},{1,5},{4,0},{5,1},{8,12},{9,13},{12,8},{13,9},{2,6},{3,7},{6... | collective-permute-start | bytes 12296 | tf_op jit(solution)/shard_map/ppermute | solution.py:48
  37.3 5.2 %collective-permute-start.16 = (bf16[32,1152]{1,0:T(8,128)(2,1)S(1)}, bf16[32,1152]{1,0:T(8,128)(2,1)S(1)}, u32[]{:S(2)}, u32[]{:S(2)}) collective-permute-start(bf16[32,1152]{1,0:T(8,128)(2,1)S(1)} %get-tuple-element.65), channel_id=1, source_target_pairs={{0,4},{1,5},{4,0},{5,1},{8,12},{9,13},{12,8},{13,9},{2,6},{3,7},{6... | collective-permute-start | bytes 221192 | tf_op jit(solution)/shard_map/ppermute | solution.py:48
  38.1 6.6 %collective-permute-start.15 = (bf16[32,1152]{1,0:T(8,128)(2,1)S(1)}, bf16[32,1152]{1,0:T(8,128)(2,1)S(1)}, u32[]{:S(2)}, u32[]{:S(2)}) collective-permute-start(bf16[32,1152]{1,0:T(8,128)(2,1)S(1)} %get-tuple-element.64), channel_id=1, source_target_pairs={{0,8},{1,9},{4,12},{5,13},{8,0},{9,1},{12,4},{13,5},{2,10},{3,11},... | collective-permute-start | bytes 221192 | tf_op jit(solution)/shard_map/ppermute | solution.py:48
  39.5 6.2 %collective-permute-start.14 = (bf16[32,1152]{1,0:T(8,128)(2,1)S(1)}, bf16[32,1152]{1,0:T(8,128)(2,1)S(1)}, u32[]{:S(2)}, u32[]{:S(2)}) collective-permute-start(bf16[32,1152]{1,0:T(8,128)(2,1)S(1)} %get-tuple-element.63), channel_id=1, source_target_pairs={{0,12},{1,13},{4,8},{5,9},{8,4},{9,5},{12,0},{13,1},{2,14},{3,15},... | collective-permute-start | bytes 221192 | tf_op jit(solution)/shard_map/ppermute | solution.py:48

commit v9 on v8

--- a/solution.py
+++ b/solution.py
@@ -347,17 +347,20 @@
     out[...] = left[...] + right[...]
 
 
-def share_kernel(select, norms, *refs, dp):
-    grads, outs, scales = refs[:dp], refs[dp : 2 * dp], refs[-1]
+def share_kernel(select, norms, *refs, slots, dp):
+    grads, outs, scales = refs[:dp], refs[dp:-1], refs[-1]
     norm_sq = jnp.sum(norms[...], axis=1, keepdims=True)
     scales[...] = jnp.broadcast_to(1.0 / jnp.maximum(1.0, jnp.sqrt(norm_sq)), scales.shape)
     scale = [scales[pl.ds(partner("blocks", j, dp), 1), :] for j in range(dp)]
-    for i, out in enumerate(outs):
-        factor = [scale[j] * select[i * dp + j : i * dp + j + 1, :] for j in range(dp)]
-        for at in range(0, out.shape[1], LANES):
+    factors = [
+        [scale[j] * select[i * dp + j : i * dp + j + 1, :] for j in range(dp)] for i in slots
+    ]
+    for at in range(0, outs[0].shape[1], LANES):
+        parts = [grad[:, at : at + LANES] for grad in grads]
+        for out, factor in zip(outs, factors):
             total = None
-            for grad, weight in zip(grads, factor):
-                term = grad[:, at : at + LANES] * weight
+            for part, weight in zip(parts, factor):
+                term = part * weight
                 total = term if total is None else total + term
             out[:, at : at + LANES] = total.astype(jnp.bfloat16)
 
@@ -430,16 +433,20 @@
     for slot in range(1, dp):
         other = to_partner(squares, "norms", slot, dp)
         (total,) = kernel(add_kernel, (total, other), [((8, LANES), jnp.float32)])
-    shares = pl.pallas_call(
-        functools.partial(share_kernel, dp=dp),
-        in_specs=[VMEM] * (2 + dp),
-        out_specs=[VMEM] * dp,
-        out_shape=[jax.ShapeDtypeStruct((rows, columns), jnp.bfloat16)] * dp,
-        scratch_shapes=[pltpu.VMEM((8, LANES), jnp.float32)],
-        compiler_params=small,
-    )(select, total, *grads)
+    shares = {}
+    for slots in (range(1, dp), range(1))[dp == 1 :]:
+        parts = pl.pallas_call(
+            functools.partial(share_kernel, slots=slots, dp=dp),
+            in_specs=[VMEM] * (2 + dp),
+            out_specs=[VMEM] * len(slots),
+            out_shape=[jax.ShapeDtypeStruct((rows, columns), jnp.bfloat16)] * len(slots),
+            scratch_shapes=[pltpu.VMEM((8, LANES), jnp.float32)],
+            compiler_params=small,
+        )(select, total, *grads)
+        shares.update(zip(slots, parts))
     result = []
-    for slot, share in enumerate(shares):
+    for slot in range(dp):
+        share = shares[slot]
         if slot:
             share = to_partner(share, "shares", slot, dp)
         result = [

time: 46.5 us -> 46.4 us (level)
  no operation moved by 1% of the time
where the time goes in v9:
time: 46.4 us; the launch traced here: 46.3 us
  starting transfers between devices  21.3 us (46%)
  Pallas kernels  15.1 us (33%)
  waiting for transfers between devices  9.61 us (21%)
    ppermute x9, starting transfers between devices, to_partner(): return lax.ppermute(array, ('dp', 'seq'), pairs)  14.5 us
    ppermute x4, starting transfers between devices, tail_by_permutes(): far = lax.ppermute(near, 'tensor', swap)  5.7 us
    pallas_call x1, Pallas kernels, prompt_value_grad(): pl.pallas_call(functools.partial(attention_kernel, turn=bool(weights)), i...  4.42 us
    ppermute x9, waiting for transfers between devices, to_partner(): return lax.ppermute(array, ('dp', 'seq'), pairs)  3.95 us
    ppermute x4, waiting for transfers between devices, tail_by_permutes(): far = lax.ppermute(near, 'tensor', swap)  3.53 us
    pallas_call x4, Pallas kernels, tail_by_permutes(): pl.pallas_call(functools.partial(update_kernel, slot=slot, dp=dp), in_spe...  2.81 us
    pallas_call x1, Pallas kernels, own_triangle(): pl.pallas_call(triangle_kernel, in_specs=[HBM] * 3 + [VMEM] * 2, out_spec...  2.8 us
    pallas_call x4, Pallas kernels, tail_by_permutes(): pl.pallas_call(partial_kernel, in_specs=[VMEM] * 2, out_specs=[VMEM], out...  2 us
  transfers between devices with their start and end apart: 17, of which 10 were waited for; matrix products, arithmetic and copies ran while one was open for 0% of the time, Pallas kernels for 26%

profile of v9, /device:TPU:0, one launch (start us, length us, event | category | flops | bytes accessed | tf_op | source)
XLA Modules:
  0.0 46.3 jit_solution(11291263006252734466)
XLA Ops:
  0.0 1.5 %shard_map.82 = (bf16[512,1536]{1,0:T(8,128)(2,1)S(1)}, bf16[512,256]{1,0:T(8,128)(2,1)S(1)}, bf16[512,128]{1,0:T(8,128)(2,1)S(1)}) custom-call(bf16[512,2048]{1,0:T(8,128)(2,1)} %bitcast.3, bf16[512,1024]{1,0:T(8,128)(2,1)} %bitcast.5), custom_call_target="tpu_custom_call" | custom-call | tf_op jit(solution)/shard_map/pallas_call | solution.py:302
  2.0 2.8 %shard_map.83 = (f32[4,8,1024]{2,1,0:T(8,128)S(1)}, f32[4,64,1024]{2,1,0:T(8,128)S(1)}, bf16[4,512,256]{2,1,0:T(8,128)(2,1)S(1)}, bf16[4,512,128]{2,1,0:T(8,128)(2,1)S(1)}, bf16[512,1024]{1,0:T(8,128)(2,1)S(1)}) custom-call(bf16[512,2048]{1,0:T(8,128)(2,1)} %bitcast.4, bf16[512,1024]{1,0:T(8,128)(2,1)} %bitcast.6, bf16[512,2048]{1,0:T(8,128)(2,1)} %bitcast.7, ...), custom_call_target="tpu_custom_call" | custom-call | flops 536870912 | bytes 3145728 | tf_op jit(solution)/shard_map/pallas_call | solution.py:137
  5.1 4.4 %shard_map.84 = (bf16[4,2,64,1024]{3,2,1,0:T(8,128)(2,1)S(1)}, bf16[512,1024]{1,0:T(8,128)(2,1)S(1)}, bf16[1024,1152]{1,0:T(8,128)(2,1)S(1)}) custom-call(f32[4,8,1024]{2,1,0:T(8,128)S(1)} %get-tuple-element.37.refs_0_, f32[4,64,1024]{2,1,0:T(8,128)S(1)} %get-tuple-element.38.refs_1_, bf16[4,512,256]{2,1,0:T(8,128)(2,1)S(1)} %get-tuple-element.39.refs_2_, ...), custom_call_target="tpu_custom_call" | custom-call | flops 1610612736 | bytes 3145728 | tf_op jit(solution)/shard_map/pallas_call | solution.py:242
  10.4 0.9 %collective-permute-done.2 = bf16[32,512]{1,0:T(8,128)(2,1)S(1)} collective-permute-done((bf16[32,512]{1,0:T(8,128)(2,1)S(1)}, bf16[32,512]{1,0:T(8,128)(2,1)S(1)}, u32[]{:S(2)}, u32[]{:S(2)}) %collective-permute-start.2) | collective-permute-done | bytes 32800 | tf_op jit(solution)/shard_map/ppermute | solution.py:507
  11.3 5.0 %collective-permute-start.3 = (bf16[32,1024]{1,0:T(8,128)(2,1)S(1)}, bf16[32,1024]{1,0:T(8,128)(2,1)S(1)}, u32[]{:S(2)}, u32[]{:S(2)}) collective-permute-start(bf16[32,1024]{1,0:T(8,128)(2,1)S(1)} %pad_maximum_fusion.block), channel_id=1, source_target_pairs={{0,12},{1,13},{4,8},{5,9},{8,4},{9,5},{12,0},{13,1},{2,14},{3,15},... | collective-permute-start | bytes 196616 | tf_op jit(solution)/shard_map/ppermute | solution.py:48
  16.3 0.6 %collective-permute-start.8 = (bf16[32,1024]{1,0:T(8,128)(2,1)S(1)}, bf16[32,1024]{1,0:T(8,128)(2,1)S(1)}, u32[]{:S(2)}, u32[]{:S(2)}) collective-permute-start(bf16[32,1024]{1,0:T(8,128)(2,1)S(1)} %pad_maximum_fusion.block), channel_id=1, source_target_pairs={{0,8},{1,9},{4,12},{5,13},{8,0},{9,1},{12,4},{13,5},{2,10},{3,11},... | collective-permute-start | bytes 196616 | tf_op jit(solution)/shard_map/ppermute | solution.py:48
  17.5 1.7 %collective-permute-start.4 = (bf16[32,1152]{1,0:T(8,128)(2,1)S(1)}, bf16[32,1152]{1,0:T(8,128)(2,1)S(1)}, u32[]{:S(2)}, u32[]{:S(2)}) collective-permute-start(bf16[32,1152]{1,0:T(8,128)(2,1)S(1)} %shard_map.87.near), channel_id=1, source_target_pairs={{0,2},{2,0},{1,3},{3,1},{4,6},{6,4},{5,7},{7,5},{8,10},{10,8},{9,1... | collective-permute-start | bytes 221192 | tf_op jit(solution)/shard_map/ppermute | solution.py:421
  19.7 1.8 %collective-permute-start.5 = (bf16[32,1152]{1,0:T(8,128)(2,1)S(1)}, bf16[32,1152]{1,0:T(8,128)(2,1)S(1)}, u32[]{:S(2)}, u32[]{:S(2)}) collective-permute-start(bf16[32,1152]{1,0:T(8,128)(2,1)S(1)} %shard_map.89.near), channel_id=1, source_target_pairs={{0,2},{2,0},{1,3},{3,1},{4,6},{6,4},{5,7},{7,5},{8,10},{10,8},{9,1... | collective-permute-start | bytes 221192 | tf_op jit(solution)/shard_map/ppermute | solution.py:421
  22.1 1.4 %collective-permute-start.7 = (bf16[32,1152]{1,0:T(8,128)(2,1)S(1)}, bf16[32,1152]{1,0:T(8,128)(2,1)S(1)}, u32[]{:S(2)}, u32[]{:S(2)}) collective-permute-start(bf16[32,1152]{1,0:T(8,128)(2,1)S(1)} %shard_map.91.near), channel_id=1, source_target_pairs={{0,2},{2,0},{1,3},{3,1},{4,6},{6,4},{5,7},{7,5},{8,10},{10,8},{9,1... | collective-permute-start | bytes 221192 | tf_op jit(solution)/shard_map/ppermute | solution.py:421
  24.0 0.8 %collective-permute-start.9 = (bf16[32,1152]{1,0:T(8,128)(2,1)S(1)}, bf16[32,1152]{1,0:T(8,128)(2,1)S(1)}, u32[]{:S(2)}, u32[]{:S(2)}) collective-permute-start(bf16[32,1152]{1,0:T(8,128)(2,1)S(1)} %shard_map.93.near), channel_id=1, source_target_pairs={{0,2},{2,0},{1,3},{3,1},{4,6},{6,4},{5,7},{7,5},{8,10},{10,8},{9,1... | collective-permute-start | bytes 221192 | tf_op jit(solution)/shard_map/ppermute | solution.py:421
  24.9 2.4 %collective-permute-done.7.far = bf16[32,1152]{1,0:T(8,128)(2,1)S(1)} collective-permute-done((bf16[32,1152]{1,0:T(8,128)(2,1)S(1)}, bf16[32,1152]{1,0:T(8,128)(2,1)S(1)}, u32[]{:S(2)}, u32[]{:S(2)}) %collective-permute-start.7) | collective-permute-done | bytes 73760 | tf_op jit(solution)/shard_map/ppermute | solution.py:421
  27.3 1.1 %collective-permute-done.9.far = bf16[32,1152]{1,0:T(8,128)(2,1)S(1)} collective-permute-done((bf16[32,1152]{1,0:T(8,128)(2,1)S(1)}, bf16[32,1152]{1,0:T(8,128)(2,1)S(1)}, u32[]{:S(2)}, u32[]{:S(2)}) %collective-permute-start.9) | collective-permute-done | bytes 73760 | tf_op jit(solution)/shard_map/ppermute | solution.py:421
  28.6 1.2 %collective-permute-done.10 = f32[8,128]{1,0:T(8,128)S(1)} collective-permute-done((f32[8,128]{1,0:T(8,128)S(1)}, f32[8,128]{1,0:T(8,128)S(1)}, u32[]{:S(2)}, u32[]{:S(2)}) %collective-permute-start.10) | collective-permute-done | bytes 4128 | tf_op jit(solution)/shard_map/ppermute | solution.py:431
  29.7 2.8 %collective-permute-start.11 = (f32[8,128]{1,0:T(8,128)S(1)}, f32[8,128]{1,0:T(8,128)S(1)}, u32[]{:S(2)}, u32[]{:S(2)}) collective-permute-start(f32[8,128]{1,0:T(8,128)S(1)} %add.15.left), channel_id=1, source_target_pairs={{0,12},{1,13},{4,8},{5,9},{8,4},{9,5},{12,0},{13,1},{2,14},{3,15},... | collective-permute-start | bytes 12296 | tf_op jit(solution)/shard_map/ppermute | solution.py:48
  32.5 1.6 %collective-permute-start.13 = (f32[8,128]{1,0:T(8,128)S(1)}, f32[8,128]{1,0:T(8,128)S(1)}, u32[]{:S(2)}, u32[]{:S(2)}) collective-permute-start(f32[8,128]{1,0:T(8,128)S(1)} %add.15.left), channel_id=1, source_target_pairs={{0,4},{1,5},{4,0},{5,1},{8,12},{9,13},{12,8},{13,9},{2,6},{3,7},{6... | collective-permute-start | bytes 12296 | tf_op jit(solution)/shard_map/ppermute | solution.py:48
  35.1 1.9 %collective-permute-done.12.right = f32[8,128]{1,0:T(8,128)S(1)} collective-permute-done((f32[8,128]{1,0:T(8,128)S(1)}, f32[8,128]{1,0:T(8,128)S(1)}, u32[]{:S(2)}, u32[]{:S(2)}) %collective-permute-start.12) | collective-permute-done | bytes 4128 | tf_op jit(solution)/shard_map/ppermute | solution.py:48
  37.2 0.8 %collective-permute-start.16 = (bf16[32,1152]{1,0:T(8,128)(2,1)S(1)}, bf16[32,1152]{1,0:T(8,128)(2,1)S(1)}, u32[]{:S(2)}, u32[]{:S(2)}) collective-permute-start(bf16[32,1152]{1,0:T(8,128)(2,1)S(1)} %get-tuple-element.64), channel_id=1, source_target_pairs={{0,4},{1,5},{4,0},{5,1},{8,12},{9,13},{12,8},{13,9},{2,6},{3,7},{6... | collective-permute-start | bytes 221192 | tf_op jit(solution)/shard_map/ppermute | solution.py:48
  38.0 1.4 %collective-permute-start.15 = (bf16[32,1152]{1,0:T(8,128)(2,1)S(1)}, bf16[32,1152]{1,0:T(8,128)(2,1)S(1)}, u32[]{:S(2)}, u32[]{:S(2)}) collective-permute-start(bf16[32,1152]{1,0:T(8,128)(2,1)S(1)} %get-tuple-element.63), channel_id=1, source_target_pairs={{0,8},{1,9},{4,12},{5,13},{8,0},{9,1},{12,4},{13,5},{2,10},{3,11},... | collective-permute-start | bytes 221192 | tf_op jit(solution)/shard_map/ppermute | solution.py:48
  39.4 2.3 %collective-permute-start.14 = (bf16[32,1152]{1,0:T(8,128)(2,1)S(1)}, bf16[32,1152]{1,0:T(8,128)(2,1)S(1)}, u32[]{:S(2)}, u32[]{:S(2)}) collective-permute-start(bf16[32,1152]{1,0:T(8,128)(2,1)S(1)} %get-tuple-element.62), channel_id=1, source_target_pairs={{0,12},{1,13},{4,8},{5,9},{8,4},{9,5},{12,0},{13,1},{2,14},{3,15},... | collective-permute-start | bytes 221192 | tf_op jit(solution)/shard_map/ppermute | solution.py:48
  41.8 0.7 %shard_map.100.refs_0_ = f32[1,32,4608]{2,1,0:T(8,128)} custom-call(f32[1,128]{1,0:T(1,128)S(1)} %get-tuple-element.48.count, bf16[32,1152]{1,0:T(8,128)(2,1)S(1)} %shard_map.99.share, f32[1,32,4608]{2,1,0:T(8,128)S(1)} %copy-done), custom_call_target="tpu_custom_call" | custom-call | tf_op jit(solution)/shard_map/pallas_call | solution.py:453
  42.6 0.7 %shard_map.101.refs_0_ = f32[1,32,4608]{2,1,0:T(8,128)} custom-call(f32[1,128]{1,0:T(1,128)S(1)} %get-tuple-element.48.count, bf16[32,1152]{1,0:T(8,128)(2,1)S(1)} %collective-permute-done.16.share, f32[1,32,4608]{2,1,0:T(8,128)S(1)} %copy-done, f32[1,32,4608]{2,1,0:T(8,128)} %shard_map.100.refs_0_), custom_call_target="tpu_custom_call", output_to_operand_aliasing={{}: (3, {})} | custom-call | tf_op jit(solution)/shard_map/pallas_call | solution.py:453
  43.3 1.4 %collective-permute-done.15.share = bf16[32,1152]{1,0:T(8,128)(2,1)S(1)} collective-permute-done((bf16[32,1152]{1,0:T(8,128)(2,1)S(1)}, bf16[32,1152]{1,0:T(8,128)(2,1)S(1)}, u32[]{:S(2)}, u32[]{:S(2)}) %collective-permute-start.15) | collective-permute-done | bytes 73760 | tf_op jit(solution)/shard_map/ppermute | solution.py:48
  44.7 0.7 %shard_map.102.refs_0_ = f32[1,32,4608]{2,1,0:T(8,128)} custom-call(f32[1,128]{1,0:T(1,128)S(1)} %get-tuple-element.48.count, bf16[32,1152]{1,0:T(8,128)(2,1)S(1)} %collective-permute-done.15.share, f32[1,32,4608]{2,1,0:T(8,128)S(1)} %copy-done, f32[1,32,4608]{2,1,0:T(8,128)} %shard_map.101.refs_0_), custom_call_target="tpu_custom_call", output_to_operand_aliasing={{}: (3, {})} | custom-call | tf_op jit(solution)/shard_map/pallas_call | solution.py:453
  45.6 0.7 %shard_map.103 = f32[1,32,4608]{2,1,0:T(8,128)} custom-call(f32[1,128]{1,0:T(1,128)S(1)} %get-tuple-element.48.count, bf16[32,1152]{1,0:T(8,128)(2,1)S(1)} %collective-permute-done.14.share, f32[1,32,4608]{2,1,0:T(8,128)S(1)} %copy-done, f32[1,32,4608]{2,1,0:T(8,128)} %shard_map.102.refs_0_), custom_call_target="tpu_custom_call", output_to_operand_aliasing={{}: (3, {})} | custom-call | tf_op jit(solution)/shard_map/pallas_call | solution.py:453
  (46 shorter events, 5.6 us)
Async XLA Ops:
  1.5 3.6 %collective-permute-start = (bf16[512,1536]{1,0:T(8,128)(2,1)S(1)}, bf16[512,1536]{1,0:T(8,128)(2,1)S(1)}, u32[]{:S(2)}, u32[]{:S(2)}) collective-permute-start(bf16[512,1536]{1,0:T(8,128)(2,1)S(1)} %get-tuple-element.41), channel_id=1, source_target_pairs={{0,1},{1,0},{2,3},{3,2},{4,5},{5,4},{6,7},{7,6},{8,9},{9,8},{10,11... | collective-permute-start | bytes 4718600 | tf_op jit(solution)/shard_map/ppermute | solution.py:499
  2.0 3.0 %copy-start.1 = (bf16[1152,1024]{1,0:T(8,128)(2,1)S(1)}, bf16[1152,1024]{1,0:T(8,128)(2,1)}, u32[]{:S(2)}) copy-start(bf16[1152,1024]{1,0:T(8,128)(2,1)} %refs_6_.1) | copy-start | bytes 7077892
  4.8 4.7 %collective-permute-start.1 = (bf16[512,1024]{1,0:T(8,128)(2,1)S(1)}, bf16[512,1024]{1,0:T(8,128)(2,1)S(1)}, u32[]{:S(2)}, u32[]{:S(2)}) collective-permute-start(bf16[512,1024]{1,0:T(8,128)(2,1)S(1)} %get-tuple-element.44), channel_id=1, source_target_pairs={{0,1},{1,0},{2,3},{3,2},{4,5},{5,4},{6,7},{7,6},{8,9},{9,8},{10,11... | collective-permute-start | bytes 3145736 | tf_op jit(solution)/shard_map/ppermute | solution.py:503
  10.0 1.3 %collective-permute-start.2 = (bf16[32,512]{1,0:T(8,128)(2,1)S(1)}, bf16[32,512]{1,0:T(8,128)(2,1)S(1)}, u32[]{:S(2)}, u32[]{:S(2)}) collective-permute-start(bf16[32,512]{1,0:T(8,128)(2,1)S(1)} %get-tuple-element.46), channel_id=1, source_target_pairs={{0,1},{1,0},{2,3},{3,2},{4,5},{5,4},{6,7},{7,6},{8,9},{9,8},{10,11... | collective-permute-start | bytes 98312 | tf_op jit(solution)/shard_map/ppermute | solution.py:507
  11.3 7.9 %collective-permute-start.3 = (bf16[32,1024]{1,0:T(8,128)(2,1)S(1)}, bf16[32,1024]{1,0:T(8,128)(2,1)S(1)}, u32[]{:S(2)}, u32[]{:S(2)}) collective-permute-start(bf16[32,1024]{1,0:T(8,128)(2,1)S(1)} %pad_maximum_fusion.block), channel_id=1, source_target_pairs={{0,12},{1,13},{4,8},{5,9},{8,4},{9,5},{12,0},{13,1},{2,14},{3,15},... | collective-permute-start | bytes 196616 | tf_op jit(solution)/shard_map/ppermute | solution.py:48
  16.3 5.3 %collective-permute-start.6 = (bf16[32,1024]{1,0:T(8,128)(2,1)S(1)}, bf16[32,1024]{1,0:T(8,128)(2,1)S(1)}, u32[]{:S(2)}, u32[]{:S(2)}) collective-permute-start(bf16[32,1024]{1,0:T(8,128)(2,1)S(1)} %pad_maximum_fusion.block), channel_id=1, source_target_pairs={{0,4},{1,5},{4,0},{5,1},{8,12},{9,13},{12,8},{13,9},{2,6},{3,7},{6... | collective-permute-start | bytes 196616 | tf_op jit(solution)/shard_map/ppermute | solution.py:48
  16.3 7.2 %collective-permute-start.8 = (bf16[32,1024]{1,0:T(8,128)(2,1)S(1)}, bf16[32,1024]{1,0:T(8,128)(2,1)S(1)}, u32[]{:S(2)}, u32[]{:S(2)}) collective-permute-start(bf16[32,1024]{1,0:T(8,128)(2,1)S(1)} %pad_maximum_fusion.block), channel_id=1, source_target_pairs={{0,8},{1,9},{4,12},{5,13},{8,0},{9,1},{12,4},{13,5},{2,10},{3,11},... | collective-permute-start | bytes 196616 | tf_op jit(solution)/shard_map/ppermute | solution.py:48
  17.5 7.3 %collective-permute-start.4 = (bf16[32,1152]{1,0:T(8,128)(2,1)S(1)}, bf16[32,1152]{1,0:T(8,128)(2,1)S(1)}, u32[]{:S(2)}, u32[]{:S(2)}) collective-permute-start(bf16[32,1152]{1,0:T(8,128)(2,1)S(1)} %shard_map.87.near), channel_id=1, source_target_pairs={{0,2},{2,0},{1,3},{3,1},{4,6},{6,4},{5,7},{7,5},{8,10},{10,8},{9,1... | collective-permute-start | bytes 221192 | tf_op jit(solution)/shard_map/ppermute | solution.py:421
  19.7 5.1 %collective-permute-start.5 = (bf16[32,1152]{1,0:T(8,128)(2,1)S(1)}, bf16[32,1152]{1,0:T(8,128)(2,1)S(1)}, u32[]{:S(2)}, u32[]{:S(2)}) collective-permute-start(bf16[32,1152]{1,0:T(8,128)(2,1)S(1)} %shard_map.89.near), channel_id=1, source_target_pairs={{0,2},{2,0},{1,3},{3,1},{4,6},{6,4},{5,7},{7,5},{8,10},{10,8},{9,1... | collective-permute-start | bytes 221192 | tf_op jit(solution)/shard_map/ppermute | solution.py:421
  22.1 12.1 %copy-start.2 = (s32[4]{0:T(128)S(1)}, s32[4]{0:T(128)}, u32[]{:S(2)}) copy-start(s32[4]{0:T(128)} %tenant_of) | copy-start | bytes 52
  22.1 12.0 %copy-start.3 = (s32[4]{0:T(128)S(1)}, s32[4]{0:T(128)}, u32[]{:S(2)}) copy-start(s32[4]{0:T(128)} %owner_of.1) | copy-start | bytes 52
  22.1 12.0 %copy-start.4 = (s32[4]{0:T(128)S(1)}, s32[4]{0:T(128)}, u32[]{:S(2)}) copy-start(s32[4]{0:T(128)} %counts.1) | copy-start | bytes 52
  22.1 19.7 %copy-start = (f32[1,32,4608]{2,1,0:T(8,128)S(1)}, f32[1,32,4608]{2,1,0:T(8,128)}, u32[]{:S(2)}) copy-start(f32[1,32,4608]{2,1,0:T(8,128)} %noise.7) | copy-start | bytes 1769476
  22.1 5.2 %collective-permute-start.7 = (bf16[32,1152]{1,0:T(8,128)(2,1)S(1)}, bf16[32,1152]{1,0:T(8,128)(2,1)S(1)}, u32[]{:S(2)}, u32[]{:S(2)}) collective-permute-start(bf16[32,1152]{1,0:T(8,128)(2,1)S(1)} %shard_map.91.near), channel_id=1, source_target_pairs={{0,2},{2,0},{1,3},{3,1},{4,6},{6,4},{5,7},{7,5},{8,10},{10,8},{9,1... | collective-permute-start | bytes 221192 | tf_op jit(solution)/shard_map/ppermute | solution.py:421
  24.0 4.4 %collective-permute-start.9 = (bf16[32,1152]{1,0:T(8,128)(2,1)S(1)}, bf16[32,1152]{1,0:T(8,128)(2,1)S(1)}, u32[]{:S(2)}, u32[]{:S(2)}) collective-permute-start(bf16[32,1152]{1,0:T(8,128)(2,1)S(1)} %shard_map.93.near), channel_id=1, source_target_pairs={{0,2},{2,0},{1,3},{3,1},{4,6},{6,4},{5,7},{7,5},{8,10},{10,8},{9,1... | collective-permute-start | bytes 221192 | tf_op jit(solution)/shard_map/ppermute | solution.py:421
  28.5 1.2 %collective-permute-start.10 = (f32[8,128]{1,0:T(8,128)S(1)}, f32[8,128]{1,0:T(8,128)S(1)}, u32[]{:S(2)}, u32[]{:S(2)}) collective-permute-start(f32[8,128]{1,0:T(8,128)S(1)} %add_add_fusion), channel_id=1, source_target_pairs={{0,1},{1,0},{2,3},{3,2},{4,5},{5,4},{6,7},{7,6},{8,9},{9,8},{10,11... | collective-permute-start | bytes 12296 | tf_op jit(solution)/shard_map/ppermute | solution.py:431
  29.7 5.4 %collective-permute-start.11 = (f32[8,128]{1,0:T(8,128)S(1)}, f32[8,128]{1,0:T(8,128)S(1)}, u32[]{:S(2)}, u32[]{:S(2)}) collective-permute-start(f32[8,128]{1,0:T(8,128)S(1)} %add.15.left), channel_id=1, source_target_pairs={{0,12},{1,13},{4,8},{5,9},{8,4},{9,5},{12,0},{13,1},{2,14},{3,15},... | collective-permute-start | bytes 12296 | tf_op jit(solution)/shard_map/ppermute | solution.py:48
  32.5 4.5 %collective-permute-start.12 = (f32[8,128]{1,0:T(8,128)S(1)}, f32[8,128]{1,0:T(8,128)S(1)}, u32[]{:S(2)}, u32[]{:S(2)}) collective-permute-start(f32[8,128]{1,0:T(8,128)S(1)} %add.15.left), channel_id=1, source_target_pairs={{0,8},{1,9},{4,12},{5,13},{8,0},{9,1},{12,4},{13,5},{2,10},{3,11},... | collective-permute-start | bytes 12296 | tf_op jit(solution)/shard_map/ppermute | solution.py:48
  32.5 4.5 %collective-permute-start.13 = (f32[8,128]{1,0:T(8,128)S(1)}, f32[8,128]{1,0:T(8,128)S(1)}, u32[]{:S(2)}, u32[]{:S(2)}) collective-permute-start(f32[8,128]{1,0:T(8,128)S(1)} %add.15.left), channel_id=1, source_target_pairs={{0,4},{1,5},{4,0},{5,1},{8,12},{9,13},{12,8},{13,9},{2,6},{3,7},{6... | collective-permute-start | bytes 12296 | tf_op jit(solution)/shard_map/ppermute | solution.py:48
  37.2 5.3 %collective-permute-start.16 = (bf16[32,1152]{1,0:T(8,128)(2,1)S(1)}, bf16[32,1152]{1,0:T(8,128)(2,1)S(1)}, u32[]{:S(2)}, u32[]{:S(2)}) collective-permute-start(bf16[32,1152]{1,0:T(8,128)(2,1)S(1)} %get-tuple-element.64), channel_id=1, source_target_pairs={{0,4},{1,5},{4,0},{5,1},{8,12},{9,13},{12,8},{13,9},{2,6},{3,7},{6... | collective-permute-start | bytes 221192 | tf_op jit(solution)/shard_map/ppermute | solution.py:48
  38.0 6.6 %collective-permute-start.15 = (bf16[32,1152]{1,0:T(8,128)(2,1)S(1)}, bf16[32,1152]{1,0:T(8,128)(2,1)S(1)}, u32[]{:S(2)}, u32[]{:S(2)}) collective-permute-start(bf16[32,1152]{1,0:T(8,128)(2,1)S(1)} %get-tuple-element.63), channel_id=1, source_target_pairs={{0,8},{1,9},{4,12},{5,13},{8,0},{9,1},{12,4},{13,5},{2,10},{3,11},... | collective-permute-start | bytes 221192 | tf_op jit(solution)/shard_map/ppermute | solution.py:48
  39.4 6.2 %collective-permute-start.14 = (bf16[32,1152]{1,0:T(8,128)(2,1)S(1)}, bf16[32,1152]{1,0:T(8,128)(2,1)S(1)}, u32[]{:S(2)}, u32[]{:S(2)}) collective-permute-start(bf16[32,1152]{1,0:T(8,128)(2,1)S(1)} %get-tuple-element.62), channel_id=1, source_target_pairs={{0,12},{1,13},{4,8},{5,9},{8,4},{9,5},{12,0},{13,1},{2,14},{3,15},... | collective-permute-start | bytes 221192 | tf_op jit(solution)/shard_map/ppermute | solution.py:48

commit v10 on v9

--- a/solution.py
+++ b/solution.py
@@ -347,9 +347,9 @@
     out[...] = left[...] + right[...]
 
 
-def share_kernel(select, norms, *refs, slots, dp):
+def share_kernel(select, norms, last, *refs, slots, dp):
     grads, outs, scales = refs[:dp], refs[dp:-1], refs[-1]
-    norm_sq = jnp.sum(norms[...], axis=1, keepdims=True)
+    norm_sq = jnp.sum(norms[...] + last[...], axis=1, keepdims=True)
     scales[...] = jnp.broadcast_to(1.0 / jnp.maximum(1.0, jnp.sqrt(norm_sq)), scales.shape)
     scale = [scales[pl.ds(partner("blocks", j, dp), 1), :] for j in range(dp)]
     factors = [
@@ -430,19 +430,21 @@
         squares = square if squares is None else squares + square
     squares = squares + lax.ppermute(squares, "seq", swap)
     total = squares
+    last = jnp.zeros_like(squares)
     for slot in range(1, dp):
-        other = to_partner(squares, "norms", slot, dp)
-        (total,) = kernel(add_kernel, (total, other), [((8, LANES), jnp.float32)])
+        if slot > 1:
+            (total,) = kernel(add_kernel, (total, last), [((8, LANES), jnp.float32)])
+        last = to_partner(squares, "norms", slot, dp)
     shares = {}
     for slots in (range(1, dp), range(1))[dp == 1 :]:
         parts = pl.pallas_call(
             functools.partial(share_kernel, slots=slots, dp=dp),
-            in_specs=[VMEM] * (2 + dp),
+            in_specs=[VMEM] * (3 + dp),
             out_specs=[VMEM] * len(slots),
             out_shape=[jax.ShapeDtypeStruct((rows, columns), jnp.bfloat16)] * len(slots),
             scratch_shapes=[pltpu.VMEM((8, LANES), jnp.float32)],
             compiler_params=small,
-        )(select, total, *grads)
+        )(select, total, last, *grads)
         shares.update(zip(slots, parts))
     result = []
     for slot in range(dp):

time: 46.4 us -> 46.4 us (level)
  no operation moved by 1% of the time
where the time goes in v10:
time: 46.4 us; the launch traced here: 46.3 us
  starting transfers between devices  21.3 us (46%)
  Pallas kernels  15.1 us (33%)
  waiting for transfers between devices  9.61 us (21%)
    ppermute x9, starting transfers between devices, to_partner(): return lax.ppermute(array, ('dp', 'seq'), pairs)  14.5 us
    ppermute x4, starting transfers between devices, tail_by_permutes(): far = lax.ppermute(near, 'tensor', swap)  5.7 us
    pallas_call x1, Pallas kernels, prompt_value_grad(): pl.pallas_call(functools.partial(attention_kernel, turn=bool(weights)), i...  4.42 us
    ppermute x9, waiting for transfers between devices, to_partner(): return lax.ppermute(array, ('dp', 'seq'), pairs)  3.95 us
    ppermute x4, waiting for transfers between devices, tail_by_permutes(): far = lax.ppermute(near, 'tensor', swap)  3.53 us
    pallas_call x4, Pallas kernels, tail_by_permutes(): pl.pallas_call(functools.partial(update_kernel, slot=slot, dp=dp), in_spe...  2.81 us
    pallas_call x1, Pallas kernels, own_triangle(): pl.pallas_call(triangle_kernel, in_specs=[HBM] * 3 + [VMEM] * 2, out_spec...  2.8 us
    pallas_call x4, Pallas kernels, tail_by_permutes(): pl.pallas_call(partial_kernel, in_specs=[VMEM] * 2, out_specs=[VMEM], out...  2 us
  transfers between devices with their start and end apart: 17, of which 10 were waited for; matrix products, arithmetic and copies ran while one was open for 0% of the time, Pallas kernels for 26%

profile of v10, /device:TPU:0, one launch (start us, length us, event | category | flops | bytes accessed | tf_op | source)
XLA Modules:
  0.0 46.3 jit_solution(4845114706849736057)
XLA Ops:
  0.0 1.5 %shard_map.82 = (bf16[512,1536]{1,0:T(8,128)(2,1)S(1)}, bf16[512,256]{1,0:T(8,128)(2,1)S(1)}, bf16[512,128]{1,0:T(8,128)(2,1)S(1)}) custom-call(bf16[512,2048]{1,0:T(8,128)(2,1)} %bitcast.3, bf16[512,1024]{1,0:T(8,128)(2,1)} %bitcast.5), custom_call_target="tpu_custom_call" | custom-call | tf_op jit(solution)/shard_map/pallas_call | solution.py:302
  2.0 2.8 %shard_map.83 = (f32[4,8,1024]{2,1,0:T(8,128)S(1)}, f32[4,64,1024]{2,1,0:T(8,128)S(1)}, bf16[4,512,256]{2,1,0:T(8,128)(2,1)S(1)}, bf16[4,512,128]{2,1,0:T(8,128)(2,1)S(1)}, bf16[512,1024]{1,0:T(8,128)(2,1)S(1)}) custom-call(bf16[512,2048]{1,0:T(8,128)(2,1)} %bitcast.4, bf16[512,1024]{1,0:T(8,128)(2,1)} %bitcast.6, bf16[512,2048]{1,0:T(8,128)(2,1)} %bitcast.7, ...), custom_call_target="tpu_custom_call" | custom-call | flops 536870912 | bytes 3145728 | tf_op jit(solution)/shard_map/pallas_call | solution.py:137
  5.1 4.4 %shard_map.84 = (bf16[4,2,64,1024]{3,2,1,0:T(8,128)(2,1)S(1)}, bf16[512,1024]{1,0:T(8,128)(2,1)S(1)}, bf16[1024,1152]{1,0:T(8,128)(2,1)S(1)}) custom-call(f32[4,8,1024]{2,1,0:T(8,128)S(1)} %get-tuple-element.37.refs_0_, f32[4,64,1024]{2,1,0:T(8,128)S(1)} %get-tuple-element.38.refs_1_, bf16[4,512,256]{2,1,0:T(8,128)(2,1)S(1)} %get-tuple-element.39.refs_2_, ...), custom_call_target="tpu_custom_call" | custom-call | flops 1610612736 | bytes 3145728 | tf_op jit(solution)/shard_map/pallas_call | solution.py:242
  10.4 0.9 %collective-permute-done.2 = bf16[32,512]{1,0:T(8,128)(2,1)S(1)} collective-permute-done((bf16[32,512]{1,0:T(8,128)(2,1)S(1)}, bf16[32,512]{1,0:T(8,128)(2,1)S(1)}, u32[]{:S(2)}, u32[]{:S(2)}) %collective-permute-start.2) | collective-permute-done | bytes 32800 | tf_op jit(solution)/shard_map/ppermute | solution.py:509
  11.3 5.0 %collective-permute-start.3 = (bf16[32,1024]{1,0:T(8,128)(2,1)S(1)}, bf16[32,1024]{1,0:T(8,128)(2,1)S(1)}, u32[]{:S(2)}, u32[]{:S(2)}) collective-permute-start(bf16[32,1024]{1,0:T(8,128)(2,1)S(1)} %pad_maximum_fusion.block), channel_id=1, source_target_pairs={{0,12},{1,13},{4,8},{5,9},{8,4},{9,5},{12,0},{13,1},{2,14},{3,15},... | collective-permute-start | bytes 196616 | tf_op jit(solution)/shard_map/ppermute | solution.py:48
  16.3 0.6 %collective-permute-start.8 = (bf16[32,1024]{1,0:T(8,128)(2,1)S(1)}, bf16[32,1024]{1,0:T(8,128)(2,1)S(1)}, u32[]{:S(2)}, u32[]{:S(2)}) collective-permute-start(bf16[32,1024]{1,0:T(8,128)(2,1)S(1)} %pad_maximum_fusion.block), channel_id=1, source_target_pairs={{0,8},{1,9},{4,12},{5,13},{8,0},{9,1},{12,4},{13,5},{2,10},{3,11},... | collective-permute-start | bytes 196616 | tf_op jit(solution)/shard_map/ppermute | solution.py:48
  17.5 1.7 %collective-permute-start.4 = (bf16[32,1152]{1,0:T(8,128)(2,1)S(1)}, bf16[32,1152]{1,0:T(8,128)(2,1)S(1)}, u32[]{:S(2)}, u32[]{:S(2)}) collective-permute-start(bf16[32,1152]{1,0:T(8,128)(2,1)S(1)} %shard_map.87.near), channel_id=1, source_target_pairs={{0,2},{2,0},{1,3},{3,1},{4,6},{6,4},{5,7},{7,5},{8,10},{10,8},{9,1... | collective-permute-start | bytes 221192 | tf_op jit(solution)/shard_map/ppermute | solution.py:421
  19.7 1.8 %collective-permute-start.5 = (bf16[32,1152]{1,0:T(8,128)(2,1)S(1)}, bf16[32,1152]{1,0:T(8,128)(2,1)S(1)}, u32[]{:S(2)}, u32[]{:S(2)}) collective-permute-start(bf16[32,1152]{1,0:T(8,128)(2,1)S(1)} %shard_map.89.near), channel_id=1, source_target_pairs={{0,2},{2,0},{1,3},{3,1},{4,6},{6,4},{5,7},{7,5},{8,10},{10,8},{9,1... | collective-permute-start | bytes 221192 | tf_op jit(solution)/shard_map/ppermute | solution.py:421
  22.1 1.4 %collective-permute-start.7 = (bf16[32,1152]{1,0:T(8,128)(2,1)S(1)}, bf16[32,1152]{1,0:T(8,128)(2,1)S(1)}, u32[]{:S(2)}, u32[]{:S(2)}) collective-permute-start(bf16[32,1152]{1,0:T(8,128)(2,1)S(1)} %shard_map.91.near), channel_id=1, source_target_pairs={{0,2},{2,0},{1,3},{3,1},{4,6},{6,4},{5,7},{7,5},{8,10},{10,8},{9,1... | collective-permute-start | bytes 221192 | tf_op jit(solution)/shard_map/ppermute | solution.py:421
  24.0 0.8 %collective-permute-start.9 = (bf16[32,1152]{1,0:T(8,128)(2,1)S(1)}, bf16[32,1152]{1,0:T(8,128)(2,1)S(1)}, u32[]{:S(2)}, u32[]{:S(2)}) collective-permute-start(bf16[32,1152]{1,0:T(8,128)(2,1)S(1)} %shard_map.93.near), channel_id=1, source_target_pairs={{0,2},{2,0},{1,3},{3,1},{4,6},{6,4},{5,7},{7,5},{8,10},{10,8},{9,1... | collective-permute-start | bytes 221192 | tf_op jit(solution)/shard_map/ppermute | solution.py:421
  24.9 2.4 %collective-permute-done.7.far = bf16[32,1152]{1,0:T(8,128)(2,1)S(1)} collective-permute-done((bf16[32,1152]{1,0:T(8,128)(2,1)S(1)}, bf16[32,1152]{1,0:T(8,128)(2,1)S(1)}, u32[]{:S(2)}, u32[]{:S(2)}) %collective-permute-start.7) | collective-permute-done | bytes 73760 | tf_op jit(solution)/shard_map/ppermute | solution.py:421
  27.3 1.1 %collective-permute-done.9.far = bf16[32,1152]{1,0:T(8,128)(2,1)S(1)} collective-permute-done((bf16[32,1152]{1,0:T(8,128)(2,1)S(1)}, bf16[32,1152]{1,0:T(8,128)(2,1)S(1)}, u32[]{:S(2)}, u32[]{:S(2)}) %collective-permute-start.9) | collective-permute-done | bytes 73760 | tf_op jit(solution)/shard_map/ppermute | solution.py:421
  28.6 1.2 %collective-permute-done.10 = f32[8,128]{1,0:T(8,128)S(1)} collective-permute-done((f32[8,128]{1,0:T(8,128)S(1)}, f32[8,128]{1,0:T(8,128)S(1)}, u32[]{:S(2)}, u32[]{:S(2)}) %collective-permute-start.10) | collective-permute-done | bytes 4128 | tf_op jit(solution)/shard_map/ppermute | solution.py:431
  29.7 2.8 %collective-permute-start.11 = (f32[8,128]{1,0:T(8,128)S(1)}, f32[8,128]{1,0:T(8,128)S(1)}, u32[]{:S(2)}, u32[]{:S(2)}) collective-permute-start(f32[8,128]{1,0:T(8,128)S(1)} %add.15.left), channel_id=1, source_target_pairs={{0,12},{1,13},{4,8},{5,9},{8,4},{9,5},{12,0},{13,1},{2,14},{3,15},... | collective-permute-start | bytes 12296 | tf_op jit(solution)/shard_map/ppermute | solution.py:48
  32.5 1.6 %collective-permute-start.13 = (f32[8,128]{1,0:T(8,128)S(1)}, f32[8,128]{1,0:T(8,128)S(1)}, u32[]{:S(2)}, u32[]{:S(2)}) collective-permute-start(f32[8,128]{1,0:T(8,128)S(1)} %add.15.left), channel_id=1, source_target_pairs={{0,4},{1,5},{4,0},{5,1},{8,12},{9,13},{12,8},{13,9},{2,6},{3,7},{6... | collective-permute-start | bytes 12296 | tf_op jit(solution)/shard_map/ppermute | solution.py:48
  35.1 1.9 %collective-permute-done.12.right = f32[8,128]{1,0:T(8,128)S(1)} collective-permute-done((f32[8,128]{1,0:T(8,128)S(1)}, f32[8,128]{1,0:T(8,128)S(1)}, u32[]{:S(2)}, u32[]{:S(2)}) %collective-permute-start.12) | collective-permute-done | bytes 4128 | tf_op jit(solution)/shard_map/ppermute | solution.py:48
  37.2 0.8 %collective-permute-start.16 = (bf16[32,1152]{1,0:T(8,128)(2,1)S(1)}, bf16[32,1152]{1,0:T(8,128)(2,1)S(1)}, u32[]{:S(2)}, u32[]{:S(2)}) collective-permute-start(bf16[32,1152]{1,0:T(8,128)(2,1)S(1)} %get-tuple-element.64), channel_id=1, source_target_pairs={{0,4},{1,5},{4,0},{5,1},{8,12},{9,13},{12,8},{13,9},{2,6},{3,7},{6... | collective-permute-start | bytes 221192 | tf_op jit(solution)/shard_map/ppermute | solution.py:48
  38.0 1.4 %collective-permute-start.15 = (bf16[32,1152]{1,0:T(8,128)(2,1)S(1)}, bf16[32,1152]{1,0:T(8,128)(2,1)S(1)}, u32[]{:S(2)}, u32[]{:S(2)}) collective-permute-start(bf16[32,1152]{1,0:T(8,128)(2,1)S(1)} %get-tuple-element.63), channel_id=1, source_target_pairs={{0,8},{1,9},{4,12},{5,13},{8,0},{9,1},{12,4},{13,5},{2,10},{3,11},... | collective-permute-start | bytes 221192 | tf_op jit(solution)/shard_map/ppermute | solution.py:48
  39.4 2.3 %collective-permute-start.14 = (bf16[32,1152]{1,0:T(8,128)(2,1)S(1)}, bf16[32,1152]{1,0:T(8,128)(2,1)S(1)}, u32[]{:S(2)}, u32[]{:S(2)}) collective-permute-start(bf16[32,1152]{1,0:T(8,128)(2,1)S(1)} %get-tuple-element.62), channel_id=1, source_target_pairs={{0,12},{1,13},{4,8},{5,9},{8,4},{9,5},{12,0},{13,1},{2,14},{3,15},... | collective-permute-start | bytes 221192 | tf_op jit(solution)/shard_map/ppermute | solution.py:48
  41.8 0.7 %shard_map.99.refs_0_ = f32[1,32,4608]{2,1,0:T(8,128)} custom-call(f32[1,128]{1,0:T(1,128)S(1)} %get-tuple-element.48.count, bf16[32,1152]{1,0:T(8,128)(2,1)S(1)} %shard_map.98.share, f32[1,32,4608]{2,1,0:T(8,128)S(1)} %copy-done), custom_call_target="tpu_custom_call" | custom-call | tf_op jit(solution)/shard_map/pallas_call | solution.py:455
  42.6 0.7 %shard_map.100.refs_0_ = f32[1,32,4608]{2,1,0:T(8,128)} custom-call(f32[1,128]{1,0:T(1,128)S(1)} %get-tuple-element.48.count, bf16[32,1152]{1,0:T(8,128)(2,1)S(1)} %collective-permute-done.16.share, f32[1,32,4608]{2,1,0:T(8,128)S(1)} %copy-done, f32[1,32,4608]{2,1,0:T(8,128)} %shard_map.99.refs_0_), custom_call_target="tpu_custom_call", output_to_operand_aliasing={{}: (3, {})} | custom-call | tf_op jit(solution)/shard_map/pallas_call | solution.py:455
  43.3 1.4 %collective-permute-done.15.share = bf16[32,1152]{1,0:T(8,128)(2,1)S(1)} collective-permute-done((bf16[32,1152]{1,0:T(8,128)(2,1)S(1)}, bf16[32,1152]{1,0:T(8,128)(2,1)S(1)}, u32[]{:S(2)}, u32[]{:S(2)}) %collective-permute-start.15) | collective-permute-done | bytes 73760 | tf_op jit(solution)/shard_map/ppermute | solution.py:48
  44.7 0.7 %shard_map.101.refs_0_ = f32[1,32,4608]{2,1,0:T(8,128)} custom-call(f32[1,128]{1,0:T(1,128)S(1)} %get-tuple-element.48.count, bf16[32,1152]{1,0:T(8,128)(2,1)S(1)} %collective-permute-done.15.share, f32[1,32,4608]{2,1,0:T(8,128)S(1)} %copy-done, f32[1,32,4608]{2,1,0:T(8,128)} %shard_map.100.refs_0_), custom_call_target="tpu_custom_call", output_to_operand_aliasing={{}: (3, {})} | custom-call | tf_op jit(solution)/shard_map/pallas_call | solution.py:455
  45.6 0.7 %shard_map.102 = f32[1,32,4608]{2,1,0:T(8,128)} custom-call(f32[1,128]{1,0:T(1,128)S(1)} %get-tuple-element.48.count, bf16[32,1152]{1,0:T(8,128)(2,1)S(1)} %collective-permute-done.14.share, f32[1,32,4608]{2,1,0:T(8,128)S(1)} %copy-done, f32[1,32,4608]{2,1,0:T(8,128)} %shard_map.101.refs_0_), custom_call_target="tpu_custom_call", output_to_operand_aliasing={{}: (3, {})} | custom-call | tf_op jit(solution)/shard_map/pallas_call | solution.py:455
  (45 shorter events, 5.6 us)
Async XLA Ops:
  1.5 3.6 %collective-permute-start = (bf16[512,1536]{1,0:T(8,128)(2,1)S(1)}, bf16[512,1536]{1,0:T(8,128)(2,1)S(1)}, u32[]{:S(2)}, u32[]{:S(2)}) collective-permute-start(bf16[512,1536]{1,0:T(8,128)(2,1)S(1)} %get-tuple-element.41), channel_id=1, source_target_pairs={{0,1},{1,0},{2,3},{3,2},{4,5},{5,4},{6,7},{7,6},{8,9},{9,8},{10,11... | collective-permute-start | bytes 4718600 | tf_op jit(solution)/shard_map/ppermute | solution.py:501
  2.0 3.0 %copy-start.1 = (bf16[1152,1024]{1,0:T(8,128)(2,1)S(1)}, bf16[1152,1024]{1,0:T(8,128)(2,1)}, u32[]{:S(2)}) copy-start(bf16[1152,1024]{1,0:T(8,128)(2,1)} %refs_6_.1) | copy-start | bytes 7077892
  4.8 4.7 %collective-permute-start.1 = (bf16[512,1024]{1,0:T(8,128)(2,1)S(1)}, bf16[512,1024]{1,0:T(8,128)(2,1)S(1)}, u32[]{:S(2)}, u32[]{:S(2)}) collective-permute-start(bf16[512,1024]{1,0:T(8,128)(2,1)S(1)} %get-tuple-element.44), channel_id=1, source_target_pairs={{0,1},{1,0},{2,3},{3,2},{4,5},{5,4},{6,7},{7,6},{8,9},{9,8},{10,11... | collective-permute-start | bytes 3145736 | tf_op jit(solution)/shard_map/ppermute | solution.py:505
  10.0 1.3 %collective-permute-start.2 = (bf16[32,512]{1,0:T(8,128)(2,1)S(1)}, bf16[32,512]{1,0:T(8,128)(2,1)S(1)}, u32[]{:S(2)}, u32[]{:S(2)}) collective-permute-start(bf16[32,512]{1,0:T(8,128)(2,1)S(1)} %get-tuple-element.46), channel_id=1, source_target_pairs={{0,1},{1,0},{2,3},{3,2},{4,5},{5,4},{6,7},{7,6},{8,9},{9,8},{10,11... | collective-permute-start | bytes 98312 | tf_op jit(solution)/shard_map/ppermute | solution.py:509
  11.3 7.9 %collective-permute-start.3 = (bf16[32,1024]{1,0:T(8,128)(2,1)S(1)}, bf16[32,1024]{1,0:T(8,128)(2,1)S(1)}, u32[]{:S(2)}, u32[]{:S(2)}) collective-permute-start(bf16[32,1024]{1,0:T(8,128)(2,1)S(1)} %pad_maximum_fusion.block), channel_id=1, source_target_pairs={{0,12},{1,13},{4,8},{5,9},{8,4},{9,5},{12,0},{13,1},{2,14},{3,15},... | collective-permute-start | bytes 196616 | tf_op jit(solution)/shard_map/ppermute | solution.py:48
  16.3 5.3 %collective-permute-start.6 = (bf16[32,1024]{1,0:T(8,128)(2,1)S(1)}, bf16[32,1024]{1,0:T(8,128)(2,1)S(1)}, u32[]{:S(2)}, u32[]{:S(2)}) collective-permute-start(bf16[32,1024]{1,0:T(8,128)(2,1)S(1)} %pad_maximum_fusion.block), channel_id=1, source_target_pairs={{0,4},{1,5},{4,0},{5,1},{8,12},{9,13},{12,8},{13,9},{2,6},{3,7},{6... | collective-permute-start | bytes 196616 | tf_op jit(solution)/shard_map/ppermute | solution.py:48
  16.3 7.2 %collective-permute-start.8 = (bf16[32,1024]{1,0:T(8,128)(2,1)S(1)}, bf16[32,1024]{1,0:T(8,128)(2,1)S(1)}, u32[]{:S(2)}, u32[]{:S(2)}) collective-permute-start(bf16[32,1024]{1,0:T(8,128)(2,1)S(1)} %pad_maximum_fusion.block), channel_id=1, source_target_pairs={{0,8},{1,9},{4,12},{5,13},{8,0},{9,1},{12,4},{13,5},{2,10},{3,11},... | collective-permute-start | bytes 196616 | tf_op jit(solution)/shard_map/ppermute | solution.py:48
  17.5 7.3 %collective-permute-start.4 = (bf16[32,1152]{1,0:T(8,128)(2,1)S(1)}, bf16[32,1152]{1,0:T(8,128)(2,1)S(1)}, u32[]{:S(2)}, u32[]{:S(2)}) collective-permute-start(bf16[32,1152]{1,0:T(8,128)(2,1)S(1)} %shard_map.87.near), channel_id=1, source_target_pairs={{0,2},{2,0},{1,3},{3,1},{4,6},{6,4},{5,7},{7,5},{8,10},{10,8},{9,1... | collective-permute-start | bytes 221192 | tf_op jit(solution)/shard_map/ppermute | solution.py:421
  19.7 5.1 %collective-permute-start.5 = (bf16[32,1152]{1,0:T(8,128)(2,1)S(1)}, bf16[32,1152]{1,0:T(8,128)(2,1)S(1)}, u32[]{:S(2)}, u32[]{:S(2)}) collective-permute-start(bf16[32,1152]{1,0:T(8,128)(2,1)S(1)} %shard_map.89.near), channel_id=1, source_target_pairs={{0,2},{2,0},{1,3},{3,1},{4,6},{6,4},{5,7},{7,5},{8,10},{10,8},{9,1... | collective-permute-start | bytes 221192 | tf_op jit(solution)/shard_map/ppermute | solution.py:421
  22.1 12.1 %copy-start.2 = (s32[4]{0:T(128)S(1)}, s32[4]{0:T(128)}, u32[]{:S(2)}) copy-start(s32[4]{0:T(128)} %tenant_of) | copy-start | bytes 52
  22.1 12.0 %copy-start.3 = (s32[4]{0:T(128)S(1)}, s32[4]{0:T(128)}, u32[]{:S(2)}) copy-start(s32[4]{0:T(128)} %owner_of.1) | copy-start | bytes 52
  22.1 12.0 %copy-start.4 = (s32[4]{0:T(128)S(1)}, s32[4]{0:T(128)}, u32[]{:S(2)}) copy-start(s32[4]{0:T(128)} %counts.1) | copy-start | bytes 52
  22.1 19.7 %copy-start = (f32[1,32,4608]{2,1,0:T(8,128)S(1)}, f32[1,32,4608]{2,1,0:T(8,128)}, u32[]{:S(2)}) copy-start(f32[1,32,4608]{2,1,0:T(8,128)} %noise.7) | copy-start | bytes 1769476
  22.1 5.2 %collective-permute-start.7 = (bf16[32,1152]{1,0:T(8,128)(2,1)S(1)}, bf16[32,1152]{1,0:T(8,128)(2,1)S(1)}, u32[]{:S(2)}, u32[]{:S(2)}) collective-permute-start(bf16[32,1152]{1,0:T(8,128)(2,1)S(1)} %shard_map.91.near), channel_id=1, source_target_pairs={{0,2},{2,0},{1,3},{3,1},{4,6},{6,4},{5,7},{7,5},{8,10},{10,8},{9,1... | collective-permute-start | bytes 221192 | tf_op jit(solution)/shard_map/ppermute | solution.py:421
  24.0 4.4 %collective-permute-start.9 = (bf16[32,1152]{1,0:T(8,128)(2,1)S(1)}, bf16[32,1152]{1,0:T(8,128)(2,1)S(1)}, u32[]{:S(2)}, u32[]{:S(2)}) collective-permute-start(bf16[32,1152]{1,0:T(8,128)(2,1)S(1)} %shard_map.93.near), channel_id=1, source_target_pairs={{0,2},{2,0},{1,3},{3,1},{4,6},{6,4},{5,7},{7,5},{8,10},{10,8},{9,1... | collective-permute-start | bytes 221192 | tf_op jit(solution)/shard_map/ppermute | solution.py:421
  28.5 1.2 %collective-permute-start.10 = (f32[8,128]{1,0:T(8,128)S(1)}, f32[8,128]{1,0:T(8,128)S(1)}, u32[]{:S(2)}, u32[]{:S(2)}) collective-permute-start(f32[8,128]{1,0:T(8,128)S(1)} %add_add_fusion), channel_id=1, source_target_pairs={{0,1},{1,0},{2,3},{3,2},{4,5},{5,4},{6,7},{7,6},{8,9},{9,8},{10,11... | collective-permute-start | bytes 12296 | tf_op jit(solution)/shard_map/ppermute | solution.py:431
  29.7 5.4 %collective-permute-start.11 = (f32[8,128]{1,0:T(8,128)S(1)}, f32[8,128]{1,0:T(8,128)S(1)}, u32[]{:S(2)}, u32[]{:S(2)}) collective-permute-start(f32[8,128]{1,0:T(8,128)S(1)} %add.15.left), channel_id=1, source_target_pairs={{0,12},{1,13},{4,8},{5,9},{8,4},{9,5},{12,0},{13,1},{2,14},{3,15},... | collective-permute-start | bytes 12296 | tf_op jit(solution)/shard_map/ppermute | solution.py:48
  32.5 4.5 %collective-permute-start.12 = (f32[8,128]{1,0:T(8,128)S(1)}, f32[8,128]{1,0:T(8,128)S(1)}, u32[]{:S(2)}, u32[]{:S(2)}) collective-permute-start(f32[8,128]{1,0:T(8,128)S(1)} %add.15.left), channel_id=1, source_target_pairs={{0,8},{1,9},{4,12},{5,13},{8,0},{9,1},{12,4},{13,5},{2,10},{3,11},... | collective-permute-start | bytes 12296 | tf_op jit(solution)/shard_map/ppermute | solution.py:48
  32.5 4.5 %collective-permute-start.13 = (f32[8,128]{1,0:T(8,128)S(1)}, f32[8,128]{1,0:T(8,128)S(1)}, u32[]{:S(2)}, u32[]{:S(2)}) collective-permute-start(f32[8,128]{1,0:T(8,128)S(1)} %add.15.left), channel_id=1, source_target_pairs={{0,4},{1,5},{4,0},{5,1},{8,12},{9,13},{12,8},{13,9},{2,6},{3,7},{6... | collective-permute-start | bytes 12296 | tf_op jit(solution)/shard_map/ppermute | solution.py:48
  37.2 5.3 %collective-permute-start.16 = (bf16[32,1152]{1,0:T(8,128)(2,1)S(1)}, bf16[32,1152]{1,0:T(8,128)(2,1)S(1)}, u32[]{:S(2)}, u32[]{:S(2)}) collective-permute-start(bf16[32,1152]{1,0:T(8,128)(2,1)S(1)} %get-tuple-element.64), channel_id=1, source_target_pairs={{0,4},{1,5},{4,0},{5,1},{8,12},{9,13},{12,8},{13,9},{2,6},{3,7},{6... | collective-permute-start | bytes 221192 | tf_op jit(solution)/shard_map/ppermute | solution.py:48
  38.0 6.6 %collective-permute-start.15 = (bf16[32,1152]{1,0:T(8,128)(2,1)S(1)}, bf16[32,1152]{1,0:T(8,128)(2,1)S(1)}, u32[]{:S(2)}, u32[]{:S(2)}) collective-permute-start(bf16[32,1152]{1,0:T(8,128)(2,1)S(1)} %get-tuple-element.63), channel_id=1, source_target_pairs={{0,8},{1,9},{4,12},{5,13},{8,0},{9,1},{12,4},{13,5},{2,10},{3,11},... | collective-permute-start | bytes 221192 | tf_op jit(solution)/shard_map/ppermute | solution.py:48
  39.4 6.2 %collective-permute-start.14 = (bf16[32,1152]{1,0:T(8,128)(2,1)S(1)}, bf16[32,1152]{1,0:T(8,128)(2,1)S(1)}, u32[]{:S(2)}, u32[]{:S(2)}) collective-permute-start(bf16[32,1152]{1,0:T(8,128)(2,1)S(1)} %get-tuple-element.62), channel_id=1, source_target_pairs={{0,12},{1,13},{4,8},{5,9},{8,4},{9,5},{12,0},{13,1},{2,14},{3,15},... | collective-permute-start | bytes 221192 | tf_op jit(solution)/shard_map/ppermute | solution.py:48

commit v11 on v9

--- a/solution.py
+++ b/solution.py
@@ -24,7 +24,7 @@
 ORDER = {
     "blocks": ((3, 1, 2), (3, 1, 2)),
     "norms": ((3, 2, 1), (3, 2, 1)),
-    "shares": ((1, 2, 3), (1, 2, 3)),
+    "shares": ((1, 2, 3), (1, 3, 2)),
 }
 
 

time: 46.4 us -> 46.5 us (level)
  no operation moved by 1% of the time
where the time goes in v11:
time: 46.5 us; the launch traced here: 46.4 us
  starting transfers between devices  21.3 us (46%)
  Pallas kernels  15.1 us (32%)
  waiting for transfers between devices  9.66 us (21%)
    ppermute x9, starting transfers between devices, to_partner(): return lax.ppermute(array, ('dp', 'seq'), pairs)  14.5 us
    ppermute x4, starting transfers between devices, tail_by_permutes(): far = lax.ppermute(near, 'tensor', swap)  5.7 us
    pallas_call x1, Pallas kernels, prompt_value_grad(): pl.pallas_call(functools.partial(attention_kernel, turn=bool(weights)), i...  4.42 us
    ppermute x9, waiting for transfers between devices, to_partner(): return lax.ppermute(array, ('dp', 'seq'), pairs)  4 us
    ppermute x4, waiting for transfers between devices, tail_by_permutes(): far = lax.ppermute(near, 'tensor', swap)  3.53 us
    pallas_call x4, Pallas kernels, tail_by_permutes(): pl.pallas_call(functools.partial(update_kernel, slot=slot, dp=dp), in_spe...  2.81 us
    pallas_call x1, Pallas kernels, own_triangle(): pl.pallas_call(triangle_kernel, in_specs=[HBM] * 3 + [VMEM] * 2, out_spec...  2.8 us
    pallas_call x4, Pallas kernels, tail_by_permutes(): pl.pallas_call(partial_kernel, in_specs=[VMEM] * 2, out_specs=[VMEM], out...  2 us
  transfers between devices with their start and end apart: 17, of which 10 were waited for; matrix products, arithmetic and copies ran while one was open for 0% of the time, Pallas kernels for 26%

profile of v11, /device:TPU:0, one launch (start us, length us, event | category | flops | bytes accessed | tf_op | source)
XLA Modules:
  0.0 46.4 jit_solution(7536295814850820900)
XLA Ops:
  0.0 1.5 %shard_map.82 = (bf16[512,1536]{1,0:T(8,128)(2,1)S(1)}, bf16[512,256]{1,0:T(8,128)(2,1)S(1)}, bf16[512,128]{1,0:T(8,128)(2,1)S(1)}) custom-call(bf16[512,2048]{1,0:T(8,128)(2,1)} %bitcast.3, bf16[512,1024]{1,0:T(8,128)(2,1)} %bitcast.5), custom_call_target="tpu_custom_call" | custom-call | tf_op jit(solution)/shard_map/pallas_call | solution.py:302
  2.0 2.8 %shard_map.83 = (f32[4,8,1024]{2,1,0:T(8,128)S(1)}, f32[4,64,1024]{2,1,0:T(8,128)S(1)}, bf16[4,512,256]{2,1,0:T(8,128)(2,1)S(1)}, bf16[4,512,128]{2,1,0:T(8,128)(2,1)S(1)}, bf16[512,1024]{1,0:T(8,128)(2,1)S(1)}) custom-call(bf16[512,2048]{1,0:T(8,128)(2,1)} %bitcast.4, bf16[512,1024]{1,0:T(8,128)(2,1)} %bitcast.6, bf16[512,2048]{1,0:T(8,128)(2,1)} %bitcast.7, ...), custom_call_target="tpu_custom_call" | custom-call | flops 536870912 | bytes 3145728 | tf_op jit(solution)/shard_map/pallas_call | solution.py:137
  5.1 4.4 %shard_map.84 = (bf16[4,2,64,1024]{3,2,1,0:T(8,128)(2,1)S(1)}, bf16[512,1024]{1,0:T(8,128)(2,1)S(1)}, bf16[1024,1152]{1,0:T(8,128)(2,1)S(1)}) custom-call(f32[4,8,1024]{2,1,0:T(8,128)S(1)} %get-tuple-element.37.refs_0_, f32[4,64,1024]{2,1,0:T(8,128)S(1)} %get-tuple-element.38.refs_1_, bf16[4,512,256]{2,1,0:T(8,128)(2,1)S(1)} %get-tuple-element.39.refs_2_, ...), custom_call_target="tpu_custom_call" | custom-call | flops 1610612736 | bytes 3145728 | tf_op jit(solution)/shard_map/pallas_call | solution.py:242
  10.4 0.9 %collective-permute-done.2 = bf16[32,512]{1,0:T(8,128)(2,1)S(1)} collective-permute-done((bf16[32,512]{1,0:T(8,128)(2,1)S(1)}, bf16[32,512]{1,0:T(8,128)(2,1)S(1)}, u32[]{:S(2)}, u32[]{:S(2)}) %collective-permute-start.2) | collective-permute-done | bytes 32800 | tf_op jit(solution)/shard_map/ppermute | solution.py:507
  11.3 5.0 %collective-permute-start.3 = (bf16[32,1024]{1,0:T(8,128)(2,1)S(1)}, bf16[32,1024]{1,0:T(8,128)(2,1)S(1)}, u32[]{:S(2)}, u32[]{:S(2)}) collective-permute-start(bf16[32,1024]{1,0:T(8,128)(2,1)S(1)} %pad_maximum_fusion.block), channel_id=1, source_target_pairs={{0,12},{1,13},{4,8},{5,9},{8,4},{9,5},{12,0},{13,1},{2,14},{3,15},... | collective-permute-start | bytes 196616 | tf_op jit(solution)/shard_map/ppermute | solution.py:48
  16.3 0.6 %collective-permute-start.8 = (bf16[32,1024]{1,0:T(8,128)(2,1)S(1)}, bf16[32,1024]{1,0:T(8,128)(2,1)S(1)}, u32[]{:S(2)}, u32[]{:S(2)}) collective-permute-start(bf16[32,1024]{1,0:T(8,128)(2,1)S(1)} %pad_maximum_fusion.block), channel_id=1, source_target_pairs={{0,8},{1,9},{4,12},{5,13},{8,0},{9,1},{12,4},{13,5},{2,10},{3,11},... | collective-permute-start | bytes 196616 | tf_op jit(solution)/shard_map/ppermute | solution.py:48
  17.5 1.7 %collective-permute-start.4 = (bf16[32,1152]{1,0:T(8,128)(2,1)S(1)}, bf16[32,1152]{1,0:T(8,128)(2,1)S(1)}, u32[]{:S(2)}, u32[]{:S(2)}) collective-permute-start(bf16[32,1152]{1,0:T(8,128)(2,1)S(1)} %shard_map.87.near), channel_id=1, source_target_pairs={{0,2},{2,0},{1,3},{3,1},{4,6},{6,4},{5,7},{7,5},{8,10},{10,8},{9,1... | collective-permute-start | bytes 221192 | tf_op jit(solution)/shard_map/ppermute | solution.py:421
  19.7 1.8 %collective-permute-start.5 = (bf16[32,1152]{1,0:T(8,128)(2,1)S(1)}, bf16[32,1152]{1,0:T(8,128)(2,1)S(1)}, u32[]{:S(2)}, u32[]{:S(2)}) collective-permute-start(bf16[32,1152]{1,0:T(8,128)(2,1)S(1)} %shard_map.89.near), channel_id=1, source_target_pairs={{0,2},{2,0},{1,3},{3,1},{4,6},{6,4},{5,7},{7,5},{8,10},{10,8},{9,1... | collective-permute-start | bytes 221192 | tf_op jit(solution)/shard_map/ppermute | solution.py:421
  22.1 1.4 %collective-permute-start.7 = (bf16[32,1152]{1,0:T(8,128)(2,1)S(1)}, bf16[32,1152]{1,0:T(8,128)(2,1)S(1)}, u32[]{:S(2)}, u32[]{:S(2)}) collective-permute-start(bf16[32,1152]{1,0:T(8,128)(2,1)S(1)} %shard_map.91.near), channel_id=1, source_target_pairs={{0,2},{2,0},{1,3},{3,1},{4,6},{6,4},{5,7},{7,5},{8,10},{10,8},{9,1... | collective-permute-start | bytes 221192 | tf_op jit(solution)/shard_map/ppermute | solution.py:421
  24.0 0.8 %collective-permute-start.9 = (bf16[32,1152]{1,0:T(8,128)(2,1)S(1)}, bf16[32,1152]{1,0:T(8,128)(2,1)S(1)}, u32[]{:S(2)}, u32[]{:S(2)}) collective-permute-start(bf16[32,1152]{1,0:T(8,128)(2,1)S(1)} %shard_map.93.near), channel_id=1, source_target_pairs={{0,2},{2,0},{1,3},{3,1},{4,6},{6,4},{5,7},{7,5},{8,10},{10,8},{9,1... | collective-permute-start | bytes 221192 | tf_op jit(solution)/shard_map/ppermute | solution.py:421
  24.9 2.4 %collective-permute-done.7.far = bf16[32,1152]{1,0:T(8,128)(2,1)S(1)} collective-permute-done((bf16[32,1152]{1,0:T(8,128)(2,1)S(1)}, bf16[32,1152]{1,0:T(8,128)(2,1)S(1)}, u32[]{:S(2)}, u32[]{:S(2)}) %collective-permute-start.7) | collective-permute-done | bytes 73760 | tf_op jit(solution)/shard_map/ppermute | solution.py:421
  27.3 1.1 %collective-permute-done.9.far = bf16[32,1152]{1,0:T(8,128)(2,1)S(1)} collective-permute-done((bf16[32,1152]{1,0:T(8,128)(2,1)S(1)}, bf16[32,1152]{1,0:T(8,128)(2,1)S(1)}, u32[]{:S(2)}, u32[]{:S(2)}) %collective-permute-start.9) | collective-permute-done | bytes 73760 | tf_op jit(solution)/shard_map/ppermute | solution.py:421
  28.6 1.2 %collective-permute-done.10 = f32[8,128]{1,0:T(8,128)S(1)} collective-permute-done((f32[8,128]{1,0:T(8,128)S(1)}, f32[8,128]{1,0:T(8,128)S(1)}, u32[]{:S(2)}, u32[]{:S(2)}) %collective-permute-start.10) | collective-permute-done | bytes 4128 | tf_op jit(solution)/shard_map/ppermute | solution.py:431
  29.7 2.8 %collective-permute-start.11 = (f32[8,128]{1,0:T(8,128)S(1)}, f32[8,128]{1,0:T(8,128)S(1)}, u32[]{:S(2)}, u32[]{:S(2)}) collective-permute-start(f32[8,128]{1,0:T(8,128)S(1)} %add.15.left), channel_id=1, source_target_pairs={{0,12},{1,13},{4,8},{5,9},{8,4},{9,5},{12,0},{13,1},{2,14},{3,15},... | collective-permute-start | bytes 12296 | tf_op jit(solution)/shard_map/ppermute | solution.py:48
  32.5 1.6 %collective-permute-start.13 = (f32[8,128]{1,0:T(8,128)S(1)}, f32[8,128]{1,0:T(8,128)S(1)}, u32[]{:S(2)}, u32[]{:S(2)}) collective-permute-start(f32[8,128]{1,0:T(8,128)S(1)} %add.15.left), channel_id=1, source_target_pairs={{0,4},{1,5},{4,0},{5,1},{8,12},{9,13},{12,8},{13,9},{2,6},{3,7},{6... | collective-permute-start | bytes 12296 | tf_op jit(solution)/shard_map/ppermute | solution.py:48
  35.1 1.9 %collective-permute-done.12.right = f32[8,128]{1,0:T(8,128)S(1)} collective-permute-done((f32[8,128]{1,0:T(8,128)S(1)}, f32[8,128]{1,0:T(8,128)S(1)}, u32[]{:S(2)}, u32[]{:S(2)}) %collective-permute-start.12) | collective-permute-done | bytes 4128 | tf_op jit(solution)/shard_map/ppermute | solution.py:48
  37.2 0.8 %collective-permute-start.16 = (bf16[32,1152]{1,0:T(8,128)(2,1)S(1)}, bf16[32,1152]{1,0:T(8,128)(2,1)S(1)}, u32[]{:S(2)}, u32[]{:S(2)}) collective-permute-start(bf16[32,1152]{1,0:T(8,128)(2,1)S(1)} %get-tuple-element.64), channel_id=1, source_target_pairs={{0,4},{1,5},{4,0},{5,1},{8,12},{9,13},{12,8},{13,9},{2,6},{3,7},{6... | collective-permute-start | bytes 221192 | tf_op jit(solution)/shard_map/ppermute | solution.py:48
  38.0 1.4 %collective-permute-start.15 = (bf16[32,1152]{1,0:T(8,128)(2,1)S(1)}, bf16[32,1152]{1,0:T(8,128)(2,1)S(1)}, u32[]{:S(2)}, u32[]{:S(2)}) collective-permute-start(bf16[32,1152]{1,0:T(8,128)(2,1)S(1)} %get-tuple-element.63), channel_id=1, source_target_pairs={{0,8},{1,13},{4,12},{5,9},{8,0},{9,5},{12,4},{13,1},{2,10},{3,15},... | collective-permute-start | bytes 221192 | tf_op jit(solution)/shard_map/ppermute | solution.py:48
  39.4 2.3 %collective-permute-start.14 = (bf16[32,1152]{1,0:T(8,128)(2,1)S(1)}, bf16[32,1152]{1,0:T(8,128)(2,1)S(1)}, u32[]{:S(2)}, u32[]{:S(2)}) collective-permute-start(bf16[32,1152]{1,0:T(8,128)(2,1)S(1)} %get-tuple-element.62), channel_id=1, source_target_pairs={{0,12},{1,9},{4,8},{5,13},{8,4},{9,1},{12,0},{13,5},{2,14},{3,11},... | collective-permute-start | bytes 221192 | tf_op jit(solution)/shard_map/ppermute | solution.py:48
  41.8 0.7 %shard_map.100.refs_0_ = f32[1,32,4608]{2,1,0:T(8,128)} custom-call(f32[1,128]{1,0:T(1,128)S(1)} %get-tuple-element.48.count, bf16[32,1152]{1,0:T(8,128)(2,1)S(1)} %shard_map.99.share, f32[1,32,4608]{2,1,0:T(8,128)S(1)} %copy-done), custom_call_target="tpu_custom_call" | custom-call | tf_op jit(solution)/shard_map/pallas_call | solution.py:453
  42.6 0.7 %shard_map.101.refs_0_ = f32[1,32,4608]{2,1,0:T(8,128)} custom-call(f32[1,128]{1,0:T(1,128)S(1)} %get-tuple-element.48.count, bf16[32,1152]{1,0:T(8,128)(2,1)S(1)} %collective-permute-done.16.share, f32[1,32,4608]{2,1,0:T(8,128)S(1)} %copy-done, f32[1,32,4608]{2,1,0:T(8,128)} %shard_map.100.refs_0_), custom_call_target="tpu_custom_call", output_to_operand_aliasing={{}: (3, {})} | custom-call | tf_op jit(solution)/shard_map/pallas_call | solution.py:453
  43.3 1.3 %collective-permute-done.15.share = bf16[32,1152]{1,0:T(8,128)(2,1)S(1)} collective-permute-done((bf16[32,1152]{1,0:T(8,128)(2,1)S(1)}, bf16[32,1152]{1,0:T(8,128)(2,1)S(1)}, u32[]{:S(2)}, u32[]{:S(2)}) %collective-permute-start.15) | collective-permute-done | bytes 73760 | tf_op jit(solution)/shard_map/ppermute | solution.py:48
  44.5 0.7 %shard_map.102.refs_0_ = f32[1,32,4608]{2,1,0:T(8,128)} custom-call(f32[1,128]{1,0:T(1,128)S(1)} %get-tuple-element.48.count, bf16[32,1152]{1,0:T(8,128)(2,1)S(1)} %collective-permute-done.15.share, f32[1,32,4608]{2,1,0:T(8,128)S(1)} %copy-done, f32[1,32,4608]{2,1,0:T(8,128)} %shard_map.101.refs_0_), custom_call_target="tpu_custom_call", output_to_operand_aliasing={{}: (3, {})} | custom-call | tf_op jit(solution)/shard_map/pallas_call | solution.py:453
  45.7 0.7 %shard_map.103 = f32[1,32,4608]{2,1,0:T(8,128)} custom-call(f32[1,128]{1,0:T(1,128)S(1)} %get-tuple-element.48.count, bf16[32,1152]{1,0:T(8,128)(2,1)S(1)} %collective-permute-done.14.share, f32[1,32,4608]{2,1,0:T(8,128)S(1)} %copy-done, f32[1,32,4608]{2,1,0:T(8,128)} %shard_map.102.refs_0_), custom_call_target="tpu_custom_call", output_to_operand_aliasing={{}: (3, {})} | custom-call | tf_op jit(solution)/shard_map/pallas_call | solution.py:453
  (46 shorter events, 5.8 us)
Async XLA Ops:
  1.5 3.6 %collective-permute-start = (bf16[512,1536]{1,0:T(8,128)(2,1)S(1)}, bf16[512,1536]{1,0:T(8,128)(2,1)S(1)}, u32[]{:S(2)}, u32[]{:S(2)}) collective-permute-start(bf16[512,1536]{1,0:T(8,128)(2,1)S(1)} %get-tuple-element.41), channel_id=1, source_target_pairs={{0,1},{1,0},{2,3},{3,2},{4,5},{5,4},{6,7},{7,6},{8,9},{9,8},{10,11... | collective-permute-start | bytes 4718600 | tf_op jit(solution)/shard_map/ppermute | solution.py:499
  2.0 3.0 %copy-start.1 = (bf16[1152,1024]{1,0:T(8,128)(2,1)S(1)}, bf16[1152,1024]{1,0:T(8,128)(2,1)}, u32[]{:S(2)}) copy-start(bf16[1152,1024]{1,0:T(8,128)(2,1)} %refs_6_.1) | copy-start | bytes 7077892
  4.8 4.7 %collective-permute-start.1 = (bf16[512,1024]{1,0:T(8,128)(2,1)S(1)}, bf16[512,1024]{1,0:T(8,128)(2,1)S(1)}, u32[]{:S(2)}, u32[]{:S(2)}) collective-permute-start(bf16[512,1024]{1,0:T(8,128)(2,1)S(1)} %get-tuple-element.44), channel_id=1, source_target_pairs={{0,1},{1,0},{2,3},{3,2},{4,5},{5,4},{6,7},{7,6},{8,9},{9,8},{10,11... | collective-permute-start | bytes 3145736 | tf_op jit(solution)/shard_map/ppermute | solution.py:503
  10.0 1.3 %collective-permute-start.2 = (bf16[32,512]{1,0:T(8,128)(2,1)S(1)}, bf16[32,512]{1,0:T(8,128)(2,1)S(1)}, u32[]{:S(2)}, u32[]{:S(2)}) collective-permute-start(bf16[32,512]{1,0:T(8,128)(2,1)S(1)} %get-tuple-element.46), channel_id=1, source_target_pairs={{0,1},{1,0},{2,3},{3,2},{4,5},{5,4},{6,7},{7,6},{8,9},{9,8},{10,11... | collective-permute-start | bytes 98312 | tf_op jit(solution)/shard_map/ppermute | solution.py:507
  11.3 7.9 %collective-permute-start.3 = (bf16[32,1024]{1,0:T(8,128)(2,1)S(1)}, bf16[32,1024]{1,0:T(8,128)(2,1)S(1)}, u32[]{:S(2)}, u32[]{:S(2)}) collective-permute-start(bf16[32,1024]{1,0:T(8,128)(2,1)S(1)} %pad_maximum_fusion.block), channel_id=1, source_target_pairs={{0,12},{1,13},{4,8},{5,9},{8,4},{9,5},{12,0},{13,1},{2,14},{3,15},... | collective-permute-start | bytes 196616 | tf_op jit(solution)/shard_map/ppermute | solution.py:48
  16.3 5.3 %collective-permute-start.6 = (bf16[32,1024]{1,0:T(8,128)(2,1)S(1)}, bf16[32,1024]{1,0:T(8,128)(2,1)S(1)}, u32[]{:S(2)}, u32[]{:S(2)}) collective-permute-start(bf16[32,1024]{1,0:T(8,128)(2,1)S(1)} %pad_maximum_fusion.block), channel_id=1, source_target_pairs={{0,4},{1,5},{4,0},{5,1},{8,12},{9,13},{12,8},{13,9},{2,6},{3,7},{6... | collective-permute-start | bytes 196616 | tf_op jit(solution)/shard_map/ppermute | solution.py:48
  16.3 7.2 %collective-permute-start.8 = (bf16[32,1024]{1,0:T(8,128)(2,1)S(1)}, bf16[32,1024]{1,0:T(8,128)(2,1)S(1)}, u32[]{:S(2)}, u32[]{:S(2)}) collective-permute-start(bf16[32,1024]{1,0:T(8,128)(2,1)S(1)} %pad_maximum_fusion.block), channel_id=1, source_target_pairs={{0,8},{1,9},{4,12},{5,13},{8,0},{9,1},{12,4},{13,5},{2,10},{3,11},... | collective-permute-start | bytes 196616 | tf_op jit(solution)/shard_map/ppermute | solution.py:48
  17.5 7.3 %collective-permute-start.4 = (bf16[32,1152]{1,0:T(8,128)(2,1)S(1)}, bf16[32,1152]{1,0:T(8,128)(2,1)S(1)}, u32[]{:S(2)}, u32[]{:S(2)}) collective-permute-start(bf16[32,1152]{1,0:T(8,128)(2,1)S(1)} %shard_map.87.near), channel_id=1, source_target_pairs={{0,2},{2,0},{1,3},{3,1},{4,6},{6,4},{5,7},{7,5},{8,10},{10,8},{9,1... | collective-permute-start | bytes 221192 | tf_op jit(solution)/shard_map/ppermute | solution.py:421
  19.7 5.1 %collective-permute-start.5 = (bf16[32,1152]{1,0:T(8,128)(2,1)S(1)}, bf16[32,1152]{1,0:T(8,128)(2,1)S(1)}, u32[]{:S(2)}, u32[]{:S(2)}) collective-permute-start(bf16[32,1152]{1,0:T(8,128)(2,1)S(1)} %shard_map.89.near), channel_id=1, source_target_pairs={{0,2},{2,0},{1,3},{3,1},{4,6},{6,4},{5,7},{7,5},{8,10},{10,8},{9,1... | collective-permute-start | bytes 221192 | tf_op jit(solution)/shard_map/ppermute | solution.py:421
  22.1 12.1 %copy-start.2 = (s32[4]{0:T(128)S(1)}, s32[4]{0:T(128)}, u32[]{:S(2)}) copy-start(s32[4]{0:T(128)} %tenant_of) | copy-start | bytes 52
  22.1 12.0 %copy-start.3 = (s32[4]{0:T(128)S(1)}, s32[4]{0:T(128)}, u32[]{:S(2)}) copy-start(s32[4]{0:T(128)} %owner_of.1) | copy-start | bytes 52
  22.1 12.0 %copy-start.4 = (s32[4]{0:T(128)S(1)}, s32[4]{0:T(128)}, u32[]{:S(2)}) copy-start(s32[4]{0:T(128)} %counts.1) | copy-start | bytes 52
  22.1 19.7 %copy-start = (f32[1,32,4608]{2,1,0:T(8,128)S(1)}, f32[1,32,4608]{2,1,0:T(8,128)}, u32[]{:S(2)}) copy-start(f32[1,32,4608]{2,1,0:T(8,128)} %noise.7) | copy-start | bytes 1769476
  22.1 5.2 %collective-permute-start.7 = (bf16[32,1152]{1,0:T(8,128)(2,1)S(1)}, bf16[32,1152]{1,0:T(8,128)(2,1)S(1)}, u32[]{:S(2)}, u32[]{:S(2)}) collective-permute-start(bf16[32,1152]{1,0:T(8,128)(2,1)S(1)} %shard_map.91.near), channel_id=1, source_target_pairs={{0,2},{2,0},{1,3},{3,1},{4,6},{6,4},{5,7},{7,5},{8,10},{10,8},{9,1... | collective-permute-start | bytes 221192 | tf_op jit(solution)/shard_map/ppermute | solution.py:421
  24.0 4.4 %collective-permute-start.9 = (bf16[32,1152]{1,0:T(8,128)(2,1)S(1)}, bf16[32,1152]{1,0:T(8,128)(2,1)S(1)}, u32[]{:S(2)}, u32[]{:S(2)}) collective-permute-start(bf16[32,1152]{1,0:T(8,128)(2,1)S(1)} %shard_map.93.near), channel_id=1, source_target_pairs={{0,2},{2,0},{1,3},{3,1},{4,6},{6,4},{5,7},{7,5},{8,10},{10,8},{9,1... | collective-permute-start | bytes 221192 | tf_op jit(solution)/shard_map/ppermute | solution.py:421
  28.5 1.2 %collective-permute-start.10 = (f32[8,128]{1,0:T(8,128)S(1)}, f32[8,128]{1,0:T(8,128)S(1)}, u32[]{:S(2)}, u32[]{:S(2)}) collective-permute-start(f32[8,128]{1,0:T(8,128)S(1)} %add_add_fusion), channel_id=1, source_target_pairs={{0,1},{1,0},{2,3},{3,2},{4,5},{5,4},{6,7},{7,6},{8,9},{9,8},{10,11... | collective-permute-start | bytes 12296 | tf_op jit(solution)/shard_map/ppermute | solution.py:431
  29.7 5.4 %collective-permute-start.11 = (f32[8,128]{1,0:T(8,128)S(1)}, f32[8,128]{1,0:T(8,128)S(1)}, u32[]{:S(2)}, u32[]{:S(2)}) collective-permute-start(f32[8,128]{1,0:T(8,128)S(1)} %add.15.left), channel_id=1, source_target_pairs={{0,12},{1,13},{4,8},{5,9},{8,4},{9,5},{12,0},{13,1},{2,14},{3,15},... | collective-permute-start | bytes 12296 | tf_op jit(solution)/shard_map/ppermute | solution.py:48
  32.5 4.5 %collective-permute-start.12 = (f32[8,128]{1,0:T(8,128)S(1)}, f32[8,128]{1,0:T(8,128)S(1)}, u32[]{:S(2)}, u32[]{:S(2)}) collective-permute-start(f32[8,128]{1,0:T(8,128)S(1)} %add.15.left), channel_id=1, source_target_pairs={{0,8},{1,9},{4,12},{5,13},{8,0},{9,1},{12,4},{13,5},{2,10},{3,11},... | collective-permute-start | bytes 12296 | tf_op jit(solution)/shard_map/ppermute | solution.py:48
  32.5 4.5 %collective-permute-start.13 = (f32[8,128]{1,0:T(8,128)S(1)}, f32[8,128]{1,0:T(8,128)S(1)}, u32[]{:S(2)}, u32[]{:S(2)}) collective-permute-start(f32[8,128]{1,0:T(8,128)S(1)} %add.15.left), channel_id=1, source_target_pairs={{0,4},{1,5},{4,0},{5,1},{8,12},{9,13},{12,8},{13,9},{2,6},{3,7},{6... | collective-permute-start | bytes 12296 | tf_op jit(solution)/shard_map/ppermute | solution.py:48
  37.2 5.3 %collective-permute-start.16 = (bf16[32,1152]{1,0:T(8,128)(2,1)S(1)}, bf16[32,1152]{1,0:T(8,128)(2,1)S(1)}, u32[]{:S(2)}, u32[]{:S(2)}) collective-permute-start(bf16[32,1152]{1,0:T(8,128)(2,1)S(1)} %get-tuple-element.64), channel_id=1, source_target_pairs={{0,4},{1,5},{4,0},{5,1},{8,12},{9,13},{12,8},{13,9},{2,6},{3,7},{6... | collective-permute-start | bytes 221192 | tf_op jit(solution)/shard_map/ppermute | solution.py:48
  38.0 6.5 %collective-permute-start.15 = (bf16[32,1152]{1,0:T(8,128)(2,1)S(1)}, bf16[32,1152]{1,0:T(8,128)(2,1)S(1)}, u32[]{:S(2)}, u32[]{:S(2)}) collective-permute-start(bf16[32,1152]{1,0:T(8,128)(2,1)S(1)} %get-tuple-element.63), channel_id=1, source_target_pairs={{0,8},{1,13},{4,12},{5,9},{8,0},{9,5},{12,4},{13,1},{2,10},{3,15},... | collective-permute-start | bytes 221192 | tf_op jit(solution)/shard_map/ppermute | solution.py:48
  39.4 6.3 %collective-permute-start.14 = (bf16[32,1152]{1,0:T(8,128)(2,1)S(1)}, bf16[32,1152]{1,0:T(8,128)(2,1)S(1)}, u32[]{:S(2)}, u32[]{:S(2)}) collective-permute-start(bf16[32,1152]{1,0:T(8,128)(2,1)S(1)} %get-tuple-element.62), channel_id=1, source_target_pairs={{0,12},{1,9},{4,8},{5,13},{8,4},{9,1},{12,0},{13,5},{2,14},{3,11},... | collective-permute-start | bytes 221192 | tf_op jit(solution)/shard_map/ppermute | solution.py:48
